TPU v7x, 128 devices: a whole 4x4x4 slice. The times are simulated.
128 devices in a mesh: rad: 32 (over x, z_hi, y), az: 4 (over z_lo, core).
Axes of the slice: x: 4, y: 4, z: 4 (z_hi: 2, z_lo: 2; z = z_hi * 2 + z_lo), core: 2. Of those that a mesh axis runs over, the one named last changes fastest.
Arguments:
- surface_mass: float32 [1024, 16384], P('rad', 'az'), may hold values from 0.5 to 2
- outward_drift: float32 [1024, 16384], P('rad', 'az'), may hold values from -1.2 to 1.2
- leftover_angular_drift: float32 [1024, 16384], P('rad', 'az'), may hold values from -1.2 to 1.2
- angular_offsets: int32 [1024], P('rad'), may hold values from 0 to 16383
- planetesimal_loop_number: int32 [32], replicated, may hold values from 0 to 1023
- planetesimal_angle_bin: int32 [32], replicated, may hold values from 0 to 16383
- planetesimal_weights: float32 [32], replicated, may hold values from 0.001 to 0.01
Outputs:
- transported_density: float32 [1024, 16384], P('rad', 'az')
- kicked_radial_velocity: float32 [1024, 16384], P('rad', 'az')
- kicked_azimuthal_velocity: float32 [1024, 16384], P('rad', 'az')
- embryo_disk_acceleration: float32 [2, 32], replicated
All inputs are finite; a program needn't handle non-finite values.
Results may differ from a plain program's by a relative error of at most 0.0003.
Values sent between devices are 32-bit elements; how exact they have to be, the bound alone decides.
No kernel may reach another device: no remote copies, remote signals or barrier semaphores. Data moves between devices by JAX's collectives and lax.ppermute only.
A program may use at most 64 MiB of HBM per device.

v0:
```python
import functools

import jax
import jax.numpy as jnp
import ml_dtypes
import numpy as np
from jax import lax
from jax.experimental import pallas as pl
from jax.experimental.pallas import tpu as pltpu
from jax.sharding import Mesh
from jax.sharding import PartitionSpec as P

ANGULAR_BINS = 16384
MODES = 256
EMB = 32
RAD = ("rad_0", "rad_1", "rad_2")
AZ = ("az_0", "az_1")
F32 = jnp.float32
BF16 = jnp.bfloat16

gravity = 1.0
timestep_length = 0.05
courant = 0.4
softening = 0.02
cell_step = 2.0 * np.pi / ANGULAR_BINS

ROWS = 32
CHUNKS = 32
GROUPS = 4
SPAN = 8 * CHUNKS
RING = 8 * (5 * CHUNKS + 8)
WIDE = 256
BLOCKS = 16


def split_bf16(table):
    high = table.astype(np.float32).astype(ml_dtypes.bfloat16)
    low = (table - high.astype(np.float64)).astype(np.float32).astype(ml_dtypes.bfloat16)
    return high, low


def constant_tables():
    orders = np.arange(MODES)
    inner = np.arange(WIDE)
    phases = orders[None, :] * (2 * inner[:, None] + 1) % (2 * ANGULAR_BINS) * (np.pi / ANGULAR_BINS)
    basis = np.concatenate([np.cos(phases), np.sin(phases)], axis=1)
    starts = np.arange(ANGULAR_BINS // WIDE) * WIDE
    turns = orders[None, :] * starts[:, None] % ANGULAR_BINS * (2 * np.pi / ANGULAR_BINS)
    twiddle = np.concatenate([np.cos(turns), np.sin(turns)], axis=1).astype(np.float32)
    halves = (2 * np.arange(ANGULAR_BINS) + 1) * (0.5 * np.pi / ANGULAR_BINS)
    wholes = 2 * halves
    angles = np.stack([np.cos(halves), np.sin(halves), np.cos(wholes), np.sin(wholes)])
    angles = angles.reshape(4, 4, CHUNKS, 128).transpose(1, 0, 2, 3).reshape(16, CHUNKS, 128)
    decays = np.tile((orders + 0.5) * cell_step, 2)
    rows = np.arange(ROWS)
    lift = np.exp(-decays[None, :] * (rows[:, None] + 1))
    drop = np.exp(-decays[None, :] * (ROWS - rows[:, None]))
    doubled = np.tile(np.where(orders > 0, 2.0, 1.0), 2)
    radial = -(gravity / cell_step) * doubled * decays * decays
    azim = gravity * np.concatenate([orders * doubled[:MODES], -orders * doubled[:MODES]])
    azim = azim * decays
    vectors = np.zeros((8, 2 * MODES))
    vectors[0] = np.exp(-decays)
    vectors[1] = radial
    vectors[2] = azim
    return (
        split_bf16(basis),
        split_bf16(basis.T),
        twiddle,
        angles.astype(np.float32),
        lift.astype(np.float32),
        drop.astype(np.float32),
        vectors.astype(np.float32),
        decays,
    )


def to_tiles(value):
    return value.reshape(GROUPS, 8, CHUNKS, 128).transpose(0, 2, 1, 3).reshape(GROUPS, SPAN, 128)


def from_tiles(value):
    return value.reshape(GROUPS, CHUNKS, 8, 128).transpose(0, 2, 1, 3).reshape(ROWS, CHUNKS * 128)


def vmem():
    return pl.BlockSpec(memory_space=pltpu.VMEM)


def smem():
    return pl.BlockSpec(memory_space=pltpu.SMEM)


def anywhere():
    return pl.BlockSpec(memory_space=pl.ANY)


def params():
    return pltpu.CompilerParams(vmem_limit_bytes=40 * 1024 * 1024)


def cost(us):
    return pl.CostEstimate(flops=int(us * 1e6), bytes_accessed=int(us * 2.5e6), transcendentals=0)


def donor_flux(speeds, upstream, downstream):
    return jnp.where(speeds > 0, speeds * upstream, speeds * downstream)


def azimuth_kernel(dens_ref, phi_ref, vrad_ref, left_ref, right_ref, offs_ref, out_ref, up_ref, down_ref):
    lane = lax.broadcasted_iota(jnp.int32, (1, 8, 128), 2)

    def following(value):
        turned = pltpu.roll(value, 127, 2)
        return jnp.where(lane == 127, turned[1:], turned[:-1])

    def widened(ref, group, base):
        rows = slice(base + 8 * group, base + 8 * group + 8)
        middle = ref[group].reshape(CHUNKS, 8, 128)
        return jnp.concatenate([left_ref[rows, :][None], middle, right_ref[rows, :][None]], axis=0)

    for group in range(GROUPS):
        dens = widened(dens_ref, group, 0)
        phi = widened(phi_ref, group, ROWS)
        speeds = 0.5 * (phi[:-1] + following(phi))
        flux = donor_flux(speeds, dens[:-1], following(dens))
        turned = pltpu.roll(flux, 1, 2)
        before = jnp.where(lane == 0, turned[:-1], turned[1:])
        stepped = dens[1:-1] - courant * (flux[1:] - before)
        out_ref[group] = stepped.reshape(SPAN, 128)
    up_ref[0:32, :] = out_ref[3, pl.ds(7, CHUNKS, stride=8), :]
    up_ref[32:64, :] = vrad_ref[3, pl.ds(7, CHUNKS, stride=8), :]
    up_ref[64:72, :] = jnp.full((8, 128), offs_ref[31].astype(F32), F32)
    down_ref[0:32, :] = out_ref[0, pl.ds(0, CHUNKS, stride=8), :]
    down_ref[32:64, :] = vrad_ref[0, pl.ds(0, CHUNKS, stride=8), :]
    down_ref[64:72, :] = jnp.full((8, 128), offs_ref[0].astype(F32), F32)


def fill_ring(own_ref, mate_ref, cross_ref, far_ref, ring_ref, sems, unit):
    odd = lax.axis_index(AZ) % 2
    places = ((own_ref, 0), (own_ref, 4), (cross_ref, 2), (mate_ref, 1 + 2 * odd), (far_ref, 3 - 2 * odd))
    copies = []
    for index, (source, place) in enumerate(places):
        where = pl.ds(pl.multiple_of(place * unit, unit), unit)
        copies.append(pltpu.make_async_copy(source, ring_ref.at[:, where, :], sems.at[index]))
    for copy in copies:
        copy.start()
    return copies


def shift_row(ring_ref, group, step, row, offset):
    start = ANGULAR_BINS - offset
    chunk = start // 128
    turn = (128 - start % 128) % 128
    lane = lax.broadcasted_iota(jnp.int32, (CHUNKS, 128), 1)
    first = ring_ref[group, pl.ds(chunk * step + row, CHUNKS, stride=step), :]
    second = ring_ref[group, pl.ds((chunk + 1) * step + row, CHUNKS, stride=step), :]
    return jnp.where(
        lane < 128 - start % 128, pltpu.roll(first, turn, 1), pltpu.roll(second, turn, 1)
    )


def shift_kernel(offs_ref, own_ref, mate_ref, cross_ref, far_ref, out_ref, ring_ref, sems):
    for copy in fill_ring(own_ref, mate_ref, cross_ref, far_ref, ring_ref, sems, SPAN):
        copy.wait()

    @pl.loop(0, GROUPS)
    def _(group):
        for row in range(8):
            moved = shift_row(ring_ref, group, 8, row, offs_ref[group * 8 + row])
            out_ref[group, pl.ds(row, CHUNKS, stride=8), :] = moved


def shifted(offsets, own, mate, cross, far, name):
    return pl.pallas_call(
        shift_kernel,
        out_shape=jax.ShapeDtypeStruct((GROUPS, SPAN, 128), F32),
        in_specs=[smem(), anywhere(), anywhere(), anywhere(), anywhere()],
        out_specs=vmem(),
        scratch_shapes=[pltpu.VMEM((GROUPS, RING, 128), F32), pltpu.SemaphoreType.DMA((5,))],
        compiler_params=params(),
        cost_estimate=cost(2),
        name=name,
    )(offsets, own, mate, cross, far)


def split_value(value):
    high = value.astype(BF16)
    return high, (value - high.astype(F32)).astype(BF16)


def dot(left, right):
    return jnp.dot(left, right, preferred_element_type=F32)


def transport_kernel(
    offs_ref, own_ref, mate_ref, cross_ref, far_ref,
    edge_own_ref, edge_mate_ref, edge_cross_ref, edge_far_ref,
    vrad_ref, high_ref, low_ref, twiddle_ref,
    dens_ref, spectra_ref,
    ring_ref, edge_ref, moved_ref, speed_ref, sems, edge_sems,
):
    copies = fill_ring(own_ref, mate_ref, cross_ref, far_ref, ring_ref, sems, SPAN)
    copies += fill_ring(
        edge_own_ref, edge_mate_ref, edge_cross_ref, edge_far_ref, edge_ref, edge_sems, CHUNKS
    )
    for copy in copies:
        copy.wait()

    @pl.loop(0, GROUPS)
    def _(group):
        for row in range(8):
            moved = shift_row(ring_ref, group, 8, row, offs_ref[group * 8 + row])
            moved_ref[group + 1, pl.ds(row, CHUNKS, stride=8), :] = moved

    for side, (place, row) in enumerate(((0, 7), (5, 0))):
        offset = offs_ref[ROWS + side]
        moved_ref[place, pl.ds(row, CHUNKS, stride=8), :] = shift_row(edge_ref, 2 * side, 1, 0, offset)
        speed_ref[side, pl.ds(row, CHUNKS, stride=8), :] = shift_row(edge_ref, 2 * side + 1, 1, 0, offset)

    sub = lax.broadcasted_iota(jnp.int32, (1, 8, 128), 1)
    own_index = lax.axis_index(RAD)
    bottom = own_index == 0
    top = own_index == lax.axis_size(RAD) - 1

    def above(value, following):
        return jnp.where(sub == 7, pltpu.roll(following, 7, 1), pltpu.roll(value, 7, 1))

    def below(value, previous):
        return jnp.where(sub == 0, pltpu.roll(previous, 1, 1), pltpu.roll(value, 1, 1))

    step = 4
    for group in range(GROUPS):

        @pl.loop(0, CHUNKS // step)
        def _(part):
            where = pl.ds(pl.multiple_of(part * 8 * step, 8 * step), 8 * step)

            def tiles(ref, index):
                return ref[index, where, :].reshape(step, 8, 128)

            dens = tiles(moved_ref, group + 1)
            dens_above = above(dens, tiles(moved_ref, group + 2))
            dens_below = below(dens, tiles(moved_ref, group))
            speed = tiles(vrad_ref, group)
            upper = tiles(vrad_ref, group + 1) if group < 3 else tiles(speed_ref, 1)
            lower = tiles(vrad_ref, group - 1) if group > 0 else tiles(speed_ref, 0)
            flux_above = donor_flux(0.5 * (speed + above(speed, upper)), dens, dens_above)
            flux_below = donor_flux(0.5 * (below(speed, lower) + speed), dens_below, dens)
            if group == 3:
                flux_above = jnp.where((sub == 7) & top, 0.0, flux_above)
            if group == 0:
                flux_below = jnp.where((sub == 0) & bottom, 0.0, flux_below)
            stepped = dens - courant * (flux_above - flux_below)
            dens_ref[group, where, :] = stepped.reshape(8 * step, 128)

    sector = lax.axis_index(AZ)
    cos_sum = jnp.zeros((ROWS, MODES), F32)
    sin_sum = jnp.zeros((ROWS, MODES), F32)
    together = 4
    for first in range(0, BLOCKS, together):
        pieces = []
        for block in range(first, first + together):
            halves = [
                dens_ref[:, 8 * chunk : 8 * chunk + 8, :].reshape(ROWS, 128)
                for chunk in (2 * block, 2 * block + 1)
            ]
            pieces.append(jnp.concatenate(halves, axis=1))
        high, low = split_value(jnp.concatenate(pieces, axis=0))
        part = dot(high, high_ref[...]) + (dot(low, high_ref[...]) + dot(high, low_ref[...]))
        for index in range(together):
            turn = twiddle_ref[pl.ds(sector * BLOCKS + first + index, 1), :]
            cosine, sine = turn[:, :MODES], turn[:, MODES:]
            rows = slice(index * ROWS, index * ROWS + ROWS)
            cos_part, sin_part = part[rows, :MODES], part[rows, MODES:]
            cos_sum += cosine * cos_part - sine * sin_part
            sin_sum += sine * cos_part + cosine * sin_part
    spectra_ref[:, :MODES] = cos_sum * cell_step
    spectra_ref[:, MODES:] = sin_sum * cell_step


def field_kernel(
    members_ref, radius_ref, angles_ref, radial_ref, azim_ref,
    gap_ref, pull_ref, chord_ref, lift_ref, side_ref,
):
    sector = lax.axis_index(AZ)
    half_cos = angles_ref[sector * 4]
    half_sin = angles_ref[sector * 4 + 1]
    radius = radius_ref[...]

    @pl.loop(0, EMB)
    def _(member):
        embryo_radius = members_ref[0, member]
        weight = members_ref[1, member]
        cosine = members_ref[2, member]
        sine = members_ref[3, member]
        gap = radius - embryo_radius
        soft = softening * embryo_radius
        rows = pl.ds(pl.multiple_of(member * 32, 32), 32)
        gap_ref[rows, :] = gap * gap + soft * soft
        pull_ref[rows, :] = weight * gap
        near = half_sin * cosine - half_cos * sine
        far = half_cos * cosine + half_sin * sine
        chord = (2.0 * embryo_radius) * (near * near)
        chord_ref[rows, :] = chord
        lift_ref[rows, :] = weight * chord
        side_ref[rows, :] = (2.0 * weight * embryo_radius) * (near * far)

    twice = [2.0 * radius[8 * g : 8 * g + 8] for g in range(GROUPS)]

    @pl.loop(0, CHUNKS)
    def _(chunk):
        zero = jnp.zeros((8, 128), F32)

        def visit(member, carried):
            radial, azim = list(carried[0]), list(carried[1])
            row = pl.ds(member * 32 + chunk, 1)
            chord = jnp.broadcast_to(chord_ref[row, :], (8, 128))
            lift = jnp.broadcast_to(lift_ref[row, :], (8, 128))
            side = jnp.broadcast_to(side_ref[row, :], (8, 128))
            for g in range(GROUPS):
                rows = pl.ds(pl.multiple_of(member * 32 + 8 * g, 8), 8)
                inverse = lax.rsqrt(gap_ref[rows, :] + twice[g] * chord)
                cubed = inverse * inverse * inverse
                radial[g] = radial[g] + cubed * (pull_ref[rows, :] + lift)
                azim[g] = azim[g] + cubed * side
            return tuple(radial), tuple(azim)

        radial, azim = lax.fori_loop(
            0, EMB, visit, ((zero,) * GROUPS, (zero,) * GROUPS), unroll=4
        )
        where = pl.ds(pl.multiple_of(chunk * 8, 8), 8)
        for g in range(GROUPS):
            radial_ref[g, where, :] = radial[g]
            azim_ref[g, where, :] = azim[g]


def push_kernel(
    members_ref, radius_ref, angles_ref, dens_ref, out_ref,
    mass_ref,
):
    sector = lax.axis_index(AZ)
    radius = radius_ref[...]
    pieces = [radius[8 * g : 8 * g + 8] for g in range(GROUPS)]
    twice = [2.0 * piece for piece in pieces]
    for g in range(GROUPS):
        area = pieces[g] * pieces[g] * (cell_step * cell_step)
        mass_ref[g] = (dens_ref[g].reshape(CHUNKS, 8, 128) * area[None]).reshape(SPAN, 128)
    half_cos = angles_ref[sector * 4]
    half_sin = angles_ref[sector * 4 + 1]

    def chunk_row(index, chunk):
        return jnp.broadcast_to(angles_ref[index, chunk : chunk + 1, :], (8, 128))

    @pl.loop(0, EMB)
    def _(member):
        embryo_radius = members_ref[0, member]
        cosine = members_ref[2, member]
        sine = members_ref[3, member]
        soft = softening * embryo_radius
        gaps = []
        for g in range(GROUPS):
            gap = pieces[g] - embryo_radius
            gaps.append(gap * gap + soft * soft)
        near = half_sin * cosine - half_cos * sine
        chords = (2.0 * embryo_radius) * (near * near)
        push_x = jnp.zeros((8, 128), F32)
        push_y = jnp.zeros((8, 128), F32)
        total = jnp.zeros((8, 128), F32)
        for chunk in range(CHUNKS):
            chord = jnp.broadcast_to(chords[chunk : chunk + 1, :], (8, 128))
            plain = jnp.zeros((8, 128), F32)
            moved = jnp.zeros((8, 128), F32)
            for g in range(GROUPS):
                inverse = lax.rsqrt(gaps[g] + twice[g] * chord)
                cubed = inverse * inverse * inverse
                term = cubed * mass_ref[g, 8 * chunk : 8 * chunk + 8, :]
                plain = plain + term
                moved = moved + pieces[g] * term
            push_x = push_x + moved * chunk_row(sector * 4 + 2, chunk)
            push_y = push_y + moved * chunk_row(sector * 4 + 3, chunk)
            total = total + plain
        place_x = embryo_radius * members_ref[4, member]
        place_y = embryo_radius * members_ref[5, member]
        out_ref[pl.ds(member, 1), :] = jnp.sum(push_x - place_x * total, axis=0, keepdims=True)
        out_ref[pl.ds(EMB + member, 1), :] = jnp.sum(push_y - place_y * total, axis=0, keepdims=True)


def moment_kernel(a_ref, b_ref, c_ref, d_ref, push_ref, lift_ref, drop_ref, vectors_ref, spectra_ref, packed_ref):
    spectra = (a_ref[...] + b_ref[...]) + (c_ref[...] + d_ref[...])
    spectra_ref[...] = spectra
    factor = vectors_ref[0:1, :]
    up = jnp.sum(spectra * drop_ref[...], axis=0, keepdims=True) / factor
    down = jnp.sum(spectra * lift_ref[...], axis=0, keepdims=True) / factor
    for part in range(4):
        packed_ref[part : part + 1, :] = up[:, 128 * part : 128 * part + 128]
        packed_ref[4 + part : 5 + part, :] = down[:, 128 * part : 128 * part + 128]
    packed_ref[8:72, :] = push_ref[...]


def kick_kernel(
    spectra_ref, terms_ref_0, terms_ref_1, terms_ref_2, terms_ref_3, terms_ref_4, terms_ref_5, terms_ref_6,
    weights_ref, radius_ref, vectors_ref, lift_ref, drop_ref, twiddle_ref, high_ref, low_ref,
    radial_ref, azim_ref, vrad_ref, vphi_ref,
    out_radial_ref, out_azim_ref,
    lower_ref, upper_ref,
):
    terms = (
        terms_ref_0, terms_ref_1, terms_ref_2, terms_ref_3, terms_ref_4, terms_ref_5, terms_ref_6,
    )
    outside = jnp.zeros((8, 128), F32)
    for index, term in enumerate(terms):
        outside += weights_ref[index] * term[0:8, :]
    lower = jnp.concatenate([outside[k : k + 1] for k in range(4)], axis=1)
    upper = jnp.concatenate([outside[k : k + 1] for k in range(4, 8)], axis=1)
    factor = vectors_ref[0:1, :]
    spectra = spectra_ref[...]
    for row in range(ROWS):
        lower = spectra[row : row + 1] + factor * lower
        lower_ref[row : row + 1, :] = lower
        back = ROWS - 1 - row
        upper = spectra[back : back + 1] + factor * upper
        upper_ref[back : back + 1, :] = upper
    lower = lower_ref[...]
    upper = upper_ref[...]
    inverse = 1.0 / radius_ref[:, 0:1]
    even = lower + upper - spectra
    odd = lower - upper
    radial = odd * vectors_ref[1:2, :] * inverse
    swapped = jnp.concatenate([even[:, MODES:], even[:, :MODES]], axis=1)
    azim = swapped * vectors_ref[2:3, :] * inverse
    sector = lax.axis_index(AZ)
    for block in range(BLOCKS):
        turn = twiddle_ref[pl.ds(sector * BLOCKS + block, 1), :]
        cosine, sine = turn[:, :MODES], turn[:, MODES:]
        pieces = []
        for coef in (radial, azim):
            cos_coef, sin_coef = coef[:, :MODES], coef[:, MODES:]
            pieces.append(
                jnp.concatenate(
                    [cos_coef * cosine + sin_coef * sine, sin_coef * cosine - cos_coef * sine], axis=1
                )
            )
        high, low = split_value(jnp.concatenate(pieces, axis=0))
        part = dot(high, high_ref[...]) + (dot(low, high_ref[...]) + dot(high, low_ref[...]))
        for half in range(2):
            where = slice(8 * (2 * block + half), 8 * (2 * block + half) + 8)
            columns = slice(128 * half, 128 * half + 128)
            disk = part[:ROWS, columns].reshape(GROUPS, 8, 128)
            out_radial_ref[:, where, :] = vrad_ref[:, where, :] + timestep_length * (
                disk - radial_ref[:, where, :]
            )
            disk = part[ROWS:, columns].reshape(GROUPS, 8, 128)
            out_azim_ref[:, where, :] = vphi_ref[:, where, :] + timestep_length * (
                disk - azim_ref[:, where, :]
            )


def across(value, axis, target):
    count = lax.axis_size(axis)
    return lax.ppermute(value, axis, [(source, target(source)) for source in range(count)])


def after(value, *others):
    return lax.optimization_barrier((value, *others))[0]


def stage_weights(decays):
    x, z, y = (lax.axis_index(name) for name in RAD)
    rate = jnp.asarray((decays * ROWS).astype(np.float32)).reshape(4, 128)
    ones = jnp.ones((64, 128), F32)

    def decayed(count):
        return jnp.where(count >= 0, jnp.exp(-rate * jnp.maximum(count, 0).astype(F32)), 0.0)

    joins, sides = [], []
    for shift in range(4):
        source = (y - shift) % 4
        joins.append(jnp.concatenate([decayed(3 - source), decayed(source), ones]))
        if shift:
            sides.append(jnp.concatenate([decayed(y - 1 - source), decayed(source - y - 1)]))
    pair = []
    for source in (z, 1 - z):
        pair.append(jnp.concatenate([decayed(4 * (1 - source)), decayed(4 * source), ones]))
    never = jnp.int32(-1)
    sides.append(
        jnp.concatenate(
            [decayed(jnp.where(z == 1, y, never)), decayed(jnp.where(z == 0, 3 - y, never))]
        )
    )
    for shift in range(1, 4):
        source = (x - shift) % 4
        gap = x - source
        within = 4 * z + y
        sides.append(
            jnp.concatenate(
                [
                    decayed(jnp.where(gap > 0, 8 * (gap - 1) + within, never)),
                    decayed(jnp.where(gap < 0, 8 * (-gap - 1) + 7 - within, never)),
                ]
            )
        )
    return jnp.stack(joins), jnp.stack(pair), jnp.stack(sides)


def on_device(
    surface_mass,
    outward_drift,
    leftover_angular_drift,
    angular_offsets,
    planetesimal_loop_number,
    planetesimal_angle_bin,
    planetesimal_weights,
):
    (basis_high, basis_low), (back_high, back_low), twiddle, angles, lift, drop, vectors, decays = (
        constant_tables()
    )
    tiles = jax.ShapeDtypeStruct((GROUPS, SPAN, 128), F32)
    dens = to_tiles(surface_mass)
    vrad = to_tiles(outward_drift)
    vphi = to_tiles(leftover_angular_drift)

    ends = jnp.concatenate([surface_mass[:, -128:], leftover_angular_drift[:, -128:]])
    begins = jnp.concatenate([surface_mass[:, :128], leftover_angular_drift[:, :128]])
    left = across(ends, AZ, lambda i: (i + 1) % 4)
    right = across(begins, AZ, lambda i: (i - 1) % 4)
    vrad_cross = across(vrad, AZ, lambda i: i ^ 2)
    vrad_mate = across(vrad, AZ, lambda i: i ^ 1)

    cell = np.float32(cell_step)
    cycles = lax.axis_index(RAD) * ROWS + jnp.arange(ROWS, dtype=jnp.int32)
    radius = jnp.broadcast_to(jnp.exp((cycles.astype(F32) + 0.5) * cell)[:, None], (ROWS, 128))
    embryo_angles = (2 * planetesimal_angle_bin + 1).astype(F32) * np.float32(np.pi / ANGULAR_BINS)
    members = jnp.stack(
        [
            jnp.exp((planetesimal_loop_number.astype(F32) + 0.5) * cell),
            planetesimal_weights,
            jnp.cos(0.5 * embryo_angles),
            jnp.sin(0.5 * embryo_angles),
            jnp.cos(embryo_angles),
            jnp.sin(embryo_angles),
        ]
    )
    joins, pair, sides = stage_weights(decays)

    dens_two, edge_up, edge_down = pl.pallas_call(
        azimuth_kernel,
        out_shape=(tiles, jax.ShapeDtypeStruct((72, 128), F32), jax.ShapeDtypeStruct((72, 128), F32)),
        in_specs=[vmem()] * 5 + [smem()],
        out_specs=(vmem(), vmem(), vmem()),
        compiler_params=params(),
        cost_estimate=cost(1),
        name="azimuth",
    )(dens, vphi, vrad, left, right, angular_offsets)

    rad_count = lax.axis_size(RAD)
    edge_low = lax.ppermute(edge_up, RAD, [(i, i + 1) for i in range(rad_count - 1)])
    edge_high = lax.ppermute(edge_down, RAD, [(i + 1, i) for i in range(rad_count - 1)])
    edges = jnp.concatenate([edge_low[:64], edge_high[:64]]).reshape(4, CHUNKS, 128)
    offsets = jnp.concatenate(
        [angular_offsets, edge_low[64:65, 0].astype(jnp.int32), edge_high[64:65, 0].astype(jnp.int32)]
    )
    edges_cross, edges_mate, edges_far = (
        across(edges, AZ, lambda i, k=k: i ^ k) for k in (2, 1, 3)
    )

    dens_mate = across(dens_two, AZ, lambda i: i ^ 1)
    dens_two_later = after(dens_two, vrad_cross)
    dens_cross = across(dens_two_later, AZ, lambda i: i ^ 2)
    vrad_far = across(vrad_cross, AZ, lambda i: i ^ 1)
    vrad_one = shifted(angular_offsets, vrad, vrad_mate, vrad_cross, vrad_far, "shift_vrad")

    radial_field, azim_field = pl.pallas_call(
        field_kernel,
        out_shape=(tiles, tiles),
        in_specs=[smem(), vmem(), vmem()],
        out_specs=(vmem(), vmem()),
        scratch_shapes=[pltpu.VMEM((EMB * 32, 128), F32)] * 5,
        compiler_params=params(),
        cost_estimate=cost(6),
        name="field",
    )(members, radius, angles)

    dens_far = across(dens_cross, AZ, lambda i: i ^ 1)
    vphi_later = after(vphi, dens_cross)
    vphi_cross = across(vphi_later, AZ, lambda i: i ^ 2)
    vphi_mate = across(vphi_later, AZ, lambda i: i ^ 1)

    transported, part = pl.pallas_call(
        transport_kernel,
        out_shape=(tiles, jax.ShapeDtypeStruct((ROWS, 2 * MODES), F32)),
        in_specs=[smem()] + [anywhere()] * 8 + [vmem()] * 4,
        out_specs=(vmem(), vmem()),
        scratch_shapes=[
            pltpu.VMEM((GROUPS, RING, 128), F32),
            pltpu.VMEM((4, RING // 8, 128), F32),
            pltpu.VMEM((GROUPS + 2, SPAN, 128), F32),
            pltpu.VMEM((2, SPAN, 128), F32),
            pltpu.SemaphoreType.DMA((5,)),
            pltpu.SemaphoreType.DMA((5,)),
        ],
        compiler_params=params(),
        cost_estimate=cost(3),
        name="transport",
    )(
        offsets, dens_two, dens_mate, dens_cross, dens_far,
        edges, edges_mate, edges_cross, edges_far,
        vrad_one, basis_high, basis_low, twiddle,
    )

    others = [across(part, AZ, lambda i, k=k: i ^ k) for k in (2, 3, 1)]
    push = pl.pallas_call(
        push_kernel,
        out_shape=jax.ShapeDtypeStruct((2 * EMB, 128), F32),
        in_specs=[smem(), vmem(), vmem(), vmem()],
        out_specs=vmem(),
        scratch_shapes=[pltpu.VMEM((GROUPS, SPAN, 128), F32)],
        compiler_params=params(),
        cost_estimate=cost(6),
        name="push",
    )(members, radius, angles, transported)

    packed_shape = jax.ShapeDtypeStruct((72, 128), F32)
    spectra, packed = pl.pallas_call(
        moment_kernel,
        out_shape=(jax.ShapeDtypeStruct((ROWS, 2 * MODES), F32), packed_shape),
        in_specs=[vmem()] * 8,
        out_specs=(vmem(), vmem()),
        compiler_params=params(),
        cost_estimate=cost(1),
        name="moments",
    )(part, *others, push, lift, drop, vectors)

    def from_shift(value, axis, shift):
        return across(value, axis, lambda i: (i + shift) % lax.axis_size(axis))

    near = [from_shift(packed, "rad_2", shift) for shift in (1, 2, 3)]
    four = joins[0] * packed + joins[1] * near[0] + joins[2] * near[1] + joins[3] * near[2]
    other = from_shift(four, "rad_1", 1)
    eight = pair[0] * four + pair[1] * other
    distant = [from_shift(eight, "rad_0", shift) for shift in (1, 2, 3)]
    push_part = eight[8:] + distant[0][8:] + distant[1][8:] + distant[2][8:]
    push_others = [across(push_part, AZ, lambda i, k=k: i ^ k) for k in (2, 3, 1)]

    vphi_far = across(vphi_cross, AZ, lambda i: i ^ 1)
    vphi_one = shifted(angular_offsets, vphi_later, vphi_mate, vphi_cross, vphi_far, "shift_vphi")

    kicked_radial, kicked_azim = pl.pallas_call(
        kick_kernel,
        out_shape=(tiles, tiles),
        in_specs=[vmem()] * 20,
        out_specs=(vmem(), vmem()),
        scratch_shapes=[pltpu.VMEM((ROWS, 2 * MODES), F32)] * 2,
        compiler_params=params(),
        cost_estimate=cost(5),
        name="kick",
    )(
        spectra, *near, other, *distant,
        sides, radius, vectors, lift, drop, twiddle, back_high, back_low,
        radial_field, azim_field, vrad_one, vphi_one,
    )

    push_sum = (push_part + push_others[0]) + (push_others[1] + push_others[2])
    embryo_disk_acceleration = jnp.sum(push_sum, axis=1).reshape(2, EMB)
    return (
        from_tiles(transported),
        from_tiles(kicked_radial),
        from_tiles(kicked_azim),
        embryo_disk_acceleration,
    )


def solution(mesh):
    torus = Mesh(mesh.devices.reshape(4, 2, 4, 2, 2), RAD + AZ)
    placed = (P(RAD, AZ), P(RAD, AZ), P(RAD, AZ), P(RAD), P(), P(), P())
    return jax.shard_map(
        on_device,
        mesh=torus,
        in_specs=placed,
        out_specs=(P(RAD, AZ), P(RAD, AZ), P(RAD, AZ), P()),
        check_vma=False,
    )
```

profile of v0, /device:TPU:0, one launch (start us, length us, event | category | flops | bytes accessed | tf_op | source)
XLA Modules:
  0.0 121.9 jit_solution(15685261096430623847)
XLA Ops:
  0.7 2.1 %collective-permute-start.5 = (f32[4,256,128]{2,1,0:T(8,128)}, f32[4,256,128]{2,1,0:T(8,128)S(1)}, u32[]{:S(2)}, u32[]{:S(2)}) collective-permute-start(f32[4,256,128]{2,1,0:T(8,128)} %bitcast.124), channel_id=1, source_target_pairs={{0,2},{1,3},{2,0},{3,1},{4,6},{5,7},{6,4},{7,5},{8,10},{9,11},{10,... | collective-permute-start | bytes 1572872 | tf_op jit(solution)/shard_map/ppermute | solution.py:461
  2.7 0.8 fusion.4
  4.2 0.6 select_bitcast_fusion.9
  4.8 0.6 select_bitcast_fusion.19
  5.4 9.4 %collective-permute-done.1.right_ref = f32[64,128]{1,0:T(8,128)S(1)} collective-permute-done((f32[64,128]{1,0:T(8,128)S(1)}, f32[64,128]{1,0:T(8,128)S(1)}, u32[]{:S(2)}, u32[]{:S(2)}) %collective-permute-start.1) | collective-permute-done | bytes 32800 | tf_op jit(solution)/shard_map/ppermute | solution.py:461
  14.8 0.7 copy-done.24
  15.5 1.0 copy-done.1
  16.5 1.0 copy-done.4
  17.6 2.0 %azimuth.1 = (f32[4,256,128]{2,1,0:T(8,128)}, f32[72,128]{1,0:T(8,128)S(1)}, f32[72,128]{1,0:T(8,128)S(1)}) custom-call(f32[4,256,128]{2,1,0:T(8,128)S(1)} %bitcast.128, f32[4,256,128]{2,1,0:T(8,128)S(1)} %bitcast.120, f32[4,256,128]{2,1,0:T(8,128)S(1)} %bitcast.126, f32[64,128]{1,0:T(8,128)S(1)} %collective-permute-done.left_ref, ...), custom_call_target="tpu_custom_call" | custom-call | flops 1000000 | bytes 2500000 | tf_op jit(solution)/shard_map/azimuth/pallas_call | solution.py:546
  19.6 1.3 %collective-permute-start.6 = (f32[4,256,128]{2,1,0:T(8,128)}, f32[4,256,128]{2,1,0:T(8,128)}, u32[]{:S(2)}, u32[]{:S(2)}) collective-permute-start(f32[4,256,128]{2,1,0:T(8,128)} %get-tuple-element.20.own_ref), channel_id=1, source_target_pairs={{0,2},{1,3},{2,0},{3,1},{4,6},{5,7},{6,4},{7,5},{8,10},{9,11},{10,... | collective-permute-start | bytes 1572872 | tf_op jit(solution)/shard_map/ppermute | solution.py:461
  21.1 0.6 select_bitcast_fusion.1
  21.8 0.7 collective-permute-start.12
  22.5 11.7 %collective-permute-done.6.cross_ref = f32[4,256,128]{2,1,0:T(8,128)} collective-permute-done((f32[4,256,128]{2,1,0:T(8,128)}, f32[4,256,128]{2,1,0:T(8,128)}, u32[]{:S(2)}, u32[]{:S(2)}) %collective-permute-start.6) | collective-permute-done | bytes 524320 | tf_op jit(solution)/shard_map/ppermute | solution.py:461
  34.9 3.5 %collective-permute-start.2 = (f32[72,128]{1,0:T(8,128)S(1)}, f32[72,128]{1,0:T(8,128)S(1)}, u32[]{:S(2)}, u32[]{:S(2)}) collective-permute-start(f32[72,128]{1,0:T(8,128)S(1)} %get-tuple-element.17), channel_id=1, source_target_pairs={{0,4},{4,8},{8,12},{12,16},{16,20},{20,24},{24,28},{28,32},{32,36}... | collective-permute-start | bytes 110600 | tf_op jit(solution)/shard_map/ppermute | solution.py:557
  38.9 1.0 collective-permute-done.2
  40.0 1.3 %collective-permute-start.3 = (f32[72,128]{1,0:T(8,128)S(1)}, f32[72,128]{1,0:T(8,128)S(1)}, u32[]{:S(2)}, u32[]{:S(2)}) collective-permute-start(f32[72,128]{1,0:T(8,128)S(1)} %get-tuple-element.18), channel_id=1, source_target_pairs={{4,0},{8,4},{12,8},{16,12},{20,16},{24,20},{28,24},{32,28},{36,32}... | collective-permute-start | bytes 110600 | tf_op jit(solution)/shard_map/ppermute | solution.py:558
  41.3 0.6 constant_dynamic-update-slice_fusion.4
  41.9 4.2 %collective-permute-done.3 = f32[72,128]{1,0:T(8,128)S(1)} collective-permute-done((f32[72,128]{1,0:T(8,128)S(1)}, f32[72,128]{1,0:T(8,128)S(1)}, u32[]{:S(2)}, u32[]{:S(2)}) %collective-permute-start.3) | collective-permute-done | bytes 36896 | tf_op jit(solution)/shard_map/ppermute | solution.py:558
  48.6 2.0 %collective-permute-start.8 = (f32[4,32,128]{2,1,0:T(8,128)S(1)}, f32[4,32,128]{2,1,0:T(8,128)S(1)}, u32[]{:S(2)}, u32[]{:S(2)}) collective-permute-start(f32[4,32,128]{2,1,0:T(8,128)S(1)} %bitcast.131), channel_id=1, source_target_pairs={{0,1},{1,0},{2,3},{3,2},{4,5},{5,4},{6,7},{7,6},{8,9},{9,8},{10,11... | collective-permute-start | bytes 196616 | tf_op jit(solution)/shard_map/ppermute | solution.py:461
  50.9 1.4 %shift_vrad.1.vrad_ref = f32[4,256,128]{2,1,0:T(8,128)S(1)} custom-call(s32[32]{0:T(128)S(1)} %copy-done.24, f32[4,256,128]{2,1,0:T(8,128)S(1)} %bitcast.127, f32[4,256,128]{2,1,0:T(8,128)S(1)} %collective-permute-done.11.mate_ref, f32[4,256,128]{2,1,0:T(8,128)S(1)} %collective-permute-done.5.cross_ref, f32[4,256,128]{2,1,0:T(8,128)S(1)} %collective-permute-done.12.far_ref), custom_call_target="tpu_custom_call" | custom-call | flops 2000000 | bytes 5000000 | tf_op jit(solution)/shard_map/shift_vrad/pallas_call | solution.py:175
  52.3 1.9 %collective-permute-start.24 = (f32[4,256,128]{2,1,0:T(8,128)S(1)}, f32[4,256,128]{2,1,0:T(8,128)S(1)}, u32[]{:S(2)}, u32[]{:S(2)}) collective-permute-start(f32[4,256,128]{2,1,0:T(8,128)S(1)} %bitcast.121), channel_id=1, source_target_pairs={{0,2},{1,3},{2,0},{3,1},{4,6},{5,7},{6,4},{7,5},{8,10},{9,11},{10,... | collective-permute-start | bytes 1572872 | tf_op jit(solution)/shard_map/ppermute | solution.py:461
  54.2 0.6 collective-permute-done.9.edge_cross_ref
  54.9 5.0 %transport.1 = (f32[4,256,128]{2,1,0:T(8,128)}, f32[32,512]{1,0:T(8,128)S(1)}) custom-call(s32[34]{0:T(128)S(1)} %pad_add_fusion.offs_ref, f32[4,256,128]{2,1,0:T(8,128)} %get-tuple-element.20.own_ref, f32[4,256,128]{2,1,0:T(8,128)} %collective-permute-done.4.mate_ref, f32[4,256,128]{2,1,0:T(8,128)} %collective-permute-done.6.cross_ref, ...), custom_call_target="tpu_custom_call" | custom-call | flops 3000000 | bytes 7500000 | tf_op jit(solution)/shard_map/transport/pallas_call | solution.py:589
  60.3 1.8 %collective-permute-start.15 = (f32[32,512]{1,0:T(8,128)S(1)}, f32[32,512]{1,0:T(8,128)S(1)}, u32[]{:S(2)}, u32[]{:S(2)}) collective-permute-start(f32[32,512]{1,0:T(8,128)S(1)} %get-tuple-element.22.a_ref), channel_id=1, source_target_pairs={{0,1},{1,0},{2,3},{3,2},{4,5},{5,4},{6,7},{7,6},{8,9},{9,8},{10,11... | collective-permute-start | bytes 196616 | tf_op jit(solution)/shard_map/ppermute | solution.py:461
  62.2 1.0 copy-done.5
  63.3 7.7 %push.1.push_ref = f32[64,128]{1,0:T(8,128)S(1)} custom-call(f32[6,32]{1,0:T(8,128)S(1)} %stack.51.members_ref, f32[32,128]{1,0:T(8,128)S(1)} %broadcast_in_dim.38.radius_ref, f32[16,32,128]{2,1,0:T(8,128)S(1)} %copy-done.3, f32[4,256,128]{2,1,0:T(8,128)S(1)} %copy-done.5), custom_call_target="tpu_custom_call" | custom-call | flops 6000000 | bytes 15000000 | tf_op jit(solution)/shard_map/push/pallas_call | solution.py:612
  71.1 0.6 copy-done.22
  71.7 2.0 %collective-permute-start.16 = (f32[72,128]{1,0:T(8,128)S(1)}, f32[72,128]{1,0:T(8,128)S(1)}, u32[]{:S(2)}, u32[]{:S(2)}) collective-permute-start(f32[72,128]{1,0:T(8,128)S(1)} %get-tuple-element.24), channel_id=1, source_target_pairs={{0,4},{4,8},{8,12},{12,0},{1,5},{5,9},{9,13},{13,1},{2,6},{6,10},{... | collective-permute-start | bytes 110600 | tf_op jit(solution)/shard_map/ppermute | solution.py:461
  73.7 7.1 %collective-permute-start.17 = (f32[72,128]{1,0:T(8,128)S(1)}, f32[72,128]{1,0:T(8,128)S(1)}, u32[]{:S(2)}, u32[]{:S(2)}) collective-permute-start(f32[72,128]{1,0:T(8,128)S(1)} %get-tuple-element.24), channel_id=1, source_target_pairs={{0,8},{4,12},{8,0},{12,4},{1,9},{5,13},{9,1},{13,5},{2,10},{6,14},... | collective-permute-start | bytes 110600 | tf_op jit(solution)/shard_map/ppermute | solution.py:461
  81.6 1.6 %collective-permute-done.17.terms_ref_1 = f32[72,128]{1,0:T(8,128)S(1)} collective-permute-done((f32[72,128]{1,0:T(8,128)S(1)}, f32[72,128]{1,0:T(8,128)S(1)}, u32[]{:S(2)}, u32[]{:S(2)}) %collective-permute-start.17) | collective-permute-done | bytes 36896 | tf_op jit(solution)/shard_map/ppermute | solution.py:461
  83.2 1.6 %collective-permute-done.18.terms_ref_2 = f32[72,128]{1,0:T(8,128)S(1)} collective-permute-done((f32[72,128]{1,0:T(8,128)S(1)}, f32[72,128]{1,0:T(8,128)S(1)}, u32[]{:S(2)}, u32[]{:S(2)}) %collective-permute-start.18) | collective-permute-done | bytes 36896 | tf_op jit(solution)/shard_map/ppermute | solution.py:461
  84.9 0.6 copy-done.28
  85.6 0.6 copy-done.13
  86.2 3.9 %collective-permute-start.19 = (f32[72,128]{1,0:T(8,128)S(1)}, f32[72,128]{1,0:T(8,128)S(1)}, u32[]{:S(2)}, u32[]{:S(2)}) collective-permute-start(f32[72,128]{1,0:T(8,128)S(1)} %fusion.2), channel_id=1, source_target_pairs={{0,16},{16,0},{1,17},{17,1},{2,18},{18,2},{3,19},{19,3},{4,20},{20... | collective-permute-start | bytes 110600 | tf_op jit(solution)/shard_map/ppermute | solution.py:461
  91.2 0.8 collective-permute-done.19.terms_ref_3
  92.1 1.6 %collective-permute-start.20 = (f32[72,128]{1,0:T(8,128)S(1)}, f32[72,128]{1,0:T(8,128)S(1)}, u32[]{:S(2)}, u32[]{:S(2)}) collective-permute-start(f32[72,128]{1,0:T(8,128)S(1)} %fusion.3), channel_id=1, source_target_pairs={{0,32},{32,64},{64,96},{96,0},{1,33},{33,65},{65,97},{97,1},{2,34}... | collective-permute-start | bytes 110600 | tf_op jit(solution)/shard_map/ppermute | solution.py:461
  93.7 2.5 %collective-permute-start.21 = (f32[72,128]{1,0:T(8,128)S(1)}, f32[72,128]{1,0:T(8,128)S(1)}, u32[]{:S(2)}, u32[]{:S(2)}) collective-permute-start(f32[72,128]{1,0:T(8,128)S(1)} %fusion.3), channel_id=1, source_target_pairs={{0,64},{32,96},{64,0},{96,32},{1,65},{33,97},{65,1},{97,33},{2,66}... | collective-permute-start | bytes 110600 | tf_op jit(solution)/shard_map/ppermute | solution.py:461
  96.2 1.7 %collective-permute-start.22 = (f32[72,128]{1,0:T(8,128)S(1)}, f32[72,128]{1,0:T(8,128)S(1)}, u32[]{:S(2)}, u32[]{:S(2)}) collective-permute-start(f32[72,128]{1,0:T(8,128)S(1)} %fusion.3), channel_id=1, source_target_pairs={{0,96},{32,0},{64,32},{96,64},{1,97},{33,1},{65,33},{97,65},{2,98}... | collective-permute-start | bytes 110600 | tf_op jit(solution)/shard_map/ppermute | solution.py:461
  98.5 0.7 collective-permute-done.21.terms_ref_5
  99.2 1.0 collective-permute-done.22.terms_ref_6
  100.8 0.8 collective-permute-start.26
  101.6 1.4 %collective-permute-start.28 = (f32[64,128]{1,0:T(8,128)S(1)}, f32[64,128]{1,0:T(8,128)S(1)}, u32[]{:S(2)}, u32[]{:S(2)}) collective-permute-start(f32[64,128]{1,0:T(8,128)S(1)} %slice_add_fusion), channel_id=1, source_target_pairs={{0,1},{1,0},{2,3},{3,2},{4,5},{5,4},{6,7},{7,6},{8,9},{9,8},{10,11... | collective-permute-start | bytes 98312 | tf_op jit(solution)/shard_map/ppermute | solution.py:461
  102.9 0.6 constant_dynamic-update-slice_fusion.weights_ref
  103.5 9.3 %field.1 = (f32[4,256,128]{2,1,0:T(8,128)S(1)}, f32[4,256,128]{2,1,0:T(8,128)S(1)}) custom-call(f32[6,32]{1,0:T(8,128)S(1)} %stack.51.members_ref, f32[32,128]{1,0:T(8,128)S(1)} %broadcast_in_dim.38.radius_ref, f32[16,32,128]{2,1,0:T(8,128)S(1)} %copy-done.3), custom_call_target="tpu_custom_call" | custom-call | flops 6000000 | bytes 15000000 | tf_op jit(solution)/shard_map/field/pallas_call | solution.py:573
  112.8 0.7 add_reduce_fusion
  113.5 1.3 %reshape.219 = f32[2,32]{1,0:T(2,128)} reshape(f32[64]{0:T(128)} %add_reduce_fusion) | data formatting | bytes 512 | tf_op jit(solution)/shard_map/reshape | solution.py:664
  114.9 2.4 %shift_vphi.1.vphi_ref = f32[4,256,128]{2,1,0:T(8,128)S(1)} custom-call(s32[32]{0:T(128)S(1)} %copy-done.25, f32[4,256,128]{2,1,0:T(8,128)S(1)} %bitcast.123, f32[4,256,128]{2,1,0:T(8,128)S(1)} %collective-permute-done.23.mate_ref, f32[4,256,128]{2,1,0:T(8,128)S(1)} %collective-permute-done.24.cross_ref, f32[4,256,128]{2,1,0:T(8,128)} %collective-permute-done.25.far_ref), custom_call_target="tpu_custom_call" | custom-call | flops 2000000 | bytes 5000000 | tf_op jit(solution)/shard_map/shift_vphi/pallas_call | solution.py:175
  117.4 4.5 %kick.1 = (f32[4,256,128]{2,1,0:T(8,128)}, f32[4,256,128]{2,1,0:T(8,128)}) custom-call(f32[32,512]{1,0:T(8,128)S(1)} %copy-done.23, f32[72,128]{1,0:T(8,128)S(1)} %collective-permute-done.16.terms_ref_0, f32[72,128]{1,0:T(8,128)S(1)} %collective-permute-done.17.terms_ref_1, f32[72,128]{1,0:T(8,128)S(1)} %copy-done.14, ...), custom_call_target="tpu_custom_call" | custom-call | flops 5000000 | bytes 12500000 | tf_op jit(solution)/shard_map/kick/pallas_call | solution.py:648
  (145 shorter events, 7.3 us)
Async XLA Ops:
  0.6 14.2 %copy-start = (f32[32,4096]{1,0:T(8,128)S(1)}, f32[32,4096]{1,0:T(8,128)}, u32[]{:S(2)}) copy-start(f32[32,4096]{1,0:T(8,128)} %param.19) | copy-start | bytes 1572868
  0.7 18.9 %collective-permute-start.5 = (f32[4,256,128]{2,1,0:T(8,128)}, f32[4,256,128]{2,1,0:T(8,128)S(1)}, u32[]{:S(2)}, u32[]{:S(2)}) collective-permute-start(f32[4,256,128]{2,1,0:T(8,128)} %bitcast.124), channel_id=1, source_target_pairs={{0,2},{1,3},{2,0},{3,1},{4,6},{5,7},{6,4},{7,5},{8,10},{9,11},{10,... | collective-permute-start | bytes 1572872 | tf_op jit(solution)/shard_map/ppermute | solution.py:461
  2.7 45.8 %collective-permute-start.11 = (f32[4,256,128]{2,1,0:T(8,128)}, f32[4,256,128]{2,1,0:T(8,128)S(1)}, u32[]{:S(2)}, u32[]{:S(2)}) collective-permute-start(f32[4,256,128]{2,1,0:T(8,128)} %bitcast.125), channel_id=1, source_target_pairs={{0,1},{1,0},{2,3},{3,2},{4,5},{5,4},{6,7},{7,6},{8,9},{9,8},{10,11... | collective-permute-start | bytes 1572872 | tf_op jit(solution)/shard_map/ppermute | solution.py:461
  3.5 11.3 %collective-permute-start.1 = (f32[64,128]{1,0:T(8,128)S(1)}, f32[64,128]{1,0:T(8,128)S(1)}, u32[]{:S(2)}, u32[]{:S(2)}) collective-permute-start(f32[64,128]{1,0:T(8,128)S(1)} %pad_maximum_fusion.2), channel_id=1, source_target_pairs={{0,3},{1,0},{2,1},{3,2},{4,7},{5,4},{6,5},{7,6},{8,11},{9,8},{10,9... | collective-permute-start | bytes 98312 | tf_op jit(solution)/shard_map/ppermute | solution.py:461
  3.8 11.0 %collective-permute-start = (f32[64,128]{1,0:T(8,128)S(1)}, f32[64,128]{1,0:T(8,128)S(1)}, u32[]{:S(2)}, u32[]{:S(2)}) collective-permute-start(f32[64,128]{1,0:T(8,128)S(1)} %pad_maximum_fusion.1), channel_id=1, source_target_pairs={{0,1},{1,2},{2,3},{3,0},{4,5},{5,6},{6,7},{7,4},{8,9},{9,10},{10,1... | collective-permute-start | bytes 98312 | tf_op jit(solution)/shard_map/ppermute | solution.py:461
  17.6 4.9 %copy-start.47 = (s32[32]{0:T(128)S(1)}, s32[32]{0:T(128)}, u32[]{:S(2)}) copy-start(s32[32]{0:T(128)} %param.21) | copy-start | bytes 388
  17.6 24.3 %copy-start.45 = (f32[32]{0:T(128)S(1)}, f32[32]{0:T(128)}, u32[]{:S(2)}) copy-start(f32[32]{0:T(128)} %param.23) | copy-start | bytes 388
  19.6 31.3 %copy-start.2 = (f32[32,4096]{1,0:T(8,128)S(1)}, f32[32,4096]{1,0:T(8,128)}, u32[]{:S(2)}) copy-start(f32[32,4096]{1,0:T(8,128)} %param.18) | copy-start | bytes 1572868
  19.6 14.7 %collective-permute-start.6 = (f32[4,256,128]{2,1,0:T(8,128)}, f32[4,256,128]{2,1,0:T(8,128)}, u32[]{:S(2)}, u32[]{:S(2)}) collective-permute-start(f32[4,256,128]{2,1,0:T(8,128)} %get-tuple-element.20.own_ref), channel_id=1, source_target_pairs={{0,2},{1,3},{2,0},{3,1},{4,6},{5,7},{6,4},{7,5},{8,10},{9,11},{10,... | collective-permute-start | bytes 1572872 | tf_op jit(solution)/shard_map/ppermute | solution.py:461
  21.8 28.9 %collective-permute-start.12 = (f32[4,256,128]{2,1,0:T(8,128)S(1)}, f32[4,256,128]{2,1,0:T(8,128)S(1)}, u32[]{:S(2)}, u32[]{:S(2)}) collective-permute-start(f32[4,256,128]{2,1,0:T(8,128)S(1)} %collective-permute-done.5.cross_ref), channel_id=1, source_target_pairs={{0,1},{1,0},{2,3},{3,2},{4,5},{5,4},{6,7},{7,6},{8,9},{9,8},{10,11... | collective-permute-start | bytes 1572872 | tf_op jit(solution)/shard_map/ppermute | solution.py:461
  22.5 32.4 %collective-permute-start.4 = (f32[4,256,128]{2,1,0:T(8,128)}, f32[4,256,128]{2,1,0:T(8,128)}, u32[]{:S(2)}, u32[]{:S(2)}) collective-permute-start(f32[4,256,128]{2,1,0:T(8,128)} %get-tuple-element.20.own_ref), channel_id=1, source_target_pairs={{0,1},{1,0},{2,3},{3,2},{4,5},{5,4},{6,7},{7,6},{8,9},{9,8},{10,11... | collective-permute-start | bytes 1572872 | tf_op jit(solution)/shard_map/ppermute | solution.py:461
  34.3 20.6 %collective-permute-start.7 = (f32[4,256,128]{2,1,0:T(8,128)}, f32[4,256,128]{2,1,0:T(8,128)}, u32[]{:S(2)}, u32[]{:S(2)}) collective-permute-start(f32[4,256,128]{2,1,0:T(8,128)} %collective-permute-done.6.cross_ref), channel_id=1, source_target_pairs={{0,1},{1,0},{2,3},{3,2},{4,5},{5,4},{6,7},{7,6},{8,9},{9,8},{10,11... | collective-permute-start | bytes 1572872 | tf_op jit(solution)/shard_map/ppermute | solution.py:461
  34.9 5.1 %collective-permute-start.2 = (f32[72,128]{1,0:T(8,128)S(1)}, f32[72,128]{1,0:T(8,128)S(1)}, u32[]{:S(2)}, u32[]{:S(2)}) collective-permute-start(f32[72,128]{1,0:T(8,128)S(1)} %get-tuple-element.17), channel_id=1, source_target_pairs={{0,4},{4,8},{8,12},{12,16},{16,20},{20,24},{24,28},{28,32},{32,36}... | collective-permute-start | bytes 110600 | tf_op jit(solution)/shard_map/ppermute | solution.py:557
  40.0 6.1 %collective-permute-start.3 = (f32[72,128]{1,0:T(8,128)S(1)}, f32[72,128]{1,0:T(8,128)S(1)}, u32[]{:S(2)}, u32[]{:S(2)}) collective-permute-start(f32[72,128]{1,0:T(8,128)S(1)} %get-tuple-element.18), channel_id=1, source_target_pairs={{4,0},{8,4},{12,8},{16,12},{20,16},{24,20},{28,24},{32,28},{36,32}... | collective-permute-start | bytes 110600 | tf_op jit(solution)/shard_map/ppermute | solution.py:558
  46.1 6.2 %collective-permute-start.10 = (f32[4,32,128]{2,1,0:T(8,128)S(1)}, f32[4,32,128]{2,1,0:T(8,128)S(1)}, u32[]{:S(2)}, u32[]{:S(2)}) collective-permute-start(f32[4,32,128]{2,1,0:T(8,128)S(1)} %bitcast.130), channel_id=1, source_target_pairs={{0,3},{1,2},{2,1},{3,0},{4,7},{5,6},{6,5},{7,4},{8,11},{9,10},{10,... | collective-permute-start | bytes 196616 | tf_op jit(solution)/shard_map/ppermute | solution.py:461
  48.6 5.7 %collective-permute-start.8 = (f32[4,32,128]{2,1,0:T(8,128)S(1)}, f32[4,32,128]{2,1,0:T(8,128)S(1)}, u32[]{:S(2)}, u32[]{:S(2)}) collective-permute-start(f32[4,32,128]{2,1,0:T(8,128)S(1)} %bitcast.131), channel_id=1, source_target_pairs={{0,1},{1,0},{2,3},{3,2},{4,5},{5,4},{6,7},{7,6},{8,9},{9,8},{10,11... | collective-permute-start | bytes 196616 | tf_op jit(solution)/shard_map/ppermute | solution.py:461
  50.6 4.3 %collective-permute-start.9 = (f32[4,32,128]{2,1,0:T(8,128)S(1)}, f32[4,32,128]{2,1,0:T(8,128)S(1)}, u32[]{:S(2)}, u32[]{:S(2)}) collective-permute-start(f32[4,32,128]{2,1,0:T(8,128)S(1)} %bitcast.132), channel_id=1, source_target_pairs={{0,2},{1,3},{2,0},{3,1},{4,6},{5,7},{6,4},{7,5},{8,10},{9,11},{10,... | collective-permute-start | bytes 196616 | tf_op jit(solution)/shard_map/ppermute | solution.py:461
  52.3 9.9 %copy-start.3 = (f32[16,32,128]{2,1,0:T(8,128)S(1)}, f32[16,32,128]{2,1,0:T(8,128)}, u32[]{:S(2)}) copy-start(f32[16,32,128]{2,1,0:T(8,128)} %constant.118.clone.angles_ref) | copy-start | bytes 786436
  52.3 38.4 %collective-permute-start.24 = (f32[4,256,128]{2,1,0:T(8,128)S(1)}, f32[4,256,128]{2,1,0:T(8,128)S(1)}, u32[]{:S(2)}, u32[]{:S(2)}) collective-permute-start(f32[4,256,128]{2,1,0:T(8,128)S(1)} %bitcast.121), channel_id=1, source_target_pairs={{0,2},{1,3},{2,0},{3,1},{4,6},{5,7},{6,4},{7,5},{8,10},{9,11},{10,... | collective-permute-start | bytes 1572872 | tf_op jit(solution)/shard_map/ppermute | solution.py:461
  59.9 11.0 %collective-permute-start.13 = (f32[32,512]{1,0:T(8,128)S(1)}, f32[32,512]{1,0:T(8,128)S(1)}, u32[]{:S(2)}, u32[]{:S(2)}) collective-permute-start(f32[32,512]{1,0:T(8,128)S(1)} %get-tuple-element.22.a_ref), channel_id=1, source_target_pairs={{0,2},{1,3},{2,0},{3,1},{4,6},{5,7},{6,4},{7,5},{8,10},{9,11},{10,... | collective-permute-start | bytes 196616 | tf_op jit(solution)/shard_map/ppermute | solution.py:461
  60.2 10.8 %collective-permute-start.14 = (f32[32,512]{1,0:T(8,128)S(1)}, f32[32,512]{1,0:T(8,128)S(1)}, u32[]{:S(2)}, u32[]{:S(2)}) collective-permute-start(f32[32,512]{1,0:T(8,128)S(1)} %get-tuple-element.22.a_ref), channel_id=1, source_target_pairs={{0,3},{1,2},{2,1},{3,0},{4,7},{5,6},{6,5},{7,4},{8,11},{9,10},{10,... | collective-permute-start | bytes 196616 | tf_op jit(solution)/shard_map/ppermute | solution.py:461
  60.3 10.7 %collective-permute-start.15 = (f32[32,512]{1,0:T(8,128)S(1)}, f32[32,512]{1,0:T(8,128)S(1)}, u32[]{:S(2)}, u32[]{:S(2)}) collective-permute-start(f32[32,512]{1,0:T(8,128)S(1)} %get-tuple-element.22.a_ref), channel_id=1, source_target_pairs={{0,1},{1,0},{2,3},{3,2},{4,5},{5,4},{6,7},{7,6},{8,9},{9,8},{10,11... | collective-permute-start | bytes 196616 | tf_op jit(solution)/shard_map/ppermute | solution.py:461
  63.3 7.7 %copy-start.9 = (f32[32,512]{1,0:T(8,128)S(1)}, f32[32,512]{1,0:T(8,128)}, u32[]{:S(2)}) copy-start(f32[32,512]{1,0:T(8,128)} %constant.122.clone.lift_ref) | copy-start | bytes 196612
  63.3 7.7 %copy-start.10 = (f32[32,512]{1,0:T(8,128)S(1)}, f32[32,512]{1,0:T(8,128)}, u32[]{:S(2)}) copy-start(f32[32,512]{1,0:T(8,128)} %constant.123.clone.drop_ref) | copy-start | bytes 196612
  63.3 7.7 %copy-start.21 = (f32[8,512]{1,0:T(8,128)S(1)}, f32[8,512]{1,0:T(8,128)}, u32[]{:S(2)}) copy-start(f32[8,512]{1,0:T(8,128)} %constant.124.clone.vectors_ref) | copy-start | bytes 49156
  71.0 13.9 %copy-start.29 = (f32[4,128]{1,0:T(4,128)S(1)}, f32[4,128]{1,0:T(4,128)}, u32[]{:S(2)}) copy-start(f32[4,128]{1,0:T(4,128)} %get-tuple-element.54) | copy-start | bytes 6148
  71.0 13.8 %copy-start.30 = (f32[4,128]{1,0:T(4,128)S(1)}, f32[4,128]{1,0:T(4,128)}, u32[]{:S(2)}) copy-start(f32[4,128]{1,0:T(4,128)} %get-tuple-element.55) | copy-start | bytes 6148
  71.0 13.8 %copy-start.31 = (f32[4,128]{1,0:T(4,128)S(1)}, f32[4,128]{1,0:T(4,128)}, u32[]{:S(2)}) copy-start(f32[4,128]{1,0:T(4,128)} %get-tuple-element.56) | copy-start | bytes 6148
  71.0 13.8 %copy-start.32 = (f32[4,128]{1,0:T(4,128)S(1)}, f32[4,128]{1,0:T(4,128)}, u32[]{:S(2)}) copy-start(f32[4,128]{1,0:T(4,128)} %get-tuple-element.57) | copy-start | bytes 6148
  71.0 13.8 %copy-start.35 = (f32[4,128]{1,0:T(4,128)S(1)}, f32[4,128]{1,0:T(4,128)}, u32[]{:S(2)}) copy-start(f32[4,128]{1,0:T(4,128)} %get-tuple-element.50) | copy-start | bytes 6148
  71.0 13.8 %copy-start.36 = (f32[4,128]{1,0:T(4,128)S(1)}, f32[4,128]{1,0:T(4,128)}, u32[]{:S(2)}) copy-start(f32[4,128]{1,0:T(4,128)} %get-tuple-element.51) | copy-start | bytes 6148
  71.7 9.2 %copy-start.44 = (f32[4,128]{1,0:T(4,128)S(1)}, f32[4,128]{1,0:T(4,128)}, u32[]{:S(2)}) copy-start(f32[4,128]{1,0:T(4,128)} %get-tuple-element.41) | copy-start | bytes 6148
  71.7 9.2 %copy-start.43 = (f32[4,128]{1,0:T(4,128)S(1)}, f32[4,128]{1,0:T(4,128)}, u32[]{:S(2)}) copy-start(f32[4,128]{1,0:T(4,128)} %get-tuple-element.40) | copy-start | bytes 6148
  71.7 9.8 %collective-permute-start.16 = (f32[72,128]{1,0:T(8,128)S(1)}, f32[72,128]{1,0:T(8,128)S(1)}, u32[]{:S(2)}, u32[]{:S(2)}) collective-permute-start(f32[72,128]{1,0:T(8,128)S(1)} %get-tuple-element.24), channel_id=1, source_target_pairs={{0,4},{4,8},{8,12},{12,0},{1,5},{5,9},{9,13},{13,1},{2,6},{6,10},{... | collective-permute-start | bytes 110600 | tf_op jit(solution)/shard_map/ppermute | solution.py:461
  73.7 9.5 %collective-permute-start.17 = (f32[72,128]{1,0:T(8,128)S(1)}, f32[72,128]{1,0:T(8,128)S(1)}, u32[]{:S(2)}, u32[]{:S(2)}) collective-permute-start(f32[72,128]{1,0:T(8,128)S(1)} %get-tuple-element.24), channel_id=1, source_target_pairs={{0,8},{4,12},{8,0},{12,4},{1,9},{5,13},{9,1},{13,5},{2,10},{6,14},... | collective-permute-start | bytes 110600 | tf_op jit(solution)/shard_map/ppermute | solution.py:461
  80.9 4.0 %collective-permute-start.18 = (f32[72,128]{1,0:T(8,128)S(1)}, f32[72,128]{1,0:T(8,128)S(1)}, u32[]{:S(2)}, u32[]{:S(2)}) collective-permute-start(f32[72,128]{1,0:T(8,128)S(1)} %get-tuple-element.24), channel_id=1, source_target_pairs={{0,12},{4,0},{8,4},{12,8},{1,13},{5,1},{9,5},{13,9},{2,14},{6,2},{... | collective-permute-start | bytes 110600 | tf_op jit(solution)/shard_map/ppermute | solution.py:461
  85.5 4.6 %copy-start.42 = (f32[4,128]{1,0:T(4,128)S(1)}, f32[4,128]{1,0:T(4,128)}, u32[]{:S(2)}) copy-start(f32[4,128]{1,0:T(4,128)} %get-tuple-element.39) | copy-start | bytes 6148
  86.2 5.8 %collective-permute-start.19 = (f32[72,128]{1,0:T(8,128)S(1)}, f32[72,128]{1,0:T(8,128)S(1)}, u32[]{:S(2)}, u32[]{:S(2)}) collective-permute-start(f32[72,128]{1,0:T(8,128)S(1)} %fusion.2), channel_id=1, source_target_pairs={{0,16},{16,0},{1,17},{17,1},{2,18},{18,2},{3,19},{19,3},{4,20},{20... | collective-permute-start | bytes 110600 | tf_op jit(solution)/shard_map/ppermute | solution.py:461
  90.7 24.2 %collective-permute-start.23 = (f32[4,256,128]{2,1,0:T(8,128)S(1)}, f32[4,256,128]{2,1,0:T(8,128)S(1)}, u32[]{:S(2)}, u32[]{:S(2)}) collective-permute-start(f32[4,256,128]{2,1,0:T(8,128)S(1)} %bitcast.122), channel_id=1, source_target_pairs={{0,1},{1,0},{2,3},{3,2},{4,5},{5,4},{6,7},{7,6},{8,9},{9,8},{10,11... | collective-permute-start | bytes 1572872 | tf_op jit(solution)/shard_map/ppermute | solution.py:461
  90.7 24.2 %collective-permute-start.25 = (f32[4,256,128]{2,1,0:T(8,128)S(1)}, f32[4,256,128]{2,1,0:T(8,128)}, u32[]{:S(2)}, u32[]{:S(2)}) collective-permute-start(f32[4,256,128]{2,1,0:T(8,128)S(1)} %collective-permute-done.24.cross_ref), channel_id=1, source_target_pairs={{0,1},{1,0},{2,3},{3,2},{4,5},{5,4},{6,7},{7,6},{8,9},{9,8},{10,11... | collective-permute-start | bytes 1572872 | tf_op jit(solution)/shard_map/ppermute | solution.py:461
  92.0 5.8 %copy-start.40 = (f32[4,128]{1,0:T(4,128)S(1)}, f32[4,128]{1,0:T(4,128)}, u32[]{:S(2)}) copy-start(f32[4,128]{1,0:T(4,128)} %get-tuple-element.37) | copy-start | bytes 6148
  92.1 5.7 %copy-start.39 = (f32[4,128]{1,0:T(4,128)S(1)}, f32[4,128]{1,0:T(4,128)}, u32[]{:S(2)}) copy-start(f32[4,128]{1,0:T(4,128)} %get-tuple-element.36) | copy-start | bytes 6148
  92.1 6.3 %collective-permute-start.20 = (f32[72,128]{1,0:T(8,128)S(1)}, f32[72,128]{1,0:T(8,128)S(1)}, u32[]{:S(2)}, u32[]{:S(2)}) collective-permute-start(f32[72,128]{1,0:T(8,128)S(1)} %fusion.3), channel_id=1, source_target_pairs={{0,32},{32,64},{64,96},{96,0},{1,33},{33,65},{65,97},{97,1},{2,34}... | collective-permute-start | bytes 110600 | tf_op jit(solution)/shard_map/ppermute | solution.py:461
  93.7 5.5 %collective-permute-start.21 = (f32[72,128]{1,0:T(8,128)S(1)}, f32[72,128]{1,0:T(8,128)S(1)}, u32[]{:S(2)}, u32[]{:S(2)}) collective-permute-start(f32[72,128]{1,0:T(8,128)S(1)} %fusion.3), channel_id=1, source_target_pairs={{0,64},{32,96},{64,0},{96,32},{1,65},{33,97},{65,1},{97,33},{2,66}... | collective-permute-start | bytes 110600 | tf_op jit(solution)/shard_map/ppermute | solution.py:461
  96.2 4.0 %collective-permute-start.22 = (f32[72,128]{1,0:T(8,128)S(1)}, f32[72,128]{1,0:T(8,128)S(1)}, u32[]{:S(2)}, u32[]{:S(2)}) collective-permute-start(f32[72,128]{1,0:T(8,128)S(1)} %fusion.3), channel_id=1, source_target_pairs={{0,96},{32,0},{64,32},{96,64},{1,97},{33,1},{65,33},{97,65},{2,98}... | collective-permute-start | bytes 110600 | tf_op jit(solution)/shard_map/ppermute | solution.py:461
  100.8 12.0 %collective-permute-start.26 = (f32[64,128]{1,0:T(8,128)S(1)}, f32[64,128]{1,0:T(8,128)S(1)}, u32[]{:S(2)}, u32[]{:S(2)}) collective-permute-start(f32[64,128]{1,0:T(8,128)S(1)} %slice_add_fusion), channel_id=1, source_target_pairs={{0,2},{1,3},{2,0},{3,1},{4,6},{5,7},{6,4},{7,5},{8,10},{9,11},{10,... | collective-permute-start | bytes 98312 | tf_op jit(solution)/shard_map/ppermute | solution.py:461
  101.6 11.3 %collective-permute-start.27 = (f32[64,128]{1,0:T(8,128)S(1)}, f32[64,128]{1,0:T(8,128)S(1)}, u32[]{:S(2)}, u32[]{:S(2)}) collective-permute-start(f32[64,128]{1,0:T(8,128)S(1)} %slice_add_fusion), channel_id=1, source_target_pairs={{0,3},{1,2},{2,1},{3,0},{4,7},{5,6},{6,5},{7,4},{8,11},{9,10},{10,... | collective-permute-start | bytes 98312 | tf_op jit(solution)/shard_map/ppermute | solution.py:461
  101.6 11.3 %collective-permute-start.28 = (f32[64,128]{1,0:T(8,128)S(1)}, f32[64,128]{1,0:T(8,128)S(1)}, u32[]{:S(2)}, u32[]{:S(2)}) collective-permute-start(f32[64,128]{1,0:T(8,128)S(1)} %slice_add_fusion), channel_id=1, source_target_pairs={{0,1},{1,0},{2,3},{3,2},{4,5},{5,4},{6,7},{7,6},{8,9},{9,8},{10,11... | collective-permute-start | bytes 98312 | tf_op jit(solution)/shard_map/ppermute | solution.py:461
  (29 other events, 59.7 us)
where the time goes:
time: 123 us; the launch traced here: 122 us
  starting transfers between devices  37.5 us (30%)
  waiting for transfers between devices  32.8 us (27%)
  Pallas kernels  32.2 us (26%)
  local copies, waits for them, and re-layouts  9.71 us (8%)
  other arithmetic  7.1 us (6%)
  between operations  2.59 us (2%)
    ppermute x27, starting transfers between devices, across(): lax.ppermute(value, axis, [(source, target(source)) for source in range(c...  32.7 us
    ppermute x27, waiting for transfers between devices, across(): lax.ppermute(value, axis, [(source, target(source)) for source in range(c...  27.6 us
    pallas_call x1, Pallas kernels, on_device(): pl.pallas_call(field_kernel, out_shape=(tiles, tiles), in_specs=[smem(),...  9.27 us
    pallas_call x1, Pallas kernels, on_device(): pl.pallas_call(push_kernel, out_shape=jax.ShapeDtypeStruct((2 * EMB, 128)...  7.66 us
    unnamed x96, local copies, waits for them, and re-layouts  6.39 us
    pallas_call x1, Pallas kernels, on_device(): pl.pallas_call(transport_kernel, out_shape=(tiles, jax.ShapeDtypeStruct((...  4.99 us
    pallas_call x1, Pallas kernels, on_device(): pl.pallas_call(kick_kernel, out_shape=(tiles, tiles), in_specs=[vmem()] *...  4.48 us
    ppermute x1, waiting for transfers between devices, on_device(): lax.ppermute(edge_down, RAD, [(i + 1, i) for i in range(rad_count - 1)])  4.22 us
  transfers between devices with their start and end apart: 29, of which 10 were waited for; matrix products, arithmetic and copies ran while one was open for 9% of the time, Pallas kernels for 21%

commit v1 on v0

--- a/solution.py
+++ b/solution.py
@@ -71,7 +71,7 @@
         lift.astype(np.float32),
         drop.astype(np.float32),
         vectors.astype(np.float32),
-        decays,
+        np.tile((decays * ROWS).astype(np.float32).reshape(4, 128), (2, 1)),
     )
 
 
@@ -335,22 +335,17 @@
             azim_ref[g, where, :] = azim[g]
 
 
-def push_kernel(
-    members_ref, radius_ref, angles_ref, dens_ref, out_ref,
-    mass_ref,
-):
+def push_kernel(members_ref, radius_ref, angles_ref, dens_ref, out_ref, mass_ref, chord_ref):
     sector = lax.axis_index(AZ)
     radius = radius_ref[...]
     pieces = [radius[8 * g : 8 * g + 8] for g in range(GROUPS)]
-    twice = [2.0 * piece for piece in pieces]
+    halves = [0.5 / piece for piece in pieces]
     for g in range(GROUPS):
-        area = pieces[g] * pieces[g] * (cell_step * cell_step)
+        scale = lax.rsqrt(2.0 * pieces[g])
+        area = pieces[g] * pieces[g] * (cell_step * cell_step) * (scale * scale * scale)
         mass_ref[g] = (dens_ref[g].reshape(CHUNKS, 8, 128) * area[None]).reshape(SPAN, 128)
     half_cos = angles_ref[sector * 4]
     half_sin = angles_ref[sector * 4 + 1]
-
-    def chunk_row(index, chunk):
-        return jnp.broadcast_to(angles_ref[index, chunk : chunk + 1, :], (8, 128))
 
     @pl.loop(0, EMB)
     def _(member):
@@ -361,24 +356,24 @@
         gaps = []
         for g in range(GROUPS):
             gap = pieces[g] - embryo_radius
-            gaps.append(gap * gap + soft * soft)
+            gaps.append((gap * gap + soft * soft) * halves[g])
         near = half_sin * cosine - half_cos * sine
-        chords = (2.0 * embryo_radius) * (near * near)
+        chord_ref[...] = (2.0 * embryo_radius) * (near * near)
         push_x = jnp.zeros((8, 128), F32)
         push_y = jnp.zeros((8, 128), F32)
         total = jnp.zeros((8, 128), F32)
         for chunk in range(CHUNKS):
-            chord = jnp.broadcast_to(chords[chunk : chunk + 1, :], (8, 128))
-            plain = jnp.zeros((8, 128), F32)
-            moved = jnp.zeros((8, 128), F32)
+            chord = jnp.broadcast_to(chord_ref[chunk : chunk + 1, :], (8, 128))
+            plain, moved = None, None
             for g in range(GROUPS):
-                inverse = lax.rsqrt(gaps[g] + twice[g] * chord)
+                inverse = lax.rsqrt(gaps[g] + chord)
                 cubed = inverse * inverse * inverse
                 term = cubed * mass_ref[g, 8 * chunk : 8 * chunk + 8, :]
-                plain = plain + term
-                moved = moved + pieces[g] * term
-            push_x = push_x + moved * chunk_row(sector * 4 + 2, chunk)
-            push_y = push_y + moved * chunk_row(sector * 4 + 3, chunk)
+                plain = term if g == 0 else plain + term
+                moved = pieces[g] * term if g == 0 else moved + pieces[g] * term
+            row = slice(chunk, chunk + 1)
+            push_x = push_x + moved * jnp.broadcast_to(angles_ref[sector * 4 + 2, row, :], (8, 128))
+            push_y = push_y + moved * jnp.broadcast_to(angles_ref[sector * 4 + 3, row, :], (8, 128))
             total = total + plain
         place_x = embryo_radius * members_ref[4, member]
         place_y = embryo_radius * members_ref[5, member]
@@ -386,7 +381,10 @@
         out_ref[pl.ds(EMB + member, 1), :] = jnp.sum(push_y - place_y * total, axis=0, keepdims=True)
 
 
-def moment_kernel(a_ref, b_ref, c_ref, d_ref, push_ref, lift_ref, drop_ref, vectors_ref, spectra_ref, packed_ref):
+def moment_kernel(
+    a_ref, b_ref, c_ref, d_ref, push_a_ref, push_b_ref, push_c_ref, push_d_ref,
+    lift_ref, drop_ref, vectors_ref, spectra_ref, packed_ref,
+):
     spectra = (a_ref[...] + b_ref[...]) + (c_ref[...] + d_ref[...])
     spectra_ref[...] = spectra
     factor = vectors_ref[0:1, :]
@@ -395,22 +393,46 @@
     for part in range(4):
         packed_ref[part : part + 1, :] = up[:, 128 * part : 128 * part + 128]
         packed_ref[4 + part : 5 + part, :] = down[:, 128 * part : 128 * part + 128]
-    packed_ref[8:72, :] = push_ref[...]
+    push = (push_a_ref[...] + push_b_ref[...]) + (push_c_ref[...] + push_d_ref[...])
+    push = jnp.broadcast_to(jnp.sum(push, axis=1, keepdims=True), (2 * EMB, 128))
+    row = lax.broadcasted_iota(jnp.int32, (2 * EMB, 128), 0)
+    lane = lax.broadcasted_iota(jnp.int32, (2 * EMB, 128), 1)
+    push = jnp.sum(jnp.where(row == lane, push, 0.0), axis=0, keepdims=True)
+    packed_ref[8:16, :] = jnp.broadcast_to(push, (8, 128))
 
 
 def kick_kernel(
-    spectra_ref, terms_ref_0, terms_ref_1, terms_ref_2, terms_ref_3, terms_ref_4, terms_ref_5, terms_ref_6,
-    weights_ref, radius_ref, vectors_ref, lift_ref, drop_ref, twiddle_ref, high_ref, low_ref,
+    spectra_ref, near_1_ref, near_2_ref, near_3_ref, other_ref, distant_1_ref, distant_2_ref, distant_3_ref,
+    eight_ref, rate_ref, radius_ref, vectors_ref, lift_ref, drop_ref, twiddle_ref, high_ref, low_ref,
     radial_ref, azim_ref, vrad_ref, vphi_ref,
-    out_radial_ref, out_azim_ref,
+    out_radial_ref, out_azim_ref, out_push_ref,
     lower_ref, upper_ref,
 ):
-    terms = (
-        terms_ref_0, terms_ref_1, terms_ref_2, terms_ref_3, terms_ref_4, terms_ref_5, terms_ref_6,
-    )
+    x, z, y = (lax.axis_index(name) for name in RAD)
+    counts = []
+    for shift in range(1, 4):
+        source = (y - shift) % 4
+        counts.append((y - 1 - source, source - y - 1))
+    counts.append((jnp.where(z == 1, y, -1), jnp.where(z == 0, 3 - y, -1)))
+    for shift in range(1, 4):
+        gap = x - (x - shift) % 4
+        within = 4 * z + y
+        counts.append(
+            (
+                jnp.where(gap > 0, 8 * (gap - 1) + within, -1),
+                jnp.where(gap < 0, 8 * (-gap - 1) + 7 - within, -1),
+            )
+        )
+    distant = (distant_1_ref, distant_2_ref, distant_3_ref)
+    row = lax.broadcasted_iota(jnp.int32, (8, 128), 0)
     outside = jnp.zeros((8, 128), F32)
-    for index, term in enumerate(terms):
-        outside += weights_ref[index] * term[0:8, :]
+    for count, term in zip(counts, (near_1_ref, near_2_ref, near_3_ref, other_ref) + distant):
+        many = jnp.where(row < 4, count[0], count[1])
+        weight = jnp.exp(-rate_ref[...] * jnp.maximum(many, 0).astype(F32))
+        outside += jnp.where(many >= 0, weight, 0.0) * term[0:8, :]
+    push = (eight_ref[8:9, :] + distant[1][8:9, :]) + (distant[0][8:9, :] + distant[2][8:9, :])
+    out_push_ref[0:1, :] = push[:, :EMB]
+    out_push_ref[1:2, :] = push[:, EMB : 2 * EMB]
     lower = jnp.concatenate([outside[k : k + 1] for k in range(4)], axis=1)
     upper = jnp.concatenate([outside[k : k + 1] for k in range(4, 8)], axis=1)
     factor = vectors_ref[0:1, :]
@@ -465,42 +487,9 @@
     return lax.optimization_barrier((value, *others))[0]
 
 
-def stage_weights(decays):
-    x, z, y = (lax.axis_index(name) for name in RAD)
-    rate = jnp.asarray((decays * ROWS).astype(np.float32)).reshape(4, 128)
-    ones = jnp.ones((64, 128), F32)
-
-    def decayed(count):
-        return jnp.where(count >= 0, jnp.exp(-rate * jnp.maximum(count, 0).astype(F32)), 0.0)
-
-    joins, sides = [], []
-    for shift in range(4):
-        source = (y - shift) % 4
-        joins.append(jnp.concatenate([decayed(3 - source), decayed(source), ones]))
-        if shift:
-            sides.append(jnp.concatenate([decayed(y - 1 - source), decayed(source - y - 1)]))
-    pair = []
-    for source in (z, 1 - z):
-        pair.append(jnp.concatenate([decayed(4 * (1 - source)), decayed(4 * source), ones]))
-    never = jnp.int32(-1)
-    sides.append(
-        jnp.concatenate(
-            [decayed(jnp.where(z == 1, y, never)), decayed(jnp.where(z == 0, 3 - y, never))]
-        )
-    )
-    for shift in range(1, 4):
-        source = (x - shift) % 4
-        gap = x - source
-        within = 4 * z + y
-        sides.append(
-            jnp.concatenate(
-                [
-                    decayed(jnp.where(gap > 0, 8 * (gap - 1) + within, never)),
-                    decayed(jnp.where(gap < 0, 8 * (-gap - 1) + 7 - within, never)),
-                ]
-            )
-        )
-    return jnp.stack(joins), jnp.stack(pair), jnp.stack(sides)
+def decayed(rate, up_count, down_count):
+    count = jnp.stack([up_count] * 4 + [down_count] * 4 + [0] * 8).astype(F32)
+    return jnp.exp(-rate * count[:, None])
 
 
 def on_device(
@@ -512,7 +501,7 @@
     planetesimal_angle_bin,
     planetesimal_weights,
 ):
-    (basis_high, basis_low), (back_high, back_low), twiddle, angles, lift, drop, vectors, decays = (
+    (basis_high, basis_low), (back_high, back_low), twiddle, angles, lift, drop, vectors, rate = (
         constant_tables()
     )
     tiles = jax.ShapeDtypeStruct((GROUPS, SPAN, 128), F32)
@@ -524,7 +513,7 @@
     begins = jnp.concatenate([surface_mass[:, :128], leftover_angular_drift[:, :128]])
     left = across(ends, AZ, lambda i: (i + 1) % 4)
     right = across(begins, AZ, lambda i: (i - 1) % 4)
-    vrad_cross = across(vrad, AZ, lambda i: i ^ 2)
+    vrad_cross = across(after(vrad, left, right), AZ, lambda i: i ^ 2)
     vrad_mate = across(vrad, AZ, lambda i: i ^ 1)
 
     cell = np.float32(cell_step)
@@ -541,7 +530,6 @@
             jnp.sin(embryo_angles),
         ]
     )
-    joins, pair, sides = stage_weights(decays)
 
     dens_two, edge_up, edge_down = pl.pallas_call(
         azimuth_kernel,
@@ -565,7 +553,7 @@
     )
 
     dens_mate = across(dens_two, AZ, lambda i: i ^ 1)
-    dens_two_later = after(dens_two, vrad_cross)
+    dens_two_later = after(dens_two, vrad_cross, edge_low, edge_high)
     dens_cross = across(dens_two_later, AZ, lambda i: i ^ 2)
     vrad_far = across(vrad_cross, AZ, lambda i: i ^ 1)
     vrad_one = shifted(angular_offsets, vrad, vrad_mate, vrad_cross, vrad_far, "shift_vrad")
@@ -581,6 +569,9 @@
         name="field",
     )(members, radius, angles)
 
+    dens_cross = after(
+        dens_cross, edges_cross, edges_mate, edges_far, dens_mate, vrad_one, radial_field
+    )
     dens_far = across(dens_cross, AZ, lambda i: i ^ 1)
     vphi_later = after(vphi, dens_cross)
     vphi_cross = across(vphi_later, AZ, lambda i: i ^ 2)
@@ -608,60 +599,65 @@
         vrad_one, basis_high, basis_low, twiddle,
     )
 
-    others = [across(part, AZ, lambda i, k=k: i ^ k) for k in (2, 3, 1)]
     push = pl.pallas_call(
         push_kernel,
         out_shape=jax.ShapeDtypeStruct((2 * EMB, 128), F32),
         in_specs=[smem(), vmem(), vmem(), vmem()],
         out_specs=vmem(),
-        scratch_shapes=[pltpu.VMEM((GROUPS, SPAN, 128), F32)],
+        scratch_shapes=[pltpu.VMEM((GROUPS, SPAN, 128), F32), pltpu.VMEM((CHUNKS, 128), F32)],
         compiler_params=params(),
         cost_estimate=cost(6),
         name="push",
     )(members, radius, angles, transported)
-
-    packed_shape = jax.ShapeDtypeStruct((72, 128), F32)
+    part_later, push_later = lax.optimization_barrier((part, push, vphi_cross))[:2]
+    part_others = [across(part_later, AZ, lambda i, k=k: i ^ k) for k in (2, 3, 1)]
+    push_others = [across(push_later, AZ, lambda i, k=k: i ^ k) for k in (2, 3, 1)]
+
     spectra, packed = pl.pallas_call(
         moment_kernel,
-        out_shape=(jax.ShapeDtypeStruct((ROWS, 2 * MODES), F32), packed_shape),
-        in_specs=[vmem()] * 8,
+        out_shape=(
+            jax.ShapeDtypeStruct((ROWS, 2 * MODES), F32),
+            jax.ShapeDtypeStruct((16, 128), F32),
+        ),
+        in_specs=[vmem()] * 11,
         out_specs=(vmem(), vmem()),
         compiler_params=params(),
         cost_estimate=cost(1),
         name="moments",
-    )(part, *others, push, lift, drop, vectors)
+    )(part, *part_others, push, *push_others, lift, drop, vectors)
 
     def from_shift(value, axis, shift):
         return across(value, axis, lambda i: (i + shift) % lax.axis_size(axis))
 
+    _, z, y = (lax.axis_index(name) for name in RAD)
+    rates = np.concatenate([rate, np.zeros((8, 128), np.float32)])
     near = [from_shift(packed, "rad_2", shift) for shift in (1, 2, 3)]
-    four = joins[0] * packed + joins[1] * near[0] + joins[2] * near[1] + joins[3] * near[2]
+    parts = []
+    for shift, piece in enumerate([packed] + near):
+        source = (y - shift) % 4
+        parts.append(decayed(rates, 3 - source, source) * piece)
+    four = (parts[0] + parts[2]) + (parts[1] + parts[3])
     other = from_shift(four, "rad_1", 1)
-    eight = pair[0] * four + pair[1] * other
+    eight = decayed(rates, 4 * (1 - z), 4 * z) * four + decayed(rates, 4 * z, 4 * (1 - z)) * other
     distant = [from_shift(eight, "rad_0", shift) for shift in (1, 2, 3)]
-    push_part = eight[8:] + distant[0][8:] + distant[1][8:] + distant[2][8:]
-    push_others = [across(push_part, AZ, lambda i, k=k: i ^ k) for k in (2, 3, 1)]
 
     vphi_far = across(vphi_cross, AZ, lambda i: i ^ 1)
     vphi_one = shifted(angular_offsets, vphi_later, vphi_mate, vphi_cross, vphi_far, "shift_vphi")
 
-    kicked_radial, kicked_azim = pl.pallas_call(
+    kicked_radial, kicked_azim, embryo_disk_acceleration = pl.pallas_call(
         kick_kernel,
-        out_shape=(tiles, tiles),
-        in_specs=[vmem()] * 20,
-        out_specs=(vmem(), vmem()),
+        out_shape=(tiles, tiles, jax.ShapeDtypeStruct((2, EMB), F32)),
+        in_specs=[vmem()] * 21,
+        out_specs=(vmem(), vmem(), vmem()),
         scratch_shapes=[pltpu.VMEM((ROWS, 2 * MODES), F32)] * 2,
         compiler_params=params(),
         cost_estimate=cost(5),
         name="kick",
     )(
-        spectra, *near, other, *distant,
-        sides, radius, vectors, lift, drop, twiddle, back_high, back_low,
+        spectra, *near, other, *distant, eight,
+        rate, radius, vectors, lift, drop, twiddle, back_high, back_low,
         radial_field, azim_field, vrad_one, vphi_one,
     )
-
-    push_sum = (push_part + push_others[0]) + (push_others[1] + push_others[2])
-    embryo_disk_acceleration = jnp.sum(push_sum, axis=1).reshape(2, EMB)
     return (
         from_tiles(transported),
         from_tiles(kicked_radial),

time: 123 us -> 99.1 us (0.81)
  waiting for transfers between devices: 32.8 us -> 11.3 us
  other arithmetic: 7.1 us -> 0.36 us
  starting transfers between devices: 37.5 us -> 41.1 us
  local copies, waits for them, and re-layouts: 9.71 us -> 11.2 us
    ppermute x27, waiting for transfers between devices: 27.6 us -> 10.3 us  [across(): lax.ppermute(value, axis, [(source, target(source)) for source in range(c...]
    ppermute x1, waiting for transfers between devices: 4.22 us -> 0.01 us  [on_device(): lax.ppermute(edge_down, RAD, [(i + 1, i) for i in range(rad_count - 1)])]
    unnamed x6 -> x0, other arithmetic: 3.57 us -> none
    ppermute x27, starting transfers between devices: 32.7 us -> 35.1 us  [across(): lax.ppermute(value, axis, [(source, target(source)) for source in range(c...]
    select_n x3 -> x0, other arithmetic: 1.89 us -> none  [decayed(): jnp.where(count >= 0, jnp.exp(-rate * jnp.maximum(count, 0).astype(F32)),...]
    pallas_call x1, Pallas kernels: 7.66 us -> 6.29 us  [on_device(): pl.pallas_call(push_kernel, out_shape=jax.ShapeDtypeStruct((2 * EMB, 128)...]
    reshape x1 -> x0, local copies, waits for them, and re-layouts: 1.33 us -> none  [on_device(): embryo_disk_acceleration = jnp.sum(push_sum, axis=1).reshape(2, EMB)]
    unnamed x96 -> x80, local copies, waits for them, and re-layouts: 6.39 us -> 7.44 us
  transfers between devices with their start and end apart: 29 -> 29, of which waited for: 10 -> 9; matrix products, arithmetic and copies ran while one was open for 9% -> 3% of each run, Pallas kernels for 21% -> 28%
where the time goes in v1:
time: 99.1 us; the launch traced here: 98.2 us
  starting transfers between devices  41.1 us (41%)
  Pallas kernels  31.7 us (32%)
  waiting for transfers between devices  11.3 us (11%)
  local copies, waits for them, and re-layouts  11.2 us (11%)
  between operations  2.5 us (3%)
    ppermute x27, starting transfers between devices, across(): lax.ppermute(value, axis, [(source, target(source)) for source in range(c...  35.1 us
    ppermute x27, waiting for transfers between devices, across(): lax.ppermute(value, axis, [(source, target(source)) for source in range(c...  10.3 us
    pallas_call x1, Pallas kernels, on_device(): pl.pallas_call(field_kernel, out_shape=(tiles, tiles), in_specs=[smem(),...  9.28 us
    unnamed x80, local copies, waits for them, and re-layouts  7.44 us
    pallas_call x1, Pallas kernels, on_device(): pl.pallas_call(push_kernel, out_shape=jax.ShapeDtypeStruct((2 * EMB, 128)...  6.29 us
    pallas_call x2, Pallas kernels, shifted(): pl.pallas_call(shift_kernel, out_shape=jax.ShapeDtypeStruct((GROUPS, SPAN...  4.89 us
    pallas_call x1, Pallas kernels, on_device(): pl.pallas_call(transport_kernel, out_shape=(tiles, jax.ShapeDtypeStruct((...  4.88 us
    ppermute x1, starting transfers between devices, on_device(): lax.ppermute(edge_up, RAD, [(i, i + 1) for i in range(rad_count - 1)])  4.55 us
  transfers between devices with their start and end apart: 29, of which 9 were waited for; matrix products, arithmetic and copies ran while one was open for 3% of the time, Pallas kernels for 28%

profile of v1, /device:TPU:0, one launch (start us, length us, event | category | flops | bytes accessed | tf_op | source)
XLA Modules:
  0.0 98.2 jit_solution(10302653695561143508)
XLA Ops:
  0.6 0.8 fusion
  1.5 1.7 %collective-permute-start.1 = (f32[64,128]{1,0:T(8,128)S(1)}, f32[64,128]{1,0:T(8,128)S(1)}, u32[]{:S(2)}, u32[]{:S(2)}) collective-permute-start(f32[64,128]{1,0:T(8,128)S(1)} %pad_maximum_fusion.2), channel_id=1, source_target_pairs={{0,3},{1,0},{2,1},{3,2},{4,7},{5,4},{6,5},{7,6},{8,11},{9,8},{10,9... | collective-permute-start | bytes 98312 | tf_op jit(solution)/shard_map/ppermute | solution.py:483
  3.2 1.6 %collective-permute-done.left_ref = f32[64,128]{1,0:T(8,128)S(1)} collective-permute-done((f32[64,128]{1,0:T(8,128)S(1)}, f32[64,128]{1,0:T(8,128)S(1)}, u32[]{:S(2)}, u32[]{:S(2)}) %collective-permute-start) | collective-permute-done | bytes 32800 | tf_op jit(solution)/shard_map/ppermute | solution.py:483
  4.8 2.0 %collective-permute-start.5 = (f32[4,256,128]{2,1,0:T(8,128)}, f32[4,256,128]{2,1,0:T(8,128)S(1)}, u32[]{:S(2)}, u32[]{:S(2)}) collective-permute-start(f32[4,256,128]{2,1,0:T(8,128)} %bitcast.8.vrad_ref.own_ref), channel_id=1, source_target_pairs={{0,2},{1,3},{2,0},{3,1},{4,6},{5,7},{6,4},{7,5},{8,10},{9,11},{10,... | collective-permute-start | bytes 1572872 | tf_op jit(solution)/shard_map/ppermute | solution.py:483
  6.9 0.7 copy-done.30
  7.5 1.0 %copy-done = f32[32,4096]{1,0:T(8,128)S(1)} copy-done((f32[32,4096]{1,0:T(8,128)S(1)}, f32[32,4096]{1,0:T(8,128)}, u32[]{:S(2)}) %copy-start) | copy-done | bytes 524312
  8.6 1.0 %copy-done.3 = f32[32,4096]{1,0:T(8,128)S(1)} copy-done((f32[32,4096]{1,0:T(8,128)S(1)}, f32[32,4096]{1,0:T(8,128)}, u32[]{:S(2)}) %copy-start.3) | copy-done | bytes 524312
  9.6 2.5 %azimuth.1 = (f32[4,256,128]{2,1,0:T(8,128)}, f32[72,128]{1,0:T(8,128)S(1)}, f32[72,128]{1,0:T(8,128)S(1)}) custom-call(f32[4,256,128]{2,1,0:T(8,128)S(1)} %bitcast.58, f32[4,256,128]{2,1,0:T(8,128)S(1)} %bitcast.54, f32[4,256,128]{2,1,0:T(8,128)} %bitcast.8.vrad_ref.own_ref, f32[64,128]{1,0:T(8,128)S(1)} %collective-permute-done.left_ref, ...), custom_call_target="tpu_custom_call" | custom-call | flops 1000000 | bytes 2500000 | tf_op jit(solution)/shard_map/azimuth/pallas_call | solution.py:534
  12.1 1.4 %collective-permute-start.3 = (f32[72,128]{1,0:T(8,128)S(1)}, f32[72,128]{1,0:T(8,128)S(1)}, u32[]{:S(2)}, u32[]{:S(2)}) collective-permute-start(f32[72,128]{1,0:T(8,128)S(1)} %get-tuple-element.23), channel_id=1, source_target_pairs={{4,0},{8,4},{12,8},{16,12},{20,16},{24,20},{28,24},{32,28},{36,32}... | collective-permute-start | bytes 110600 | tf_op jit(solution)/shard_map/ppermute | solution.py:546
  13.6 4.5 %collective-permute-start.2 = (f32[72,128]{1,0:T(8,128)S(1)}, f32[72,128]{1,0:T(8,128)S(1)}, u32[]{:S(2)}, u32[]{:S(2)}) collective-permute-start(f32[72,128]{1,0:T(8,128)S(1)} %get-tuple-element.22), channel_id=1, source_target_pairs={{0,4},{4,8},{8,12},{12,16},{16,20},{20,24},{24,28},{28,32},{32,36}... | collective-permute-start | bytes 110600 | tf_op jit(solution)/shard_map/ppermute | solution.py:545
  18.2 0.5 collective-permute-start.4
  18.7 1.0 %collective-permute-done.2 = f32[72,128]{1,0:T(8,128)S(1)} collective-permute-done((f32[72,128]{1,0:T(8,128)S(1)}, f32[72,128]{1,0:T(8,128)S(1)}, u32[]{:S(2)}, u32[]{:S(2)}) %collective-permute-start.2) | collective-permute-done | bytes 36896 | tf_op jit(solution)/shard_map/ppermute | solution.py:545
  19.7 1.5 %collective-permute-start.6 = (f32[4,256,128]{2,1,0:T(8,128)}, f32[4,256,128]{2,1,0:T(8,128)}, u32[]{:S(2)}, u32[]{:S(2)}) collective-permute-start(f32[4,256,128]{2,1,0:T(8,128)} %get-tuple-element.26.own_ref), channel_id=1, source_target_pairs={{0,2},{1,3},{2,0},{3,1},{4,6},{5,7},{6,4},{7,5},{8,10},{9,11},{10,... | collective-permute-start | bytes 1572872 | tf_op jit(solution)/shard_map/ppermute | solution.py:483
  21.5 0.6 collective-permute-start.7
  22.3 0.9 collective-permute-done.11.far_ref
  23.2 0.8 copy-done.5
  24.0 0.5 collective-permute-start.9
  24.6 9.3 %field.1 = (f32[4,256,128]{2,1,0:T(8,128)S(1)}, f32[4,256,128]{2,1,0:T(8,128)S(1)}) custom-call(f32[6,32]{1,0:T(8,128)S(1)} %stack.54.members_ref, f32[32,128]{1,0:T(8,128)S(1)} %broadcast_in_dim.2.radius_ref, f32[16,32,128]{2,1,0:T(8,128)S(1)} %copy-done.2), custom_call_target="tpu_custom_call" | custom-call | flops 6000000 | bytes 15000000 | tf_op jit(solution)/shard_map/field/pallas_call | solution.py:561
  33.9 1.0 %copy-done.6 = f32[4,256,128]{2,1,0:T(8,128)S(1)} copy-done((f32[4,256,128]{2,1,0:T(8,128)S(1)}, f32[4,256,128]{2,1,0:T(8,128)}, u32[]{:S(2)}) %copy-start.6) | copy-done | bytes 524312
  34.9 2.5 %shift_vrad.1.vrad_ref = f32[4,256,128]{2,1,0:T(8,128)S(1)} custom-call(s32[32]{0:T(128)S(1)} %copy-done.31, f32[4,256,128]{2,1,0:T(8,128)} %bitcast.8.vrad_ref.own_ref, f32[4,256,128]{2,1,0:T(8,128)S(1)} %collective-permute-done.10.mate_ref, f32[4,256,128]{2,1,0:T(8,128)S(1)} %collective-permute-done.5.cross_ref, f32[4,256,128]{2,1,0:T(8,128)S(1)} %copy-done.6), custom_call_target="tpu_custom_call" | custom-call | flops 2000000 | bytes 5000000 | tf_op jit(solution)/shard_map/shift_vrad/pallas_call | solution.py:175
  37.8 1.4 %collective-permute-start.13 = (f32[4,256,128]{2,1,0:T(8,128)S(1)}, f32[4,256,128]{2,1,0:T(8,128)S(1)}, u32[]{:S(2)}, u32[]{:S(2)}) collective-permute-start(f32[4,256,128]{2,1,0:T(8,128)S(1)} %bitcast.55), channel_id=1, source_target_pairs={{0,2},{1,3},{2,0},{3,1},{4,6},{5,7},{6,4},{7,5},{8,10},{9,11},{10,... | collective-permute-start | bytes 1572872 | tf_op jit(solution)/shard_map/ppermute | solution.py:483
  39.2 1.2 %slice.33 = f32[1,1]{1,0:T(1,128)} slice(f32[72,128]{1,0:T(8,128)} %copy-done.35), slice={[64:65], [0:1]} | slice | bytes 8 | tf_op jit(solution)/shard_map/slice | solution.py:549
  41.0 1.2 %slice.32 = f32[1,1]{1,0:T(1,128)} slice(f32[72,128]{1,0:T(8,128)} %copy-done.36), slice={[64:65], [0:1]} | slice | bytes 8 | tf_op jit(solution)/shard_map/slice | solution.py:549
  43.0 4.9 %transport.1 = (f32[4,256,128]{2,1,0:T(8,128)}, f32[32,512]{1,0:T(8,128)S(1)}) custom-call(s32[34]{0:T(128)S(1)} %pad_add_fusion.offs_ref, f32[4,256,128]{2,1,0:T(8,128)} %get-tuple-element.26.own_ref, f32[4,256,128]{2,1,0:T(8,128)} %collective-permute-done.4.mate_ref, f32[4,256,128]{2,1,0:T(8,128)} %collective-permute-done.6.cross_ref, ...), custom_call_target="tpu_custom_call" | custom-call | flops 3000000 | bytes 7500000 | tf_op jit(solution)/shard_map/transport/pallas_call | solution.py:580
  47.9 1.0 %copy-done.4 = f32[4,256,128]{2,1,0:T(8,128)S(1)} copy-done((f32[4,256,128]{2,1,0:T(8,128)S(1)}, f32[4,256,128]{2,1,0:T(8,128)}, u32[]{:S(2)}) %copy-start.4) | copy-done | bytes 524312
  49.0 6.3 %push.1.push_a_ref = f32[64,128]{1,0:T(8,128)S(1)} custom-call(f32[6,32]{1,0:T(8,128)S(1)} %copy-done.21, f32[32,128]{1,0:T(8,128)S(1)} %broadcast_in_dim.2.radius_ref, f32[16,32,128]{2,1,0:T(8,128)S(1)} %copy-done.2, f32[4,256,128]{2,1,0:T(8,128)S(1)} %copy-done.4), custom_call_target="tpu_custom_call" | custom-call | flops 6000000 | bytes 15000000 | tf_op jit(solution)/shard_map/push/pallas_call | solution.py:602
  55.3 0.7 collective-permute-start.17
  55.9 0.6 collective-permute-start.18
  56.5 0.9 collective-permute-start.19
  57.5 0.6 collective-permute-start.14
  58.1 0.7 collective-permute-start.15
  58.8 0.7 collective-permute-done.17.push_b_ref
  59.6 0.5 collective-permute-start.27
  60.2 2.2 %collective-permute-done.14.b_ref = f32[32,512]{1,0:T(8,128)S(1)} collective-permute-done((f32[32,512]{1,0:T(8,128)S(1)}, f32[32,512]{1,0:T(8,128)S(1)}, u32[]{:S(2)}, u32[]{:S(2)}) %collective-permute-start.14) | collective-permute-done | bytes 65568 | tf_op jit(solution)/shard_map/ppermute | solution.py:483
  62.6 0.6 copy-done.18
  63.2 2.2 %collective-permute-start.20 = (f32[16,128]{1,0:T(8,128)S(1)}, f32[16,128]{1,0:T(8,128)S(1)}, u32[]{:S(2)}, u32[]{:S(2)}) collective-permute-start(f32[16,128]{1,0:T(8,128)S(1)} %get-tuple-element.35), channel_id=1, source_target_pairs={{0,4},{4,8},{8,12},{12,0},{1,5},{5,9},{9,13},{13,1},{2,6},{6,10},{... | collective-permute-start | bytes 24584 | tf_op jit(solution)/shard_map/ppermute | solution.py:483
  65.4 5.7 %collective-permute-start.21 = (f32[16,128]{1,0:T(8,128)S(1)}, f32[16,128]{1,0:T(8,128)S(1)}, u32[]{:S(2)}, u32[]{:S(2)}) collective-permute-start(f32[16,128]{1,0:T(8,128)S(1)} %get-tuple-element.35), channel_id=1, source_target_pairs={{0,8},{4,12},{8,0},{12,4},{1,9},{5,13},{9,1},{13,5},{2,10},{6,14},... | collective-permute-start | bytes 24584 | tf_op jit(solution)/shard_map/ppermute | solution.py:483
  71.5 1.3 %collective-permute-done.21.near_2_ref = f32[16,128]{1,0:T(8,128)S(1)} collective-permute-done((f32[16,128]{1,0:T(8,128)S(1)}, f32[16,128]{1,0:T(8,128)S(1)}, u32[]{:S(2)}, u32[]{:S(2)}) %collective-permute-start.21) | collective-permute-done | bytes 8224 | tf_op jit(solution)/shard_map/ppermute | solution.py:483
  72.8 1.9 %collective-permute-done.22.near_3_ref = f32[16,128]{1,0:T(8,128)S(1)} collective-permute-done((f32[16,128]{1,0:T(8,128)S(1)}, f32[16,128]{1,0:T(8,128)S(1)}, u32[]{:S(2)}, u32[]{:S(2)}) %collective-permute-start.22) | collective-permute-done | bytes 8224 | tf_op jit(solution)/shard_map/ppermute | solution.py:483
  74.9 0.5 copy-done.26
  75.3 4.5 %collective-permute-start.23 = (f32[16,128]{1,0:T(8,128)S(1)}, f32[16,128]{1,0:T(8,128)S(1)}, u32[]{:S(2)}, u32[]{:S(2)}) collective-permute-start(f32[16,128]{1,0:T(8,128)S(1)} %add_add_fusion), channel_id=1, source_target_pairs={{0,16},{16,0},{1,17},{17,1},{2,18},{18,2},{3,19},{19,3},{4,20},{20... | collective-permute-start | bytes 24584 | tf_op jit(solution)/shard_map/ppermute | solution.py:483
  80.0 1.4 %collective-permute-done.23.other_ref = f32[16,128]{1,0:T(8,128)S(1)} collective-permute-done((f32[16,128]{1,0:T(8,128)S(1)}, f32[16,128]{1,0:T(8,128)S(1)}, u32[]{:S(2)}, u32[]{:S(2)}) %collective-permute-start.23) | collective-permute-done | bytes 8224 | tf_op jit(solution)/shard_map/ppermute | solution.py:483
  81.6 0.6 copy-done.28
  82.2 5.5 %collective-permute-start.24 = (f32[16,128]{1,0:T(8,128)S(1)}, f32[16,128]{1,0:T(8,128)S(1)}, u32[]{:S(2)}, u32[]{:S(2)}) collective-permute-start(f32[16,128]{1,0:T(8,128)S(1)} %multiply_add_fusion.eight_ref), channel_id=1, source_target_pairs={{0,32},{32,64},{64,96},{96,0},{1,33},{33,65},{65,97},{97,1},{2,34}... | collective-permute-start | bytes 24584 | tf_op jit(solution)/shard_map/ppermute | solution.py:483
  87.7 3.0 %collective-permute-start.25 = (f32[16,128]{1,0:T(8,128)S(1)}, f32[16,128]{1,0:T(8,128)S(1)}, u32[]{:S(2)}, u32[]{:S(2)}) collective-permute-start(f32[16,128]{1,0:T(8,128)S(1)} %multiply_add_fusion.eight_ref), channel_id=1, source_target_pairs={{0,64},{32,96},{64,0},{96,32},{1,65},{33,97},{65,1},{97,33},{2,66}... | collective-permute-start | bytes 24584 | tf_op jit(solution)/shard_map/ppermute | solution.py:483
  90.7 1.1 %collective-permute-start.26 = (f32[16,128]{1,0:T(8,128)S(1)}, f32[16,128]{1,0:T(8,128)S(1)}, u32[]{:S(2)}, u32[]{:S(2)}) collective-permute-start(f32[16,128]{1,0:T(8,128)S(1)} %multiply_add_fusion.eight_ref), channel_id=1, source_target_pairs={{0,96},{32,0},{64,32},{96,64},{1,97},{33,1},{65,33},{97,65},{2,98}... | collective-permute-start | bytes 24584 | tf_op jit(solution)/shard_map/ppermute | solution.py:483
  91.9 2.4 %shift_vphi.1.vphi_ref = f32[4,256,128]{2,1,0:T(8,128)S(1)} custom-call(s32[32]{0:T(128)S(1)} %copy-done.32, f32[4,256,128]{2,1,0:T(8,128)S(1)} %bitcast.57, f32[4,256,128]{2,1,0:T(8,128)S(1)} %collective-permute-done.27.mate_ref, f32[4,256,128]{2,1,0:T(8,128)S(1)} %collective-permute-done.13.cross_ref, f32[4,256,128]{2,1,0:T(8,128)} %collective-permute-done.28.far_ref), custom_call_target="tpu_custom_call" | custom-call | flops 2000000 | bytes 5000000 | tf_op jit(solution)/shard_map/shift_vphi/pallas_call | solution.py:175
  94.4 3.7 %kick.1 = (f32[4,256,128]{2,1,0:T(8,128)}, f32[4,256,128]{2,1,0:T(8,128)}, f32[2,32]{1,0:T(2,128)}) custom-call(f32[32,512]{1,0:T(8,128)S(1)} %copy-done.19, f32[16,128]{1,0:T(8,128)S(1)} %copy-done.23, f32[16,128]{1,0:T(8,128)S(1)} %copy-done.25, f32[16,128]{1,0:T(8,128)S(1)} %copy-done.27, f32[16,128]{1,0:T(8,128)S(1)} %copy-done.29, ...), custom_call_target="tpu_custom_call" | custom-call | flops 5000000 | bytes 12500000 | tf_op jit(solution)/shard_map/kick/pallas_call | solution.py:647
  (127 shorter events, 2.2 us)
Async XLA Ops:
  1.4 3.4 %collective-permute-start = (f32[64,128]{1,0:T(8,128)S(1)}, f32[64,128]{1,0:T(8,128)S(1)}, u32[]{:S(2)}, u32[]{:S(2)}) collective-permute-start(f32[64,128]{1,0:T(8,128)S(1)} %pad_maximum_fusion.1), channel_id=1, source_target_pairs={{0,1},{1,2},{2,3},{3,0},{4,5},{5,6},{6,7},{7,4},{8,9},{9,10},{10,1... | collective-permute-start | bytes 98312 | tf_op jit(solution)/shard_map/ppermute | solution.py:483
  1.5 3.3 %collective-permute-start.1 = (f32[64,128]{1,0:T(8,128)S(1)}, f32[64,128]{1,0:T(8,128)S(1)}, u32[]{:S(2)}, u32[]{:S(2)}) collective-permute-start(f32[64,128]{1,0:T(8,128)S(1)} %pad_maximum_fusion.2), channel_id=1, source_target_pairs={{0,3},{1,0},{2,1},{3,2},{4,7},{5,4},{6,5},{7,6},{8,11},{9,8},{10,9... | collective-permute-start | bytes 98312 | tf_op jit(solution)/shard_map/ppermute | solution.py:483
  4.8 14.9 %collective-permute-start.5 = (f32[4,256,128]{2,1,0:T(8,128)}, f32[4,256,128]{2,1,0:T(8,128)S(1)}, u32[]{:S(2)}, u32[]{:S(2)}) collective-permute-start(f32[4,256,128]{2,1,0:T(8,128)} %bitcast.8.vrad_ref.own_ref), channel_id=1, source_target_pairs={{0,2},{1,3},{2,0},{3,1},{4,6},{5,7},{6,4},{7,5},{8,10},{9,11},{10,... | collective-permute-start | bytes 1572872 | tf_op jit(solution)/shard_map/ppermute | solution.py:483
  9.6 11.7 %copy-start.39 = (s32[32]{0:T(128)S(1)}, s32[32]{0:T(128)}, u32[]{:S(2)}) copy-start(s32[32]{0:T(128)} %param.27) | copy-start | bytes 388
  9.6 11.7 %copy-start.38 = (s32[32]{0:T(128)S(1)}, s32[32]{0:T(128)}, u32[]{:S(2)}) copy-start(s32[32]{0:T(128)} %param.28) | copy-start | bytes 388
  9.6 11.8 %copy-start.37 = (f32[32]{0:T(128)S(1)}, f32[32]{0:T(128)}, u32[]{:S(2)}) copy-start(f32[32]{0:T(128)} %param.29) | copy-start | bytes 388
  12.1 12.4 %copy-start.2 = (f32[16,32,128]{2,1,0:T(8,128)S(1)}, f32[16,32,128]{2,1,0:T(8,128)}, u32[]{:S(2)}) copy-start(f32[16,32,128]{2,1,0:T(8,128)} %constant.88.clone.angles_ref) | copy-start | bytes 786436
  12.1 6.6 %collective-permute-start.3 = (f32[72,128]{1,0:T(8,128)S(1)}, f32[72,128]{1,0:T(8,128)S(1)}, u32[]{:S(2)}, u32[]{:S(2)}) collective-permute-start(f32[72,128]{1,0:T(8,128)S(1)} %get-tuple-element.23), channel_id=1, source_target_pairs={{4,0},{8,4},{12,8},{16,12},{20,16},{24,20},{28,24},{32,28},{36,32}... | collective-permute-start | bytes 110600 | tf_op jit(solution)/shard_map/ppermute | solution.py:546
  13.6 6.2 %collective-permute-start.2 = (f32[72,128]{1,0:T(8,128)S(1)}, f32[72,128]{1,0:T(8,128)S(1)}, u32[]{:S(2)}, u32[]{:S(2)}) collective-permute-start(f32[72,128]{1,0:T(8,128)S(1)} %get-tuple-element.22), channel_id=1, source_target_pairs={{0,4},{4,8},{8,12},{12,16},{16,20},{20,24},{24,28},{28,32},{32,36}... | collective-permute-start | bytes 110600 | tf_op jit(solution)/shard_map/ppermute | solution.py:545
  18.1 3.9 %collective-permute-start.10 = (f32[4,256,128]{2,1,0:T(8,128)}, f32[4,256,128]{2,1,0:T(8,128)S(1)}, u32[]{:S(2)}, u32[]{:S(2)}) collective-permute-start(f32[4,256,128]{2,1,0:T(8,128)} %bitcast.8.vrad_ref.own_ref), channel_id=1, source_target_pairs={{0,1},{1,0},{2,3},{3,2},{4,5},{5,4},{6,7},{7,6},{8,9},{9,8},{10,11... | collective-permute-start | bytes 1572872 | tf_op jit(solution)/shard_map/ppermute | solution.py:483
  18.2 19.3 %collective-permute-start.4 = (f32[4,256,128]{2,1,0:T(8,128)}, f32[4,256,128]{2,1,0:T(8,128)}, u32[]{:S(2)}, u32[]{:S(2)}) collective-permute-start(f32[4,256,128]{2,1,0:T(8,128)} %get-tuple-element.26.own_ref), channel_id=1, source_target_pairs={{0,1},{1,0},{2,3},{3,2},{4,5},{5,4},{6,7},{7,6},{8,9},{9,8},{10,11... | collective-permute-start | bytes 1572872 | tf_op jit(solution)/shard_map/ppermute | solution.py:483
  19.7 17.7 %collective-permute-start.6 = (f32[4,256,128]{2,1,0:T(8,128)}, f32[4,256,128]{2,1,0:T(8,128)}, u32[]{:S(2)}, u32[]{:S(2)}) collective-permute-start(f32[4,256,128]{2,1,0:T(8,128)} %get-tuple-element.26.own_ref), channel_id=1, source_target_pairs={{0,2},{1,3},{2,0},{3,1},{4,6},{5,7},{6,4},{7,5},{8,10},{9,11},{10,... | collective-permute-start | bytes 1572872 | tf_op jit(solution)/shard_map/ppermute | solution.py:483
  21.3 1.9 %collective-permute-start.11 = (f32[4,256,128]{2,1,0:T(8,128)S(1)}, f32[4,256,128]{2,1,0:T(8,128)S(1)}, u32[]{:S(2)}, u32[]{:S(2)}) collective-permute-start(f32[4,256,128]{2,1,0:T(8,128)S(1)} %collective-permute-done.5.cross_ref), channel_id=1, source_target_pairs={{0,1},{1,0},{2,3},{3,2},{4,5},{5,4},{6,7},{7,6},{8,9},{9,8},{10,11... | collective-permute-start | bytes 1572872 | tf_op jit(solution)/shard_map/ppermute | solution.py:483
  21.5 16.0 %collective-permute-start.7 = (f32[4,32,128]{2,1,0:T(8,128)S(1)}, f32[4,32,128]{2,1,0:T(8,128)S(1)}, u32[]{:S(2)}, u32[]{:S(2)}) collective-permute-start(f32[4,32,128]{2,1,0:T(8,128)S(1)} %bitcast.60), channel_id=1, source_target_pairs={{0,2},{1,3},{2,0},{3,1},{4,6},{5,7},{6,4},{7,5},{8,10},{9,11},{10,... | collective-permute-start | bytes 196616 | tf_op jit(solution)/shard_map/ppermute | solution.py:483
  22.0 15.4 %collective-permute-start.8 = (f32[4,32,128]{2,1,0:T(8,128)S(1)}, f32[4,32,128]{2,1,0:T(8,128)S(1)}, u32[]{:S(2)}, u32[]{:S(2)}) collective-permute-start(f32[4,32,128]{2,1,0:T(8,128)S(1)} %bitcast.61), channel_id=1, source_target_pairs={{0,1},{1,0},{2,3},{3,2},{4,5},{5,4},{6,7},{7,6},{8,9},{9,8},{10,11... | collective-permute-start | bytes 196616 | tf_op jit(solution)/shard_map/ppermute | solution.py:483
  24.0 13.5 %collective-permute-start.9 = (f32[4,32,128]{2,1,0:T(8,128)S(1)}, f32[4,32,128]{2,1,0:T(8,128)S(1)}, u32[]{:S(2)}, u32[]{:S(2)}) collective-permute-start(f32[4,32,128]{2,1,0:T(8,128)S(1)} %bitcast.62), channel_id=1, source_target_pairs={{0,3},{1,2},{2,1},{3,0},{4,7},{5,6},{6,5},{7,4},{8,11},{9,10},{10,... | collective-permute-start | bytes 196616 | tf_op jit(solution)/shard_map/ppermute | solution.py:483
  24.6 9.3 %copy-start.31 = (s32[32]{0:T(128)S(1)}, s32[32]{0:T(128)}, u32[]{:S(2)}) copy-start(s32[32]{0:T(128)} %offs_ref.5) | copy-start | bytes 388
  34.9 8.1 %copy-start.7 = (f32[64,512]{1,0:T(8,128)S(1)}, f32[64,512]{1,0:T(8,128)}, u32[]{:S(2)}) copy-start(f32[64,512]{1,0:T(8,128)} %constant.91.clone.twiddle_ref) | copy-start | bytes 393220
  34.9 8.1 %copy-start.14 = (bf16[256,512]{1,0:T(8,128)(2,1)S(1)}, bf16[256,512]{1,0:T(8,128)(2,1)}, u32[]{:S(2)}) copy-start(bf16[256,512]{1,0:T(8,128)(2,1)} %constant.89.clone.high_ref) | copy-start | bytes 786436
  34.9 8.1 %copy-start.15 = (bf16[256,512]{1,0:T(8,128)(2,1)S(1)}, bf16[256,512]{1,0:T(8,128)(2,1)}, u32[]{:S(2)}) copy-start(bf16[256,512]{1,0:T(8,128)(2,1)} %constant.90.clone.low_ref) | copy-start | bytes 786436
  37.5 5.5 %collective-permute-start.12 = (f32[4,256,128]{2,1,0:T(8,128)}, f32[4,256,128]{2,1,0:T(8,128)S(1)}, u32[]{:S(2)}, u32[]{:S(2)}) collective-permute-start(f32[4,256,128]{2,1,0:T(8,128)} %collective-permute-done.6.cross_ref), channel_id=1, source_target_pairs={{0,1},{1,0},{2,3},{3,2},{4,5},{5,4},{6,7},{7,6},{8,9},{9,8},{10,11... | collective-permute-start | bytes 1572872 | tf_op jit(solution)/shard_map/ppermute | solution.py:483
  37.8 17.5 %collective-permute-start.13 = (f32[4,256,128]{2,1,0:T(8,128)S(1)}, f32[4,256,128]{2,1,0:T(8,128)S(1)}, u32[]{:S(2)}, u32[]{:S(2)}) collective-permute-start(f32[4,256,128]{2,1,0:T(8,128)S(1)} %bitcast.55), channel_id=1, source_target_pairs={{0,2},{1,3},{2,0},{3,1},{4,6},{5,7},{6,4},{7,5},{8,10},{9,11},{10,... | collective-permute-start | bytes 1572872 | tf_op jit(solution)/shard_map/ppermute | solution.py:483
  43.0 4.9 %copy-start.21 = (f32[6,32]{1,0:T(8,128)S(1)}, f32[6,32]{1,0:T(8,128)}, u32[]{:S(2)}) copy-start(f32[6,32]{1,0:T(8,128)} %copy-done.20) | copy-start | bytes 2308
  48.9 13.5 %copy-start.10 = (f32[32,512]{1,0:T(8,128)S(1)}, f32[32,512]{1,0:T(8,128)}, u32[]{:S(2)}) copy-start(f32[32,512]{1,0:T(8,128)} %constant.92.clone.lift_ref) | copy-start | bytes 196612
  49.0 13.5 %copy-start.12 = (f32[32,512]{1,0:T(8,128)S(1)}, f32[32,512]{1,0:T(8,128)}, u32[]{:S(2)}) copy-start(f32[32,512]{1,0:T(8,128)} %constant.93.clone.drop_ref) | copy-start | bytes 196612
  49.0 13.5 %copy-start.16 = (f32[8,512]{1,0:T(8,128)S(1)}, f32[8,512]{1,0:T(8,128)}, u32[]{:S(2)}) copy-start(f32[8,512]{1,0:T(8,128)} %constant.94.clone.vectors_ref) | copy-start | bytes 49156
  55.3 4.3 %collective-permute-start.17 = (f32[64,128]{1,0:T(8,128)S(1)}, f32[64,128]{1,0:T(8,128)S(1)}, u32[]{:S(2)}, u32[]{:S(2)}) collective-permute-start(f32[64,128]{1,0:T(8,128)S(1)} %push.1.push_a_ref), channel_id=1, source_target_pairs={{0,2},{1,3},{2,0},{3,1},{4,6},{5,7},{6,4},{7,5},{8,10},{9,11},{10,... | collective-permute-start | bytes 98312 | tf_op jit(solution)/shard_map/ppermute | solution.py:483
  55.9 3.7 %collective-permute-start.18 = (f32[64,128]{1,0:T(8,128)S(1)}, f32[64,128]{1,0:T(8,128)S(1)}, u32[]{:S(2)}, u32[]{:S(2)}) collective-permute-start(f32[64,128]{1,0:T(8,128)S(1)} %push.1.push_a_ref), channel_id=1, source_target_pairs={{0,3},{1,2},{2,1},{3,0},{4,7},{5,6},{6,5},{7,4},{8,11},{9,10},{10,... | collective-permute-start | bytes 98312 | tf_op jit(solution)/shard_map/ppermute | solution.py:483
  56.5 3.5 %collective-permute-start.19 = (f32[64,128]{1,0:T(8,128)S(1)}, f32[64,128]{1,0:T(8,128)S(1)}, u32[]{:S(2)}, u32[]{:S(2)}) collective-permute-start(f32[64,128]{1,0:T(8,128)S(1)} %push.1.push_a_ref), channel_id=1, source_target_pairs={{0,1},{1,0},{2,3},{3,2},{4,5},{5,4},{6,7},{7,6},{8,9},{9,8},{10,11... | collective-permute-start | bytes 98312 | tf_op jit(solution)/shard_map/ppermute | solution.py:483
  57.5 4.9 %collective-permute-start.14 = (f32[32,512]{1,0:T(8,128)S(1)}, f32[32,512]{1,0:T(8,128)S(1)}, u32[]{:S(2)}, u32[]{:S(2)}) collective-permute-start(f32[32,512]{1,0:T(8,128)S(1)} %get-tuple-element.32.a_ref), channel_id=1, source_target_pairs={{0,2},{1,3},{2,0},{3,1},{4,6},{5,7},{6,4},{7,5},{8,10},{9,11},{10,... | collective-permute-start | bytes 196616 | tf_op jit(solution)/shard_map/ppermute | solution.py:483
  58.1 4.4 %collective-permute-start.15 = (f32[32,512]{1,0:T(8,128)S(1)}, f32[32,512]{1,0:T(8,128)S(1)}, u32[]{:S(2)}, u32[]{:S(2)}) collective-permute-start(f32[32,512]{1,0:T(8,128)S(1)} %get-tuple-element.32.a_ref), channel_id=1, source_target_pairs={{0,3},{1,2},{2,1},{3,0},{4,7},{5,6},{6,5},{7,4},{8,11},{9,10},{10,... | collective-permute-start | bytes 196616 | tf_op jit(solution)/shard_map/ppermute | solution.py:483
  59.6 2.9 %collective-permute-start.16 = (f32[32,512]{1,0:T(8,128)S(1)}, f32[32,512]{1,0:T(8,128)S(1)}, u32[]{:S(2)}, u32[]{:S(2)}) collective-permute-start(f32[32,512]{1,0:T(8,128)S(1)} %get-tuple-element.32.a_ref), channel_id=1, source_target_pairs={{0,1},{1,0},{2,3},{3,2},{4,5},{5,4},{6,7},{7,6},{8,9},{9,8},{10,11... | collective-permute-start | bytes 196616 | tf_op jit(solution)/shard_map/ppermute | solution.py:483
  59.6 32.2 %collective-permute-start.27 = (f32[4,256,128]{2,1,0:T(8,128)S(1)}, f32[4,256,128]{2,1,0:T(8,128)S(1)}, u32[]{:S(2)}, u32[]{:S(2)}) collective-permute-start(f32[4,256,128]{2,1,0:T(8,128)S(1)} %bitcast.56), channel_id=1, source_target_pairs={{0,1},{1,0},{2,3},{3,2},{4,5},{5,4},{6,7},{7,6},{8,9},{9,8},{10,11... | collective-permute-start | bytes 1572872 | tf_op jit(solution)/shard_map/ppermute | solution.py:483
  60.1 31.8 %collective-permute-start.28 = (f32[4,256,128]{2,1,0:T(8,128)S(1)}, f32[4,256,128]{2,1,0:T(8,128)}, u32[]{:S(2)}, u32[]{:S(2)}) collective-permute-start(f32[4,256,128]{2,1,0:T(8,128)S(1)} %collective-permute-done.13.cross_ref), channel_id=1, source_target_pairs={{0,1},{1,0},{2,3},{3,2},{4,5},{5,4},{6,7},{7,6},{8,9},{9,8},{10,11... | collective-permute-start | bytes 1572872 | tf_op jit(solution)/shard_map/ppermute | solution.py:483
  63.2 8.3 %collective-permute-start.20 = (f32[16,128]{1,0:T(8,128)S(1)}, f32[16,128]{1,0:T(8,128)S(1)}, u32[]{:S(2)}, u32[]{:S(2)}) collective-permute-start(f32[16,128]{1,0:T(8,128)S(1)} %get-tuple-element.35), channel_id=1, source_target_pairs={{0,4},{4,8},{8,12},{12,0},{1,5},{5,9},{9,13},{13,1},{2,6},{6,10},{... | collective-permute-start | bytes 24584 | tf_op jit(solution)/shard_map/ppermute | solution.py:483
  65.4 7.4 %collective-permute-start.21 = (f32[16,128]{1,0:T(8,128)S(1)}, f32[16,128]{1,0:T(8,128)S(1)}, u32[]{:S(2)}, u32[]{:S(2)}) collective-permute-start(f32[16,128]{1,0:T(8,128)S(1)} %get-tuple-element.35), channel_id=1, source_target_pairs={{0,8},{4,12},{8,0},{12,4},{1,9},{5,13},{9,1},{13,5},{2,10},{6,14},... | collective-permute-start | bytes 24584 | tf_op jit(solution)/shard_map/ppermute | solution.py:483
  71.1 3.7 %collective-permute-start.22 = (f32[16,128]{1,0:T(8,128)S(1)}, f32[16,128]{1,0:T(8,128)S(1)}, u32[]{:S(2)}, u32[]{:S(2)}) collective-permute-start(f32[16,128]{1,0:T(8,128)S(1)} %get-tuple-element.35), channel_id=1, source_target_pairs={{0,12},{4,0},{8,4},{12,8},{1,13},{5,1},{9,5},{13,9},{2,14},{6,2},{... | collective-permute-start | bytes 24584 | tf_op jit(solution)/shard_map/ppermute | solution.py:483
  75.3 6.1 %collective-permute-start.23 = (f32[16,128]{1,0:T(8,128)S(1)}, f32[16,128]{1,0:T(8,128)S(1)}, u32[]{:S(2)}, u32[]{:S(2)}) collective-permute-start(f32[16,128]{1,0:T(8,128)S(1)} %add_add_fusion), channel_id=1, source_target_pairs={{0,16},{16,0},{1,17},{17,1},{2,18},{18,2},{3,19},{19,3},{4,20},{20... | collective-permute-start | bytes 24584 | tf_op jit(solution)/shard_map/ppermute | solution.py:483
  80.0 11.8 %copy-start.32 = (s32[32]{0:T(128)S(1)}, s32[32]{0:T(128)}, u32[]{:S(2)}) copy-start(s32[32]{0:T(128)} %offs_ref.5) | copy-start | bytes 388
  82.1 12.2 %copy-start.8 = (bf16[512,256]{1,0:T(8,128)(2,1)S(1)}, bf16[512,256]{1,0:T(8,128)(2,1)}, u32[]{:S(2)}) copy-start(bf16[512,256]{1,0:T(8,128)(2,1)} %constant.97.clone.high_ref) | copy-start | bytes 786436
  82.1 12.2 %copy-start.9 = (bf16[512,256]{1,0:T(8,128)(2,1)S(1)}, bf16[512,256]{1,0:T(8,128)(2,1)}, u32[]{:S(2)}) copy-start(bf16[512,256]{1,0:T(8,128)(2,1)} %constant.98.clone.low_ref) | copy-start | bytes 786436
  82.2 12.2 %copy-start.11 = (f32[32,512]{1,0:T(8,128)S(1)}, f32[32,512]{1,0:T(8,128)}, u32[]{:S(2)}) copy-start(f32[32,512]{1,0:T(8,128)} %constant.92.clone.lift_ref) | copy-start | bytes 196612
  82.2 12.2 %copy-start.13 = (f32[32,512]{1,0:T(8,128)S(1)}, f32[32,512]{1,0:T(8,128)}, u32[]{:S(2)}) copy-start(f32[32,512]{1,0:T(8,128)} %constant.93.clone.drop_ref) | copy-start | bytes 196612
  82.2 12.2 %copy-start.17 = (f32[8,512]{1,0:T(8,128)S(1)}, f32[8,512]{1,0:T(8,128)}, u32[]{:S(2)}) copy-start(f32[8,512]{1,0:T(8,128)} %constant.94.clone.vectors_ref) | copy-start | bytes 49156
  82.2 12.2 %copy-start.19 = (f32[32,512]{1,0:T(8,128)S(1)}, f32[32,512]{1,0:T(8,128)}, u32[]{:S(2)}) copy-start(f32[32,512]{1,0:T(8,128)} %copy-done.18) | copy-start | bytes 196612
  82.2 12.1 %collective-permute-start.24 = (f32[16,128]{1,0:T(8,128)S(1)}, f32[16,128]{1,0:T(8,128)S(1)}, u32[]{:S(2)}, u32[]{:S(2)}) collective-permute-start(f32[16,128]{1,0:T(8,128)S(1)} %multiply_add_fusion.eight_ref), channel_id=1, source_target_pairs={{0,32},{32,64},{64,96},{96,0},{1,33},{33,65},{65,97},{97,1},{2,34}... | collective-permute-start | bytes 24584 | tf_op jit(solution)/shard_map/ppermute | solution.py:483
  87.7 6.6 %collective-permute-start.25 = (f32[16,128]{1,0:T(8,128)S(1)}, f32[16,128]{1,0:T(8,128)S(1)}, u32[]{:S(2)}, u32[]{:S(2)}) collective-permute-start(f32[16,128]{1,0:T(8,128)S(1)} %multiply_add_fusion.eight_ref), channel_id=1, source_target_pairs={{0,64},{32,96},{64,0},{96,32},{1,65},{33,97},{65,1},{97,33},{2,66}... | collective-permute-start | bytes 24584 | tf_op jit(solution)/shard_map/ppermute | solution.py:483
  90.7 3.7 %collective-permute-start.26 = (f32[16,128]{1,0:T(8,128)S(1)}, f32[16,128]{1,0:T(8,128)S(1)}, u32[]{:S(2)}, u32[]{:S(2)}) collective-permute-start(f32[16,128]{1,0:T(8,128)S(1)} %multiply_add_fusion.eight_ref), channel_id=1, source_target_pairs={{0,96},{32,0},{64,32},{96,64},{1,97},{33,1},{65,33},{97,65},{2,98}... | collective-permute-start | bytes 24584 | tf_op jit(solution)/shard_map/ppermute | solution.py:483
  (21 other events, 39.3 us)

commit v2 on v1

--- a/solution.py
+++ b/solution.py
@@ -96,7 +96,7 @@
 
 
 def params():
-    return pltpu.CompilerParams(vmem_limit_bytes=40 * 1024 * 1024)
+    return pltpu.CompilerParams(vmem_limit_bytes=14 * 1024 * 1024)
 
 
 def cost(us):
@@ -107,8 +107,26 @@
     return jnp.where(speeds > 0, speeds * upstream, speeds * downstream)
 
 
-def azimuth_kernel(dens_ref, phi_ref, vrad_ref, left_ref, right_ref, offs_ref, out_ref, up_ref, down_ref):
+def azimuth_kernel(
+    dens_ref, phi_ref, vrad_ref, left_ref, right_ref, offs_ref, out_ref, up_ref, down_ref,
+    dens_buf, phi_buf, vrad_buf, sems,
+):
     lane = lax.broadcasted_iota(jnp.int32, (1, 8, 128), 2)
+    copies = []
+    for group in range(GROUPS):
+        copies.append(
+            (
+                pltpu.make_async_copy(dens_ref.at[group], dens_buf.at[group], sems.at[2 * group]),
+                pltpu.make_async_copy(phi_ref.at[group], phi_buf.at[group], sems.at[2 * group + 1]),
+            )
+        )
+    ends = (
+        pltpu.make_async_copy(vrad_ref.at[0], vrad_buf.at[0], sems.at[8]),
+        pltpu.make_async_copy(vrad_ref.at[3], vrad_buf.at[1], sems.at[9]),
+    )
+    for pair in copies + [ends]:
+        for copy in pair:
+            copy.start()
 
     def following(value):
         turned = pltpu.roll(value, 127, 2)
@@ -120,54 +138,50 @@
         return jnp.concatenate([left_ref[rows, :][None], middle, right_ref[rows, :][None]], axis=0)
 
     for group in range(GROUPS):
-        dens = widened(dens_ref, group, 0)
-        phi = widened(phi_ref, group, ROWS)
+        for copy in copies[group]:
+            copy.wait()
+        dens = widened(dens_buf, group, 0)
+        phi = widened(phi_buf, group, ROWS)
         speeds = 0.5 * (phi[:-1] + following(phi))
         flux = donor_flux(speeds, dens[:-1], following(dens))
         turned = pltpu.roll(flux, 1, 2)
         before = jnp.where(lane == 0, turned[:-1], turned[1:])
         stepped = dens[1:-1] - courant * (flux[1:] - before)
         out_ref[group] = stepped.reshape(SPAN, 128)
-    up_ref[0:32, :] = out_ref[3, pl.ds(7, CHUNKS, stride=8), :]
-    up_ref[32:64, :] = vrad_ref[3, pl.ds(7, CHUNKS, stride=8), :]
-    up_ref[64:72, :] = jnp.full((8, 128), offs_ref[31].astype(F32), F32)
-    down_ref[0:32, :] = out_ref[0, pl.ds(0, CHUNKS, stride=8), :]
-    down_ref[32:64, :] = vrad_ref[0, pl.ds(0, CHUNKS, stride=8), :]
-    down_ref[64:72, :] = jnp.full((8, 128), offs_ref[0].astype(F32), F32)
-
-
-def fill_ring(own_ref, mate_ref, cross_ref, far_ref, ring_ref, sems, unit):
+    for copy in ends:
+        copy.wait()
+    for side, (ref, group, row) in enumerate(((down_ref, 0, 0), (up_ref, 3, 7))):
+        ref[pl.ds(0, CHUNKS, stride=2), :] = out_ref[group, pl.ds(row, CHUNKS, stride=8), :]
+        ref[pl.ds(1, CHUNKS, stride=2), :] = vrad_buf[side, pl.ds(row, CHUNKS, stride=8), :]
+        ref[64:72, :] = jnp.full((8, 128), offs_ref[8 * group + row].astype(F32), F32)
+
+
+def fill_ring(group, own_ref, mate_ref, cross_ref, far_ref, ring_ref, unit):
     odd = lax.axis_index(AZ) % 2
     places = ((own_ref, 0), (own_ref, 4), (cross_ref, 2), (mate_ref, 1 + 2 * odd), (far_ref, 3 - 2 * odd))
-    copies = []
-    for index, (source, place) in enumerate(places):
+    for source, place in places:
         where = pl.ds(pl.multiple_of(place * unit, unit), unit)
-        copies.append(pltpu.make_async_copy(source, ring_ref.at[:, where, :], sems.at[index]))
-    for copy in copies:
-        copy.start()
-    return copies
-
-
-def shift_row(ring_ref, group, step, row, offset):
+        ring_ref[where, :] = source[group, 0:unit, :]
+
+
+def shift_row(ring_ref, step, row, offset):
     start = ANGULAR_BINS - offset
     chunk = start // 128
     turn = (128 - start % 128) % 128
     lane = lax.broadcasted_iota(jnp.int32, (CHUNKS, 128), 1)
-    first = ring_ref[group, pl.ds(chunk * step + row, CHUNKS, stride=step), :]
-    second = ring_ref[group, pl.ds((chunk + 1) * step + row, CHUNKS, stride=step), :]
+    first = ring_ref[pl.ds(chunk * step + row, CHUNKS, stride=step), :]
+    second = ring_ref[pl.ds((chunk + 1) * step + row, CHUNKS, stride=step), :]
     return jnp.where(
         lane < 128 - start % 128, pltpu.roll(first, turn, 1), pltpu.roll(second, turn, 1)
     )
 
 
-def shift_kernel(offs_ref, own_ref, mate_ref, cross_ref, far_ref, out_ref, ring_ref, sems):
-    for copy in fill_ring(own_ref, mate_ref, cross_ref, far_ref, ring_ref, sems, SPAN):
-        copy.wait()
-
+def shift_kernel(offs_ref, own_ref, mate_ref, cross_ref, far_ref, out_ref, ring_ref):
     @pl.loop(0, GROUPS)
     def _(group):
+        fill_ring(group, own_ref, mate_ref, cross_ref, far_ref, ring_ref, SPAN)
         for row in range(8):
-            moved = shift_row(ring_ref, group, 8, row, offs_ref[group * 8 + row])
+            moved = shift_row(ring_ref, 8, row, offs_ref[group * 8 + row])
             out_ref[group, pl.ds(row, CHUNKS, stride=8), :] = moved
 
 
@@ -175,9 +189,9 @@
     return pl.pallas_call(
         shift_kernel,
         out_shape=jax.ShapeDtypeStruct((GROUPS, SPAN, 128), F32),
-        in_specs=[smem(), anywhere(), anywhere(), anywhere(), anywhere()],
+        in_specs=[smem(), vmem(), vmem(), vmem(), vmem()],
         out_specs=vmem(),
-        scratch_shapes=[pltpu.VMEM((GROUPS, RING, 128), F32), pltpu.SemaphoreType.DMA((5,))],
+        scratch_shapes=[pltpu.VMEM((RING, 128), F32)],
         compiler_params=params(),
         cost_estimate=cost(2),
         name=name,
@@ -197,26 +211,23 @@
     offs_ref, own_ref, mate_ref, cross_ref, far_ref,
     edge_own_ref, edge_mate_ref, edge_cross_ref, edge_far_ref,
     vrad_ref, high_ref, low_ref, twiddle_ref,
-    dens_ref, spectra_ref,
-    ring_ref, edge_ref, moved_ref, speed_ref, sems, edge_sems,
+    whole_ref, dens_ref, spectra_ref,
+    ring_ref, edge_ref, moved_ref, speed_ref, whole_sem,
 ):
-    copies = fill_ring(own_ref, mate_ref, cross_ref, far_ref, ring_ref, sems, SPAN)
-    copies += fill_ring(
-        edge_own_ref, edge_mate_ref, edge_cross_ref, edge_far_ref, edge_ref, edge_sems, CHUNKS
-    )
-    for copy in copies:
-        copy.wait()
+    for side, (place, row) in enumerate(((0, 7), (5, 0))):
+        fill_ring(
+            side, edge_own_ref, edge_mate_ref, edge_cross_ref, edge_far_ref, edge_ref, 2 * CHUNKS
+        )
+        offset = jnp.max(edge_own_ref[side, 64:72, :]).astype(jnp.int32)
+        moved_ref[place, pl.ds(row, CHUNKS, stride=8), :] = shift_row(edge_ref, 2, 0, offset)
+        speed_ref[side, pl.ds(row, CHUNKS, stride=8), :] = shift_row(edge_ref, 2, 1, offset)
 
     @pl.loop(0, GROUPS)
     def _(group):
+        fill_ring(group, own_ref, mate_ref, cross_ref, far_ref, ring_ref, SPAN)
         for row in range(8):
-            moved = shift_row(ring_ref, group, 8, row, offs_ref[group * 8 + row])
+            moved = shift_row(ring_ref, 8, row, offs_ref[group * 8 + row])
             moved_ref[group + 1, pl.ds(row, CHUNKS, stride=8), :] = moved
-
-    for side, (place, row) in enumerate(((0, 7), (5, 0))):
-        offset = offs_ref[ROWS + side]
-        moved_ref[place, pl.ds(row, CHUNKS, stride=8), :] = shift_row(edge_ref, 2 * side, 1, 0, offset)
-        speed_ref[side, pl.ds(row, CHUNKS, stride=8), :] = shift_row(edge_ref, 2 * side + 1, 1, 0, offset)
 
     sub = lax.broadcasted_iota(jnp.int32, (1, 8, 128), 1)
     own_index = lax.axis_index(RAD)
@@ -254,6 +265,8 @@
             stepped = dens - courant * (flux_above - flux_below)
             dens_ref[group, where, :] = stepped.reshape(8 * step, 128)
 
+    whole = pltpu.make_async_copy(dens_ref, whole_ref, whole_sem)
+    whole.start()
     sector = lax.axis_index(AZ)
     cos_sum = jnp.zeros((ROWS, MODES), F32)
     sin_sum = jnp.zeros((ROWS, MODES), F32)
@@ -277,65 +290,80 @@
             sin_sum += sine * cos_part + cosine * sin_part
     spectra_ref[:, :MODES] = cos_sum * cell_step
     spectra_ref[:, MODES:] = sin_sum * cell_step
+    whole.wait()
 
 
 def field_kernel(
     members_ref, radius_ref, angles_ref, radial_ref, azim_ref,
-    gap_ref, pull_ref, chord_ref, lift_ref, side_ref,
+    gap_ref, chord_ref, lift_ref, side_ref,
 ):
     sector = lax.axis_index(AZ)
     half_cos = angles_ref[sector * 4]
     half_sin = angles_ref[sector * 4 + 1]
     radius = radius_ref[...]
-
-    @pl.loop(0, EMB)
+    halves = 0.5 / radius
+
+    @pl.loop(0, EMB, unroll=4)
     def _(member):
         embryo_radius = members_ref[0, member]
-        weight = members_ref[1, member]
+        scale = members_ref[1, member]
         cosine = members_ref[2, member]
         sine = members_ref[3, member]
         gap = radius - embryo_radius
         soft = softening * embryo_radius
         rows = pl.ds(pl.multiple_of(member * 32, 32), 32)
-        gap_ref[rows, :] = gap * gap + soft * soft
-        pull_ref[rows, :] = weight * gap
+        gap_ref[rows, :] = (gap * gap + soft * soft) * halves * scale
         near = half_sin * cosine - half_cos * sine
         far = half_cos * cosine + half_sin * sine
         chord = (2.0 * embryo_radius) * (near * near)
-        chord_ref[rows, :] = chord
-        lift_ref[rows, :] = weight * chord
-        side_ref[rows, :] = (2.0 * weight * embryo_radius) * (near * far)
-
-    twice = [2.0 * radius[8 * g : 8 * g + 8] for g in range(GROUPS)]
-
-    @pl.loop(0, CHUNKS)
-    def _(chunk):
+        chord_ref[rows, :] = chord * scale
+        lift_ref[rows, :] = chord - embryo_radius
+        side_ref[rows, :] = (2.0 * embryo_radius) * (near * far)
+
+    pieces = [radius[8 * g : 8 * g + 8] for g in range(GROUPS)]
+    ends = []
+    for g in range(GROUPS):
+        root = lax.rsqrt(2.0 * pieces[g])
+        ends.append(root * root * root)
+    together = 2
+
+    @pl.loop(0, CHUNKS // together)
+    def _(part):
         zero = jnp.zeros((8, 128), F32)
 
         def visit(member, carried):
             radial, azim = list(carried[0]), list(carried[1])
-            row = pl.ds(member * 32 + chunk, 1)
-            chord = jnp.broadcast_to(chord_ref[row, :], (8, 128))
-            lift = jnp.broadcast_to(lift_ref[row, :], (8, 128))
-            side = jnp.broadcast_to(side_ref[row, :], (8, 128))
+            rows = []
+            for k in range(together):
+                row = pl.ds(member * 32 + part * together + k, 1)
+                rows.append(
+                    [jnp.broadcast_to(ref[row, :], (8, 128)) for ref in (chord_ref, lift_ref, side_ref)]
+                )
             for g in range(GROUPS):
-                rows = pl.ds(pl.multiple_of(member * 32 + 8 * g, 8), 8)
-                inverse = lax.rsqrt(gap_ref[rows, :] + twice[g] * chord)
-                cubed = inverse * inverse * inverse
-                radial[g] = radial[g] + cubed * (pull_ref[rows, :] + lift)
-                azim[g] = azim[g] + cubed * side
+                gap = gap_ref[pl.ds(pl.multiple_of(member * 32 + 8 * g, 8), 8), :]
+                for k in range(together):
+                    chord, lift, side = rows[k]
+                    inverse = lax.rsqrt(gap + chord)
+                    cubed = inverse * inverse * inverse
+                    at = k * GROUPS + g
+                    radial[at] = radial[at] + cubed * (pieces[g] + lift)
+                    azim[at] = azim[at] + cubed * side
             return tuple(radial), tuple(azim)
 
-        radial, azim = lax.fori_loop(
-            0, EMB, visit, ((zero,) * GROUPS, (zero,) * GROUPS), unroll=4
-        )
-        where = pl.ds(pl.multiple_of(chunk * 8, 8), 8)
-        for g in range(GROUPS):
-            radial_ref[g, where, :] = radial[g]
-            azim_ref[g, where, :] = azim[g]
-
-
-def push_kernel(members_ref, radius_ref, angles_ref, dens_ref, out_ref, mass_ref, chord_ref):
+        count = together * GROUPS
+        radial, azim = lax.fori_loop(0, EMB, visit, ((zero,) * count, (zero,) * count), unroll=4)
+        for k in range(together):
+            where = pl.ds(pl.multiple_of((part * together + k) * 8, 8), 8)
+            for g in range(GROUPS):
+                radial_ref[g, where, :] = radial[k * GROUPS + g] * ends[g]
+                azim_ref[g, where, :] = azim[k * GROUPS + g] * ends[g]
+
+
+def push_kernel(
+    members_ref, radius_ref, angles_ref, dens_ref, spectra_ref, out_ref, mass_ref, chord_ref
+):
+    for part in range(4):
+        out_ref[ROWS * part : ROWS * part + ROWS, :] = spectra_ref[:, 128 * part : 128 * part + 128]
     sector = lax.axis_index(AZ)
     radius = radius_ref[...]
     pieces = [radius[8 * g : 8 * g + 8] for g in range(GROUPS)]
@@ -377,60 +405,47 @@
             total = total + plain
         place_x = embryo_radius * members_ref[4, member]
         place_y = embryo_radius * members_ref[5, member]
-        out_ref[pl.ds(member, 1), :] = jnp.sum(push_x - place_x * total, axis=0, keepdims=True)
-        out_ref[pl.ds(EMB + member, 1), :] = jnp.sum(push_y - place_y * total, axis=0, keepdims=True)
-
-
-def moment_kernel(
-    a_ref, b_ref, c_ref, d_ref, push_a_ref, push_b_ref, push_c_ref, push_d_ref,
-    lift_ref, drop_ref, vectors_ref, spectra_ref, packed_ref,
-):
-    spectra = (a_ref[...] + b_ref[...]) + (c_ref[...] + d_ref[...])
-    spectra_ref[...] = spectra
-    factor = vectors_ref[0:1, :]
-    up = jnp.sum(spectra * drop_ref[...], axis=0, keepdims=True) / factor
-    down = jnp.sum(spectra * lift_ref[...], axis=0, keepdims=True) / factor
+        out_ref[pl.ds(4 * ROWS + member, 1), :] = jnp.sum(push_x - place_x * total, axis=0, keepdims=True)
+        out_ref[pl.ds(4 * ROWS + EMB + member, 1), :] = jnp.sum(push_y - place_y * total, axis=0, keepdims=True)
+
+
+def moment_kernel(a_ref, b_ref, c_ref, d_ref, lift_ref, drop_ref, vectors_ref, spectra_ref, packed_ref, one_ref):
+    total = (a_ref[...] + b_ref[...]) + (c_ref[...] + d_ref[...])
     for part in range(4):
-        packed_ref[part : part + 1, :] = up[:, 128 * part : 128 * part + 128]
-        packed_ref[4 + part : 5 + part, :] = down[:, 128 * part : 128 * part + 128]
-    push = (push_a_ref[...] + push_b_ref[...]) + (push_c_ref[...] + push_d_ref[...])
+        columns = slice(128 * part, 128 * part + 128)
+        spectra = total[ROWS * part : ROWS * part + ROWS]
+        spectra_ref[:, columns] = spectra
+        factor = vectors_ref[0:1, columns]
+        up = jnp.sum(spectra * drop_ref[:, columns], axis=0, keepdims=True) / factor
+        down = jnp.sum(spectra * lift_ref[:, columns], axis=0, keepdims=True) / factor
+        one_ref[part : part + 1, :] = up
+        one_ref[4 + part : 5 + part, :] = down
+    push = total[4 * ROWS :]
     push = jnp.broadcast_to(jnp.sum(push, axis=1, keepdims=True), (2 * EMB, 128))
     row = lax.broadcasted_iota(jnp.int32, (2 * EMB, 128), 0)
     lane = lax.broadcasted_iota(jnp.int32, (2 * EMB, 128), 1)
     push = jnp.sum(jnp.where(row == lane, push, 0.0), axis=0, keepdims=True)
-    packed_ref[8:16, :] = jnp.broadcast_to(push, (8, 128))
+    one_ref[8:16, :] = jnp.broadcast_to(push, (8, 128))
+    one = one_ref[...]
+    for copy in range(packed_ref.shape[0]):
+        packed_ref[copy] = one
 
 
 def kick_kernel(
-    spectra_ref, near_1_ref, near_2_ref, near_3_ref, other_ref, distant_1_ref, distant_2_ref, distant_3_ref,
-    eight_ref, rate_ref, radius_ref, vectors_ref, lift_ref, drop_ref, twiddle_ref, high_ref, low_ref,
+    spectra_ref, moments_ref, rate_ref, radius_ref, vectors_ref, lift_ref, drop_ref, twiddle_ref, high_ref, low_ref,
     radial_ref, azim_ref, vrad_ref, vphi_ref,
-    out_radial_ref, out_azim_ref, out_push_ref,
-    lower_ref, upper_ref,
+    whole_radial_ref, whole_azim_ref, out_push_ref,
+    lower_ref, upper_ref, out_radial_ref, out_azim_ref, sems,
 ):
-    x, z, y = (lax.axis_index(name) for name in RAD)
-    counts = []
-    for shift in range(1, 4):
-        source = (y - shift) % 4
-        counts.append((y - 1 - source, source - y - 1))
-    counts.append((jnp.where(z == 1, y, -1), jnp.where(z == 0, 3 - y, -1)))
-    for shift in range(1, 4):
-        gap = x - (x - shift) % 4
-        within = 4 * z + y
-        counts.append(
-            (
-                jnp.where(gap > 0, 8 * (gap - 1) + within, -1),
-                jnp.where(gap < 0, 8 * (-gap - 1) + 7 - within, -1),
-            )
-        )
-    distant = (distant_1_ref, distant_2_ref, distant_3_ref)
+    own_index = lax.axis_index(RAD)
     row = lax.broadcasted_iota(jnp.int32, (8, 128), 0)
     outside = jnp.zeros((8, 128), F32)
-    for count, term in zip(counts, (near_1_ref, near_2_ref, near_3_ref, other_ref) + distant):
-        many = jnp.where(row < 4, count[0], count[1])
+    push = jnp.zeros((1, 128), F32)
+    for source in range(moments_ref.shape[0]):
+        many = jnp.where(row < 4, own_index - 1 - source, source - own_index - 1)
         weight = jnp.exp(-rate_ref[...] * jnp.maximum(many, 0).astype(F32))
-        outside += jnp.where(many >= 0, weight, 0.0) * term[0:8, :]
-    push = (eight_ref[8:9, :] + distant[1][8:9, :]) + (distant[0][8:9, :] + distant[2][8:9, :])
+        outside += jnp.where(many >= 0, weight, 0.0) * moments_ref[source, 0:8, :]
+        push += moments_ref[source, 8:9, :]
     out_push_ref[0:1, :] = push[:, :EMB]
     out_push_ref[1:2, :] = push[:, EMB : 2 * EMB]
     lower = jnp.concatenate([outside[k : k + 1] for k in range(4)], axis=1)
@@ -452,6 +467,7 @@
     swapped = jnp.concatenate([even[:, MODES:], even[:, :MODES]], axis=1)
     azim = swapped * vectors_ref[2:3, :] * inverse
     sector = lax.axis_index(AZ)
+    copies = []
     for block in range(BLOCKS):
         turn = twiddle_ref[pl.ds(sector * BLOCKS + block, 1), :]
         cosine, sine = turn[:, :MODES], turn[:, MODES:]
@@ -476,6 +492,20 @@
             out_azim_ref[:, where, :] = vphi_ref[:, where, :] + timestep_length * (
                 disk - azim_ref[:, where, :]
             )
+        if block % 4 == 3:
+            quarter = block // 4
+            rows = slice(64 * quarter, 64 * quarter + 64)
+            for index, (source, target) in enumerate(
+                ((out_radial_ref, whole_radial_ref), (out_azim_ref, whole_azim_ref))
+            ):
+                copies.append(
+                    pltpu.make_async_copy(
+                        source.at[:, rows, :], target.at[:, rows, :], sems.at[index, quarter]
+                    )
+                )
+                copies[-1].start()
+    for copy in copies:
+        copy.wait()
 
 
 def across(value, axis, target):
@@ -485,11 +515,6 @@
 
 def after(value, *others):
     return lax.optimization_barrier((value, *others))[0]
-
-
-def decayed(rate, up_count, down_count):
-    count = jnp.stack([up_count] * 4 + [down_count] * 4 + [0] * 8).astype(F32)
-    return jnp.exp(-rate * count[:, None])
 
 
 def on_device(
@@ -523,7 +548,7 @@
     members = jnp.stack(
         [
             jnp.exp((planetesimal_loop_number.astype(F32) + 0.5) * cell),
-            planetesimal_weights,
+            jnp.exp(np.float32(-2.0 / 3.0) * jnp.log(planetesimal_weights)),
             jnp.cos(0.5 * embryo_angles),
             jnp.sin(0.5 * embryo_angles),
             jnp.cos(embryo_angles),
@@ -534,8 +559,14 @@
     dens_two, edge_up, edge_down = pl.pallas_call(
         azimuth_kernel,
         out_shape=(tiles, jax.ShapeDtypeStruct((72, 128), F32), jax.ShapeDtypeStruct((72, 128), F32)),
-        in_specs=[vmem()] * 5 + [smem()],
+        in_specs=[pl.BlockSpec(memory_space=pltpu.HBM)] * 3 + [vmem()] * 2 + [smem()],
         out_specs=(vmem(), vmem(), vmem()),
+        scratch_shapes=[
+            pltpu.VMEM((GROUPS, SPAN, 128), F32),
+            pltpu.VMEM((GROUPS, SPAN, 128), F32),
+            pltpu.VMEM((2, SPAN, 128), F32),
+            pltpu.SemaphoreType.DMA((10,)),
+        ],
         compiler_params=params(),
         cost_estimate=cost(1),
         name="azimuth",
@@ -544,10 +575,7 @@
     rad_count = lax.axis_size(RAD)
     edge_low = lax.ppermute(edge_up, RAD, [(i, i + 1) for i in range(rad_count - 1)])
     edge_high = lax.ppermute(edge_down, RAD, [(i + 1, i) for i in range(rad_count - 1)])
-    edges = jnp.concatenate([edge_low[:64], edge_high[:64]]).reshape(4, CHUNKS, 128)
-    offsets = jnp.concatenate(
-        [angular_offsets, edge_low[64:65, 0].astype(jnp.int32), edge_high[64:65, 0].astype(jnp.int32)]
-    )
+    edges = jnp.stack([edge_low, edge_high])
     edges_cross, edges_mate, edges_far = (
         across(edges, AZ, lambda i, k=k: i ^ k) for k in (2, 1, 3)
     )
@@ -563,7 +591,7 @@
         out_shape=(tiles, tiles),
         in_specs=[smem(), vmem(), vmem()],
         out_specs=(vmem(), vmem()),
-        scratch_shapes=[pltpu.VMEM((EMB * 32, 128), F32)] * 5,
+        scratch_shapes=[pltpu.VMEM((EMB * 32, 128), F32)] * 4,
         compiler_params=params(),
         cost_estimate=cost(6),
         name="field",
@@ -577,85 +605,77 @@
     vphi_cross = across(vphi_later, AZ, lambda i: i ^ 2)
     vphi_mate = across(vphi_later, AZ, lambda i: i ^ 1)
 
-    transported, part = pl.pallas_call(
+    transported, stepped, part = pl.pallas_call(
         transport_kernel,
-        out_shape=(tiles, jax.ShapeDtypeStruct((ROWS, 2 * MODES), F32)),
-        in_specs=[smem()] + [anywhere()] * 8 + [vmem()] * 4,
-        out_specs=(vmem(), vmem()),
+        out_shape=(tiles, tiles, jax.ShapeDtypeStruct((ROWS, 2 * MODES), F32)),
+        in_specs=[smem()] + [vmem()] * 12,
+        out_specs=(anywhere(), vmem(), vmem()),
         scratch_shapes=[
-            pltpu.VMEM((GROUPS, RING, 128), F32),
-            pltpu.VMEM((4, RING // 8, 128), F32),
+            pltpu.VMEM((RING, 128), F32),
+            pltpu.VMEM((2 * RING // 8, 128), F32),
             pltpu.VMEM((GROUPS + 2, SPAN, 128), F32),
             pltpu.VMEM((2, SPAN, 128), F32),
-            pltpu.SemaphoreType.DMA((5,)),
-            pltpu.SemaphoreType.DMA((5,)),
+            pltpu.SemaphoreType.DMA,
         ],
         compiler_params=params(),
         cost_estimate=cost(3),
         name="transport",
     )(
-        offsets, dens_two, dens_mate, dens_cross, dens_far,
+        angular_offsets, dens_two, dens_mate, dens_cross, dens_far,
         edges, edges_mate, edges_cross, edges_far,
         vrad_one, basis_high, basis_low, twiddle,
     )
 
-    push = pl.pallas_call(
+    joined_shape = jax.ShapeDtypeStruct((4 * ROWS + 2 * EMB, 128), F32)
+    joined = pl.pallas_call(
         push_kernel,
-        out_shape=jax.ShapeDtypeStruct((2 * EMB, 128), F32),
-        in_specs=[smem(), vmem(), vmem(), vmem()],
+        out_shape=joined_shape,
+        in_specs=[smem()] + [vmem()] * 4,
         out_specs=vmem(),
         scratch_shapes=[pltpu.VMEM((GROUPS, SPAN, 128), F32), pltpu.VMEM((CHUNKS, 128), F32)],
         compiler_params=params(),
         cost_estimate=cost(6),
         name="push",
-    )(members, radius, angles, transported)
-    part_later, push_later = lax.optimization_barrier((part, push, vphi_cross))[:2]
-    part_others = [across(part_later, AZ, lambda i, k=k: i ^ k) for k in (2, 3, 1)]
-    push_others = [across(push_later, AZ, lambda i, k=k: i ^ k) for k in (2, 3, 1)]
-
+    )(members, radius, angles, stepped, part)
+    joined = after(joined, vphi_cross)
+    others = [across(joined, AZ, lambda i, k=k: i ^ k) for k in (2, 3, 1)]
+
+    vphi_far = across(after(vphi_cross, joined), AZ, lambda i: i ^ 1)
+    vphi_one = shifted(angular_offsets, vphi_later, vphi_mate, vphi_cross, vphi_far, "shift_vphi")
+
+    others[0] = after(others[0], vphi_one)
     spectra, packed = pl.pallas_call(
         moment_kernel,
         out_shape=(
             jax.ShapeDtypeStruct((ROWS, 2 * MODES), F32),
-            jax.ShapeDtypeStruct((16, 128), F32),
+            jax.ShapeDtypeStruct((rad_count, 16, 128), F32),
         ),
-        in_specs=[vmem()] * 11,
+        in_specs=[vmem()] * 7,
         out_specs=(vmem(), vmem()),
+        scratch_shapes=[pltpu.VMEM((16, 128), F32)],
         compiler_params=params(),
         cost_estimate=cost(1),
         name="moments",
-    )(part, *part_others, push, *push_others, lift, drop, vectors)
-
-    def from_shift(value, axis, shift):
-        return across(value, axis, lambda i: (i + shift) % lax.axis_size(axis))
-
-    _, z, y = (lax.axis_index(name) for name in RAD)
-    rates = np.concatenate([rate, np.zeros((8, 128), np.float32)])
-    near = [from_shift(packed, "rad_2", shift) for shift in (1, 2, 3)]
-    parts = []
-    for shift, piece in enumerate([packed] + near):
-        source = (y - shift) % 4
-        parts.append(decayed(rates, 3 - source, source) * piece)
-    four = (parts[0] + parts[2]) + (parts[1] + parts[3])
-    other = from_shift(four, "rad_1", 1)
-    eight = decayed(rates, 4 * (1 - z), 4 * z) * four + decayed(rates, 4 * z, 4 * (1 - z)) * other
-    distant = [from_shift(eight, "rad_0", shift) for shift in (1, 2, 3)]
-
-    vphi_far = across(vphi_cross, AZ, lambda i: i ^ 1)
-    vphi_one = shifted(angular_offsets, vphi_later, vphi_mate, vphi_cross, vphi_far, "shift_vphi")
+    )(joined, *others, lift, drop, vectors)
+    gathered = lax.all_to_all(packed, RAD, split_axis=0, concat_axis=0, tiled=True)
 
     kicked_radial, kicked_azim, embryo_disk_acceleration = pl.pallas_call(
         kick_kernel,
         out_shape=(tiles, tiles, jax.ShapeDtypeStruct((2, EMB), F32)),
-        in_specs=[vmem()] * 21,
-        out_specs=(vmem(), vmem(), vmem()),
-        scratch_shapes=[pltpu.VMEM((ROWS, 2 * MODES), F32)] * 2,
+        in_specs=[vmem()] * 14,
+        out_specs=(anywhere(), anywhere(), vmem()),
+        scratch_shapes=[
+            pltpu.VMEM((ROWS, 2 * MODES), F32),
+            pltpu.VMEM((ROWS, 2 * MODES), F32),
+            pltpu.VMEM((GROUPS, SPAN, 128), F32),
+            pltpu.VMEM((GROUPS, SPAN, 128), F32),
+            pltpu.SemaphoreType.DMA((2, 4)),
+        ],
         compiler_params=params(),
         cost_estimate=cost(5),
         name="kick",
     )(
-        spectra, *near, other, *distant, eight,
-        rate, radius, vectors, lift, drop, twiddle, back_high, back_low,
+        spectra, gathered, rate, radius, vectors, lift, drop, twiddle, back_high, back_low,
         radial_field, azim_field, vrad_one, vphi_one,
     )
     return (

time: 99.1 us -> 87.4 us (0.88)
  starting transfers between devices: 41.1 us -> 14.8 us
  blocking collectives: 0 us -> 24.4 us
  local copies, waits for them, and re-layouts: 11.2 us -> 4.35 us
  Pallas kernels: 31.7 us -> 27.7 us
  waiting for transfers between devices: 11.3 us -> 14.8 us
  between operations: 2.5 us -> 0.87 us
    ppermute x27 -> x17, starting transfers between devices: 35.1 us -> 10.1 us  [across(): lax.ppermute(value, axis, [(source, target(source)) for source in range(c...]
    all_to_all x0 -> x1, blocking collectives: none -> 24.4 us  [on_device(): lax.all_to_all(packed, RAD, split_axis=0, concat_axis=0, tiled=True)]
    unnamed x80 -> x34, local copies, waits for them, and re-layouts: 7.44 us -> 3.47 us
    ppermute x1, waiting for transfers between devices: 0.01 us -> 3.96 us  [on_device(): lax.ppermute(edge_down, RAD, [(i + 1, i) for i in range(rad_count - 1)])]
    slice x4 -> x0, local copies, waits for them, and re-layouts: 2.4 us -> none  [the longest x1 1.2 us: on_device(): edge_high[64:65, 0].astype(jnp.int32)]
    pallas_call x1, Pallas kernels: 9.28 us -> 7.54 us  [on_device(): pl.pallas_call(field_kernel, out_shape=(tiles, tiles), in_specs=[smem(),...]
    pallas_call x2, Pallas kernels: 4.89 us -> 3.23 us  [shifted(): pl.pallas_call(shift_kernel, out_shape=jax.ShapeDtypeStruct((GROUPS, SPAN...]
    pallas_call x2, Pallas kernels: 11.2 us -> 9.71 us  [the longest x1 6.3 us: on_device(): pl.pallas_call(push_kernel, out_shape=joined_shape, in_specs=[smem()] + [...]
  transfers between devices with their start and end apart: 29 -> 19, of which waited for: 9 -> 8; matrix products, arithmetic and copies ran while one was open for 3% -> 0% of each run, Pallas kernels for 28% -> 27%
where the time goes in v2:
time: 87.4 us; the launch traced here: 87 us
  Pallas kernels  27.7 us (32%)
  blocking collectives  24.4 us (28%)
  starting transfers between devices  14.8 us (17%)
  waiting for transfers between devices  14.8 us (17%)
  local copies, waits for them, and re-layouts  4.35 us (5%)
    all_to_all x1, blocking collectives, on_device(): lax.all_to_all(packed, RAD, split_axis=0, concat_axis=0, tiled=True)  24.4 us
    ppermute x17, waiting for transfers between devices, across(): lax.ppermute(value, axis, [(source, target(source)) for source in range(c...  10.8 us
    ppermute x17, starting transfers between devices, across(): lax.ppermute(value, axis, [(source, target(source)) for source in range(c...  10.1 us
    pallas_call x1, Pallas kernels, on_device(): pl.pallas_call(field_kernel, out_shape=(tiles, tiles), in_specs=[smem(),...  7.54 us
    pallas_call x1, Pallas kernels, on_device(): pl.pallas_call(push_kernel, out_shape=joined_shape, in_specs=[smem()] + [...  6.3 us
    pallas_call x1, Pallas kernels, on_device(): pl.pallas_call(kick_kernel, out_shape=(tiles, tiles, jax.ShapeDtypeStruct...  4.14 us
    ppermute x1, waiting for transfers between devices, on_device(): lax.ppermute(edge_down, RAD, [(i + 1, i) for i in range(rad_count - 1)])  3.96 us
    ppermute x1, starting transfers between devices, on_device(): lax.ppermute(edge_up, RAD, [(i, i + 1) for i in range(rad_count - 1)])  3.48 us
  transfers between devices with their start and end apart: 19, of which 8 were waited for; matrix products, arithmetic and copies ran while one was open for 0% of the time, Pallas kernels for 27%

profile of v2, /device:TPU:0, one launch (start us, length us, event | category | flops | bytes accessed | tf_op | source)
XLA Modules:
  0.0 87.0 jit_solution(13695500903608369498)
XLA Ops:
  0.6 0.8 fusion
  1.4 1.5 %collective-permute-start.1 = (f32[64,128]{1,0:T(8,128)S(1)}, f32[64,128]{1,0:T(8,128)S(1)}, u32[]{:S(2)}, u32[]{:S(2)}) collective-permute-start(f32[64,128]{1,0:T(8,128)S(1)} %pad_maximum_fusion.2), channel_id=1, source_target_pairs={{0,3},{1,0},{2,1},{3,2},{4,7},{5,4},{6,5},{7,6},{8,11},{9,8},{10,9... | collective-permute-start | bytes 98312 | tf_op jit(solution)/shard_map/ppermute | solution.py:513
  2.9 1.7 %collective-permute-done.1.right_ref = f32[64,128]{1,0:T(8,128)S(1)} collective-permute-done((f32[64,128]{1,0:T(8,128)S(1)}, f32[64,128]{1,0:T(8,128)S(1)}, u32[]{:S(2)}, u32[]{:S(2)}) %collective-permute-start.1) | collective-permute-done | bytes 32800 | tf_op jit(solution)/shard_map/ppermute | solution.py:513
  4.6 1.6 %collective-permute-done.left_ref = f32[64,128]{1,0:T(8,128)S(1)} collective-permute-done((f32[64,128]{1,0:T(8,128)S(1)}, f32[64,128]{1,0:T(8,128)S(1)}, u32[]{:S(2)}, u32[]{:S(2)}) %collective-permute-start) | collective-permute-done | bytes 32800 | tf_op jit(solution)/shard_map/ppermute | solution.py:513
  6.3 0.9 %collective-permute-start.3 = (f32[4,256,128]{2,1,0:T(8,128)}, f32[4,256,128]{2,1,0:T(8,128)S(1)}, u32[]{:S(2)}, u32[]{:S(2)}) collective-permute-start(f32[4,256,128]{2,1,0:T(8,128)} %bitcast.8.vrad_ref.own_ref), channel_id=1, source_target_pairs={{0,2},{1,3},{2,0},{3,1},{4,6},{5,7},{6,4},{7,5},{8,10},{9,11},{10,... | collective-permute-start | bytes 1572872 | tf_op jit(solution)/shard_map/ppermute | solution.py:513
  7.2 0.7 copy-done.12
  7.8 1.0 %copy-done = f32[32,4096]{1,0:T(8,128)S(1)} copy-done((f32[32,4096]{1,0:T(8,128)S(1)}, f32[32,4096]{1,0:T(8,128)}, u32[]{:S(2)}) %copy-start) | copy-done | bytes 524312
  8.9 1.0 %copy-done.3 = f32[32,4096]{1,0:T(8,128)S(1)} copy-done((f32[32,4096]{1,0:T(8,128)S(1)}, f32[32,4096]{1,0:T(8,128)}, u32[]{:S(2)}) %copy-start.3) | copy-done | bytes 524312
  9.9 3.0 %azimuth.1 = (f32[4,256,128]{2,1,0:T(8,128)S(1)}, f32[72,128]{1,0:T(8,128)S(1)}, f32[72,128]{1,0:T(8,128)S(1)}) custom-call(f32[4,256,128]{2,1,0:T(8,128)S(1)} %bitcast.48, f32[4,256,128]{2,1,0:T(8,128)S(1)} %bitcast.44, f32[4,256,128]{2,1,0:T(8,128)} %bitcast.8.vrad_ref.own_ref, f32[64,128]{1,0:T(8,128)S(1)} %collective-permute-done.left_ref, ...), custom_call_target="tpu_custom_call" | custom-call | flops 1000000 | bytes 2500000 | tf_op jit(solution)/shard_map/azimuth/pallas_call | solution.py:559
  12.9 3.5 %collective-permute-start.4 = (f32[72,128]{1,0:T(8,128)S(1)}, f32[72,128]{1,0:T(8,128)S(1)}, u32[]{:S(2)}, u32[]{:S(2)}) collective-permute-start(f32[72,128]{1,0:T(8,128)S(1)} %get-tuple-element.26), channel_id=1, source_target_pairs={{0,4},{4,8},{8,12},{12,16},{16,20},{20,24},{24,28},{28,32},{32,36}... | collective-permute-start | bytes 110600 | tf_op jit(solution)/shard_map/ppermute | solution.py:576
  16.4 0.0 copy-start.16
  16.4 1.3 %collective-permute-start.5 = (f32[72,128]{1,0:T(8,128)S(1)}, f32[72,128]{1,0:T(8,128)S(1)}, u32[]{:S(2)}, u32[]{:S(2)}) collective-permute-start(f32[72,128]{1,0:T(8,128)S(1)} %get-tuple-element.27), channel_id=1, source_target_pairs={{4,0},{8,4},{12,8},{16,12},{20,16},{24,20},{28,24},{32,28},{36,32}... | collective-permute-start | bytes 110600 | tf_op jit(solution)/shard_map/ppermute | solution.py:577
  17.7 0.1 collective-permute-start.10
  17.8 0.5 collective-permute-start.2
  18.3 4.0 %collective-permute-done.5 = f32[72,128]{1,0:T(8,128)S(1)} collective-permute-done((f32[72,128]{1,0:T(8,128)S(1)}, f32[72,128]{1,0:T(8,128)S(1)}, u32[]{:S(2)}, u32[]{:S(2)}) %collective-permute-start.5) | collective-permute-done | bytes 36896 | tf_op jit(solution)/shard_map/ppermute | solution.py:577
  22.3 1.1 %collective-permute-start.6 = (f32[4,256,128]{2,1,0:T(8,128)S(1)}, f32[4,256,128]{2,1,0:T(8,128)S(1)}, u32[]{:S(2)}, u32[]{:S(2)}) collective-permute-start(f32[4,256,128]{2,1,0:T(8,128)S(1)} %get-tuple-element.28.own_ref), channel_id=1, source_target_pairs={{0,2},{1,3},{2,0},{3,1},{4,6},{5,7},{6,4},{7,5},{8,10},{9,11},{10,... | collective-permute-start | bytes 1572872 | tf_op jit(solution)/shard_map/ppermute | solution.py:513
  23.4 0.6 copy-done.14
  24.1 0.1 sine_bitcast_fusion
  24.2 1.0 %collective-permute-start.7 = (f32[2,72,128]{2,1,0:T(8,128)S(1)}, f32[2,72,128]{2,1,0:T(8,128)S(1)}, u32[]{:S(2)}, u32[]{:S(2)}) collective-permute-start(f32[2,72,128]{2,1,0:T(8,128)S(1)} %pad_maximum_fusion.edge_own_ref), channel_id=1, source_target_pairs={{0,2},{1,3},{2,0},{3,1},{4,6},{5,7},{6,4},{7,5},{8,10},{9,11},{10,... | collective-permute-start | bytes 221192 | tf_op jit(solution)/shard_map/ppermute | solution.py:513
  25.2 0.2 collective-permute-start.8
  25.4 1.0 %collective-permute-start.9 = (f32[2,72,128]{2,1,0:T(8,128)S(1)}, f32[2,72,128]{2,1,0:T(8,128)S(1)}, u32[]{:S(2)}, u32[]{:S(2)}) collective-permute-start(f32[2,72,128]{2,1,0:T(8,128)S(1)} %pad_maximum_fusion.edge_own_ref), channel_id=1, source_target_pairs={{0,3},{1,2},{2,1},{3,0},{4,7},{5,6},{6,5},{7,4},{8,11},{9,10},{10,... | collective-permute-start | bytes 221192 | tf_op jit(solution)/shard_map/ppermute | solution.py:513
  26.4 0.1 broadcast_in_dim.2.radius_ref
  26.5 7.5 %field.1 = (f32[4,256,128]{2,1,0:T(8,128)S(1)}, f32[4,256,128]{2,1,0:T(8,128)S(1)}) custom-call(f32[6,32]{1,0:T(8,128)S(1)} %stack.39.members_ref, f32[32,128]{1,0:T(8,128)S(1)} %broadcast_in_dim.2.radius_ref, f32[16,32,128]{2,1,0:T(8,128)S(1)} %copy-done.2), custom_call_target="tpu_custom_call" | custom-call | flops 6000000 | bytes 15000000 | tf_op jit(solution)/shard_map/field/pallas_call | solution.py:589
  34.0 0.0 copy-start.4
  34.1 0.0 copy-start.9
  34.1 0.0 copy-start.10
  34.1 1.9 %shift_vrad.1.vrad_ref = f32[4,256,128]{2,1,0:T(8,128)S(1)} custom-call(s32[32]{0:T(128)S(1)} %copy-done.12, f32[4,256,128]{2,1,0:T(8,128)} %bitcast.8.vrad_ref.own_ref, f32[4,256,128]{2,1,0:T(8,128)S(1)} %collective-permute-done.10.mate_ref, f32[4,256,128]{2,1,0:T(8,128)S(1)} %collective-permute-done.3.cross_ref, ...), custom_call_target="tpu_custom_call" | custom-call | flops 2000000 | bytes 5000000 | tf_op jit(solution)/shard_map/shift_vrad/pallas_call | solution.py:189
  36.0 0.8 collective-permute-done.7.edge_cross_ref
  36.8 0.6 collective-permute-start.12
  37.4 1.0 %collective-permute-start.13 = (f32[4,256,128]{2,1,0:T(8,128)S(1)}, f32[4,256,128]{2,1,0:T(8,128)S(1)}, u32[]{:S(2)}, u32[]{:S(2)}) collective-permute-start(f32[4,256,128]{2,1,0:T(8,128)S(1)} %bitcast.45), channel_id=1, source_target_pairs={{0,2},{1,3},{2,0},{3,1},{4,6},{5,7},{6,4},{7,5},{8,10},{9,11},{10,... | collective-permute-start | bytes 1572872 | tf_op jit(solution)/shard_map/ppermute | solution.py:513
  38.4 0.6 collective-permute-done.12.far_ref
  39.0 3.4 %transport.1 = (f32[4,256,128]{2,1,0:T(8,128)}, f32[4,256,128]{2,1,0:T(8,128)S(1)}, f32[32,512]{1,0:T(8,128)S(1)}) custom-call(s32[32]{0:T(128)S(1)} %copy-done.12, f32[4,256,128]{2,1,0:T(8,128)S(1)} %get-tuple-element.28.own_ref, f32[4,256,128]{2,1,0:T(8,128)S(1)} %collective-permute-done.2.mate_ref, f32[4,256,128]{2,1,0:T(8,128)S(1)} %collective-permute-done.6.cross_ref, ...), custom_call_target="tpu_custom_call" | custom-call | flops 3000000 | bytes 7500000 | tf_op jit(solution)/shard_map/transport/pallas_call | solution.py:608
  42.4 6.3 %push.1.a_ref = f32[192,128]{1,0:T(8,128)S(1)} custom-call(f32[6,32]{1,0:T(8,128)S(1)} %stack.39.members_ref, f32[32,128]{1,0:T(8,128)S(1)} %broadcast_in_dim.2.radius_ref, f32[16,32,128]{2,1,0:T(8,128)S(1)} %copy-done.2, f32[4,256,128]{2,1,0:T(8,128)S(1)} %get-tuple-element.32.dens_ref, f32[32,512]{1,0:T(8,128)S(1)} %get-tuple-element.33.spectra_ref), custom_call_target="tpu_custom_call" | custom-call | flops 6000000 | bytes 15000000 | tf_op jit(solution)/shard_map/push/pallas_call | solution.py:630
  48.7 0.0 copy-start.8
  48.7 0.0 copy-start.11
  48.7 2.6 %collective-permute-done.13.cross_ref = f32[4,256,128]{2,1,0:T(8,128)S(1)} collective-permute-done((f32[4,256,128]{2,1,0:T(8,128)S(1)}, f32[4,256,128]{2,1,0:T(8,128)S(1)}, u32[]{:S(2)}, u32[]{:S(2)}) %collective-permute-start.13) | collective-permute-done | bytes 524320 | tf_op jit(solution)/shard_map/ppermute | solution.py:513
  51.3 1.0 %collective-permute-start.14 = (f32[192,128]{1,0:T(8,128)S(1)}, f32[192,128]{1,0:T(8,128)S(1)}, u32[]{:S(2)}, u32[]{:S(2)}) collective-permute-start(f32[192,128]{1,0:T(8,128)S(1)} %push.1.a_ref), channel_id=1, source_target_pairs={{0,2},{1,3},{2,0},{3,1},{4,6},{5,7},{6,4},{7,5},{8,10},{9,11},{10,... | collective-permute-start | bytes 294920 | tf_op jit(solution)/shard_map/ppermute | solution.py:513
  52.3 0.9 %collective-permute-start.17 = (f32[192,128]{1,0:T(8,128)S(1)}, f32[192,128]{1,0:T(8,128)S(1)}, u32[]{:S(2)}, u32[]{:S(2)}) collective-permute-start(f32[192,128]{1,0:T(8,128)S(1)} %push.1.a_ref), channel_id=1, source_target_pairs={{0,3},{1,2},{2,1},{3,0},{4,7},{5,6},{6,5},{7,4},{8,11},{9,10},{10,... | collective-permute-start | bytes 294920 | tf_op jit(solution)/shard_map/ppermute | solution.py:513
  53.2 0.3 collective-permute-start.18
  53.5 1.3 %shift_vphi.1.vphi_ref = f32[4,256,128]{2,1,0:T(8,128)S(1)} custom-call(s32[32]{0:T(128)S(1)} %copy-done.12, f32[4,256,128]{2,1,0:T(8,128)S(1)} %bitcast.47, f32[4,256,128]{2,1,0:T(8,128)S(1)} %collective-permute-done.15.mate_ref, f32[4,256,128]{2,1,0:T(8,128)S(1)} %collective-permute-done.13.cross_ref, f32[4,256,128]{2,1,0:T(8,128)S(1)} %collective-permute-done.16.far_ref), custom_call_target="tpu_custom_call" | custom-call | flops 2000000 | bytes 5000000 | tf_op jit(solution)/shard_map/shift_vphi/pallas_call | solution.py:189
  54.8 2.1 %collective-permute-done.14.b_ref = f32[192,128]{1,0:T(8,128)S(1)} collective-permute-done((f32[192,128]{1,0:T(8,128)S(1)}, f32[192,128]{1,0:T(8,128)S(1)}, u32[]{:S(2)}, u32[]{:S(2)}) %collective-permute-start.14) | collective-permute-done | bytes 98336 | tf_op jit(solution)/shard_map/ppermute | solution.py:513
  56.9 1.3 %collective-permute-done.17.c_ref = f32[192,128]{1,0:T(8,128)S(1)} collective-permute-done((f32[192,128]{1,0:T(8,128)S(1)}, f32[192,128]{1,0:T(8,128)S(1)}, u32[]{:S(2)}, u32[]{:S(2)}) %collective-permute-start.17) | collective-permute-done | bytes 98336 | tf_op jit(solution)/shard_map/ppermute | solution.py:513
  58.3 0.0 copy-start.13
  58.3 0.1 moments.1
  58.4 0.0 copy-start.5
  58.5 0.0 copy-start.6
  58.5 24.4 %all_to_all.5.moments_ref = f32[32,16,128]{2,1,0:T(8,128)S(1)} all-to-all(f32[32,16,128]{2,1,0:T(8,128)S(1)} %get-tuple-element.39), channel_id=1, replica_groups=mesh['rad_0'=4,'rad_1'=2,'rad_2'=4,'az_0'=2,'az_1'=2] {'rad_0','rad_1','..., dimensions={0} | all-to-all | bytes 524288 | tf_op jit(solution)/shard_map/all_to_all | solution.py:660
  82.9 4.1 %kick.1 = (f32[4,256,128]{2,1,0:T(8,128)}, f32[4,256,128]{2,1,0:T(8,128)}, f32[2,32]{1,0:T(2,128)}) custom-call(f32[32,512]{1,0:T(8,128)S(1)} %get-tuple-element.38.spectra_ref, f32[32,16,128]{2,1,0:T(8,128)S(1)} %all_to_all.5.moments_ref, f32[8,128]{1,0:T(8,128)S(1)} %copy-done.13, f32[32,128]{1,0:T(8,128)S(1)} %broadcast_in_dim.2.radius_ref, ...), custom_call_target="tpu_custom_call" | custom-call | flops 5000000 | bytes 12500000 | tf_op jit(solution)/shard_map/kick/pallas_call | solution.py:662
  (42 shorter events, 0.2 us)
Async XLA Ops:
  1.4 3.2 %collective-permute-start.1 = (f32[64,128]{1,0:T(8,128)S(1)}, f32[64,128]{1,0:T(8,128)S(1)}, u32[]{:S(2)}, u32[]{:S(2)}) collective-permute-start(f32[64,128]{1,0:T(8,128)S(1)} %pad_maximum_fusion.2), channel_id=1, source_target_pairs={{0,3},{1,0},{2,1},{3,2},{4,7},{5,4},{6,5},{7,6},{8,11},{9,8},{10,9... | collective-permute-start | bytes 98312 | tf_op jit(solution)/shard_map/ppermute | solution.py:513
  2.9 3.3 %collective-permute-start = (f32[64,128]{1,0:T(8,128)S(1)}, f32[64,128]{1,0:T(8,128)S(1)}, u32[]{:S(2)}, u32[]{:S(2)}) collective-permute-start(f32[64,128]{1,0:T(8,128)S(1)} %pad_maximum_fusion.1), channel_id=1, source_target_pairs={{0,1},{1,2},{2,3},{3,0},{4,5},{5,6},{6,7},{7,4},{8,9},{9,10},{10,1... | collective-permute-start | bytes 98312 | tf_op jit(solution)/shard_map/ppermute | solution.py:513
  6.3 16.0 %collective-permute-start.3 = (f32[4,256,128]{2,1,0:T(8,128)}, f32[4,256,128]{2,1,0:T(8,128)S(1)}, u32[]{:S(2)}, u32[]{:S(2)}) collective-permute-start(f32[4,256,128]{2,1,0:T(8,128)} %bitcast.8.vrad_ref.own_ref), channel_id=1, source_target_pairs={{0,2},{1,3},{2,0},{3,1},{4,6},{5,7},{6,4},{7,5},{8,10},{9,11},{10,... | collective-permute-start | bytes 1572872 | tf_op jit(solution)/shard_map/ppermute | solution.py:513
  7.2 0.7 copy-start.12
  7.8 1.0 %copy-start = (f32[32,4096]{1,0:T(8,128)S(1)}, f32[32,4096]{1,0:T(8,128)}, u32[]{:S(2)}) copy-start(f32[32,4096]{1,0:T(8,128)} %param.19) | copy-start | bytes 1572868
  8.9 1.0 %copy-start.3 = (f32[32,4096]{1,0:T(8,128)S(1)}, f32[32,4096]{1,0:T(8,128)}, u32[]{:S(2)}) copy-start(f32[32,4096]{1,0:T(8,128)} %param.17) | copy-start | bytes 1572868
  9.9 16.6 %copy-start.2 = (f32[16,32,128]{2,1,0:T(8,128)S(1)}, f32[16,32,128]{2,1,0:T(8,128)}, u32[]{:S(2)}) copy-start(f32[16,32,128]{2,1,0:T(8,128)} %constant.55.clone.angles_ref) | copy-start | bytes 786436
  12.9 5.4 %collective-permute-start.4 = (f32[72,128]{1,0:T(8,128)S(1)}, f32[72,128]{1,0:T(8,128)S(1)}, u32[]{:S(2)}, u32[]{:S(2)}) collective-permute-start(f32[72,128]{1,0:T(8,128)S(1)} %get-tuple-element.26), channel_id=1, source_target_pairs={{0,4},{4,8},{8,12},{12,16},{16,20},{20,24},{24,28},{28,32},{32,36}... | collective-permute-start | bytes 110600 | tf_op jit(solution)/shard_map/ppermute | solution.py:576
  16.4 7.0 %copy-start.15 = (f32[32]{0:T(128)S(1)}, f32[32]{0:T(128)}, u32[]{:S(2)}) copy-start(f32[32]{0:T(128)} %param.23) | copy-start | bytes 388
  16.4 7.0 %copy-start.16 = (s32[32]{0:T(128)S(1)}, s32[32]{0:T(128)}, u32[]{:S(2)}) copy-start(s32[32]{0:T(128)} %param.21) | copy-start | bytes 388
  16.4 5.9 %collective-permute-start.5 = (f32[72,128]{1,0:T(8,128)S(1)}, f32[72,128]{1,0:T(8,128)S(1)}, u32[]{:S(2)}, u32[]{:S(2)}) collective-permute-start(f32[72,128]{1,0:T(8,128)S(1)} %get-tuple-element.27), channel_id=1, source_target_pairs={{4,0},{8,4},{12,8},{16,12},{20,16},{24,20},{28,24},{32,28},{36,32}... | collective-permute-start | bytes 110600 | tf_op jit(solution)/shard_map/ppermute | solution.py:577
  17.7 7.5 %collective-permute-start.10 = (f32[4,256,128]{2,1,0:T(8,128)}, f32[4,256,128]{2,1,0:T(8,128)S(1)}, u32[]{:S(2)}, u32[]{:S(2)}) collective-permute-start(f32[4,256,128]{2,1,0:T(8,128)} %bitcast.8.vrad_ref.own_ref), channel_id=1, source_target_pairs={{0,1},{1,0},{2,3},{3,2},{4,5},{5,4},{6,7},{7,6},{8,9},{9,8},{10,11... | collective-permute-start | bytes 1572872 | tf_op jit(solution)/shard_map/ppermute | solution.py:513
  17.8 19.0 %collective-permute-start.2 = (f32[4,256,128]{2,1,0:T(8,128)S(1)}, f32[4,256,128]{2,1,0:T(8,128)S(1)}, u32[]{:S(2)}, u32[]{:S(2)}) collective-permute-start(f32[4,256,128]{2,1,0:T(8,128)S(1)} %get-tuple-element.28.own_ref), channel_id=1, source_target_pairs={{0,1},{1,0},{2,3},{3,2},{4,5},{5,4},{6,7},{7,6},{8,9},{9,8},{10,11... | collective-permute-start | bytes 1572872 | tf_op jit(solution)/shard_map/ppermute | solution.py:513
  22.3 14.5 %collective-permute-start.6 = (f32[4,256,128]{2,1,0:T(8,128)S(1)}, f32[4,256,128]{2,1,0:T(8,128)S(1)}, u32[]{:S(2)}, u32[]{:S(2)}) collective-permute-start(f32[4,256,128]{2,1,0:T(8,128)S(1)} %get-tuple-element.28.own_ref), channel_id=1, source_target_pairs={{0,2},{1,3},{2,0},{3,1},{4,6},{5,7},{6,4},{7,5},{8,10},{9,11},{10,... | collective-permute-start | bytes 1572872 | tf_op jit(solution)/shard_map/ppermute | solution.py:513
  23.4 2.0 %collective-permute-start.11 = (f32[4,256,128]{2,1,0:T(8,128)S(1)}, f32[4,256,128]{2,1,0:T(8,128)S(1)}, u32[]{:S(2)}, u32[]{:S(2)}) collective-permute-start(f32[4,256,128]{2,1,0:T(8,128)S(1)} %collective-permute-done.3.cross_ref), channel_id=1, source_target_pairs={{0,1},{1,0},{2,3},{3,2},{4,5},{5,4},{6,7},{7,6},{8,9},{9,8},{10,11... | collective-permute-start | bytes 1572872 | tf_op jit(solution)/shard_map/ppermute | solution.py:513
  23.4 0.7 copy-start.14
  24.2 12.6 %collective-permute-start.7 = (f32[2,72,128]{2,1,0:T(8,128)S(1)}, f32[2,72,128]{2,1,0:T(8,128)S(1)}, u32[]{:S(2)}, u32[]{:S(2)}) collective-permute-start(f32[2,72,128]{2,1,0:T(8,128)S(1)} %pad_maximum_fusion.edge_own_ref), channel_id=1, source_target_pairs={{0,2},{1,3},{2,0},{3,1},{4,6},{5,7},{6,4},{7,5},{8,10},{9,11},{10,... | collective-permute-start | bytes 221192 | tf_op jit(solution)/shard_map/ppermute | solution.py:513
  25.2 11.6 %collective-permute-start.8 = (f32[2,72,128]{2,1,0:T(8,128)S(1)}, f32[2,72,128]{2,1,0:T(8,128)S(1)}, u32[]{:S(2)}, u32[]{:S(2)}) collective-permute-start(f32[2,72,128]{2,1,0:T(8,128)S(1)} %pad_maximum_fusion.edge_own_ref), channel_id=1, source_target_pairs={{0,1},{1,0},{2,3},{3,2},{4,5},{5,4},{6,7},{7,6},{8,9},{9,8},{10,11... | collective-permute-start | bytes 221192 | tf_op jit(solution)/shard_map/ppermute | solution.py:513
  25.4 11.4 %collective-permute-start.9 = (f32[2,72,128]{2,1,0:T(8,128)S(1)}, f32[2,72,128]{2,1,0:T(8,128)S(1)}, u32[]{:S(2)}, u32[]{:S(2)}) collective-permute-start(f32[2,72,128]{2,1,0:T(8,128)S(1)} %pad_maximum_fusion.edge_own_ref), channel_id=1, source_target_pairs={{0,3},{1,2},{2,1},{3,0},{4,7},{5,6},{6,5},{7,4},{8,11},{9,10},{10,... | collective-permute-start | bytes 221192 | tf_op jit(solution)/shard_map/ppermute | solution.py:513
  34.0 3.4 %copy-start.1 = (f32[32,4096]{1,0:T(8,128)S(1)}, f32[32,4096]{1,0:T(8,128)}, u32[]{:S(2)}) copy-start(f32[32,4096]{1,0:T(8,128)} %param.19) | copy-start | bytes 1572868
  34.0 4.9 %copy-start.4 = (f32[64,512]{1,0:T(8,128)S(1)}, f32[64,512]{1,0:T(8,128)}, u32[]{:S(2)}) copy-start(f32[64,512]{1,0:T(8,128)} %constant.58.clone.twiddle_ref) | copy-start | bytes 393220
  34.1 4.9 %copy-start.9 = (bf16[256,512]{1,0:T(8,128)(2,1)S(1)}, bf16[256,512]{1,0:T(8,128)(2,1)}, u32[]{:S(2)}) copy-start(bf16[256,512]{1,0:T(8,128)(2,1)} %constant.56.clone.high_ref) | copy-start | bytes 786436
  34.1 4.9 %copy-start.10 = (bf16[256,512]{1,0:T(8,128)(2,1)S(1)}, bf16[256,512]{1,0:T(8,128)(2,1)}, u32[]{:S(2)}) copy-start(bf16[256,512]{1,0:T(8,128)(2,1)} %constant.57.clone.low_ref) | copy-start | bytes 786436
  36.8 2.1 %collective-permute-start.12 = (f32[4,256,128]{2,1,0:T(8,128)S(1)}, f32[4,256,128]{2,1,0:T(8,128)S(1)}, u32[]{:S(2)}, u32[]{:S(2)}) collective-permute-start(f32[4,256,128]{2,1,0:T(8,128)S(1)} %collective-permute-done.6.cross_ref), channel_id=1, source_target_pairs={{0,1},{1,0},{2,3},{3,2},{4,5},{5,4},{6,7},{7,6},{8,9},{9,8},{10,11... | collective-permute-start | bytes 1572872 | tf_op jit(solution)/shard_map/ppermute | solution.py:513
  37.4 13.9 %collective-permute-start.13 = (f32[4,256,128]{2,1,0:T(8,128)S(1)}, f32[4,256,128]{2,1,0:T(8,128)S(1)}, u32[]{:S(2)}, u32[]{:S(2)}) collective-permute-start(f32[4,256,128]{2,1,0:T(8,128)S(1)} %bitcast.45), channel_id=1, source_target_pairs={{0,2},{1,3},{2,0},{3,1},{4,6},{5,7},{6,4},{7,5},{8,10},{9,11},{10,... | collective-permute-start | bytes 1572872 | tf_op jit(solution)/shard_map/ppermute | solution.py:513
  38.4 15.1 %collective-permute-start.15 = (f32[4,256,128]{2,1,0:T(8,128)S(1)}, f32[4,256,128]{2,1,0:T(8,128)S(1)}, u32[]{:S(2)}, u32[]{:S(2)}) collective-permute-start(f32[4,256,128]{2,1,0:T(8,128)S(1)} %bitcast.46), channel_id=1, source_target_pairs={{0,1},{1,0},{2,3},{3,2},{4,5},{5,4},{6,7},{7,6},{8,9},{9,8},{10,11... | collective-permute-start | bytes 1572872 | tf_op jit(solution)/shard_map/ppermute | solution.py:513
  48.7 9.6 %copy-start.7 = (f32[32,512]{1,0:T(8,128)S(1)}, f32[32,512]{1,0:T(8,128)}, u32[]{:S(2)}) copy-start(f32[32,512]{1,0:T(8,128)} %constant.59.clone.lift_ref) | copy-start | bytes 196612
  48.7 9.6 %copy-start.8 = (f32[32,512]{1,0:T(8,128)S(1)}, f32[32,512]{1,0:T(8,128)}, u32[]{:S(2)}) copy-start(f32[32,512]{1,0:T(8,128)} %constant.60.clone.drop_ref) | copy-start | bytes 196612
  48.7 9.6 %copy-start.11 = (f32[8,512]{1,0:T(8,128)S(1)}, f32[8,512]{1,0:T(8,128)}, u32[]{:S(2)}) copy-start(f32[8,512]{1,0:T(8,128)} %constant.61.clone.vectors_ref) | copy-start | bytes 49156
  51.3 2.2 %collective-permute-start.16 = (f32[4,256,128]{2,1,0:T(8,128)S(1)}, f32[4,256,128]{2,1,0:T(8,128)S(1)}, u32[]{:S(2)}, u32[]{:S(2)}) collective-permute-start(f32[4,256,128]{2,1,0:T(8,128)S(1)} %collective-permute-done.13.cross_ref), channel_id=1, source_target_pairs={{0,1},{1,0},{2,3},{3,2},{4,5},{5,4},{6,7},{7,6},{8,9},{9,8},{10,11... | collective-permute-start | bytes 1572872 | tf_op jit(solution)/shard_map/ppermute | solution.py:513
  51.3 5.6 %collective-permute-start.14 = (f32[192,128]{1,0:T(8,128)S(1)}, f32[192,128]{1,0:T(8,128)S(1)}, u32[]{:S(2)}, u32[]{:S(2)}) collective-permute-start(f32[192,128]{1,0:T(8,128)S(1)} %push.1.a_ref), channel_id=1, source_target_pairs={{0,2},{1,3},{2,0},{3,1},{4,6},{5,7},{6,4},{7,5},{8,10},{9,11},{10,... | collective-permute-start | bytes 294920 | tf_op jit(solution)/shard_map/ppermute | solution.py:513
  52.3 6.0 %collective-permute-start.17 = (f32[192,128]{1,0:T(8,128)S(1)}, f32[192,128]{1,0:T(8,128)S(1)}, u32[]{:S(2)}, u32[]{:S(2)}) collective-permute-start(f32[192,128]{1,0:T(8,128)S(1)} %push.1.a_ref), channel_id=1, source_target_pairs={{0,3},{1,2},{2,1},{3,0},{4,7},{5,6},{6,5},{7,4},{8,11},{9,10},{10,... | collective-permute-start | bytes 294920 | tf_op jit(solution)/shard_map/ppermute | solution.py:513
  53.2 5.1 %collective-permute-start.18 = (f32[192,128]{1,0:T(8,128)S(1)}, f32[192,128]{1,0:T(8,128)S(1)}, u32[]{:S(2)}, u32[]{:S(2)}) collective-permute-start(f32[192,128]{1,0:T(8,128)S(1)} %push.1.a_ref), channel_id=1, source_target_pairs={{0,1},{1,0},{2,3},{3,2},{4,5},{5,4},{6,7},{7,6},{8,9},{9,8},{10,11... | collective-permute-start | bytes 294920 | tf_op jit(solution)/shard_map/ppermute | solution.py:513
  58.3 24.6 %copy-start.13 = (f32[8,128]{1,0:T(8,128)S(1)}, f32[8,128]{1,0:T(8,128)}, u32[]{:S(2)}) copy-start(f32[8,128]{1,0:T(8,128)} %constant.62.clone.rate_ref) | copy-start | bytes 12292
  58.4 24.5 %copy-start.5 = (bf16[512,256]{1,0:T(8,128)(2,1)S(1)}, bf16[512,256]{1,0:T(8,128)(2,1)}, u32[]{:S(2)}) copy-start(bf16[512,256]{1,0:T(8,128)(2,1)} %constant.63.clone.high_ref) | copy-start | bytes 786436
  58.5 24.4 %copy-start.6 = (bf16[512,256]{1,0:T(8,128)(2,1)S(1)}, bf16[512,256]{1,0:T(8,128)(2,1)}, u32[]{:S(2)}) copy-start(bf16[512,256]{1,0:T(8,128)(2,1)} %constant.64.clone.low_ref) | copy-start | bytes 786436

commit v3 on v2

--- a/solution.py
+++ b/solution.py
@@ -95,6 +95,10 @@
     return pl.BlockSpec(memory_space=pl.ANY)
 
 
+def hbm(value):
+    return pltpu.with_memory_space_constraint(value, pltpu.HBM)
+
+
 def params():
     return pltpu.CompilerParams(vmem_limit_bytes=14 * 1024 * 1024)
 
@@ -107,10 +111,23 @@
     return jnp.where(speeds > 0, speeds * upstream, speeds * downstream)
 
 
-def azimuth_kernel(
-    dens_ref, phi_ref, vrad_ref, left_ref, right_ref, offs_ref, out_ref, up_ref, down_ref,
-    dens_buf, phi_buf, vrad_buf, sems,
-):
+def border_kernel(dens_ref, phi_ref, vrad_ref, out_ref, buf_ref, sems):
+    copies = []
+    for index, ref in enumerate((dens_ref, phi_ref, vrad_ref)):
+        for side, group in enumerate((0, GROUPS - 1)):
+            at = 2 * index + side
+            copies.append(pltpu.make_async_copy(ref.at[group], buf_ref.at[at], sems.at[at]))
+    for copy in copies:
+        copy.start()
+    for copy in copies:
+        copy.wait()
+    for side, row in enumerate((0, 7)):
+        for index in range(3):
+            rows = buf_ref[2 * index + side, pl.ds(row, CHUNKS, stride=8), :]
+            out_ref[side, pl.ds(index, CHUNKS, stride=3), :] = rows
+
+
+def azimuth_kernel(dens_ref, phi_ref, mate_ref, far_ref, out_ref, dens_buf, phi_buf, sems):
     lane = lax.broadcasted_iota(jnp.int32, (1, 8, 128), 2)
     copies = []
     for group in range(GROUPS):
@@ -120,40 +137,34 @@
                 pltpu.make_async_copy(phi_ref.at[group], phi_buf.at[group], sems.at[2 * group + 1]),
             )
         )
-    ends = (
-        pltpu.make_async_copy(vrad_ref.at[0], vrad_buf.at[0], sems.at[8]),
-        pltpu.make_async_copy(vrad_ref.at[3], vrad_buf.at[1], sems.at[9]),
-    )
-    for pair in copies + [ends]:
+    for pair in copies:
         for copy in pair:
             copy.start()
+
+    odd = lax.axis_index(AZ) % 2 == 1
 
     def following(value):
         turned = pltpu.roll(value, 127, 2)
         return jnp.where(lane == 127, turned[1:], turned[:-1])
 
     def widened(ref, group, base):
-        rows = slice(base + 8 * group, base + 8 * group + 8)
         middle = ref[group].reshape(CHUNKS, 8, 128)
-        return jnp.concatenate([left_ref[rows, :][None], middle, right_ref[rows, :][None]], axis=0)
+        mate, far = mate_ref[base + group][None], far_ref[base + group][None]
+        return jnp.concatenate(
+            [jnp.where(odd, mate, far), middle, jnp.where(odd, far, mate)], axis=0
+        )
 
     for group in range(GROUPS):
         for copy in copies[group]:
             copy.wait()
         dens = widened(dens_buf, group, 0)
-        phi = widened(phi_buf, group, ROWS)
+        phi = widened(phi_buf, group, GROUPS)
         speeds = 0.5 * (phi[:-1] + following(phi))
         flux = donor_flux(speeds, dens[:-1], following(dens))
         turned = pltpu.roll(flux, 1, 2)
         before = jnp.where(lane == 0, turned[:-1], turned[1:])
         stepped = dens[1:-1] - courant * (flux[1:] - before)
         out_ref[group] = stepped.reshape(SPAN, 128)
-    for copy in ends:
-        copy.wait()
-    for side, (ref, group, row) in enumerate(((down_ref, 0, 0), (up_ref, 3, 7))):
-        ref[pl.ds(0, CHUNKS, stride=2), :] = out_ref[group, pl.ds(row, CHUNKS, stride=8), :]
-        ref[pl.ds(1, CHUNKS, stride=2), :] = vrad_buf[side, pl.ds(row, CHUNKS, stride=8), :]
-        ref[64:72, :] = jnp.full((8, 128), offs_ref[8 * group + row].astype(F32), F32)
 
 
 def fill_ring(group, own_ref, mate_ref, cross_ref, far_ref, ring_ref, unit):
@@ -198,6 +209,33 @@
     )(offsets, own, mate, cross, far)
 
 
+def edge_kernel(
+    offs_ref, own_ref, mate_ref, cross_ref, far_ref, up_ref, down_ref, ring_ref, flux_ref, line_ref
+):
+    unit = 3 * CHUNKS
+    length = 5 * CHUNKS
+    lane = lax.broadcasted_iota(jnp.int32, (length, 128), 1)
+    for side, ref in enumerate((down_ref, up_ref)):
+        fill_ring(side, own_ref, mate_ref, cross_ref, far_ref, ring_ref, unit)
+        ring_ref[5 * unit : 5 * unit + 24, :] = ring_ref[unit : unit + 24, :]
+        offset = offs_ref[(ROWS - 1) * side]
+
+        def following(index):
+            here = pltpu.roll(ring_ref[pl.ds(index, length, stride=3), :], 127, 1)
+            there = pltpu.roll(ring_ref[pl.ds(index + 3, length, stride=3), :], 127, 1)
+            return jnp.where(lane == 127, there, here)
+
+        dens = ring_ref[pl.ds(0, length, stride=3), :]
+        phi = ring_ref[pl.ds(1, length, stride=3), :]
+        flux = donor_flux(0.5 * (phi + following(1)), dens, following(0))
+        flux_ref[8 : 8 + length, :] = flux
+        before = pltpu.roll(flux_ref[7 : 7 + length, :], 1, 1)
+        before = jnp.where(lane == 0, before, pltpu.roll(flux, 1, 1))
+        line_ref[0:length, :] = dens - courant * (flux - before)
+        ref[0:CHUNKS, :] = shift_row(line_ref, 1, 0, offset)
+        ref[CHUNKS : 2 * CHUNKS, :] = shift_row(ring_ref, 3, 2, offset)
+
+
 def split_value(value):
     high = value.astype(BF16)
     return high, (value - high.astype(F32)).astype(BF16)
@@ -208,26 +246,13 @@
 
 
 def transport_kernel(
-    offs_ref, own_ref, mate_ref, cross_ref, far_ref,
-    edge_own_ref, edge_mate_ref, edge_cross_ref, edge_far_ref,
-    vrad_ref, high_ref, low_ref, twiddle_ref,
+    moved_ref, low_edge_ref, high_edge_ref, vrad_ref, high_ref, low_ref, twiddle_ref,
     whole_ref, dens_ref, spectra_ref,
-    ring_ref, edge_ref, moved_ref, speed_ref, whole_sem,
+    other_ref, speed_ref, whole_sem,
 ):
-    for side, (place, row) in enumerate(((0, 7), (5, 0))):
-        fill_ring(
-            side, edge_own_ref, edge_mate_ref, edge_cross_ref, edge_far_ref, edge_ref, 2 * CHUNKS
-        )
-        offset = jnp.max(edge_own_ref[side, 64:72, :]).astype(jnp.int32)
-        moved_ref[place, pl.ds(row, CHUNKS, stride=8), :] = shift_row(edge_ref, 2, 0, offset)
-        speed_ref[side, pl.ds(row, CHUNKS, stride=8), :] = shift_row(edge_ref, 2, 1, offset)
-
-    @pl.loop(0, GROUPS)
-    def _(group):
-        fill_ring(group, own_ref, mate_ref, cross_ref, far_ref, ring_ref, SPAN)
-        for row in range(8):
-            moved = shift_row(ring_ref, 8, row, offs_ref[group * 8 + row])
-            moved_ref[group + 1, pl.ds(row, CHUNKS, stride=8), :] = moved
+    for side, (ref, row) in enumerate(((low_edge_ref, 7), (high_edge_ref, 0))):
+        other_ref[side, pl.ds(row, CHUNKS, stride=8), :] = ref[0:CHUNKS, :]
+        speed_ref[side, pl.ds(row, CHUNKS, stride=8), :] = ref[CHUNKS : 2 * CHUNKS, :]
 
     sub = lax.broadcasted_iota(jnp.int32, (1, 8, 128), 1)
     own_index = lax.axis_index(RAD)
@@ -250,9 +275,11 @@
             def tiles(ref, index):
                 return ref[index, where, :].reshape(step, 8, 128)
 
-            dens = tiles(moved_ref, group + 1)
-            dens_above = above(dens, tiles(moved_ref, group + 2))
-            dens_below = below(dens, tiles(moved_ref, group))
+            dens = tiles(moved_ref, group)
+            upper = tiles(moved_ref, group + 1) if group < 3 else tiles(other_ref, 1)
+            lower = tiles(moved_ref, group - 1) if group > 0 else tiles(other_ref, 0)
+            dens_above = above(dens, upper)
+            dens_below = below(dens, lower)
             speed = tiles(vrad_ref, group)
             upper = tiles(vrad_ref, group + 1) if group < 3 else tiles(speed_ref, 1)
             lower = tiles(vrad_ref, group - 1) if group > 0 else tiles(speed_ref, 0)
@@ -270,7 +297,7 @@
     sector = lax.axis_index(AZ)
     cos_sum = jnp.zeros((ROWS, MODES), F32)
     sin_sum = jnp.zeros((ROWS, MODES), F32)
-    together = 4
+    together = 8
     for first in range(0, BLOCKS, together):
         pieces = []
         for block in range(first, first + together):
@@ -293,13 +320,17 @@
     whole.wait()
 
 
-def field_kernel(
-    members_ref, radius_ref, angles_ref, radial_ref, azim_ref,
-    gap_ref, chord_ref, lift_ref, side_ref,
-):
+def field_kernel(members_ref, radius_ref, angles_ref, *refs, second):
+    radial_ref, azim_ref, gap_ref, chord_ref, lift_ref, side_ref = refs[-6:]
+    many = CHUNKS // 2
+    base = many * second
+    if second:
+        rows = slice(0, 8 * base)
+        radial_ref[:, rows, :] = refs[0][:, rows, :]
+        azim_ref[:, rows, :] = refs[1][:, rows, :]
     sector = lax.axis_index(AZ)
-    half_cos = angles_ref[sector * 4]
-    half_sin = angles_ref[sector * 4 + 1]
+    half_cos = angles_ref[sector * 4, base : base + many, :]
+    half_sin = angles_ref[sector * 4 + 1, base : base + many, :]
     radius = radius_ref[...]
     halves = 0.5 / radius
 
@@ -316,9 +347,10 @@
         near = half_sin * cosine - half_cos * sine
         far = half_cos * cosine + half_sin * sine
         chord = (2.0 * embryo_radius) * (near * near)
-        chord_ref[rows, :] = chord * scale
-        lift_ref[rows, :] = chord - embryo_radius
-        side_ref[rows, :] = (2.0 * embryo_radius) * (near * far)
+        columns = pl.ds(pl.multiple_of(member * many, many), many)
+        chord_ref[columns, :] = chord * scale
+        lift_ref[columns, :] = chord - embryo_radius
+        side_ref[columns, :] = (2.0 * embryo_radius) * (near * far)
 
     pieces = [radius[8 * g : 8 * g + 8] for g in range(GROUPS)]
     ends = []
@@ -327,7 +359,7 @@
         ends.append(root * root * root)
     together = 2
 
-    @pl.loop(0, CHUNKS // together)
+    @pl.loop(0, many // together)
     def _(part):
         zero = jnp.zeros((8, 128), F32)
 
@@ -335,7 +367,7 @@
             radial, azim = list(carried[0]), list(carried[1])
             rows = []
             for k in range(together):
-                row = pl.ds(member * 32 + part * together + k, 1)
+                row = pl.ds(member * many + part * together + k, 1)
                 rows.append(
                     [jnp.broadcast_to(ref[row, :], (8, 128)) for ref in (chord_ref, lift_ref, side_ref)]
                 )
@@ -353,14 +385,14 @@
         count = together * GROUPS
         radial, azim = lax.fori_loop(0, EMB, visit, ((zero,) * count, (zero,) * count), unroll=4)
         for k in range(together):
-            where = pl.ds(pl.multiple_of((part * together + k) * 8, 8), 8)
+            where = pl.ds(pl.multiple_of((base + part * together + k) * 8, 8), 8)
             for g in range(GROUPS):
                 radial_ref[g, where, :] = radial[k * GROUPS + g] * ends[g]
                 azim_ref[g, where, :] = azim[k * GROUPS + g] * ends[g]
 
 
 def push_kernel(
-    members_ref, radius_ref, angles_ref, dens_ref, spectra_ref, out_ref, mass_ref, chord_ref
+    members_ref, radius_ref, angles_ref, dens_ref, spectra_ref, out_ref, mass_ref, chord_ref, push_ref
 ):
     for part in range(4):
         out_ref[ROWS * part : ROWS * part + ROWS, :] = spectra_ref[:, 128 * part : 128 * part + 128]
@@ -405,12 +437,18 @@
             total = total + plain
         place_x = embryo_radius * members_ref[4, member]
         place_y = embryo_radius * members_ref[5, member]
-        out_ref[pl.ds(4 * ROWS + member, 1), :] = jnp.sum(push_x - place_x * total, axis=0, keepdims=True)
-        out_ref[pl.ds(4 * ROWS + EMB + member, 1), :] = jnp.sum(push_y - place_y * total, axis=0, keepdims=True)
-
-
-def moment_kernel(a_ref, b_ref, c_ref, d_ref, lift_ref, drop_ref, vectors_ref, spectra_ref, packed_ref, one_ref):
-    total = (a_ref[...] + b_ref[...]) + (c_ref[...] + d_ref[...])
+        push_ref[pl.ds(member, 1), :] = jnp.sum(push_x - place_x * total, axis=0, keepdims=True)
+        push_ref[pl.ds(EMB + member, 1), :] = jnp.sum(push_y - place_y * total, axis=0, keepdims=True)
+
+    push = jnp.broadcast_to(jnp.sum(push_ref[...], axis=1, keepdims=True), (2 * EMB, 128))
+    row = lax.broadcasted_iota(jnp.int32, (2 * EMB, 128), 0)
+    lane = lax.broadcasted_iota(jnp.int32, (2 * EMB, 128), 1)
+    push = jnp.sum(jnp.where(row == lane, push, 0.0), axis=0, keepdims=True)
+    out_ref[4 * ROWS : 4 * ROWS + 8, :] = jnp.broadcast_to(push, (8, 128))
+
+
+def moment_kernel(a_ref, b_ref, lift_ref, drop_ref, vectors_ref, spectra_ref, packed_ref, one_ref):
+    total = a_ref[...] + b_ref[...]
     for part in range(4):
         columns = slice(128 * part, 128 * part + 128)
         spectra = total[ROWS * part : ROWS * part + ROWS]
@@ -420,12 +458,7 @@
         down = jnp.sum(spectra * lift_ref[:, columns], axis=0, keepdims=True) / factor
         one_ref[part : part + 1, :] = up
         one_ref[4 + part : 5 + part, :] = down
-    push = total[4 * ROWS :]
-    push = jnp.broadcast_to(jnp.sum(push, axis=1, keepdims=True), (2 * EMB, 128))
-    row = lax.broadcasted_iota(jnp.int32, (2 * EMB, 128), 0)
-    lane = lax.broadcasted_iota(jnp.int32, (2 * EMB, 128), 1)
-    push = jnp.sum(jnp.where(row == lane, push, 0.0), axis=0, keepdims=True)
-    one_ref[8:16, :] = jnp.broadcast_to(push, (8, 128))
+    one_ref[8:16, :] = total[4 * ROWS :]
     one = one_ref[...]
     for copy in range(packed_ref.shape[0]):
         packed_ref[copy] = one
@@ -467,45 +500,52 @@
     swapped = jnp.concatenate([even[:, MODES:], even[:, :MODES]], axis=1)
     azim = swapped * vectors_ref[2:3, :] * inverse
     sector = lax.axis_index(AZ)
-    copies = []
-    for block in range(BLOCKS):
-        turn = twiddle_ref[pl.ds(sector * BLOCKS + block, 1), :]
-        cosine, sine = turn[:, :MODES], turn[:, MODES:]
+    together = 4
+
+    def whole_copies(quarter):
+        rows = pl.ds(pl.multiple_of(16 * together * quarter, 16 * together), 16 * together)
+        return [
+            pltpu.make_async_copy(source.at[:, rows, :], target.at[:, rows, :], sems.at[index, quarter])
+            for index, (source, target) in enumerate(
+                ((out_radial_ref, whole_radial_ref), (out_azim_ref, whole_azim_ref))
+            )
+        ]
+
+    @pl.loop(0, BLOCKS // together)
+    def _(quarter):
         pieces = []
-        for coef in (radial, azim):
-            cos_coef, sin_coef = coef[:, :MODES], coef[:, MODES:]
-            pieces.append(
-                jnp.concatenate(
-                    [cos_coef * cosine + sin_coef * sine, sin_coef * cosine - cos_coef * sine], axis=1
+        for index in range(together):
+            turn = twiddle_ref[pl.ds(sector * BLOCKS + quarter * together + index, 1), :]
+            cosine, sine = turn[:, :MODES], turn[:, MODES:]
+            for coef in (radial, azim):
+                cos_coef, sin_coef = coef[:, :MODES], coef[:, MODES:]
+                pieces.append(
+                    jnp.concatenate(
+                        [cos_coef * cosine + sin_coef * sine, sin_coef * cosine - cos_coef * sine], axis=1
+                    )
                 )
-            )
         high, low = split_value(jnp.concatenate(pieces, axis=0))
         part = dot(high, high_ref[...]) + (dot(low, high_ref[...]) + dot(high, low_ref[...]))
-        for half in range(2):
-            where = slice(8 * (2 * block + half), 8 * (2 * block + half) + 8)
-            columns = slice(128 * half, 128 * half + 128)
-            disk = part[:ROWS, columns].reshape(GROUPS, 8, 128)
-            out_radial_ref[:, where, :] = vrad_ref[:, where, :] + timestep_length * (
-                disk - radial_ref[:, where, :]
-            )
-            disk = part[ROWS:, columns].reshape(GROUPS, 8, 128)
-            out_azim_ref[:, where, :] = vphi_ref[:, where, :] + timestep_length * (
-                disk - azim_ref[:, where, :]
-            )
-        if block % 4 == 3:
-            quarter = block // 4
-            rows = slice(64 * quarter, 64 * quarter + 64)
-            for index, (source, target) in enumerate(
-                ((out_radial_ref, whole_radial_ref), (out_azim_ref, whole_azim_ref))
-            ):
-                copies.append(
-                    pltpu.make_async_copy(
-                        source.at[:, rows, :], target.at[:, rows, :], sems.at[index, quarter]
-                    )
+        for index in range(together):
+            for half in range(2):
+                start = 16 * together * quarter + 8 * (2 * index + half)
+                where = pl.ds(pl.multiple_of(start, 8), 8)
+                columns = slice(128 * half, 128 * half + 128)
+                rows = 2 * ROWS * index
+                disk = part[rows : rows + ROWS, columns].reshape(GROUPS, 8, 128)
+                out_radial_ref[:, where, :] = vrad_ref[:, where, :] + timestep_length * (
+                    disk - radial_ref[:, where, :]
                 )
-                copies[-1].start()
-    for copy in copies:
-        copy.wait()
+                disk = part[rows + ROWS : rows + 2 * ROWS, columns].reshape(GROUPS, 8, 128)
+                out_azim_ref[:, where, :] = vphi_ref[:, where, :] + timestep_length * (
+                    disk - azim_ref[:, where, :]
+                )
+        for copy in whole_copies(quarter):
+            copy.start()
+
+    for quarter in range(BLOCKS // together):
+        for copy in whole_copies(quarter):
+            copy.wait()
 
 
 def across(value, axis, target):
@@ -534,11 +574,26 @@
     vrad = to_tiles(outward_drift)
     vphi = to_tiles(leftover_angular_drift)
 
+    odd = lax.axis_index(AZ) % 2 == 1
     ends = jnp.concatenate([surface_mass[:, -128:], leftover_angular_drift[:, -128:]])
     begins = jnp.concatenate([surface_mass[:, :128], leftover_angular_drift[:, :128]])
-    left = across(ends, AZ, lambda i: (i + 1) % 4)
-    right = across(begins, AZ, lambda i: (i - 1) % 4)
-    vrad_cross = across(after(vrad, left, right), AZ, lambda i: i ^ 2)
+    outer = jnp.where(odd, ends, begins).reshape(2 * GROUPS, 8, 128)
+    inner = jnp.where(odd, begins, ends).reshape(2 * GROUPS, 8, 128)
+    border_far = across(outer, AZ, lambda i: i ^ 3)
+    border_mate = across(inner, AZ, lambda i: i ^ 1)
+    edge_rows = pl.pallas_call(
+        border_kernel,
+        out_shape=jax.ShapeDtypeStruct((2, 3 * CHUNKS, 128), F32),
+        in_specs=[pl.BlockSpec(memory_space=pltpu.HBM)] * 3,
+        out_specs=vmem(),
+        scratch_shapes=[pltpu.VMEM((6, SPAN, 128), F32), pltpu.SemaphoreType.DMA((6,))],
+        compiler_params=params(),
+        cost_estimate=cost(1),
+        name="borders",
+    )(hbm(dens), hbm(vphi), hbm(vrad))
+    edge_cross = across(edge_rows, AZ, lambda i: i ^ 2)
+    edge_mate = across(edge_rows, AZ, lambda i: i ^ 1)
+    vrad_cross = across(after(vrad, border_mate, border_far, edge_rows), AZ, lambda i: i ^ 2)
     vrad_mate = across(vrad, AZ, lambda i: i ^ 1)
 
     cell = np.float32(cell_step)
@@ -556,51 +611,65 @@
         ]
     )
 
-    dens_two, edge_up, edge_down = pl.pallas_call(
+    dens_two = pl.pallas_call(
         azimuth_kernel,
-        out_shape=(tiles, jax.ShapeDtypeStruct((72, 128), F32), jax.ShapeDtypeStruct((72, 128), F32)),
-        in_specs=[pl.BlockSpec(memory_space=pltpu.HBM)] * 3 + [vmem()] * 2 + [smem()],
-        out_specs=(vmem(), vmem(), vmem()),
+        out_shape=tiles,
+        in_specs=[pl.BlockSpec(memory_space=pltpu.HBM)] * 2 + [vmem()] * 2,
+        out_specs=vmem(),
         scratch_shapes=[
             pltpu.VMEM((GROUPS, SPAN, 128), F32),
             pltpu.VMEM((GROUPS, SPAN, 128), F32),
-            pltpu.VMEM((2, SPAN, 128), F32),
-            pltpu.SemaphoreType.DMA((10,)),
+            pltpu.SemaphoreType.DMA((8,)),
         ],
         compiler_params=params(),
         cost_estimate=cost(1),
         name="azimuth",
-    )(dens, vphi, vrad, left, right, angular_offsets)
-
+    )(hbm(dens), hbm(vphi), border_mate, border_far)
+
+    edge_far = across(edge_cross, AZ, lambda i: i ^ 1)
+    edge = jax.ShapeDtypeStruct((2 * CHUNKS, 128), F32)
+    edge_up, edge_down = pl.pallas_call(
+        edge_kernel,
+        out_shape=(edge, edge),
+        in_specs=[smem()] + [vmem()] * 4,
+        out_specs=(vmem(), vmem()),
+        scratch_shapes=[
+            pltpu.VMEM((3 * RING // 8, 128), F32),
+            pltpu.VMEM((RING // 8 + 8, 128), F32),
+            pltpu.VMEM((RING // 8, 128), F32),
+        ],
+        compiler_params=params(),
+        cost_estimate=cost(1),
+        name="edges",
+    )(angular_offsets, edge_rows, edge_mate, edge_cross, edge_far)
     rad_count = lax.axis_size(RAD)
     edge_low = lax.ppermute(edge_up, RAD, [(i, i + 1) for i in range(rad_count - 1)])
     edge_high = lax.ppermute(edge_down, RAD, [(i + 1, i) for i in range(rad_count - 1)])
-    edges = jnp.stack([edge_low, edge_high])
-    edges_cross, edges_mate, edges_far = (
-        across(edges, AZ, lambda i, k=k: i ^ k) for k in (2, 1, 3)
-    )
-
+
+    def field(second, *before):
+        return pl.pallas_call(
+            functools.partial(field_kernel, second=second),
+            out_shape=(tiles, tiles),
+            in_specs=[smem(), vmem(), vmem()] + [vmem()] * len(before),
+            out_specs=(vmem(), vmem()),
+            scratch_shapes=[pltpu.VMEM((EMB * 32, 128), F32)] + [pltpu.VMEM((EMB * 16, 128), F32)] * 3,
+            compiler_params=params(),
+            cost_estimate=cost(4),
+            name=f"field_{second}",
+        )(members, radius, angles, *before)
+
+    first_field = field(0)
     dens_mate = across(dens_two, AZ, lambda i: i ^ 1)
-    dens_two_later = after(dens_two, vrad_cross, edge_low, edge_high)
-    dens_cross = across(dens_two_later, AZ, lambda i: i ^ 2)
-    vrad_far = across(vrad_cross, AZ, lambda i: i ^ 1)
+    dens_cross = across(after(dens_two, vrad_cross, edge_up, *first_field), AZ, lambda i: i ^ 2)
+    vrad_far = across(after(vrad_cross, dens_two, *first_field), AZ, lambda i: i ^ 1)
     vrad_one = shifted(angular_offsets, vrad, vrad_mate, vrad_cross, vrad_far, "shift_vrad")
-
-    radial_field, azim_field = pl.pallas_call(
-        field_kernel,
-        out_shape=(tiles, tiles),
-        in_specs=[smem(), vmem(), vmem()],
-        out_specs=(vmem(), vmem()),
-        scratch_shapes=[pltpu.VMEM((EMB * 32, 128), F32)] * 4,
-        compiler_params=params(),
-        cost_estimate=cost(6),
-        name="field",
-    )(members, radius, angles)
-
-    dens_cross = after(
-        dens_cross, edges_cross, edges_mate, edges_far, dens_mate, vrad_one, radial_field
-    )
+    radial_field, azim_field = field(1, *first_field)
+    dens_cross = after(dens_cross, vrad_one, radial_field, dens_mate, edge_low, edge_high)
     dens_far = across(dens_cross, AZ, lambda i: i ^ 1)
+
+    dens_one = shifted(
+        angular_offsets, dens_two, dens_mate, dens_cross, dens_far, "shift_dens"
+    )
     vphi_later = after(vphi, dens_cross)
     vphi_cross = across(vphi_later, AZ, lambda i: i ^ 2)
     vphi_mate = across(vphi_later, AZ, lambda i: i ^ 1)
@@ -608,12 +677,10 @@
     transported, stepped, part = pl.pallas_call(
         transport_kernel,
         out_shape=(tiles, tiles, jax.ShapeDtypeStruct((ROWS, 2 * MODES), F32)),
-        in_specs=[smem()] + [vmem()] * 12,
+        in_specs=[vmem()] * 7,
         out_specs=(anywhere(), vmem(), vmem()),
         scratch_shapes=[
-            pltpu.VMEM((RING, 128), F32),
-            pltpu.VMEM((2 * RING // 8, 128), F32),
-            pltpu.VMEM((GROUPS + 2, SPAN, 128), F32),
+            pltpu.VMEM((2, SPAN, 128), F32),
             pltpu.VMEM((2, SPAN, 128), F32),
             pltpu.SemaphoreType.DMA,
         ],
@@ -621,42 +688,45 @@
         cost_estimate=cost(3),
         name="transport",
     )(
-        angular_offsets, dens_two, dens_mate, dens_cross, dens_far,
-        edges, edges_mate, edges_cross, edges_far,
+        dens_one, edge_low, edge_high,
         vrad_one, basis_high, basis_low, twiddle,
     )
 
-    joined_shape = jax.ShapeDtypeStruct((4 * ROWS + 2 * EMB, 128), F32)
+    joined_shape = jax.ShapeDtypeStruct((4 * ROWS + 8, 128), F32)
     joined = pl.pallas_call(
         push_kernel,
         out_shape=joined_shape,
         in_specs=[smem()] + [vmem()] * 4,
         out_specs=vmem(),
-        scratch_shapes=[pltpu.VMEM((GROUPS, SPAN, 128), F32), pltpu.VMEM((CHUNKS, 128), F32)],
+        scratch_shapes=[
+            pltpu.VMEM((GROUPS, SPAN, 128), F32),
+            pltpu.VMEM((CHUNKS, 128), F32),
+            pltpu.VMEM((2 * EMB, 128), F32),
+        ],
         compiler_params=params(),
         cost_estimate=cost(6),
         name="push",
     )(members, radius, angles, stepped, part)
-    joined = after(joined, vphi_cross)
-    others = [across(joined, AZ, lambda i, k=k: i ^ k) for k in (2, 3, 1)]
-
-    vphi_far = across(after(vphi_cross, joined), AZ, lambda i: i ^ 1)
+    chip = joined + across(joined, AZ, lambda i: i ^ 1)
+    chip_other = across(chip, AZ, lambda i: i ^ 2)
+
+    vphi_far = across(after(vphi_cross, chip), AZ, lambda i: i ^ 1)
     vphi_one = shifted(angular_offsets, vphi_later, vphi_mate, vphi_cross, vphi_far, "shift_vphi")
 
-    others[0] = after(others[0], vphi_one)
+    chip_later = after(chip, vphi_one)
     spectra, packed = pl.pallas_call(
         moment_kernel,
         out_shape=(
             jax.ShapeDtypeStruct((ROWS, 2 * MODES), F32),
             jax.ShapeDtypeStruct((rad_count, 16, 128), F32),
         ),
-        in_specs=[vmem()] * 7,
+        in_specs=[vmem()] * 5,
         out_specs=(vmem(), vmem()),
         scratch_shapes=[pltpu.VMEM((16, 128), F32)],
         compiler_params=params(),
         cost_estimate=cost(1),
         name="moments",
-    )(joined, *others, lift, drop, vectors)
+    )(chip_later, chip_other, lift, drop, vectors)
     gathered = lax.all_to_all(packed, RAD, split_axis=0, concat_axis=0, tiled=True)
 
     kicked_radial, kicked_azim, embryo_disk_acceleration = pl.pallas_call(

time: 87.4 us -> 81.3 us (0.930)
  blocking collectives: 24.4 us -> 20.8 us
  starting transfers between devices: 14.8 us -> 11.6 us
  local copies, waits for them, and re-layouts: 4.35 us -> 1.6 us
  waiting for transfers between devices: 14.8 us -> 17.5 us
    ppermute x17 -> x16, waiting for transfers between devices: 10.8 us -> 17.5 us  [across(): lax.ppermute(value, axis, [(source, target(source)) for source in range(c...]
    ppermute x1, waiting for transfers between devices: 3.96 us -> 0.01 us  [on_device(): lax.ppermute(edge_down, RAD, [(i + 1, i) for i in range(rad_count - 1)])]
    all_to_all x1, blocking collectives: 24.4 us -> 20.8 us  [on_device(): lax.all_to_all(packed, RAD, split_axis=0, concat_axis=0, tiled=True)]
    ppermute x17 -> x16, starting transfers between devices: 10.1 us -> 6.82 us  [across(): lax.ppermute(value, axis, [(source, target(source)) for source in range(c...]
    unnamed x34 -> x32, local copies, waits for them, and re-layouts: 3.47 us -> 0.72 us
    pallas_call x2 -> x5, Pallas kernels: 10.5 us -> 12.8 us  [the longest x2 8.4 us: field(): pl.pallas_call(functools.partial(field_kernel, second=second), out_shape=...]
    pallas_call x1, Pallas kernels: 3.41 us -> 1.99 us  [on_device(): pl.pallas_call(transport_kernel, out_shape=(tiles, tiles, jax.ShapeDtypeS...]
    pallas_call x2 -> x3, Pallas kernels: 3.23 us -> 3.94 us  [shifted(): pl.pallas_call(shift_kernel, out_shape=jax.ShapeDtypeStruct((GROUPS, SPAN...]
  transfers between devices with their start and end apart: 19 -> 18, of which waited for: 8 -> 8; matrix products, arithmetic and copies ran while one was open for 0% -> 0% of each run, Pallas kernels for 27% -> 31%
where the time goes in v3:
time: 81.3 us; the launch traced here: 81 us
  Pallas kernels  28.4 us (35%)
  blocking collectives  20.8 us (26%)
  waiting for transfers between devices  17.5 us (22%)
  starting transfers between devices  11.6 us (14%)
  local copies, waits for them, and re-layouts  1.6 us (2%)
  between operations  0.95 us (1%)
    all_to_all x1, blocking collectives, on_device(): lax.all_to_all(packed, RAD, split_axis=0, concat_axis=0, tiled=True)  20.8 us
    ppermute x16, waiting for transfers between devices, across(): lax.ppermute(value, axis, [(source, target(source)) for source in range(c...  17.5 us
    pallas_call x2, Pallas kernels, field(): pl.pallas_call(functools.partial(field_kernel, second=second), out_shape=...  8.4 us
    ppermute x16, starting transfers between devices, across(): lax.ppermute(value, axis, [(source, target(source)) for source in range(c...  6.82 us
    pallas_call x1, Pallas kernels, on_device(): pl.pallas_call(push_kernel, out_shape=joined_shape, in_specs=[smem()] + [...  6.39 us
    pallas_call x3, Pallas kernels, shifted(): pl.pallas_call(shift_kernel, out_shape=jax.ShapeDtypeStruct((GROUPS, SPAN...  3.94 us
    ppermute x1, starting transfers between devices, on_device(): lax.ppermute(edge_up, RAD, [(i, i + 1) for i in range(rad_count - 1)])  3.47 us
    pallas_call x1, Pallas kernels, on_device(): pl.pallas_call(kick_kernel, out_shape=(tiles, tiles, jax.ShapeDtypeStruct...  3.32 us
  transfers between devices with their start and end apart: 18, of which 8 were waited for; matrix products, arithmetic and copies ran while one was open for 0% of the time, Pallas kernels for 31%

profile of v3, /device:TPU:0, one launch (start us, length us, event | category | flops | bytes accessed | tf_op | source)
XLA Modules:
  0.0 81.0 jit_solution(14556707240735978105)
XLA Ops:
  0.6 0.8 fusion
  1.4 0.1 collective-permute-start
  1.5 2.1 %collective-permute-start.1 = (f32[8,8,128]{2,1,0:T(8,128)S(1)}, f32[8,8,128]{2,1,0:T(8,128)S(1)}, u32[]{:S(2)}, u32[]{:S(2)}) collective-permute-start(f32[8,8,128]{2,1,0:T(8,128)S(1)} %get-tuple-element.50), channel_id=1, source_target_pairs={{0,3},{1,2},{2,1},{3,0},{4,7},{5,6},{6,5},{7,4},{8,11},{9,10},{10,... | collective-permute-start | bytes 98312 | tf_op jit(solution)/shard_map/ppermute | solution.py:553
  3.6 0.1 collective-permute-start.8
  3.7 1.3 %borders.1.own_ref = f32[2,96,128]{2,1,0:T(8,128)S(1)} custom-call(f32[4,256,128]{2,1,0:T(8,128)} %bitcast.55, f32[4,256,128]{2,1,0:T(8,128)} %bitcast.46, f32[4,256,128]{2,1,0:T(8,128)} %bitcast.52), custom_call_target="tpu_custom_call" | custom-call | flops 1000000 | bytes 2500000 | tf_op jit(solution)/shard_map/borders/pallas_call | solution.py:584
  5.1 0.0 copy-start.14
  5.1 0.0 copy-start.15
  5.1 0.4 collective-permute-start.5
  5.5 0.2 collective-permute-start.4
  5.7 1.7 %collective-permute-start.3 = (f32[4,256,128]{2,1,0:T(8,128)S(1)}, f32[4,256,128]{2,1,0:T(8,128)S(1)}, u32[]{:S(2)}, u32[]{:S(2)}) collective-permute-start(f32[4,256,128]{2,1,0:T(8,128)S(1)} %bitcast.53), channel_id=1, source_target_pairs={{0,2},{1,3},{2,0},{3,1},{4,6},{5,7},{6,4},{7,5},{8,10},{9,11},{10,... | collective-permute-start | bytes 1572872 | tf_op jit(solution)/shard_map/ppermute | solution.py:553
  7.5 0.1 sine_bitcast_fusion
  7.6 3.2 %collective-permute-done.5.cross_ref = f32[2,96,128]{2,1,0:T(8,128)S(1)} collective-permute-done((f32[2,96,128]{2,1,0:T(8,128)S(1)}, f32[2,96,128]{2,1,0:T(8,128)S(1)}, u32[]{:S(2)}, u32[]{:S(2)}) %collective-permute-start.5) | collective-permute-done | bytes 98336 | tf_op jit(solution)/shard_map/ppermute | solution.py:553
  10.8 0.1 broadcast_in_dim.2.radius_ref
  10.9 4.2 %field_0.1 = (f32[4,256,128]{2,1,0:T(8,128)S(1)}, f32[4,256,128]{2,1,0:T(8,128)S(1)}) custom-call(f32[6,32]{1,0:T(8,128)S(1)} %stack.27.members_ref, f32[32,128]{1,0:T(8,128)S(1)} %broadcast_in_dim.2.radius_ref, f32[16,32,128]{2,1,0:T(8,128)S(1)} %copy-done.1), custom_call_target="tpu_custom_call" | custom-call | flops 4000000 | bytes 10000000 | tf_op jit(solution)/shard_map/field_0/pallas_call | solution.py:650
  15.1 1.9 %azimuth.1.own_ref = f32[4,256,128]{2,1,0:T(8,128)S(1)} custom-call(f32[4,256,128]{2,1,0:T(8,128)} %bitcast.56, f32[4,256,128]{2,1,0:T(8,128)} %bitcast.47, f32[8,8,128]{2,1,0:T(8,128)S(1)} %collective-permute-done.mate_ref, f32[8,8,128]{2,1,0:T(8,128)S(1)} %collective-permute-done.1.far_ref), custom_call_target="tpu_custom_call" | custom-call | flops 1000000 | bytes 2500000 | tf_op jit(solution)/shard_map/azimuth/pallas_call | solution.py:614
  17.0 0.6 collective-permute-start.2
  17.6 4.0 %collective-permute-done.3.cross_ref = f32[4,256,128]{2,1,0:T(8,128)S(1)} collective-permute-done((f32[4,256,128]{2,1,0:T(8,128)S(1)}, f32[4,256,128]{2,1,0:T(8,128)S(1)}, u32[]{:S(2)}, u32[]{:S(2)}) %collective-permute-start.3) | collective-permute-done | bytes 524320 | tf_op jit(solution)/shard_map/ppermute | solution.py:553
  21.6 0.6 copy-done.11
  22.2 1.1 %edges.1 = (f32[64,128]{1,0:T(8,128)S(1)}, f32[64,128]{1,0:T(8,128)S(1)}) custom-call(s32[32]{0:T(128)S(1)} %copy-done.11, f32[2,96,128]{2,1,0:T(8,128)S(1)} %borders.1.own_ref, f32[2,96,128]{2,1,0:T(8,128)S(1)} %collective-permute-done.4.mate_ref, f32[2,96,128]{2,1,0:T(8,128)S(1)} %collective-permute-done.5.cross_ref, ...), custom_call_target="tpu_custom_call" | custom-call | flops 1000000 | bytes 2500000 | tf_op jit(solution)/shard_map/edges/pallas_call | solution.py:631
  23.3 0.3 collective-permute-start.7
  23.7 3.5 %collective-permute-start.10 = (f32[64,128]{1,0:T(8,128)S(1)}, f32[64,128]{1,0:T(8,128)S(1)}, u32[]{:S(2)}, u32[]{:S(2)}) collective-permute-start(f32[64,128]{1,0:T(8,128)S(1)} %get-tuple-element.26), channel_id=1, source_target_pairs={{0,4},{4,8},{8,12},{12,16},{16,20},{20,24},{24,28},{28,32},{32,36}... | collective-permute-start | bytes 98312 | tf_op jit(solution)/shard_map/ppermute | solution.py:646
  27.2 1.3 %collective-permute-start.11 = (f32[64,128]{1,0:T(8,128)S(1)}, f32[64,128]{1,0:T(8,128)S(1)}, u32[]{:S(2)}, u32[]{:S(2)}) collective-permute-start(f32[64,128]{1,0:T(8,128)S(1)} %get-tuple-element.32), channel_id=1, source_target_pairs={{4,0},{8,4},{12,8},{16,12},{20,16},{24,20},{28,24},{32,28},{36,32}... | collective-permute-start | bytes 98312 | tf_op jit(solution)/shard_map/ppermute | solution.py:647
  28.5 4.2 %field_1.1 = (f32[4,256,128]{2,1,0:T(8,128)S(1)}, f32[4,256,128]{2,1,0:T(8,128)S(1)}) custom-call(f32[6,32]{1,0:T(8,128)S(1)} %stack.27.members_ref, f32[32,128]{1,0:T(8,128)S(1)} %broadcast_in_dim.2.radius_ref, f32[16,32,128]{2,1,0:T(8,128)S(1)} %copy-done.1, f32[4,256,128]{2,1,0:T(8,128)S(1)} %get-tuple-element.27.refs_0_, ...), custom_call_target="tpu_custom_call" | custom-call | flops 4000000 | bytes 10000000 | tf_op jit(solution)/shard_map/field_1/pallas_call | solution.py:650
  32.7 1.3 %shift_vrad.1.vrad_ref = f32[4,256,128]{2,1,0:T(8,128)S(1)} custom-call(s32[32]{0:T(128)S(1)} %copy-done.11, f32[4,256,128]{2,1,0:T(8,128)S(1)} %bitcast.54, f32[4,256,128]{2,1,0:T(8,128)S(1)} %collective-permute-done.8.mate_ref, f32[4,256,128]{2,1,0:T(8,128)S(1)} %collective-permute-done.3.cross_ref, f32[4,256,128]{2,1,0:T(8,128)S(1)} %collective-permute-done.9.far_ref), custom_call_target="tpu_custom_call" | custom-call | flops 2000000 | bytes 5000000 | tf_op jit(solution)/shard_map/shift_vrad/pallas_call | solution.py:200
  34.0 0.0 collective-permute-done.10.low_edge_ref
  34.1 3.8 %collective-permute-done.7.cross_ref = f32[4,256,128]{2,1,0:T(8,128)S(1)} collective-permute-done((f32[4,256,128]{2,1,0:T(8,128)S(1)}, f32[4,256,128]{2,1,0:T(8,128)S(1)}, u32[]{:S(2)}, u32[]{:S(2)}) %collective-permute-start.7) | collective-permute-done | bytes 524320 | tf_op jit(solution)/shard_map/ppermute | solution.py:553
  37.8 0.4 collective-permute-start.15
  38.2 1.5 %collective-permute-done.12.far_ref = f32[4,256,128]{2,1,0:T(8,128)S(1)} collective-permute-done((f32[4,256,128]{2,1,0:T(8,128)S(1)}, f32[4,256,128]{2,1,0:T(8,128)S(1)}, u32[]{:S(2)}, u32[]{:S(2)}) %collective-permute-start.12) | collective-permute-done | bytes 524320 | tf_op jit(solution)/shard_map/ppermute | solution.py:553
  39.7 1.3 %shift_dens.1.moved_ref = f32[4,256,128]{2,1,0:T(8,128)S(1)} custom-call(s32[32]{0:T(128)S(1)} %copy-done.11, f32[4,256,128]{2,1,0:T(8,128)S(1)} %azimuth.1.own_ref, f32[4,256,128]{2,1,0:T(8,128)S(1)} %collective-permute-done.2.mate_ref, f32[4,256,128]{2,1,0:T(8,128)S(1)} %collective-permute-done.7.cross_ref, f32[4,256,128]{2,1,0:T(8,128)S(1)} %collective-permute-done.12.far_ref), custom_call_target="tpu_custom_call" | custom-call | flops 2000000 | bytes 5000000 | tf_op jit(solution)/shard_map/shift_dens/pallas_call | solution.py:200
  41.0 0.0 copy-done.3
  41.1 2.0 %transport.1 = (f32[4,256,128]{2,1,0:T(8,128)}, f32[4,256,128]{2,1,0:T(8,128)S(1)}, f32[32,512]{1,0:T(8,128)S(1)}) custom-call(f32[4,256,128]{2,1,0:T(8,128)S(1)} %shift_dens.1.moved_ref, f32[64,128]{1,0:T(8,128)S(1)} %collective-permute-done.10.low_edge_ref, f32[64,128]{1,0:T(8,128)S(1)} %collective-permute-done.11.high_edge_ref, ...), custom_call_target="tpu_custom_call" | custom-call | flops 3000000 | bytes 7500000 | tf_op jit(solution)/shard_map/transport/pallas_call | solution.py:677
  43.1 6.4 %push.1 = f32[136,128]{1,0:T(8,128)S(1)} custom-call(f32[6,32]{1,0:T(8,128)S(1)} %stack.27.members_ref, f32[32,128]{1,0:T(8,128)S(1)} %broadcast_in_dim.2.radius_ref, f32[16,32,128]{2,1,0:T(8,128)S(1)} %copy-done.1, f32[4,256,128]{2,1,0:T(8,128)S(1)} %get-tuple-element.35.dens_ref, f32[32,512]{1,0:T(8,128)S(1)} %get-tuple-element.36.spectra_ref), custom_call_target="tpu_custom_call" | custom-call | flops 6000000 | bytes 15000000 | tf_op jit(solution)/shard_map/push/pallas_call | solution.py:696
  49.5 0.2 collective-permute-start.13
  49.7 0.4 collective-permute-start.14
  50.1 0.7 collective-permute-done.13
  50.8 0.0 copy-start.8
  50.8 0.0 copy-start.9
  50.8 0.0 copy-start.10
  50.9 1.3 %collective-permute-done.15.cross_ref = f32[4,256,128]{2,1,0:T(8,128)S(1)} collective-permute-done((f32[4,256,128]{2,1,0:T(8,128)S(1)}, f32[4,256,128]{2,1,0:T(8,128)S(1)}, u32[]{:S(2)}, u32[]{:S(2)}) %collective-permute-start.15) | collective-permute-done | bytes 524320 | tf_op jit(solution)/shard_map/ppermute | solution.py:553
  52.2 0.3 collective-permute-start.17
  52.5 1.6 %collective-permute-done.16.far_ref = f32[4,256,128]{2,1,0:T(8,128)S(1)} collective-permute-done((f32[4,256,128]{2,1,0:T(8,128)S(1)}, f32[4,256,128]{2,1,0:T(8,128)S(1)}, u32[]{:S(2)}, u32[]{:S(2)}) %collective-permute-start.16) | collective-permute-done | bytes 524320 | tf_op jit(solution)/shard_map/ppermute | solution.py:553
  54.1 1.3 %shift_vphi.1.vphi_ref = f32[4,256,128]{2,1,0:T(8,128)S(1)} custom-call(s32[32]{0:T(128)S(1)} %copy-done.11, f32[4,256,128]{2,1,0:T(8,128)S(1)} %bitcast.50, f32[4,256,128]{2,1,0:T(8,128)S(1)} %collective-permute-done.14.mate_ref, f32[4,256,128]{2,1,0:T(8,128)S(1)} %collective-permute-done.15.cross_ref, f32[4,256,128]{2,1,0:T(8,128)S(1)} %collective-permute-done.16.far_ref), custom_call_target="tpu_custom_call" | custom-call | flops 2000000 | bytes 5000000 | tf_op jit(solution)/shard_map/shift_vphi/pallas_call | solution.py:200
  55.4 1.4 %collective-permute-done.17.b_ref = f32[136,128]{1,0:T(8,128)S(1)} collective-permute-done((f32[136,128]{1,0:T(8,128)S(1)}, f32[136,128]{1,0:T(8,128)S(1)}, u32[]{:S(2)}, u32[]{:S(2)}) %collective-permute-start.17) | collective-permute-done | bytes 69664 | tf_op jit(solution)/shard_map/ppermute | solution.py:553
  56.8 0.0 copy-start.12
  56.9 0.0 copy-start.4
  56.9 0.0 copy-start.5
  56.9 20.8 %all_to_all.5.moments_ref = f32[32,16,128]{2,1,0:T(8,128)S(1)} all-to-all(f32[32,16,128]{2,1,0:T(8,128)S(1)} %get-tuple-element.41), channel_id=1, replica_groups=mesh['rad_0'=4,'rad_1'=2,'rad_2'=4,'az_0'=2,'az_1'=2] {'rad_0','rad_1','..., dimensions={0} | all-to-all | bytes 524288 | tf_op jit(solution)/shard_map/all_to_all | solution.py:730
  77.7 3.3 %kick.1 = (f32[4,256,128]{2,1,0:T(8,128)}, f32[4,256,128]{2,1,0:T(8,128)}, f32[2,32]{1,0:T(2,128)}) custom-call(f32[32,512]{1,0:T(8,128)S(1)} %get-tuple-element.40.spectra_ref, f32[32,16,128]{2,1,0:T(8,128)S(1)} %all_to_all.5.moments_ref, f32[8,128]{1,0:T(8,128)S(1)} %copy-done.12, f32[32,128]{1,0:T(8,128)S(1)} %broadcast_in_dim.2.radius_ref, ...), custom_call_target="tpu_custom_call" | custom-call | flops 5000000 | bytes 12500000 | tf_op jit(solution)/shard_map/kick/pallas_call | solution.py:732
  (41 shorter events, 0.2 us)
Async XLA Ops:
  1.4 4.3 %collective-permute-start = (f32[8,8,128]{2,1,0:T(8,128)S(1)}, f32[8,8,128]{2,1,0:T(8,128)S(1)}, u32[]{:S(2)}, u32[]{:S(2)}) collective-permute-start(f32[8,8,128]{2,1,0:T(8,128)S(1)} %get-tuple-element.51), channel_id=1, source_target_pairs={{0,1},{1,0},{2,3},{3,2},{4,5},{5,4},{6,7},{7,6},{8,9},{9,8},{10,11... | collective-permute-start | bytes 98312 | tf_op jit(solution)/shard_map/ppermute | solution.py:553
  1.5 4.2 %collective-permute-start.1 = (f32[8,8,128]{2,1,0:T(8,128)S(1)}, f32[8,8,128]{2,1,0:T(8,128)S(1)}, u32[]{:S(2)}, u32[]{:S(2)}) collective-permute-start(f32[8,8,128]{2,1,0:T(8,128)S(1)} %get-tuple-element.50), channel_id=1, source_target_pairs={{0,3},{1,2},{2,1},{3,0},{4,7},{5,6},{6,5},{7,4},{8,11},{9,10},{10,... | collective-permute-start | bytes 98312 | tf_op jit(solution)/shard_map/ppermute | solution.py:553
  3.6 23.5 %collective-permute-start.8 = (f32[4,256,128]{2,1,0:T(8,128)}, f32[4,256,128]{2,1,0:T(8,128)S(1)}, u32[]{:S(2)}, u32[]{:S(2)}) collective-permute-start(f32[4,256,128]{2,1,0:T(8,128)} %bitcast.51), channel_id=1, source_target_pairs={{0,1},{1,0},{2,3},{3,2},{4,5},{5,4},{6,7},{7,6},{8,9},{9,8},{10,11... | collective-permute-start | bytes 1572872 | tf_op jit(solution)/shard_map/ppermute | solution.py:553
  3.7 2.0 %copy-start.2 = (f32[32,4096]{1,0:T(8,128)S(1)}, f32[32,4096]{1,0:T(8,128)}, u32[]{:S(2)}) copy-start(f32[32,4096]{1,0:T(8,128)} %param.18) | copy-start | bytes 1572868
  3.7 3.7 %copy-start.13 = (s32[32]{0:T(128)S(1)}, s32[32]{0:T(128)}, u32[]{:S(2)}) copy-start(s32[32]{0:T(128)} %param.22) | copy-start | bytes 388
  3.7 7.2 %copy-start.1 = (f32[16,32,128]{2,1,0:T(8,128)S(1)}, f32[16,32,128]{2,1,0:T(8,128)}, u32[]{:S(2)}) copy-start(f32[16,32,128]{2,1,0:T(8,128)} %constant.71.clone.angles_ref) | copy-start | bytes 786436
  5.1 2.4 %copy-start.14 = (f32[32]{0:T(128)S(1)}, f32[32]{0:T(128)}, u32[]{:S(2)}) copy-start(f32[32]{0:T(128)} %param.23) | copy-start | bytes 388
  5.1 2.4 %copy-start.15 = (s32[32]{0:T(128)S(1)}, s32[32]{0:T(128)}, u32[]{:S(2)}) copy-start(s32[32]{0:T(128)} %param.21) | copy-start | bytes 388
  5.1 5.7 %collective-permute-start.5 = (f32[2,96,128]{2,1,0:T(8,128)S(1)}, f32[2,96,128]{2,1,0:T(8,128)S(1)}, u32[]{:S(2)}, u32[]{:S(2)}) collective-permute-start(f32[2,96,128]{2,1,0:T(8,128)S(1)} %borders.1.own_ref), channel_id=1, source_target_pairs={{0,2},{1,3},{2,0},{3,1},{4,6},{5,7},{6,4},{7,5},{8,10},{9,11},{10,... | collective-permute-start | bytes 294920 | tf_op jit(solution)/shard_map/ppermute | solution.py:553
  5.5 16.1 %collective-permute-start.4 = (f32[2,96,128]{2,1,0:T(8,128)S(1)}, f32[2,96,128]{2,1,0:T(8,128)S(1)}, u32[]{:S(2)}, u32[]{:S(2)}) collective-permute-start(f32[2,96,128]{2,1,0:T(8,128)S(1)} %borders.1.own_ref), channel_id=1, source_target_pairs={{0,1},{1,0},{2,3},{3,2},{4,5},{5,4},{6,7},{7,6},{8,9},{9,8},{10,11... | collective-permute-start | bytes 294920 | tf_op jit(solution)/shard_map/ppermute | solution.py:553
  5.7 15.8 %collective-permute-start.3 = (f32[4,256,128]{2,1,0:T(8,128)S(1)}, f32[4,256,128]{2,1,0:T(8,128)S(1)}, u32[]{:S(2)}, u32[]{:S(2)}) collective-permute-start(f32[4,256,128]{2,1,0:T(8,128)S(1)} %bitcast.53), channel_id=1, source_target_pairs={{0,2},{1,3},{2,0},{3,1},{4,6},{5,7},{6,4},{7,5},{8,10},{9,11},{10,... | collective-permute-start | bytes 1572872 | tf_op jit(solution)/shard_map/ppermute | solution.py:553
  10.8 10.8 %collective-permute-start.6 = (f32[2,96,128]{2,1,0:T(8,128)S(1)}, f32[2,96,128]{2,1,0:T(8,128)S(1)}, u32[]{:S(2)}, u32[]{:S(2)}) collective-permute-start(f32[2,96,128]{2,1,0:T(8,128)S(1)} %collective-permute-done.5.cross_ref), channel_id=1, source_target_pairs={{0,1},{1,0},{2,3},{3,2},{4,5},{5,4},{6,7},{7,6},{8,9},{9,8},{10,11... | collective-permute-start | bytes 294920 | tf_op jit(solution)/shard_map/ppermute | solution.py:553
  17.0 17.1 %collective-permute-start.2 = (f32[4,256,128]{2,1,0:T(8,128)S(1)}, f32[4,256,128]{2,1,0:T(8,128)S(1)}, u32[]{:S(2)}, u32[]{:S(2)}) collective-permute-start(f32[4,256,128]{2,1,0:T(8,128)S(1)} %azimuth.1.own_ref), channel_id=1, source_target_pairs={{0,1},{1,0},{2,3},{3,2},{4,5},{5,4},{6,7},{7,6},{8,9},{9,8},{10,11... | collective-permute-start | bytes 1572872 | tf_op jit(solution)/shard_map/ppermute | solution.py:553
  21.6 0.7 copy-start.11
  21.6 11.1 %collective-permute-start.9 = (f32[4,256,128]{2,1,0:T(8,128)S(1)}, f32[4,256,128]{2,1,0:T(8,128)S(1)}, u32[]{:S(2)}, u32[]{:S(2)}) collective-permute-start(f32[4,256,128]{2,1,0:T(8,128)S(1)} %collective-permute-done.3.cross_ref), channel_id=1, source_target_pairs={{0,1},{1,0},{2,3},{3,2},{4,5},{5,4},{6,7},{7,6},{8,9},{9,8},{10,11... | collective-permute-start | bytes 1572872 | tf_op jit(solution)/shard_map/ppermute | solution.py:553
  23.3 14.5 %collective-permute-start.7 = (f32[4,256,128]{2,1,0:T(8,128)S(1)}, f32[4,256,128]{2,1,0:T(8,128)S(1)}, u32[]{:S(2)}, u32[]{:S(2)}) collective-permute-start(f32[4,256,128]{2,1,0:T(8,128)S(1)} %azimuth.1.own_ref), channel_id=1, source_target_pairs={{0,2},{1,3},{2,0},{3,1},{4,6},{5,7},{6,4},{7,5},{8,10},{9,11},{10,... | collective-permute-start | bytes 1572872 | tf_op jit(solution)/shard_map/ppermute | solution.py:553
  23.7 10.4 %collective-permute-start.10 = (f32[64,128]{1,0:T(8,128)S(1)}, f32[64,128]{1,0:T(8,128)S(1)}, u32[]{:S(2)}, u32[]{:S(2)}) collective-permute-start(f32[64,128]{1,0:T(8,128)S(1)} %get-tuple-element.26), channel_id=1, source_target_pairs={{0,4},{4,8},{8,12},{12,16},{16,20},{20,24},{24,28},{28,32},{32,36}... | collective-permute-start | bytes 98312 | tf_op jit(solution)/shard_map/ppermute | solution.py:646
  27.2 6.9 %collective-permute-start.11 = (f32[64,128]{1,0:T(8,128)S(1)}, f32[64,128]{1,0:T(8,128)S(1)}, u32[]{:S(2)}, u32[]{:S(2)}) collective-permute-start(f32[64,128]{1,0:T(8,128)S(1)} %get-tuple-element.32), channel_id=1, source_target_pairs={{4,0},{8,4},{12,8},{16,12},{20,16},{24,20},{28,24},{32,28},{36,32}... | collective-permute-start | bytes 98312 | tf_op jit(solution)/shard_map/ppermute | solution.py:647
  32.7 5.1 %copy-start = (f32[32,4096]{1,0:T(8,128)S(1)}, f32[32,4096]{1,0:T(8,128)}, u32[]{:S(2)}) copy-start(f32[32,4096]{1,0:T(8,128)} %param.19) | copy-start | bytes 1572868
  37.8 3.2 %copy-start.3 = (f32[64,512]{1,0:T(8,128)S(1)}, f32[64,512]{1,0:T(8,128)}, u32[]{:S(2)}) copy-start(f32[64,512]{1,0:T(8,128)} %constant.74.clone.twiddle_ref) | copy-start | bytes 393220
  37.8 3.2 %copy-start.6 = (bf16[256,512]{1,0:T(8,128)(2,1)S(1)}, bf16[256,512]{1,0:T(8,128)(2,1)}, u32[]{:S(2)}) copy-start(bf16[256,512]{1,0:T(8,128)(2,1)} %constant.72.clone.high_ref) | copy-start | bytes 786436
  37.8 3.3 %copy-start.7 = (bf16[256,512]{1,0:T(8,128)(2,1)S(1)}, bf16[256,512]{1,0:T(8,128)(2,1)}, u32[]{:S(2)}) copy-start(bf16[256,512]{1,0:T(8,128)(2,1)} %constant.73.clone.low_ref) | copy-start | bytes 786436
  37.8 1.9 %collective-permute-start.12 = (f32[4,256,128]{2,1,0:T(8,128)S(1)}, f32[4,256,128]{2,1,0:T(8,128)S(1)}, u32[]{:S(2)}, u32[]{:S(2)}) collective-permute-start(f32[4,256,128]{2,1,0:T(8,128)S(1)} %collective-permute-done.7.cross_ref), channel_id=1, source_target_pairs={{0,1},{1,0},{2,3},{3,2},{4,5},{5,4},{6,7},{7,6},{8,9},{9,8},{10,11... | collective-permute-start | bytes 1572872 | tf_op jit(solution)/shard_map/ppermute | solution.py:553
  37.8 14.3 %collective-permute-start.15 = (f32[4,256,128]{2,1,0:T(8,128)S(1)}, f32[4,256,128]{2,1,0:T(8,128)S(1)}, u32[]{:S(2)}, u32[]{:S(2)}) collective-permute-start(f32[4,256,128]{2,1,0:T(8,128)S(1)} %bitcast.48), channel_id=1, source_target_pairs={{0,2},{1,3},{2,0},{3,1},{4,6},{5,7},{6,4},{7,5},{8,10},{9,11},{10,... | collective-permute-start | bytes 1572872 | tf_op jit(solution)/shard_map/ppermute | solution.py:553
  49.5 1.3 %collective-permute-start.13 = (f32[136,128]{1,0:T(8,128)S(1)}, f32[136,128]{1,0:T(8,128)S(1)}, u32[]{:S(2)}, u32[]{:S(2)}) collective-permute-start(f32[136,128]{1,0:T(8,128)S(1)} %push.1), channel_id=1, source_target_pairs={{0,1},{1,0},{2,3},{3,2},{4,5},{5,4},{6,7},{7,6},{8,9},{9,8},{10,11... | collective-permute-start | bytes 208904 | tf_op jit(solution)/shard_map/ppermute | solution.py:553
  49.7 2.8 %collective-permute-start.14 = (f32[4,256,128]{2,1,0:T(8,128)S(1)}, f32[4,256,128]{2,1,0:T(8,128)S(1)}, u32[]{:S(2)}, u32[]{:S(2)}) collective-permute-start(f32[4,256,128]{2,1,0:T(8,128)S(1)} %bitcast.49), channel_id=1, source_target_pairs={{0,1},{1,0},{2,3},{3,2},{4,5},{5,4},{6,7},{7,6},{8,9},{9,8},{10,11... | collective-permute-start | bytes 1572872 | tf_op jit(solution)/shard_map/ppermute | solution.py:553
  50.8 6.0 %copy-start.8 = (f32[32,512]{1,0:T(8,128)S(1)}, f32[32,512]{1,0:T(8,128)}, u32[]{:S(2)}) copy-start(f32[32,512]{1,0:T(8,128)} %constant.75.clone.lift_ref) | copy-start | bytes 196612
  50.8 5.9 %copy-start.9 = (f32[32,512]{1,0:T(8,128)S(1)}, f32[32,512]{1,0:T(8,128)}, u32[]{:S(2)}) copy-start(f32[32,512]{1,0:T(8,128)} %constant.76.clone.drop_ref) | copy-start | bytes 196612
  50.8 5.9 %copy-start.10 = (f32[8,512]{1,0:T(8,128)S(1)}, f32[8,512]{1,0:T(8,128)}, u32[]{:S(2)}) copy-start(f32[8,512]{1,0:T(8,128)} %constant.77.clone.vectors_ref) | copy-start | bytes 49156
  52.2 1.9 %collective-permute-start.16 = (f32[4,256,128]{2,1,0:T(8,128)S(1)}, f32[4,256,128]{2,1,0:T(8,128)S(1)}, u32[]{:S(2)}, u32[]{:S(2)}) collective-permute-start(f32[4,256,128]{2,1,0:T(8,128)S(1)} %collective-permute-done.15.cross_ref), channel_id=1, source_target_pairs={{0,1},{1,0},{2,3},{3,2},{4,5},{5,4},{6,7},{7,6},{8,9},{9,8},{10,11... | collective-permute-start | bytes 1572872 | tf_op jit(solution)/shard_map/ppermute | solution.py:553
  52.2 4.6 %collective-permute-start.17 = (f32[136,128]{1,0:T(8,128)S(1)}, f32[136,128]{1,0:T(8,128)S(1)}, u32[]{:S(2)}, u32[]{:S(2)}) collective-permute-start(f32[136,128]{1,0:T(8,128)S(1)} %add.52.a_ref), channel_id=1, source_target_pairs={{0,2},{1,3},{2,0},{3,1},{4,6},{5,7},{6,4},{7,5},{8,10},{9,11},{10,... | collective-permute-start | bytes 208904 | tf_op jit(solution)/shard_map/ppermute | solution.py:553
  56.8 20.9 %copy-start.12 = (f32[8,128]{1,0:T(8,128)S(1)}, f32[8,128]{1,0:T(8,128)}, u32[]{:S(2)}) copy-start(f32[8,128]{1,0:T(8,128)} %constant.78.clone.rate_ref) | copy-start | bytes 12292
  56.9 20.9 %copy-start.4 = (bf16[512,256]{1,0:T(8,128)(2,1)S(1)}, bf16[512,256]{1,0:T(8,128)(2,1)}, u32[]{:S(2)}) copy-start(bf16[512,256]{1,0:T(8,128)(2,1)} %constant.79.clone.high_ref) | copy-start | bytes 786436
  56.9 20.9 %copy-start.5 = (bf16[512,256]{1,0:T(8,128)(2,1)S(1)}, bf16[512,256]{1,0:T(8,128)(2,1)}, u32[]{:S(2)}) copy-start(bf16[512,256]{1,0:T(8,128)(2,1)} %constant.80.clone.low_ref) | copy-start | bytes 786436

commit v4 on v3

--- a/solution.py
+++ b/solution.py
@@ -111,12 +111,19 @@
     return jnp.where(speeds > 0, speeds * upstream, speeds * downstream)
 
 
-def border_kernel(dens_ref, phi_ref, vrad_ref, out_ref, buf_ref, sems):
+def border_kernel(dens_ref, phi_ref, vrad_ref, outer_ref, inner_ref, out_ref, buf_ref, sems):
+    odd = lax.axis_index(AZ) % 2
     copies = []
+    for index, ref in enumerate((dens_ref, phi_ref)):
+        where = slice(GROUPS * index, GROUPS * index + GROUPS)
+        outer = pl.ds(pl.multiple_of(odd * (SPAN - 8), 8), 8)
+        inner = pl.ds(pl.multiple_of((1 - odd) * (SPAN - 8), 8), 8)
+        copies.append((ref.at[:, outer, :], outer_ref.at[where]))
+        copies.append((ref.at[:, inner, :], inner_ref.at[where]))
     for index, ref in enumerate((dens_ref, phi_ref, vrad_ref)):
         for side, group in enumerate((0, GROUPS - 1)):
-            at = 2 * index + side
-            copies.append(pltpu.make_async_copy(ref.at[group], buf_ref.at[at], sems.at[at]))
+            copies.append((ref.at[group], buf_ref.at[2 * index + side]))
+    copies = [pltpu.make_async_copy(*copy, sems.at[index]) for index, copy in enumerate(copies)]
     for copy in copies:
         copy.start()
     for copy in copies:
@@ -209,13 +216,46 @@
     )(offsets, own, mate, cross, far)
 
 
+def share_kernel(offs_ref, own_ref, mate_ref, *refs, kinds):
+    odd = lax.axis_index(AZ) % 2
+    sent = (own_ref, 2), (mate_ref, 3 - 2 * odd)
+    kept = (own_ref, 0), (own_ref, 4), (mate_ref, 1 + 2 * odd)
+    out_refs, ring_refs = refs[: len(kinds)], refs[len(kinds) :]
+    for ring_ref in ring_refs:
+        ring_ref[...] = jnp.zeros_like(ring_ref)
+
+    @pl.loop(0, GROUPS)
+    def _(group):
+        for kind, out_ref, ring_ref in zip(kinds, out_refs, ring_refs):
+            for source, place in sent if kind else kept:
+                where = pl.ds(pl.multiple_of(place * SPAN, SPAN), SPAN)
+                ring_ref[where, :] = source[group]
+            for row in range(8):
+                moved = shift_row(ring_ref, 8, row, offs_ref[group * 8 + row])
+                out_ref[group, pl.ds(row, CHUNKS, stride=8), :] = moved
+
+
+def share(offsets, own, mate, kinds, name):
+    return pl.pallas_call(
+        functools.partial(share_kernel, kinds=kinds),
+        out_shape=tuple(jax.ShapeDtypeStruct((GROUPS, SPAN, 128), F32) for _ in kinds),
+        in_specs=[smem(), vmem(), vmem()],
+        out_specs=tuple(vmem() for _ in kinds),
+        scratch_shapes=[pltpu.VMEM((RING, 128), F32) for _ in kinds],
+        compiler_params=params(),
+        cost_estimate=cost(2),
+        name=name,
+    )(offsets, own, mate)
+
+
 def edge_kernel(
-    offs_ref, own_ref, mate_ref, cross_ref, far_ref, up_ref, down_ref, ring_ref, flux_ref, line_ref
+    offs_ref, own_ref, mate_ref, cross_ref, far_ref, first_ref, second_ref, ring_ref, flux_ref, line_ref
 ):
     unit = 3 * CHUNKS
     length = 5 * CHUNKS
     lane = lax.broadcasted_iota(jnp.int32, (length, 128), 1)
-    for side, ref in enumerate((down_ref, up_ref)):
+    sides = []
+    for side in range(2):
         fill_ring(side, own_ref, mate_ref, cross_ref, far_ref, ring_ref, unit)
         ring_ref[5 * unit : 5 * unit + 24, :] = ring_ref[unit : unit + 24, :]
         offset = offs_ref[(ROWS - 1) * side]
@@ -232,8 +272,13 @@
         before = pltpu.roll(flux_ref[7 : 7 + length, :], 1, 1)
         before = jnp.where(lane == 0, before, pltpu.roll(flux, 1, 1))
         line_ref[0:length, :] = dens - courant * (flux - before)
-        ref[0:CHUNKS, :] = shift_row(line_ref, 1, 0, offset)
-        ref[CHUNKS : 2 * CHUNKS, :] = shift_row(ring_ref, 3, 2, offset)
+        sides.append((shift_row(line_ref, 1, 0, offset), shift_row(ring_ref, 3, 2, offset)))
+    even = lax.axis_index(RAD) % 2 == 0
+    for index in range(2):
+        where = slice(CHUNKS * index, CHUNKS * index + CHUNKS)
+        down, up = sides[0][index], sides[1][index]
+        first_ref[where, :] = jnp.where(even, up, down)
+        second_ref[where, :] = jnp.where(even, down, up)
 
 
 def split_value(value):
@@ -246,13 +291,18 @@
 
 
 def transport_kernel(
-    moved_ref, low_edge_ref, high_edge_ref, vrad_ref, high_ref, low_ref, twiddle_ref,
+    kept_ref, sent_ref, first_ref, second_ref, vrad_ref, high_ref, low_ref, twiddle_ref,
     whole_ref, dens_ref, spectra_ref,
-    other_ref, speed_ref, whole_sem,
+    moved_ref, other_ref, speed_ref, whole_sem,
 ):
-    for side, (ref, row) in enumerate(((low_edge_ref, 7), (high_edge_ref, 0))):
-        other_ref[side, pl.ds(row, CHUNKS, stride=8), :] = ref[0:CHUNKS, :]
-        speed_ref[side, pl.ds(row, CHUNKS, stride=8), :] = ref[CHUNKS : 2 * CHUNKS, :]
+    for group in range(GROUPS):
+        moved_ref[group] = kept_ref[group] + sent_ref[group]
+    even = lax.axis_index(RAD) % 2 == 0
+    first, second = first_ref[...], second_ref[...]
+    for side, row in enumerate((7, 0)):
+        edge = jnp.where(even, second, first) if side == 0 else jnp.where(even, first, second)
+        other_ref[side, pl.ds(row, CHUNKS, stride=8), :] = edge[0:CHUNKS]
+        speed_ref[side, pl.ds(row, CHUNKS, stride=8), :] = edge[CHUNKS:]
 
     sub = lax.broadcasted_iota(jnp.int32, (1, 8, 128), 1)
     own_index = lax.axis_index(RAD)
@@ -383,7 +433,7 @@
             return tuple(radial), tuple(azim)
 
         count = together * GROUPS
-        radial, azim = lax.fori_loop(0, EMB, visit, ((zero,) * count, (zero,) * count), unroll=4)
+        radial, azim = lax.fori_loop(0, EMB, visit, ((zero,) * count, (zero,) * count), unroll=8)
         for k in range(together):
             where = pl.ds(pl.multiple_of((base + part * together + k) * 8, 8), 8)
             for g in range(GROUPS):
@@ -466,7 +516,7 @@
 
 def kick_kernel(
     spectra_ref, moments_ref, rate_ref, radius_ref, vectors_ref, lift_ref, drop_ref, twiddle_ref, high_ref, low_ref,
-    radial_ref, azim_ref, vrad_ref, vphi_ref,
+    radial_ref, azim_ref, vrad_ref, vphi_kept_ref, vphi_sent_ref,
     whole_radial_ref, whole_azim_ref, out_push_ref,
     lower_ref, upper_ref, out_radial_ref, out_azim_ref, sems,
 ):
@@ -537,7 +587,8 @@
                     disk - radial_ref[:, where, :]
                 )
                 disk = part[rows + ROWS : rows + 2 * ROWS, columns].reshape(GROUPS, 8, 128)
-                out_azim_ref[:, where, :] = vphi_ref[:, where, :] + timestep_length * (
+                vphi = vphi_kept_ref[:, where, :] + vphi_sent_ref[:, where, :]
+                out_azim_ref[:, where, :] = vphi + timestep_length * (
                     disk - azim_ref[:, where, :]
                 )
         for copy in whole_copies(quarter):
@@ -574,26 +625,22 @@
     vrad = to_tiles(outward_drift)
     vphi = to_tiles(leftover_angular_drift)
 
-    odd = lax.axis_index(AZ) % 2 == 1
-    ends = jnp.concatenate([surface_mass[:, -128:], leftover_angular_drift[:, -128:]])
-    begins = jnp.concatenate([surface_mass[:, :128], leftover_angular_drift[:, :128]])
-    outer = jnp.where(odd, ends, begins).reshape(2 * GROUPS, 8, 128)
-    inner = jnp.where(odd, begins, ends).reshape(2 * GROUPS, 8, 128)
-    border_far = across(outer, AZ, lambda i: i ^ 3)
-    border_mate = across(inner, AZ, lambda i: i ^ 1)
-    edge_rows = pl.pallas_call(
+    halo = jax.ShapeDtypeStruct((2 * GROUPS, 8, 128), F32)
+    outer, inner, edge_rows = pl.pallas_call(
         border_kernel,
-        out_shape=jax.ShapeDtypeStruct((2, 3 * CHUNKS, 128), F32),
+        out_shape=(halo, halo, jax.ShapeDtypeStruct((2, 3 * CHUNKS, 128), F32)),
         in_specs=[pl.BlockSpec(memory_space=pltpu.HBM)] * 3,
-        out_specs=vmem(),
-        scratch_shapes=[pltpu.VMEM((6, SPAN, 128), F32), pltpu.SemaphoreType.DMA((6,))],
+        out_specs=(vmem(), vmem(), vmem()),
+        scratch_shapes=[pltpu.VMEM((6, SPAN, 128), F32), pltpu.SemaphoreType.DMA((10,))],
         compiler_params=params(),
         cost_estimate=cost(1),
         name="borders",
     )(hbm(dens), hbm(vphi), hbm(vrad))
+    border_far = across(outer, AZ, lambda i: i ^ 3)
+    border_mate = across(inner, AZ, lambda i: i ^ 1)
     edge_cross = across(edge_rows, AZ, lambda i: i ^ 2)
     edge_mate = across(edge_rows, AZ, lambda i: i ^ 1)
-    vrad_cross = across(after(vrad, border_mate, border_far, edge_rows), AZ, lambda i: i ^ 2)
+    vrad_cross = across(after(vrad, edge_rows), AZ, lambda i: i ^ 2)
     vrad_mate = across(vrad, AZ, lambda i: i ^ 1)
 
     cell = np.float32(cell_step)
@@ -628,7 +675,7 @@
 
     edge_far = across(edge_cross, AZ, lambda i: i ^ 1)
     edge = jax.ShapeDtypeStruct((2 * CHUNKS, 128), F32)
-    edge_up, edge_down = pl.pallas_call(
+    edge_first, edge_second = pl.pallas_call(
         edge_kernel,
         out_shape=(edge, edge),
         in_specs=[smem()] + [vmem()] * 4,
@@ -643,8 +690,9 @@
         name="edges",
     )(angular_offsets, edge_rows, edge_mate, edge_cross, edge_far)
     rad_count = lax.axis_size(RAD)
-    edge_low = lax.ppermute(edge_up, RAD, [(i, i + 1) for i in range(rad_count - 1)])
-    edge_high = lax.ppermute(edge_down, RAD, [(i + 1, i) for i in range(rad_count - 1)])
+    inside = range(1, rad_count - 1)
+    edge_second = lax.ppermute(edge_second, RAD, [(i, i + 1 if i % 2 else i - 1) for i in inside])
+    edge_first_in = across(edge_first, RAD, lambda i: i ^ 1)
 
     def field(second, *before):
         return pl.pallas_call(
@@ -660,26 +708,27 @@
 
     first_field = field(0)
     dens_mate = across(dens_two, AZ, lambda i: i ^ 1)
-    dens_cross = across(after(dens_two, vrad_cross, edge_up, *first_field), AZ, lambda i: i ^ 2)
-    vrad_far = across(after(vrad_cross, dens_two, *first_field), AZ, lambda i: i ^ 1)
+    (dens_sent,) = share(angular_offsets, dens_two, dens_mate, (True,), "share_dens")
+    vphi_mate = across(vphi, AZ, lambda i: i ^ 1)
+    vphi_sent, vphi_kept = share(angular_offsets, vphi, vphi_mate, (True, False), "share_vphi")
+    early = (dens_sent, *first_field, edge_first, vphi_sent, vphi_kept)
+    vrad_far = across(after(vrad_cross, *early), AZ, lambda i: i ^ 1)
+    dens_cross = across(after(dens_sent, vrad_cross, *early), AZ, lambda i: i ^ 2)
+    (dens_kept,) = share(angular_offsets, dens_two, dens_mate, (False,), "keep_dens")
     vrad_one = shifted(angular_offsets, vrad, vrad_mate, vrad_cross, vrad_far, "shift_vrad")
     radial_field, azim_field = field(1, *first_field)
-    dens_cross = after(dens_cross, vrad_one, radial_field, dens_mate, edge_low, edge_high)
-    dens_far = across(dens_cross, AZ, lambda i: i ^ 1)
-
-    dens_one = shifted(
-        angular_offsets, dens_two, dens_mate, dens_cross, dens_far, "shift_dens"
+    dens_cross = after(
+        dens_cross, vrad_one, radial_field, dens_kept, vphi_sent, vphi_kept, edge_first_in, edge_second
     )
-    vphi_later = after(vphi, dens_cross)
-    vphi_cross = across(vphi_later, AZ, lambda i: i ^ 2)
-    vphi_mate = across(vphi_later, AZ, lambda i: i ^ 1)
+    vphi_cross = across(after(vphi_sent, vrad_cross), AZ, lambda i: i ^ 2)
 
     transported, stepped, part = pl.pallas_call(
         transport_kernel,
         out_shape=(tiles, tiles, jax.ShapeDtypeStruct((ROWS, 2 * MODES), F32)),
-        in_specs=[vmem()] * 7,
+        in_specs=[vmem()] * 8,
         out_specs=(anywhere(), vmem(), vmem()),
         scratch_shapes=[
+            pltpu.VMEM((GROUPS, SPAN, 128), F32),
             pltpu.VMEM((2, SPAN, 128), F32),
             pltpu.VMEM((2, SPAN, 128), F32),
             pltpu.SemaphoreType.DMA,
@@ -688,7 +737,7 @@
         cost_estimate=cost(3),
         name="transport",
     )(
-        dens_one, edge_low, edge_high,
+        dens_kept, dens_cross, edge_first_in, edge_second,
         vrad_one, basis_high, basis_low, twiddle,
     )
 
@@ -710,10 +759,7 @@
     chip = joined + across(joined, AZ, lambda i: i ^ 1)
     chip_other = across(chip, AZ, lambda i: i ^ 2)
 
-    vphi_far = across(after(vphi_cross, chip), AZ, lambda i: i ^ 1)
-    vphi_one = shifted(angular_offsets, vphi_later, vphi_mate, vphi_cross, vphi_far, "shift_vphi")
-
-    chip_later = after(chip, vphi_one)
+    chip_later = after(chip, vphi_cross)
     spectra, packed = pl.pallas_call(
         moment_kernel,
         out_shape=(
@@ -732,7 +778,7 @@
     kicked_radial, kicked_azim, embryo_disk_acceleration = pl.pallas_call(
         kick_kernel,
         out_shape=(tiles, tiles, jax.ShapeDtypeStruct((2, EMB), F32)),
-        in_specs=[vmem()] * 14,
+        in_specs=[vmem()] * 15,
         out_specs=(anywhere(), anywhere(), vmem()),
         scratch_shapes=[
             pltpu.VMEM((ROWS, 2 * MODES), F32),
@@ -746,7 +792,7 @@
         name="kick",
     )(
         spectra, gathered, rate, radius, vectors, lift, drop, twiddle, back_high, back_low,
-        radial_field, azim_field, vrad_one, vphi_one,
+        radial_field, azim_field, vrad_one, vphi_kept, vphi_cross,
     )
     return (
         from_tiles(transported),

time: 81.3 us -> 75 us (0.923)
  waiting for transfers between devices: 17.5 us -> 11.3 us
  Pallas kernels: 28.4 us -> 30.3 us
  starting transfers between devices: 11.6 us -> 9.99 us
    ppermute x16 -> x15, waiting for transfers between devices: 17.5 us -> 11.3 us  [across(): lax.ppermute(value, axis, [(source, target(source)) for source in range(c...]
    pallas_call x1 -> x4, Pallas kernels: 1.34 us -> 6.17 us  [the longest x3 4.73 us: share(): pl.pallas_call(functools.partial(share_kernel, kinds=kinds), out_shape=tu...]
    ppermute x2 -> x1, starting transfers between devices: 4.76 us -> 0.65 us  [on_device(): lax.ppermute(edge_second, RAD, [(i, i + 1 if i % 2 else i - 1) for i in i...]
    pallas_call x3 -> x1, Pallas kernels: 3.94 us -> 1.32 us  [shifted(): pl.pallas_call(shift_kernel, out_shape=jax.ShapeDtypeStruct((GROUPS, SPAN...]
    ppermute x16 -> x15, starting transfers between devices: 6.82 us -> 9.34 us  [across(): lax.ppermute(value, axis, [(source, target(source)) for source in range(c...]
    pallas_call x2, Pallas kernels: 8.4 us -> 7.55 us  [field(): pl.pallas_call(functools.partial(field_kernel, second=second), out_shape=...]
  transfers between devices with their start and end apart: 18 -> 16, of which waited for: 8 -> 6; matrix products, arithmetic and copies ran while one was open for 0% -> 0% of each run, Pallas kernels for 31% -> 34%
where the time goes in v4:
time: 75 us; the launch traced here: 74.7 us
  Pallas kernels  30.3 us (40%)
  blocking collectives  20.8 us (28%)
  waiting for transfers between devices  11.3 us (15%)
  starting transfers between devices  9.99 us (13%)
  local copies, waits for them, and re-layouts  1.26 us (2%)
  between operations  0.94 us (1%)
    all_to_all x1, blocking collectives, on_device(): lax.all_to_all(packed, RAD, split_axis=0, concat_axis=0, tiled=True)  20.8 us
    ppermute x15, waiting for transfers between devices, across(): lax.ppermute(value, axis, [(source, target(source)) for source in range(c...  11.3 us
    ppermute x15, starting transfers between devices, across(): lax.ppermute(value, axis, [(source, target(source)) for source in range(c...  9.34 us
    pallas_call x2, Pallas kernels, field(): pl.pallas_call(functools.partial(field_kernel, second=second), out_shape=...  7.55 us
    pallas_call x1, Pallas kernels, on_device(): pl.pallas_call(push_kernel, out_shape=joined_shape, in_specs=[smem()] + [...  6.39 us
    pallas_call x3, Pallas kernels, share(): pl.pallas_call(functools.partial(share_kernel, kinds=kinds), out_shape=tu...  4.73 us
    pallas_call x1, Pallas kernels, on_device(): pl.pallas_call(kick_kernel, out_shape=(tiles, tiles, jax.ShapeDtypeStruct...  3.33 us
    pallas_call x1, Pallas kernels, on_device(): pl.pallas_call(transport_kernel, out_shape=(tiles, tiles, jax.ShapeDtypeS...  2.06 us
  transfers between devices with their start and end apart: 16, of which 6 were waited for; matrix products, arithmetic and copies ran while one was open for 0% of the time, Pallas kernels for 34%

profile of v4, /device:TPU:0, one launch (start us, length us, event | category | flops | bytes accessed | tf_op | source)
XLA Modules:
  0.0 74.7 jit_solution(12386659448048017276)
XLA Ops:
  0.6 1.4 %borders.1 = (f32[8,8,128]{2,1,0:T(8,128)S(1)}, f32[8,8,128]{2,1,0:T(8,128)S(1)}, f32[2,96,128]{2,1,0:T(8,128)S(1)}) custom-call(f32[4,256,128]{2,1,0:T(8,128)} %bitcast.46, f32[4,256,128]{2,1,0:T(8,128)} %bitcast.5.phi_ref.own_ref, f32[4,256,128]{2,1,0:T(8,128)} %bitcast.42), custom_call_target="tpu_custom_call" | custom-call | flops 1000000 | bytes 2500000 | tf_op jit(solution)/shard_map/borders/pallas_call | solution.py:629
  2.1 0.1 collective-permute-start
  2.2 2.1 %collective-permute-start.1 = (f32[8,8,128]{2,1,0:T(8,128)S(1)}, f32[8,8,128]{2,1,0:T(8,128)S(1)}, u32[]{:S(2)}, u32[]{:S(2)}) collective-permute-start(f32[8,8,128]{2,1,0:T(8,128)S(1)} %get-tuple-element.30), channel_id=1, source_target_pairs={{0,3},{1,2},{2,1},{3,0},{4,7},{5,6},{6,5},{7,4},{8,11},{9,10},{10,... | collective-permute-start | bytes 98312 | tf_op jit(solution)/shard_map/ppermute | solution.py:604
  4.3 0.1 collective-permute-start.4
  4.4 0.3 collective-permute-start.5
  4.7 0.1 collective-permute-start.7
  4.8 1.8 %collective-permute-start.3 = (f32[4,256,128]{2,1,0:T(8,128)S(1)}, f32[4,256,128]{2,1,0:T(8,128)S(1)}, u32[]{:S(2)}, u32[]{:S(2)}) collective-permute-start(f32[4,256,128]{2,1,0:T(8,128)S(1)} %bitcast.43), channel_id=1, source_target_pairs={{0,2},{1,3},{2,0},{3,1},{4,6},{5,7},{6,4},{7,5},{8,10},{9,11},{10,... | collective-permute-start | bytes 1572872 | tf_op jit(solution)/shard_map/ppermute | solution.py:604
  6.6 1.9 %azimuth.1.own_ref = f32[4,256,128]{2,1,0:T(8,128)S(1)} custom-call(f32[4,256,128]{2,1,0:T(8,128)} %bitcast.47, f32[4,256,128]{2,1,0:T(8,128)} %bitcast.5.phi_ref.own_ref, f32[8,8,128]{2,1,0:T(8,128)S(1)} %collective-permute-done.mate_ref, f32[8,8,128]{2,1,0:T(8,128)S(1)} %collective-permute-done.1.far_ref), custom_call_target="tpu_custom_call" | custom-call | flops 1000000 | bytes 2500000 | tf_op jit(solution)/shard_map/azimuth/pallas_call | solution.py:661
  8.5 0.1 collective-permute-start.2
  8.7 0.1 sine_bitcast_fusion
  8.7 0.4 copy-done.15
  9.2 0.0 copy-done.16
  9.2 0.6 copy-done.9
  9.8 0.1 collective-permute-start.9
  9.9 0.2 collective-permute-done.5.cross_ref
  10.1 0.3 collective-permute-start.6
  10.4 0.1 broadcast_in_dim.2.radius_ref
  10.5 3.8 %field_0.1 = (f32[4,256,128]{2,1,0:T(8,128)S(1)}, f32[4,256,128]{2,1,0:T(8,128)S(1)}) custom-call(f32[6,32]{1,0:T(8,128)S(1)} %stack.27.members_ref, f32[32,128]{1,0:T(8,128)S(1)} %broadcast_in_dim.2.radius_ref, f32[16,32,128]{2,1,0:T(8,128)S(1)} %copy-done), custom_call_target="tpu_custom_call" | custom-call | flops 4000000 | bytes 10000000 | tf_op jit(solution)/shard_map/field_0/pallas_call | solution.py:698
  14.3 1.5 %edges.1 = (f32[64,128]{1,0:T(8,128)S(1)}, f32[64,128]{1,0:T(8,128)S(1)}) custom-call(s32[32]{0:T(128)S(1)} %copy-done.12, f32[2,96,128]{2,1,0:T(8,128)S(1)} %get-tuple-element.31.own_ref, f32[2,96,128]{2,1,0:T(8,128)S(1)} %copy-done.10, f32[2,96,128]{2,1,0:T(8,128)} %collective-permute-done.5.cross_ref, f32[2,96,128]{2,1,0:T(8,128)} %collective-permute-done.6.far_ref), custom_call_target="tpu_custom_call" | custom-call | flops 1000000 | bytes 2500000 | tf_op jit(solution)/shard_map/edges/pallas_call | solution.py:678
  15.8 2.2 %share_vphi.1 = (f32[4,256,128]{2,1,0:T(8,128)S(1)}, f32[4,256,128]{2,1,0:T(8,128)S(1)}) custom-call(s32[32]{0:T(128)S(1)} %copy-done.12, f32[4,256,128]{2,1,0:T(8,128)} %bitcast.5.phi_ref.own_ref, f32[4,256,128]{2,1,0:T(8,128)S(1)} %collective-permute-done.7.mate_ref), custom_call_target="tpu_custom_call" | custom-call | flops 2000000 | bytes 5000000 | tf_op jit(solution)/shard_map/share_vphi/pallas_call | solution.py:239
  18.0 1.3 %share_dens.1 = f32[4,256,128]{2,1,0:T(8,128)S(1)} custom-call(s32[32]{0:T(128)S(1)} %copy-done.12, f32[4,256,128]{2,1,0:T(8,128)S(1)} %azimuth.1.own_ref, f32[4,256,128]{2,1,0:T(8,128)S(1)} %collective-permute-done.2.mate_ref), custom_call_target="tpu_custom_call" | custom-call | flops 2000000 | bytes 5000000 | tf_op jit(solution)/shard_map/share_dens/pallas_call | solution.py:239
  19.3 1.5 %collective-permute-done.3.cross_ref = f32[4,256,128]{2,1,0:T(8,128)S(1)} collective-permute-done((f32[4,256,128]{2,1,0:T(8,128)S(1)}, f32[4,256,128]{2,1,0:T(8,128)S(1)}, u32[]{:S(2)}, u32[]{:S(2)}) %collective-permute-start.3) | collective-permute-done | bytes 524320 | tf_op jit(solution)/shard_map/ppermute | solution.py:604
  20.8 0.6 collective-permute-start.8
  21.4 1.4 %collective-permute-start.14 = (f32[4,256,128]{2,1,0:T(8,128)S(1)}, f32[4,256,128]{2,1,0:T(8,128)S(1)}, u32[]{:S(2)}, u32[]{:S(2)}) collective-permute-start(f32[4,256,128]{2,1,0:T(8,128)S(1)} %get-tuple-element.46), channel_id=1, source_target_pairs={{0,2},{1,3},{2,0},{3,1},{4,6},{5,7},{6,4},{7,5},{8,10},{9,11},{10,... | collective-permute-start | bytes 1572872 | tf_op jit(solution)/shard_map/ppermute | solution.py:604
  22.8 1.6 %collective-permute-start.11 = (f32[64,128]{1,0:T(8,128)S(1)}, f32[64,128]{1,0:T(8,128)S(1)}, u32[]{:S(2)}, u32[]{:S(2)}) collective-permute-start(f32[64,128]{1,0:T(8,128)S(1)} %get-tuple-element.35), channel_id=1, source_target_pairs={{0,4},{4,0},{8,12},{12,8},{16,20},{20,16},{24,28},{28,24},{32,36},... | collective-permute-start | bytes 98312 | tf_op jit(solution)/shard_map/ppermute | solution.py:604
  24.4 0.7 collective-permute-start.12
  25.0 3.8 %field_1.1 = (f32[4,256,128]{2,1,0:T(8,128)S(1)}, f32[4,256,128]{2,1,0:T(8,128)S(1)}) custom-call(f32[6,32]{1,0:T(8,128)S(1)} %stack.27.members_ref, f32[32,128]{1,0:T(8,128)S(1)} %broadcast_in_dim.2.radius_ref, f32[16,32,128]{2,1,0:T(8,128)S(1)} %copy-done, f32[4,256,128]{2,1,0:T(8,128)S(1)} %get-tuple-element.33.refs_0_, ...), custom_call_target="tpu_custom_call" | custom-call | flops 4000000 | bytes 10000000 | tf_op jit(solution)/shard_map/field_1/pallas_call | solution.py:698
  28.8 1.3 %keep_dens.1.kept_ref = f32[4,256,128]{2,1,0:T(8,128)S(1)} custom-call(s32[32]{0:T(128)S(1)} %copy-done.12, f32[4,256,128]{2,1,0:T(8,128)S(1)} %azimuth.1.own_ref, f32[4,256,128]{2,1,0:T(8,128)S(1)} %collective-permute-done.2.mate_ref), custom_call_target="tpu_custom_call" | custom-call | flops 2000000 | bytes 5000000 | tf_op jit(solution)/shard_map/keep_dens/pallas_call | solution.py:239
  30.1 0.0 copy-start.2
  30.1 0.0 copy-start.7
  30.1 0.0 copy-start.8
  30.2 1.3 %shift_vrad.1.vrad_ref = f32[4,256,128]{2,1,0:T(8,128)S(1)} custom-call(s32[32]{0:T(128)S(1)} %copy-done.12, f32[4,256,128]{2,1,0:T(8,128)S(1)} %bitcast.45, f32[4,256,128]{2,1,0:T(8,128)S(1)} %collective-permute-done.9.mate_ref, f32[4,256,128]{2,1,0:T(8,128)S(1)} %collective-permute-done.3.cross_ref, f32[4,256,128]{2,1,0:T(8,128)S(1)} %collective-permute-done.10.far_ref), custom_call_target="tpu_custom_call" | custom-call | flops 2000000 | bytes 5000000 | tf_op jit(solution)/shard_map/shift_vrad/pallas_call | solution.py:207
  31.5 0.0 collective-permute-done.11.first_ref
  31.5 4.7 %collective-permute-done.8.sent_ref = f32[4,256,128]{2,1,0:T(8,128)S(1)} collective-permute-done((f32[4,256,128]{2,1,0:T(8,128)S(1)}, f32[4,256,128]{2,1,0:T(8,128)S(1)}, u32[]{:S(2)}, u32[]{:S(2)}) %collective-permute-start.8) | collective-permute-done | bytes 524320 | tf_op jit(solution)/shard_map/ppermute | solution.py:604
  36.2 2.1 %transport.1 = (f32[4,256,128]{2,1,0:T(8,128)}, f32[4,256,128]{2,1,0:T(8,128)S(1)}, f32[32,512]{1,0:T(8,128)S(1)}) custom-call(f32[4,256,128]{2,1,0:T(8,128)S(1)} %keep_dens.1.kept_ref, f32[4,256,128]{2,1,0:T(8,128)S(1)} %collective-permute-done.8.sent_ref, f32[64,128]{1,0:T(8,128)S(1)} %collective-permute-done.11.first_ref, ...), custom_call_target="tpu_custom_call" | custom-call | flops 3000000 | bytes 7500000 | tf_op jit(solution)/shard_map/transport/pallas_call | solution.py:725
  38.3 6.4 %push.1 = f32[136,128]{1,0:T(8,128)S(1)} custom-call(f32[6,32]{1,0:T(8,128)S(1)} %stack.27.members_ref, f32[32,128]{1,0:T(8,128)S(1)} %broadcast_in_dim.2.radius_ref, f32[16,32,128]{2,1,0:T(8,128)S(1)} %copy-done, f32[4,256,128]{2,1,0:T(8,128)S(1)} %get-tuple-element.44.dens_ref, f32[32,512]{1,0:T(8,128)S(1)} %get-tuple-element.45.spectra_ref), custom_call_target="tpu_custom_call" | custom-call | flops 6000000 | bytes 15000000 | tf_op jit(solution)/shard_map/push/pallas_call | solution.py:745
  44.7 0.0 copy-start.3
  44.7 0.0 copy-start.11
  44.7 0.1 collective-permute-start.13
  44.8 1.2 %collective-permute-done.13 = f32[136,128]{1,0:T(8,128)S(1)} collective-permute-done((f32[136,128]{1,0:T(8,128)S(1)}, f32[136,128]{1,0:T(8,128)S(1)}, u32[]{:S(2)}, u32[]{:S(2)}) %collective-permute-start.13) | collective-permute-done | bytes 69664 | tf_op jit(solution)/shard_map/ppermute | solution.py:604
  46.0 0.7 collective-permute-start.15
  46.7 0.3 collective-permute-done.14.vphi_sent_ref
  47.0 3.4 %collective-permute-done.15.b_ref = f32[136,128]{1,0:T(8,128)S(1)} collective-permute-done((f32[136,128]{1,0:T(8,128)S(1)}, f32[136,128]{1,0:T(8,128)S(1)}, u32[]{:S(2)}, u32[]{:S(2)}) %collective-permute-start.15) | collective-permute-done | bytes 69664 | tf_op jit(solution)/shard_map/ppermute | solution.py:604
  50.4 0.0 copy-start.13
  50.5 0.0 copy-start.5
  50.5 0.0 copy-start.6
  50.5 20.8 %all_to_all.5.moments_ref = f32[32,16,128]{2,1,0:T(8,128)S(1)} all-to-all(f32[32,16,128]{2,1,0:T(8,128)S(1)} %get-tuple-element.49), channel_id=1, replica_groups=mesh['rad_0'=4,'rad_1'=2,'rad_2'=4,'az_0'=2,'az_1'=2] {'rad_0','rad_1','..., dimensions={0} | all-to-all | bytes 524288 | tf_op jit(solution)/shard_map/all_to_all | solution.py:776
  71.4 3.3 %kick.1 = (f32[4,256,128]{2,1,0:T(8,128)}, f32[4,256,128]{2,1,0:T(8,128)}, f32[2,32]{1,0:T(2,128)}) custom-call(f32[32,512]{1,0:T(8,128)S(1)} %get-tuple-element.48.spectra_ref, f32[32,16,128]{2,1,0:T(8,128)S(1)} %all_to_all.5.moments_ref, f32[8,128]{1,0:T(8,128)S(1)} %copy-done.13, f32[32,128]{1,0:T(8,128)S(1)} %broadcast_in_dim.2.radius_ref, ...), custom_call_target="tpu_custom_call" | custom-call | flops 5000000 | bytes 12500000 | tf_op jit(solution)/shard_map/kick/pallas_call | solution.py:778
  (38 shorter events, 0.2 us)
Async XLA Ops:
  0.6 4.2 %copy-start.1 = (f32[32,4096]{1,0:T(8,128)S(1)}, f32[32,4096]{1,0:T(8,128)}, u32[]{:S(2)}) copy-start(f32[32,4096]{1,0:T(8,128)} %param.18) | copy-start | bytes 1572868
  2.1 2.7 %collective-permute-start = (f32[8,8,128]{2,1,0:T(8,128)S(1)}, f32[8,8,128]{2,1,0:T(8,128)S(1)}, u32[]{:S(2)}, u32[]{:S(2)}) collective-permute-start(f32[8,8,128]{2,1,0:T(8,128)S(1)} %get-tuple-element.29), channel_id=1, source_target_pairs={{0,1},{1,0},{2,3},{3,2},{4,5},{5,4},{6,7},{7,6},{8,9},{9,8},{10,11... | collective-permute-start | bytes 98312 | tf_op jit(solution)/shard_map/ppermute | solution.py:604
  2.2 4.4 %collective-permute-start.1 = (f32[8,8,128]{2,1,0:T(8,128)S(1)}, f32[8,8,128]{2,1,0:T(8,128)S(1)}, u32[]{:S(2)}, u32[]{:S(2)}) collective-permute-start(f32[8,8,128]{2,1,0:T(8,128)S(1)} %get-tuple-element.30), channel_id=1, source_target_pairs={{0,3},{1,2},{2,1},{3,0},{4,7},{5,6},{6,5},{7,4},{8,11},{9,10},{10,... | collective-permute-start | bytes 98312 | tf_op jit(solution)/shard_map/ppermute | solution.py:604
  4.3 4.4 %copy-start.14 = (s32[32]{0:T(128)S(1)}, s32[32]{0:T(128)}, u32[]{:S(2)}) copy-start(s32[32]{0:T(128)} %param.22) | copy-start | bytes 388
  4.3 6.2 %copy-start = (f32[16,32,128]{2,1,0:T(8,128)S(1)}, f32[16,32,128]{2,1,0:T(8,128)}, u32[]{:S(2)}) copy-start(f32[16,32,128]{2,1,0:T(8,128)} %constant.55.clone.angles_ref) | copy-start | bytes 786436
  4.3 4.9 %collective-permute-start.4 = (f32[2,96,128]{2,1,0:T(8,128)S(1)}, f32[2,96,128]{2,1,0:T(8,128)S(1)}, u32[]{:S(2)}, u32[]{:S(2)}) collective-permute-start(f32[2,96,128]{2,1,0:T(8,128)S(1)} %get-tuple-element.31.own_ref), channel_id=1, source_target_pairs={{0,1},{1,0},{2,3},{3,2},{4,5},{5,4},{6,7},{7,6},{8,9},{9,8},{10,11... | collective-permute-start | bytes 294920 | tf_op jit(solution)/shard_map/ppermute | solution.py:604
  4.4 5.7 %collective-permute-start.5 = (f32[2,96,128]{2,1,0:T(8,128)S(1)}, f32[2,96,128]{2,1,0:T(8,128)}, u32[]{:S(2)}, u32[]{:S(2)}) collective-permute-start(f32[2,96,128]{2,1,0:T(8,128)S(1)} %get-tuple-element.31.own_ref), channel_id=1, source_target_pairs={{0,2},{1,3},{2,0},{3,1},{4,6},{5,7},{6,4},{7,5},{8,10},{9,11},{10,... | collective-permute-start | bytes 294920 | tf_op jit(solution)/shard_map/ppermute | solution.py:604
  4.7 11.1 %collective-permute-start.7 = (f32[4,256,128]{2,1,0:T(8,128)}, f32[4,256,128]{2,1,0:T(8,128)S(1)}, u32[]{:S(2)}, u32[]{:S(2)}) collective-permute-start(f32[4,256,128]{2,1,0:T(8,128)} %bitcast.5.phi_ref.own_ref), channel_id=1, source_target_pairs={{0,1},{1,0},{2,3},{3,2},{4,5},{5,4},{6,7},{7,6},{8,9},{9,8},{10,11... | collective-permute-start | bytes 1572872 | tf_op jit(solution)/shard_map/ppermute | solution.py:604
  4.8 15.9 %collective-permute-start.3 = (f32[4,256,128]{2,1,0:T(8,128)S(1)}, f32[4,256,128]{2,1,0:T(8,128)S(1)}, u32[]{:S(2)}, u32[]{:S(2)}) collective-permute-start(f32[4,256,128]{2,1,0:T(8,128)S(1)} %bitcast.43), channel_id=1, source_target_pairs={{0,2},{1,3},{2,0},{3,1},{4,6},{5,7},{6,4},{7,5},{8,10},{9,11},{10,... | collective-permute-start | bytes 1572872 | tf_op jit(solution)/shard_map/ppermute | solution.py:604
  8.5 0.7 copy-start.15
  8.5 0.7 copy-start.16
  8.5 9.5 %collective-permute-start.2 = (f32[4,256,128]{2,1,0:T(8,128)S(1)}, f32[4,256,128]{2,1,0:T(8,128)S(1)}, u32[]{:S(2)}, u32[]{:S(2)}) collective-permute-start(f32[4,256,128]{2,1,0:T(8,128)S(1)} %azimuth.1.own_ref), channel_id=1, source_target_pairs={{0,1},{1,0},{2,3},{3,2},{4,5},{5,4},{6,7},{7,6},{8,9},{9,8},{10,11... | collective-permute-start | bytes 1572872 | tf_op jit(solution)/shard_map/ppermute | solution.py:604
  9.2 0.6 copy-start.9
  9.8 14.5 %collective-permute-start.9 = (f32[4,256,128]{2,1,0:T(8,128)S(1)}, f32[4,256,128]{2,1,0:T(8,128)S(1)}, u32[]{:S(2)}, u32[]{:S(2)}) collective-permute-start(f32[4,256,128]{2,1,0:T(8,128)S(1)} %bitcast.44), channel_id=1, source_target_pairs={{0,1},{1,0},{2,3},{3,2},{4,5},{5,4},{6,7},{7,6},{8,9},{9,8},{10,11... | collective-permute-start | bytes 1572872 | tf_op jit(solution)/shard_map/ppermute | solution.py:604
  10.1 4.2 %collective-permute-start.6 = (f32[2,96,128]{2,1,0:T(8,128)}, f32[2,96,128]{2,1,0:T(8,128)}, u32[]{:S(2)}, u32[]{:S(2)}) collective-permute-start(f32[2,96,128]{2,1,0:T(8,128)} %collective-permute-done.5.cross_ref), channel_id=1, source_target_pairs={{0,1},{1,0},{2,3},{3,2},{4,5},{5,4},{6,7},{7,6},{8,9},{9,8},{10,11... | collective-permute-start | bytes 294920 | tf_op jit(solution)/shard_map/ppermute | solution.py:604
  10.5 3.8 %copy-start.10 = (f32[2,96,128]{2,1,0:T(8,128)S(1)}, f32[2,96,128]{2,1,0:T(8,128)}, u32[]{:S(2)}) copy-start(f32[2,96,128]{2,1,0:T(8,128)} %copy-done.9) | copy-start | bytes 294916
  10.5 3.8 %copy-start.12 = (s32[32]{0:T(128)S(1)}, s32[32]{0:T(128)}, u32[]{:S(2)}) copy-start(s32[32]{0:T(128)} %offs_ref.9) | copy-start | bytes 388
  20.8 9.4 %collective-permute-start.10 = (f32[4,256,128]{2,1,0:T(8,128)S(1)}, f32[4,256,128]{2,1,0:T(8,128)S(1)}, u32[]{:S(2)}, u32[]{:S(2)}) collective-permute-start(f32[4,256,128]{2,1,0:T(8,128)S(1)} %collective-permute-done.3.cross_ref), channel_id=1, source_target_pairs={{0,1},{1,0},{2,3},{3,2},{4,5},{5,4},{6,7},{7,6},{8,9},{9,8},{10,11... | collective-permute-start | bytes 1572872 | tf_op jit(solution)/shard_map/ppermute | solution.py:604
  20.8 15.4 %collective-permute-start.8 = (f32[4,256,128]{2,1,0:T(8,128)S(1)}, f32[4,256,128]{2,1,0:T(8,128)S(1)}, u32[]{:S(2)}, u32[]{:S(2)}) collective-permute-start(f32[4,256,128]{2,1,0:T(8,128)S(1)} %share_dens.1), channel_id=1, source_target_pairs={{0,2},{1,3},{2,0},{3,1},{4,6},{5,7},{6,4},{7,5},{8,10},{9,11},{10,... | collective-permute-start | bytes 1572872 | tf_op jit(solution)/shard_map/ppermute | solution.py:604
  21.4 25.7 %collective-permute-start.14 = (f32[4,256,128]{2,1,0:T(8,128)S(1)}, f32[4,256,128]{2,1,0:T(8,128)S(1)}, u32[]{:S(2)}, u32[]{:S(2)}) collective-permute-start(f32[4,256,128]{2,1,0:T(8,128)S(1)} %get-tuple-element.46), channel_id=1, source_target_pairs={{0,2},{1,3},{2,0},{3,1},{4,6},{5,7},{6,4},{7,5},{8,10},{9,11},{10,... | collective-permute-start | bytes 1572872 | tf_op jit(solution)/shard_map/ppermute | solution.py:604
  22.8 8.7 %collective-permute-start.11 = (f32[64,128]{1,0:T(8,128)S(1)}, f32[64,128]{1,0:T(8,128)S(1)}, u32[]{:S(2)}, u32[]{:S(2)}) collective-permute-start(f32[64,128]{1,0:T(8,128)S(1)} %get-tuple-element.35), channel_id=1, source_target_pairs={{0,4},{4,0},{8,12},{12,8},{16,20},{20,16},{24,28},{28,24},{32,36},... | collective-permute-start | bytes 98312 | tf_op jit(solution)/shard_map/ppermute | solution.py:604
  24.4 7.1 %collective-permute-start.12 = (f32[64,128]{1,0:T(8,128)S(1)}, f32[64,128]{1,0:T(8,128)S(1)}, u32[]{:S(2)}, u32[]{:S(2)}) collective-permute-start(f32[64,128]{1,0:T(8,128)S(1)} %get-tuple-element.41), channel_id=1, source_target_pairs={{4,8},{8,4},{12,16},{16,12},{20,24},{24,20},{28,32},{32,28},{36,40... | collective-permute-start | bytes 98312 | tf_op jit(solution)/shard_map/ppermute | solution.py:694
  30.1 6.1 %copy-start.2 = (f32[64,512]{1,0:T(8,128)S(1)}, f32[64,512]{1,0:T(8,128)}, u32[]{:S(2)}) copy-start(f32[64,512]{1,0:T(8,128)} %constant.58.clone.twiddle_ref) | copy-start | bytes 393220
  30.1 6.1 %copy-start.7 = (bf16[256,512]{1,0:T(8,128)(2,1)S(1)}, bf16[256,512]{1,0:T(8,128)(2,1)}, u32[]{:S(2)}) copy-start(bf16[256,512]{1,0:T(8,128)(2,1)} %constant.56.clone.high_ref) | copy-start | bytes 786436
  30.1 6.1 %copy-start.8 = (bf16[256,512]{1,0:T(8,128)(2,1)S(1)}, bf16[256,512]{1,0:T(8,128)(2,1)}, u32[]{:S(2)}) copy-start(bf16[256,512]{1,0:T(8,128)(2,1)} %constant.57.clone.low_ref) | copy-start | bytes 786436
  44.7 5.8 %copy-start.3 = (f32[32,512]{1,0:T(8,128)S(1)}, f32[32,512]{1,0:T(8,128)}, u32[]{:S(2)}) copy-start(f32[32,512]{1,0:T(8,128)} %constant.59.clone.lift_ref) | copy-start | bytes 196612
  44.7 5.8 %copy-start.4 = (f32[32,512]{1,0:T(8,128)S(1)}, f32[32,512]{1,0:T(8,128)}, u32[]{:S(2)}) copy-start(f32[32,512]{1,0:T(8,128)} %constant.60.clone.drop_ref) | copy-start | bytes 196612
  44.7 5.8 %copy-start.11 = (f32[8,512]{1,0:T(8,128)S(1)}, f32[8,512]{1,0:T(8,128)}, u32[]{:S(2)}) copy-start(f32[8,512]{1,0:T(8,128)} %constant.61.clone.vectors_ref) | copy-start | bytes 49156
  44.7 1.3 %collective-permute-start.13 = (f32[136,128]{1,0:T(8,128)S(1)}, f32[136,128]{1,0:T(8,128)S(1)}, u32[]{:S(2)}, u32[]{:S(2)}) collective-permute-start(f32[136,128]{1,0:T(8,128)S(1)} %push.1), channel_id=1, source_target_pairs={{0,1},{1,0},{2,3},{3,2},{4,5},{5,4},{6,7},{7,6},{8,9},{9,8},{10,11... | collective-permute-start | bytes 208904 | tf_op jit(solution)/shard_map/ppermute | solution.py:604
  46.0 4.4 %collective-permute-start.15 = (f32[136,128]{1,0:T(8,128)S(1)}, f32[136,128]{1,0:T(8,128)S(1)}, u32[]{:S(2)}, u32[]{:S(2)}) collective-permute-start(f32[136,128]{1,0:T(8,128)S(1)} %add.43.a_ref), channel_id=1, source_target_pairs={{0,2},{1,3},{2,0},{3,1},{4,6},{5,7},{6,4},{7,5},{8,10},{9,11},{10,... | collective-permute-start | bytes 208904 | tf_op jit(solution)/shard_map/ppermute | solution.py:604
  50.4 20.9 %copy-start.13 = (f32[8,128]{1,0:T(8,128)S(1)}, f32[8,128]{1,0:T(8,128)}, u32[]{:S(2)}) copy-start(f32[8,128]{1,0:T(8,128)} %constant.62.clone.rate_ref) | copy-start | bytes 12292
  50.5 20.9 %copy-start.5 = (bf16[512,256]{1,0:T(8,128)(2,1)S(1)}, bf16[512,256]{1,0:T(8,128)(2,1)}, u32[]{:S(2)}) copy-start(bf16[512,256]{1,0:T(8,128)(2,1)} %constant.63.clone.high_ref) | copy-start | bytes 786436
  50.5 20.8 %copy-start.6 = (bf16[512,256]{1,0:T(8,128)(2,1)S(1)}, bf16[512,256]{1,0:T(8,128)(2,1)}, u32[]{:S(2)}) copy-start(bf16[512,256]{1,0:T(8,128)(2,1)} %constant.64.clone.low_ref) | copy-start | bytes 786436

commit v5 on v4

--- a/solution.py
+++ b/solution.py
@@ -370,11 +370,9 @@
     whole.wait()
 
 
-def field_kernel(members_ref, radius_ref, angles_ref, *refs, second):
+def field_kernel(members_ref, radius_ref, angles_ref, *refs, base, many):
     radial_ref, azim_ref, gap_ref, chord_ref, lift_ref, side_ref = refs[-6:]
-    many = CHUNKS // 2
-    base = many * second
-    if second:
+    if base:
         rows = slice(0, 8 * base)
         radial_ref[:, rows, :] = refs[0][:, rows, :]
         azim_ref[:, rows, :] = refs[1][:, rows, :]
@@ -550,7 +548,7 @@
     swapped = jnp.concatenate([even[:, MODES:], even[:, :MODES]], axis=1)
     azim = swapped * vectors_ref[2:3, :] * inverse
     sector = lax.axis_index(AZ)
-    together = 4
+    together = 8
 
     def whole_copies(quarter):
         rows = pl.ds(pl.multiple_of(16 * together * quarter, 16 * together), 16 * together)
@@ -694,19 +692,19 @@
     edge_second = lax.ppermute(edge_second, RAD, [(i, i + 1 if i % 2 else i - 1) for i in inside])
     edge_first_in = across(edge_first, RAD, lambda i: i ^ 1)
 
-    def field(second, *before):
+    def field(base, many, *before):
         return pl.pallas_call(
-            functools.partial(field_kernel, second=second),
+            functools.partial(field_kernel, base=base, many=many),
             out_shape=(tiles, tiles),
             in_specs=[smem(), vmem(), vmem()] + [vmem()] * len(before),
             out_specs=(vmem(), vmem()),
-            scratch_shapes=[pltpu.VMEM((EMB * 32, 128), F32)] + [pltpu.VMEM((EMB * 16, 128), F32)] * 3,
+            scratch_shapes=[pltpu.VMEM((EMB * 32, 128), F32)] + [pltpu.VMEM((EMB * many, 128), F32)] * 3,
             compiler_params=params(),
-            cost_estimate=cost(4),
-            name=f"field_{second}",
+            cost_estimate=cost(many // 4),
+            name=f"field_{base}",
         )(members, radius, angles, *before)
 
-    first_field = field(0)
+    first_field = field(0, 16)
     dens_mate = across(dens_two, AZ, lambda i: i ^ 1)
     (dens_sent,) = share(angular_offsets, dens_two, dens_mate, (True,), "share_dens")
     vphi_mate = across(vphi, AZ, lambda i: i ^ 1)
@@ -716,11 +714,11 @@
     dens_cross = across(after(dens_sent, vrad_cross, *early), AZ, lambda i: i ^ 2)
     (dens_kept,) = share(angular_offsets, dens_two, dens_mate, (False,), "keep_dens")
     vrad_one = shifted(angular_offsets, vrad, vrad_mate, vrad_cross, vrad_far, "shift_vrad")
-    radial_field, azim_field = field(1, *first_field)
+    middle_field = field(16, 8, *first_field)
     dens_cross = after(
-        dens_cross, vrad_one, radial_field, dens_kept, vphi_sent, vphi_kept, edge_first_in, edge_second
+        dens_cross, vrad_one, *middle_field, dens_kept, vphi_sent, vphi_kept, edge_first_in, edge_second
     )
-    vphi_cross = across(after(vphi_sent, vrad_cross), AZ, lambda i: i ^ 2)
+    vphi_cross = across(after(vphi_sent, *middle_field), AZ, lambda i: i ^ 2)
 
     transported, stepped, part = pl.pallas_call(
         transport_kernel,
@@ -759,7 +757,8 @@
     chip = joined + across(joined, AZ, lambda i: i ^ 1)
     chip_other = across(chip, AZ, lambda i: i ^ 2)
 
-    chip_later = after(chip, vphi_cross)
+    radial_field, azim_field = field(24, 8, *middle_field)
+    chip_later = after(chip, vphi_cross, radial_field)
     spectra, packed = pl.pallas_call(
         moment_kernel,
         out_shape=(

time: 75 us -> 74.3 us (level)
  waiting for transfers between devices: 11.3 us -> 6.85 us
  starting transfers between devices: 9.99 us -> 13.7 us
    ppermute x15, waiting for transfers between devices: 11.3 us -> 6.84 us  [across(): lax.ppermute(value, axis, [(source, target(source)) for source in range(c...]
    ppermute x15, starting transfers between devices: 9.34 us -> 13.1 us  [across(): lax.ppermute(value, axis, [(source, target(source)) for source in range(c...]
    pallas_call x2 -> x3, Pallas kernels: 7.55 us -> 8.37 us  [field(): pl.pallas_call(functools.partial(field_kernel, base=base, many=many), out...]
  transfers between devices with their start and end apart: 16 -> 16, of which waited for: 6 -> 5; matrix products, arithmetic and copies ran while one was open for 0% -> 0% of each run, Pallas kernels for 34% -> 36%
where the time goes in v5:
time: 74.3 us; the launch traced here: 74 us
  Pallas kernels  30.9 us (42%)
  blocking collectives  20.8 us (28%)
  starting transfers between devices  13.7 us (18%)
  waiting for transfers between devices  6.85 us (9%)
  between operations  0.95 us (1%)
    all_to_all x1, blocking collectives, on_device(): lax.all_to_all(packed, RAD, split_axis=0, concat_axis=0, tiled=True)  20.8 us
    ppermute x15, starting transfers between devices, across(): lax.ppermute(value, axis, [(source, target(source)) for source in range(c...  13.1 us
    pallas_call x3, Pallas kernels, field(): pl.pallas_call(functools.partial(field_kernel, base=base, many=many), out...  8.37 us
    ppermute x15, waiting for transfers between devices, across(): lax.ppermute(value, axis, [(source, target(source)) for source in range(c...  6.84 us
    pallas_call x1, Pallas kernels, on_device(): pl.pallas_call(push_kernel, out_shape=joined_shape, in_specs=[smem()] + [...  6.39 us
    pallas_call x3, Pallas kernels, share(): pl.pallas_call(functools.partial(share_kernel, kinds=kinds), out_shape=tu...  4.72 us
    pallas_call x1, Pallas kernels, on_device(): pl.pallas_call(kick_kernel, out_shape=(tiles, tiles, jax.ShapeDtypeStruct...  3.07 us
    pallas_call x1, Pallas kernels, on_device(): pl.pallas_call(transport_kernel, out_shape=(tiles, tiles, jax.ShapeDtypeS...  2.05 us
  transfers between devices with their start and end apart: 16, of which 5 were waited for; matrix products, arithmetic and copies ran while one was open for 0% of the time, Pallas kernels for 36%

profile of v5, /device:TPU:0, one launch (start us, length us, event | category | flops | bytes accessed | tf_op | source)
XLA Modules:
  0.0 74.0 jit_solution(2349300059618192627)
XLA Ops:
  0.6 1.4 %borders.1 = (f32[8,8,128]{2,1,0:T(8,128)S(1)}, f32[8,8,128]{2,1,0:T(8,128)S(1)}, f32[2,96,128]{2,1,0:T(8,128)S(1)}) custom-call(f32[4,256,128]{2,1,0:T(8,128)} %bitcast.46, f32[4,256,128]{2,1,0:T(8,128)} %bitcast.5.phi_ref.own_ref, f32[4,256,128]{2,1,0:T(8,128)} %bitcast.42), custom_call_target="tpu_custom_call" | custom-call | flops 1000000 | bytes 2500000 | tf_op jit(solution)/shard_map/borders/pallas_call | solution.py:627
  2.1 0.1 collective-permute-start
  2.2 2.1 %collective-permute-start.1 = (f32[8,8,128]{2,1,0:T(8,128)S(1)}, f32[8,8,128]{2,1,0:T(8,128)S(1)}, u32[]{:S(2)}, u32[]{:S(2)}) collective-permute-start(f32[8,8,128]{2,1,0:T(8,128)S(1)} %get-tuple-element.32), channel_id=1, source_target_pairs={{0,3},{1,2},{2,1},{3,0},{4,7},{5,6},{6,5},{7,4},{8,11},{9,10},{10,... | collective-permute-start | bytes 98312 | tf_op jit(solution)/shard_map/ppermute | solution.py:602
  4.3 0.1 collective-permute-start.5
  4.4 0.1 collective-permute-start.4
  4.4 0.5 collective-permute-start.7
  4.9 1.9 %collective-permute-start.3 = (f32[4,256,128]{2,1,0:T(8,128)S(1)}, f32[4,256,128]{2,1,0:T(8,128)S(1)}, u32[]{:S(2)}, u32[]{:S(2)}) collective-permute-start(f32[4,256,128]{2,1,0:T(8,128)S(1)} %bitcast.43), channel_id=1, source_target_pairs={{0,2},{1,3},{2,0},{3,1},{4,6},{5,7},{6,4},{7,5},{8,10},{9,11},{10,... | collective-permute-start | bytes 1572872 | tf_op jit(solution)/shard_map/ppermute | solution.py:602
  6.9 1.9 %azimuth.1.own_ref = f32[4,256,128]{2,1,0:T(8,128)S(1)} custom-call(f32[4,256,128]{2,1,0:T(8,128)} %bitcast.47, f32[4,256,128]{2,1,0:T(8,128)} %bitcast.5.phi_ref.own_ref, f32[8,8,128]{2,1,0:T(8,128)S(1)} %collective-permute-done.mate_ref, f32[8,8,128]{2,1,0:T(8,128)S(1)} %collective-permute-done.1.far_ref), custom_call_target="tpu_custom_call" | custom-call | flops 1000000 | bytes 2500000 | tf_op jit(solution)/shard_map/azimuth/pallas_call | solution.py:659
  8.8 0.0 copy-start.13
  8.8 0.0 copy-start.14
  8.8 0.1 collective-permute-start.2
  8.9 0.1 sine_bitcast_fusion
  8.9 0.5 copy-done.13
  9.4 0.0 copy-done.14
  9.5 0.6 collective-permute-done.5.cross_ref
  10.1 0.5 collective-permute-start.6
  10.6 0.1 broadcast_in_dim.2.radius_ref
  10.7 3.8 %field_0.1 = (f32[4,256,128]{2,1,0:T(8,128)S(1)}, f32[4,256,128]{2,1,0:T(8,128)S(1)}) custom-call(f32[6,32]{1,0:T(8,128)S(1)} %stack.27.members_ref, f32[32,128]{1,0:T(8,128)S(1)} %broadcast_in_dim.2.radius_ref, f32[16,32,128]{2,1,0:T(8,128)S(1)} %copy-done), custom_call_target="tpu_custom_call" | custom-call | flops 4000000 | bytes 10000000 | tf_op jit(solution)/shard_map/field_0/pallas_call | solution.py:696
  14.5 1.6 %edges.1 = (f32[64,128]{1,0:T(8,128)S(1)}, f32[64,128]{1,0:T(8,128)S(1)}) custom-call(s32[32]{0:T(128)S(1)} %copy-done.10, f32[2,96,128]{2,1,0:T(8,128)S(1)} %get-tuple-element.33.own_ref, f32[2,96,128]{2,1,0:T(8,128)} %collective-permute-done.4.mate_ref, f32[2,96,128]{2,1,0:T(8,128)} %collective-permute-done.5.cross_ref, ...), custom_call_target="tpu_custom_call" | custom-call | flops 1000000 | bytes 2500000 | tf_op jit(solution)/shard_map/edges/pallas_call | solution.py:676
  16.1 2.2 %share_vphi.1 = (f32[4,256,128]{2,1,0:T(8,128)S(1)}, f32[4,256,128]{2,1,0:T(8,128)S(1)}) custom-call(s32[32]{0:T(128)S(1)} %copy-done.10, f32[4,256,128]{2,1,0:T(8,128)} %bitcast.5.phi_ref.own_ref, f32[4,256,128]{2,1,0:T(8,128)S(1)} %collective-permute-done.7.mate_ref), custom_call_target="tpu_custom_call" | custom-call | flops 2000000 | bytes 5000000 | tf_op jit(solution)/shard_map/share_vphi/pallas_call | solution.py:239
  18.3 1.3 %share_dens.1 = f32[4,256,128]{2,1,0:T(8,128)S(1)} custom-call(s32[32]{0:T(128)S(1)} %copy-done.10, f32[4,256,128]{2,1,0:T(8,128)S(1)} %azimuth.1.own_ref, f32[4,256,128]{2,1,0:T(8,128)S(1)} %collective-permute-done.2.mate_ref), custom_call_target="tpu_custom_call" | custom-call | flops 2000000 | bytes 5000000 | tf_op jit(solution)/shard_map/share_dens/pallas_call | solution.py:239
  19.5 0.8 %collective-permute-done.3.cross_ref = f32[4,256,128]{2,1,0:T(8,128)S(1)} collective-permute-done((f32[4,256,128]{2,1,0:T(8,128)S(1)}, f32[4,256,128]{2,1,0:T(8,128)S(1)}, u32[]{:S(2)}, u32[]{:S(2)}) %collective-permute-start.3) | collective-permute-done | bytes 524320 | tf_op jit(solution)/shard_map/ppermute | solution.py:602
  20.3 1.0 %collective-permute-start.8 = (f32[4,256,128]{2,1,0:T(8,128)S(1)}, f32[4,256,128]{2,1,0:T(8,128)S(1)}, u32[]{:S(2)}, u32[]{:S(2)}) collective-permute-start(f32[4,256,128]{2,1,0:T(8,128)S(1)} %share_dens.1), channel_id=1, source_target_pairs={{0,2},{1,3},{2,0},{3,1},{4,6},{5,7},{6,4},{7,5},{8,10},{9,11},{10,... | collective-permute-start | bytes 1572872 | tf_op jit(solution)/shard_map/ppermute | solution.py:602
  21.3 2.3 %field_16.1 = (f32[4,256,128]{2,1,0:T(8,128)S(1)}, f32[4,256,128]{2,1,0:T(8,128)S(1)}) custom-call(f32[6,32]{1,0:T(8,128)S(1)} %stack.27.members_ref, f32[32,128]{1,0:T(8,128)S(1)} %broadcast_in_dim.2.radius_ref, f32[16,32,128]{2,1,0:T(8,128)S(1)} %copy-done, f32[4,256,128]{2,1,0:T(8,128)S(1)} %get-tuple-element.35.refs_0_, ...), custom_call_target="tpu_custom_call" | custom-call | flops 2000000 | bytes 5000000 | tf_op jit(solution)/shard_map/field_16/pallas_call | solution.py:696
  23.6 1.1 %collective-permute-start.14 = (f32[4,256,128]{2,1,0:T(8,128)S(1)}, f32[4,256,128]{2,1,0:T(8,128)S(1)}, u32[]{:S(2)}, u32[]{:S(2)}) collective-permute-start(f32[4,256,128]{2,1,0:T(8,128)S(1)} %get-tuple-element.49), channel_id=1, source_target_pairs={{0,2},{1,3},{2,0},{3,1},{4,6},{5,7},{6,4},{7,5},{8,10},{9,11},{10,... | collective-permute-start | bytes 1572872 | tf_op jit(solution)/shard_map/ppermute | solution.py:602
  24.7 0.7 collective-permute-start.12
  25.4 4.5 %collective-permute-start.11 = (f32[64,128]{1,0:T(8,128)S(1)}, f32[64,128]{1,0:T(8,128)S(1)}, u32[]{:S(2)}, u32[]{:S(2)}) collective-permute-start(f32[64,128]{1,0:T(8,128)S(1)} %get-tuple-element.37), channel_id=1, source_target_pairs={{0,4},{4,0},{8,12},{12,8},{16,20},{20,16},{24,28},{28,24},{32,36},... | collective-permute-start | bytes 98312 | tf_op jit(solution)/shard_map/ppermute | solution.py:602
  29.9 1.3 %keep_dens.1.kept_ref = f32[4,256,128]{2,1,0:T(8,128)S(1)} custom-call(s32[32]{0:T(128)S(1)} %copy-done.10, f32[4,256,128]{2,1,0:T(8,128)S(1)} %azimuth.1.own_ref, f32[4,256,128]{2,1,0:T(8,128)S(1)} %collective-permute-done.2.mate_ref), custom_call_target="tpu_custom_call" | custom-call | flops 2000000 | bytes 5000000 | tf_op jit(solution)/shard_map/keep_dens/pallas_call | solution.py:239
  31.2 0.0 copy-start.2
  31.2 0.0 copy-start.7
  31.2 0.0 copy-start.8
  31.2 1.3 %shift_vrad.1.vrad_ref = f32[4,256,128]{2,1,0:T(8,128)S(1)} custom-call(s32[32]{0:T(128)S(1)} %copy-done.10, f32[4,256,128]{2,1,0:T(8,128)S(1)} %bitcast.45, f32[4,256,128]{2,1,0:T(8,128)S(1)} %collective-permute-done.9.mate_ref, f32[4,256,128]{2,1,0:T(8,128)S(1)} %collective-permute-done.3.cross_ref, f32[4,256,128]{2,1,0:T(8,128)S(1)} %collective-permute-done.10.far_ref), custom_call_target="tpu_custom_call" | custom-call | flops 2000000 | bytes 5000000 | tf_op jit(solution)/shard_map/shift_vrad/pallas_call | solution.py:207
  32.5 0.0 collective-permute-done.12.second_ref
  32.6 3.2 %collective-permute-done.8.sent_ref = f32[4,256,128]{2,1,0:T(8,128)S(1)} collective-permute-done((f32[4,256,128]{2,1,0:T(8,128)S(1)}, f32[4,256,128]{2,1,0:T(8,128)S(1)}, u32[]{:S(2)}, u32[]{:S(2)}) %collective-permute-start.8) | collective-permute-done | bytes 524320 | tf_op jit(solution)/shard_map/ppermute | solution.py:602
  35.8 2.1 %transport.1 = (f32[4,256,128]{2,1,0:T(8,128)}, f32[4,256,128]{2,1,0:T(8,128)S(1)}, f32[32,512]{1,0:T(8,128)S(1)}) custom-call(f32[4,256,128]{2,1,0:T(8,128)S(1)} %keep_dens.1.kept_ref, f32[4,256,128]{2,1,0:T(8,128)S(1)} %collective-permute-done.8.sent_ref, f32[64,128]{1,0:T(8,128)S(1)} %collective-permute-done.11.first_ref, ...), custom_call_target="tpu_custom_call" | custom-call | flops 3000000 | bytes 7500000 | tf_op jit(solution)/shard_map/transport/pallas_call | solution.py:723
  37.8 6.4 %push.1 = f32[136,128]{1,0:T(8,128)S(1)} custom-call(f32[6,32]{1,0:T(8,128)S(1)} %stack.27.members_ref, f32[32,128]{1,0:T(8,128)S(1)} %broadcast_in_dim.2.radius_ref, f32[16,32,128]{2,1,0:T(8,128)S(1)} %copy-done, f32[4,256,128]{2,1,0:T(8,128)S(1)} %get-tuple-element.47.dens_ref, f32[32,512]{1,0:T(8,128)S(1)} %get-tuple-element.48.spectra_ref), custom_call_target="tpu_custom_call" | custom-call | flops 6000000 | bytes 15000000 | tf_op jit(solution)/shard_map/push/pallas_call | solution.py:743
  44.2 0.1 collective-permute-start.13
  44.3 1.2 %collective-permute-done.13 = f32[136,128]{1,0:T(8,128)S(1)} collective-permute-done((f32[136,128]{1,0:T(8,128)S(1)}, f32[136,128]{1,0:T(8,128)S(1)}, u32[]{:S(2)}, u32[]{:S(2)}) %collective-permute-start.13) | collective-permute-done | bytes 69664 | tf_op jit(solution)/shard_map/ppermute | solution.py:602
  45.6 0.0 copy-start.3
  45.6 0.0 copy-start.4
  45.6 0.0 copy-start.9
  45.6 1.1 %collective-permute-start.15 = (f32[136,128]{1,0:T(8,128)S(1)}, f32[136,128]{1,0:T(8,128)S(1)}, u32[]{:S(2)}, u32[]{:S(2)}) collective-permute-start(f32[136,128]{1,0:T(8,128)S(1)} %add.43.a_ref), channel_id=1, source_target_pairs={{0,2},{1,3},{2,0},{3,1},{4,6},{5,7},{6,4},{7,5},{8,10},{9,11},{10,... | collective-permute-start | bytes 208904 | tf_op jit(solution)/shard_map/ppermute | solution.py:602
  46.7 2.3 %field_24.1 = (f32[4,256,128]{2,1,0:T(8,128)S(1)}, f32[4,256,128]{2,1,0:T(8,128)S(1)}) custom-call(f32[6,32]{1,0:T(8,128)S(1)} %stack.27.members_ref, f32[32,128]{1,0:T(8,128)S(1)} %broadcast_in_dim.2.radius_ref, f32[16,32,128]{2,1,0:T(8,128)S(1)} %copy-done, f32[4,256,128]{2,1,0:T(8,128)S(1)} %get-tuple-element.42.refs_0_, ...), custom_call_target="tpu_custom_call" | custom-call | flops 2000000 | bytes 5000000 | tf_op jit(solution)/shard_map/field_24/pallas_call | solution.py:696
  49.0 1.0 %collective-permute-done.15.b_ref = f32[136,128]{1,0:T(8,128)S(1)} collective-permute-done((f32[136,128]{1,0:T(8,128)S(1)}, f32[136,128]{1,0:T(8,128)S(1)}, u32[]{:S(2)}, u32[]{:S(2)}) %collective-permute-start.15) | collective-permute-done | bytes 69664 | tf_op jit(solution)/shard_map/ppermute | solution.py:602
  50.0 0.0 copy-start.11
  50.1 0.0 copy-start.6
  50.1 20.8 %all_to_all.5.moments_ref = f32[32,16,128]{2,1,0:T(8,128)S(1)} all-to-all(f32[32,16,128]{2,1,0:T(8,128)S(1)} %get-tuple-element.53), channel_id=1, replica_groups=mesh['rad_0'=4,'rad_1'=2,'rad_2'=4,'az_0'=2,'az_1'=2] {'rad_0','rad_1','..., dimensions={0} | all-to-all | bytes 524288 | tf_op jit(solution)/shard_map/all_to_all | solution.py:775
  70.9 3.1 %kick.1 = (f32[4,256,128]{2,1,0:T(8,128)}, f32[4,256,128]{2,1,0:T(8,128)}, f32[2,32]{1,0:T(2,128)}) custom-call(f32[32,512]{1,0:T(8,128)S(1)} %get-tuple-element.52.spectra_ref, f32[32,16,128]{2,1,0:T(8,128)S(1)} %all_to_all.5.moments_ref, f32[8,128]{1,0:T(8,128)S(1)} %copy-done.11, f32[32,128]{1,0:T(8,128)S(1)} %broadcast_in_dim.2.radius_ref, ...), custom_call_target="tpu_custom_call" | custom-call | flops 5000000 | bytes 12500000 | tf_op jit(solution)/shard_map/kick/pallas_call | solution.py:777
  (35 shorter events, 0.2 us)
Async XLA Ops:
  0.6 4.3 %copy-start.1 = (f32[32,4096]{1,0:T(8,128)S(1)}, f32[32,4096]{1,0:T(8,128)}, u32[]{:S(2)}) copy-start(f32[32,4096]{1,0:T(8,128)} %param.18) | copy-start | bytes 1572868
  2.1 2.8 %collective-permute-start = (f32[8,8,128]{2,1,0:T(8,128)S(1)}, f32[8,8,128]{2,1,0:T(8,128)S(1)}, u32[]{:S(2)}, u32[]{:S(2)}) collective-permute-start(f32[8,8,128]{2,1,0:T(8,128)S(1)} %get-tuple-element.31), channel_id=1, source_target_pairs={{0,1},{1,0},{2,3},{3,2},{4,5},{5,4},{6,7},{7,6},{8,9},{9,8},{10,11... | collective-permute-start | bytes 98312 | tf_op jit(solution)/shard_map/ppermute | solution.py:602
  2.2 4.7 %collective-permute-start.1 = (f32[8,8,128]{2,1,0:T(8,128)S(1)}, f32[8,8,128]{2,1,0:T(8,128)S(1)}, u32[]{:S(2)}, u32[]{:S(2)}) collective-permute-start(f32[8,8,128]{2,1,0:T(8,128)S(1)} %get-tuple-element.32), channel_id=1, source_target_pairs={{0,3},{1,2},{2,1},{3,0},{4,7},{5,6},{6,5},{7,4},{8,11},{9,10},{10,... | collective-permute-start | bytes 98312 | tf_op jit(solution)/shard_map/ppermute | solution.py:602
  4.3 4.6 %copy-start.12 = (s32[32]{0:T(128)S(1)}, s32[32]{0:T(128)}, u32[]{:S(2)}) copy-start(s32[32]{0:T(128)} %param.22) | copy-start | bytes 388
  4.3 6.4 %copy-start = (f32[16,32,128]{2,1,0:T(8,128)S(1)}, f32[16,32,128]{2,1,0:T(8,128)}, u32[]{:S(2)}) copy-start(f32[16,32,128]{2,1,0:T(8,128)} %constant.55.clone.angles_ref) | copy-start | bytes 786436
  4.3 5.8 %collective-permute-start.5 = (f32[2,96,128]{2,1,0:T(8,128)S(1)}, f32[2,96,128]{2,1,0:T(8,128)}, u32[]{:S(2)}, u32[]{:S(2)}) collective-permute-start(f32[2,96,128]{2,1,0:T(8,128)S(1)} %get-tuple-element.33.own_ref), channel_id=1, source_target_pairs={{0,2},{1,3},{2,0},{3,1},{4,6},{5,7},{6,4},{7,5},{8,10},{9,11},{10,... | collective-permute-start | bytes 294920 | tf_op jit(solution)/shard_map/ppermute | solution.py:602
  4.4 5.7 %collective-permute-start.4 = (f32[2,96,128]{2,1,0:T(8,128)S(1)}, f32[2,96,128]{2,1,0:T(8,128)}, u32[]{:S(2)}, u32[]{:S(2)}) collective-permute-start(f32[2,96,128]{2,1,0:T(8,128)S(1)} %get-tuple-element.33.own_ref), channel_id=1, source_target_pairs={{0,1},{1,0},{2,3},{3,2},{4,5},{5,4},{6,7},{7,6},{8,9},{9,8},{10,11... | collective-permute-start | bytes 294920 | tf_op jit(solution)/shard_map/ppermute | solution.py:602
  4.4 11.6 %collective-permute-start.7 = (f32[4,256,128]{2,1,0:T(8,128)}, f32[4,256,128]{2,1,0:T(8,128)S(1)}, u32[]{:S(2)}, u32[]{:S(2)}) collective-permute-start(f32[4,256,128]{2,1,0:T(8,128)} %bitcast.5.phi_ref.own_ref), channel_id=1, source_target_pairs={{0,1},{1,0},{2,3},{3,2},{4,5},{5,4},{6,7},{7,6},{8,9},{9,8},{10,11... | collective-permute-start | bytes 1572872 | tf_op jit(solution)/shard_map/ppermute | solution.py:602
  4.9 15.4 %collective-permute-start.3 = (f32[4,256,128]{2,1,0:T(8,128)S(1)}, f32[4,256,128]{2,1,0:T(8,128)S(1)}, u32[]{:S(2)}, u32[]{:S(2)}) collective-permute-start(f32[4,256,128]{2,1,0:T(8,128)S(1)} %bitcast.43), channel_id=1, source_target_pairs={{0,2},{1,3},{2,0},{3,1},{4,6},{5,7},{6,4},{7,5},{8,10},{9,11},{10,... | collective-permute-start | bytes 1572872 | tf_op jit(solution)/shard_map/ppermute | solution.py:602
  8.8 0.7 copy-start.13
  8.8 0.7 copy-start.14
  8.8 9.5 %collective-permute-start.2 = (f32[4,256,128]{2,1,0:T(8,128)S(1)}, f32[4,256,128]{2,1,0:T(8,128)S(1)}, u32[]{:S(2)}, u32[]{:S(2)}) collective-permute-start(f32[4,256,128]{2,1,0:T(8,128)S(1)} %azimuth.1.own_ref), channel_id=1, source_target_pairs={{0,1},{1,0},{2,3},{3,2},{4,5},{5,4},{6,7},{7,6},{8,9},{9,8},{10,11... | collective-permute-start | bytes 1572872 | tf_op jit(solution)/shard_map/ppermute | solution.py:602
  10.1 15.3 %collective-permute-start.9 = (f32[4,256,128]{2,1,0:T(8,128)S(1)}, f32[4,256,128]{2,1,0:T(8,128)S(1)}, u32[]{:S(2)}, u32[]{:S(2)}) collective-permute-start(f32[4,256,128]{2,1,0:T(8,128)S(1)} %bitcast.44), channel_id=1, source_target_pairs={{0,1},{1,0},{2,3},{3,2},{4,5},{5,4},{6,7},{7,6},{8,9},{9,8},{10,11... | collective-permute-start | bytes 1572872 | tf_op jit(solution)/shard_map/ppermute | solution.py:602
  10.1 4.4 %collective-permute-start.6 = (f32[2,96,128]{2,1,0:T(8,128)}, f32[2,96,128]{2,1,0:T(8,128)}, u32[]{:S(2)}, u32[]{:S(2)}) collective-permute-start(f32[2,96,128]{2,1,0:T(8,128)} %collective-permute-done.5.cross_ref), channel_id=1, source_target_pairs={{0,1},{1,0},{2,3},{3,2},{4,5},{5,4},{6,7},{7,6},{8,9},{9,8},{10,11... | collective-permute-start | bytes 294920 | tf_op jit(solution)/shard_map/ppermute | solution.py:602
  10.7 3.8 %copy-start.10 = (s32[32]{0:T(128)S(1)}, s32[32]{0:T(128)}, u32[]{:S(2)}) copy-start(s32[32]{0:T(128)} %offs_ref.9) | copy-start | bytes 388
  20.3 10.9 %collective-permute-start.10 = (f32[4,256,128]{2,1,0:T(8,128)S(1)}, f32[4,256,128]{2,1,0:T(8,128)S(1)}, u32[]{:S(2)}, u32[]{:S(2)}) collective-permute-start(f32[4,256,128]{2,1,0:T(8,128)S(1)} %collective-permute-done.3.cross_ref), channel_id=1, source_target_pairs={{0,1},{1,0},{2,3},{3,2},{4,5},{5,4},{6,7},{7,6},{8,9},{9,8},{10,11... | collective-permute-start | bytes 1572872 | tf_op jit(solution)/shard_map/ppermute | solution.py:602
  20.3 15.4 %collective-permute-start.8 = (f32[4,256,128]{2,1,0:T(8,128)S(1)}, f32[4,256,128]{2,1,0:T(8,128)S(1)}, u32[]{:S(2)}, u32[]{:S(2)}) collective-permute-start(f32[4,256,128]{2,1,0:T(8,128)S(1)} %share_dens.1), channel_id=1, source_target_pairs={{0,2},{1,3},{2,0},{3,1},{4,6},{5,7},{6,4},{7,5},{8,10},{9,11},{10,... | collective-permute-start | bytes 1572872 | tf_op jit(solution)/shard_map/ppermute | solution.py:602
  23.6 25.4 %collective-permute-start.14 = (f32[4,256,128]{2,1,0:T(8,128)S(1)}, f32[4,256,128]{2,1,0:T(8,128)S(1)}, u32[]{:S(2)}, u32[]{:S(2)}) collective-permute-start(f32[4,256,128]{2,1,0:T(8,128)S(1)} %get-tuple-element.49), channel_id=1, source_target_pairs={{0,2},{1,3},{2,0},{3,1},{4,6},{5,7},{6,4},{7,5},{8,10},{9,11},{10,... | collective-permute-start | bytes 1572872 | tf_op jit(solution)/shard_map/ppermute | solution.py:602
  24.7 7.8 %collective-permute-start.12 = (f32[64,128]{1,0:T(8,128)S(1)}, f32[64,128]{1,0:T(8,128)S(1)}, u32[]{:S(2)}, u32[]{:S(2)}) collective-permute-start(f32[64,128]{1,0:T(8,128)S(1)} %get-tuple-element.44), channel_id=1, source_target_pairs={{4,8},{8,4},{12,16},{16,12},{20,24},{24,20},{28,32},{32,28},{36,40... | collective-permute-start | bytes 98312 | tf_op jit(solution)/shard_map/ppermute | solution.py:692
  25.4 7.1 %collective-permute-start.11 = (f32[64,128]{1,0:T(8,128)S(1)}, f32[64,128]{1,0:T(8,128)S(1)}, u32[]{:S(2)}, u32[]{:S(2)}) collective-permute-start(f32[64,128]{1,0:T(8,128)S(1)} %get-tuple-element.37), channel_id=1, source_target_pairs={{0,4},{4,0},{8,12},{12,8},{16,20},{20,16},{24,28},{28,24},{32,36},... | collective-permute-start | bytes 98312 | tf_op jit(solution)/shard_map/ppermute | solution.py:602
  31.2 4.6 %copy-start.2 = (f32[64,512]{1,0:T(8,128)S(1)}, f32[64,512]{1,0:T(8,128)}, u32[]{:S(2)}) copy-start(f32[64,512]{1,0:T(8,128)} %constant.58.clone.twiddle_ref) | copy-start | bytes 393220
  31.2 4.6 %copy-start.7 = (bf16[256,512]{1,0:T(8,128)(2,1)S(1)}, bf16[256,512]{1,0:T(8,128)(2,1)}, u32[]{:S(2)}) copy-start(bf16[256,512]{1,0:T(8,128)(2,1)} %constant.57.clone.low_ref) | copy-start | bytes 786436
  31.2 4.6 %copy-start.8 = (bf16[256,512]{1,0:T(8,128)(2,1)S(1)}, bf16[256,512]{1,0:T(8,128)(2,1)}, u32[]{:S(2)}) copy-start(bf16[256,512]{1,0:T(8,128)(2,1)} %constant.56.clone.high_ref) | copy-start | bytes 786436
  44.2 1.3 %collective-permute-start.13 = (f32[136,128]{1,0:T(8,128)S(1)}, f32[136,128]{1,0:T(8,128)S(1)}, u32[]{:S(2)}, u32[]{:S(2)}) collective-permute-start(f32[136,128]{1,0:T(8,128)S(1)} %push.1), channel_id=1, source_target_pairs={{0,1},{1,0},{2,3},{3,2},{4,5},{5,4},{6,7},{7,6},{8,9},{9,8},{10,11... | collective-permute-start | bytes 208904 | tf_op jit(solution)/shard_map/ppermute | solution.py:602
  45.6 4.4 %copy-start.3 = (f32[32,512]{1,0:T(8,128)S(1)}, f32[32,512]{1,0:T(8,128)}, u32[]{:S(2)}) copy-start(f32[32,512]{1,0:T(8,128)} %constant.60.clone.drop_ref) | copy-start | bytes 196612
  45.6 4.4 %copy-start.4 = (f32[32,512]{1,0:T(8,128)S(1)}, f32[32,512]{1,0:T(8,128)}, u32[]{:S(2)}) copy-start(f32[32,512]{1,0:T(8,128)} %constant.59.clone.lift_ref) | copy-start | bytes 196612
  45.6 4.4 %copy-start.9 = (f32[8,512]{1,0:T(8,128)S(1)}, f32[8,512]{1,0:T(8,128)}, u32[]{:S(2)}) copy-start(f32[8,512]{1,0:T(8,128)} %constant.61.clone.vectors_ref) | copy-start | bytes 49156
  45.6 4.4 %collective-permute-start.15 = (f32[136,128]{1,0:T(8,128)S(1)}, f32[136,128]{1,0:T(8,128)S(1)}, u32[]{:S(2)}, u32[]{:S(2)}) collective-permute-start(f32[136,128]{1,0:T(8,128)S(1)} %add.43.a_ref), channel_id=1, source_target_pairs={{0,2},{1,3},{2,0},{3,1},{4,6},{5,7},{6,4},{7,5},{8,10},{9,11},{10,... | collective-permute-start | bytes 208904 | tf_op jit(solution)/shard_map/ppermute | solution.py:602
  50.0 20.9 %copy-start.11 = (f32[8,128]{1,0:T(8,128)S(1)}, f32[8,128]{1,0:T(8,128)}, u32[]{:S(2)}) copy-start(f32[8,128]{1,0:T(8,128)} %constant.62.clone.rate_ref) | copy-start | bytes 12292
  50.1 20.9 %copy-start.5 = (bf16[512,256]{1,0:T(8,128)(2,1)S(1)}, bf16[512,256]{1,0:T(8,128)(2,1)}, u32[]{:S(2)}) copy-start(bf16[512,256]{1,0:T(8,128)(2,1)} %constant.64.clone.low_ref) | copy-start | bytes 786436
  50.1 20.8 %copy-start.6 = (bf16[512,256]{1,0:T(8,128)(2,1)S(1)}, bf16[512,256]{1,0:T(8,128)(2,1)}, u32[]{:S(2)}) copy-start(bf16[512,256]{1,0:T(8,128)(2,1)} %constant.63.clone.high_ref) | copy-start | bytes 786436

commit v6 on v5

--- a/solution.py
+++ b/solution.py
@@ -455,23 +455,25 @@
     half_cos = angles_ref[sector * 4]
     half_sin = angles_ref[sector * 4 + 1]
 
-    @pl.loop(0, EMB)
+    @pl.loop(0, EMB, unroll=4)
+    def _(member):
+        near = half_sin * members_ref[2, member] - half_cos * members_ref[3, member]
+        rows = pl.ds(pl.multiple_of(member * CHUNKS, CHUNKS), CHUNKS)
+        chord_ref[rows, :] = (2.0 * members_ref[0, member]) * (near * near)
+
+    @pl.loop(0, EMB, unroll=2)
     def _(member):
         embryo_radius = members_ref[0, member]
-        cosine = members_ref[2, member]
-        sine = members_ref[3, member]
         soft = softening * embryo_radius
         gaps = []
         for g in range(GROUPS):
             gap = pieces[g] - embryo_radius
             gaps.append((gap * gap + soft * soft) * halves[g])
-        near = half_sin * cosine - half_cos * sine
-        chord_ref[...] = (2.0 * embryo_radius) * (near * near)
         push_x = jnp.zeros((8, 128), F32)
         push_y = jnp.zeros((8, 128), F32)
         total = jnp.zeros((8, 128), F32)
         for chunk in range(CHUNKS):
-            chord = jnp.broadcast_to(chord_ref[chunk : chunk + 1, :], (8, 128))
+            chord = jnp.broadcast_to(chord_ref[pl.ds(member * CHUNKS + chunk, 1), :], (8, 128))
             plain, moved = None, None
             for g in range(GROUPS):
                 inverse = lax.rsqrt(gaps[g] + chord)
@@ -485,10 +487,11 @@
             total = total + plain
         place_x = embryo_radius * members_ref[4, member]
         place_y = embryo_radius * members_ref[5, member]
-        push_ref[pl.ds(member, 1), :] = jnp.sum(push_x - place_x * total, axis=0, keepdims=True)
-        push_ref[pl.ds(EMB + member, 1), :] = jnp.sum(push_y - place_y * total, axis=0, keepdims=True)
-
-    push = jnp.broadcast_to(jnp.sum(push_ref[...], axis=1, keepdims=True), (2 * EMB, 128))
+        push_ref[member] = push_x - place_x * total
+        push_ref[EMB + member] = push_y - place_y * total
+
+    push = jnp.sum(jnp.sum(push_ref[...], axis=1), axis=1, keepdims=True)
+    push = jnp.broadcast_to(push, (2 * EMB, 128))
     row = lax.broadcasted_iota(jnp.int32, (2 * EMB, 128), 0)
     lane = lax.broadcasted_iota(jnp.int32, (2 * EMB, 128), 1)
     push = jnp.sum(jnp.where(row == lane, push, 0.0), axis=0, keepdims=True)
@@ -747,8 +750,8 @@
         out_specs=vmem(),
         scratch_shapes=[
             pltpu.VMEM((GROUPS, SPAN, 128), F32),
-            pltpu.VMEM((CHUNKS, 128), F32),
-            pltpu.VMEM((2 * EMB, 128), F32),
+            pltpu.VMEM((EMB * CHUNKS, 128), F32),
+            pltpu.VMEM((2 * EMB, 8, 128), F32),
         ],
         compiler_params=params(),
         cost_estimate=cost(6),

time: 74.3 us -> 73.9 us (level)
  transfers between devices with their start and end apart: 16 -> 16, of which waited for: 5 -> 5; matrix products, arithmetic and copies ran while one was open for 0% -> 0% of each run, Pallas kernels for 36% -> 35%
where the time goes in v6:
time: 73.9 us; the launch traced here: 73.6 us
  Pallas kernels  30.5 us (41%)
  blocking collectives  20.8 us (28%)
  starting transfers between devices  13.7 us (19%)
  waiting for transfers between devices  6.84 us (9%)
  between operations  0.95 us (1%)
    all_to_all x1, blocking collectives, on_device(): lax.all_to_all(packed, RAD, split_axis=0, concat_axis=0, tiled=True)  20.8 us
    ppermute x15, starting transfers between devices, across(): lax.ppermute(value, axis, [(source, target(source)) for source in range(c...  13 us
    pallas_call x3, Pallas kernels, field(): pl.pallas_call(functools.partial(field_kernel, base=base, many=many), out...  8.37 us
    ppermute x15, waiting for transfers between devices, across(): lax.ppermute(value, axis, [(source, target(source)) for source in range(c...  6.83 us
    pallas_call x1, Pallas kernels, on_device(): pl.pallas_call(push_kernel, out_shape=joined_shape, in_specs=[smem()] + [...  6.01 us
    pallas_call x3, Pallas kernels, share(): pl.pallas_call(functools.partial(share_kernel, kinds=kinds), out_shape=tu...  4.73 us
    pallas_call x1, Pallas kernels, on_device(): pl.pallas_call(kick_kernel, out_shape=(tiles, tiles, jax.ShapeDtypeStruct...  3.07 us
    pallas_call x1, Pallas kernels, on_device(): pl.pallas_call(transport_kernel, out_shape=(tiles, tiles, jax.ShapeDtypeS...  2.05 us
  transfers between devices with their start and end apart: 16, of which 5 were waited for; matrix products, arithmetic and copies ran while one was open for 0% of the time, Pallas kernels for 35%

profile of v6, /device:TPU:0, one launch (start us, length us, event | category | flops | bytes accessed | tf_op | source)
XLA Modules:
  0.0 73.6 jit_solution(4069156339997081195)
XLA Ops:
  0.6 1.4 %borders.1 = (f32[8,8,128]{2,1,0:T(8,128)S(1)}, f32[8,8,128]{2,1,0:T(8,128)S(1)}, f32[2,96,128]{2,1,0:T(8,128)S(1)}) custom-call(f32[4,256,128]{2,1,0:T(8,128)} %bitcast.46, f32[4,256,128]{2,1,0:T(8,128)} %bitcast.5.phi_ref.own_ref, f32[4,256,128]{2,1,0:T(8,128)} %bitcast.42), custom_call_target="tpu_custom_call" | custom-call | flops 1000000 | bytes 2500000 | tf_op jit(solution)/shard_map/borders/pallas_call | solution.py:630
  2.1 0.1 collective-permute-start
  2.2 2.1 %collective-permute-start.1 = (f32[8,8,128]{2,1,0:T(8,128)S(1)}, f32[8,8,128]{2,1,0:T(8,128)S(1)}, u32[]{:S(2)}, u32[]{:S(2)}) collective-permute-start(f32[8,8,128]{2,1,0:T(8,128)S(1)} %get-tuple-element.32), channel_id=1, source_target_pairs={{0,3},{1,2},{2,1},{3,0},{4,7},{5,6},{6,5},{7,4},{8,11},{9,10},{10,... | collective-permute-start | bytes 98312 | tf_op jit(solution)/shard_map/ppermute | solution.py:605
  4.3 0.1 collective-permute-start.5
  4.4 0.1 collective-permute-start.4
  4.4 0.5 collective-permute-start.7
  4.9 1.9 %collective-permute-start.3 = (f32[4,256,128]{2,1,0:T(8,128)S(1)}, f32[4,256,128]{2,1,0:T(8,128)S(1)}, u32[]{:S(2)}, u32[]{:S(2)}) collective-permute-start(f32[4,256,128]{2,1,0:T(8,128)S(1)} %bitcast.43), channel_id=1, source_target_pairs={{0,2},{1,3},{2,0},{3,1},{4,6},{5,7},{6,4},{7,5},{8,10},{9,11},{10,... | collective-permute-start | bytes 1572872 | tf_op jit(solution)/shard_map/ppermute | solution.py:605
  6.9 1.9 %azimuth.1.own_ref = f32[4,256,128]{2,1,0:T(8,128)S(1)} custom-call(f32[4,256,128]{2,1,0:T(8,128)} %bitcast.47, f32[4,256,128]{2,1,0:T(8,128)} %bitcast.5.phi_ref.own_ref, f32[8,8,128]{2,1,0:T(8,128)S(1)} %collective-permute-done.mate_ref, f32[8,8,128]{2,1,0:T(8,128)S(1)} %collective-permute-done.1.far_ref), custom_call_target="tpu_custom_call" | custom-call | flops 1000000 | bytes 2500000 | tf_op jit(solution)/shard_map/azimuth/pallas_call | solution.py:662
  8.8 0.0 copy-start.13
  8.8 0.0 copy-start.14
  8.8 0.1 collective-permute-start.2
  8.9 0.1 sine_bitcast_fusion
  8.9 0.5 copy-done.13
  9.4 0.0 copy-done.14
  9.5 0.6 collective-permute-done.5.cross_ref
  10.1 0.5 collective-permute-start.6
  10.6 0.1 broadcast_in_dim.2.radius_ref
  10.7 3.8 %field_0.1 = (f32[4,256,128]{2,1,0:T(8,128)S(1)}, f32[4,256,128]{2,1,0:T(8,128)S(1)}) custom-call(f32[6,32]{1,0:T(8,128)S(1)} %stack.27.members_ref, f32[32,128]{1,0:T(8,128)S(1)} %broadcast_in_dim.2.radius_ref, f32[16,32,128]{2,1,0:T(8,128)S(1)} %copy-done), custom_call_target="tpu_custom_call" | custom-call | flops 4000000 | bytes 10000000 | tf_op jit(solution)/shard_map/field_0/pallas_call | solution.py:699
  14.5 1.6 %edges.1 = (f32[64,128]{1,0:T(8,128)S(1)}, f32[64,128]{1,0:T(8,128)S(1)}) custom-call(s32[32]{0:T(128)S(1)} %copy-done.10, f32[2,96,128]{2,1,0:T(8,128)S(1)} %get-tuple-element.33.own_ref, f32[2,96,128]{2,1,0:T(8,128)} %collective-permute-done.4.mate_ref, f32[2,96,128]{2,1,0:T(8,128)} %collective-permute-done.5.cross_ref, ...), custom_call_target="tpu_custom_call" | custom-call | flops 1000000 | bytes 2500000 | tf_op jit(solution)/shard_map/edges/pallas_call | solution.py:679
  16.1 2.2 %share_vphi.1 = (f32[4,256,128]{2,1,0:T(8,128)S(1)}, f32[4,256,128]{2,1,0:T(8,128)S(1)}) custom-call(s32[32]{0:T(128)S(1)} %copy-done.10, f32[4,256,128]{2,1,0:T(8,128)} %bitcast.5.phi_ref.own_ref, f32[4,256,128]{2,1,0:T(8,128)S(1)} %collective-permute-done.7.mate_ref), custom_call_target="tpu_custom_call" | custom-call | flops 2000000 | bytes 5000000 | tf_op jit(solution)/shard_map/share_vphi/pallas_call | solution.py:239
  18.3 1.3 %share_dens.1 = f32[4,256,128]{2,1,0:T(8,128)S(1)} custom-call(s32[32]{0:T(128)S(1)} %copy-done.10, f32[4,256,128]{2,1,0:T(8,128)S(1)} %azimuth.1.own_ref, f32[4,256,128]{2,1,0:T(8,128)S(1)} %collective-permute-done.2.mate_ref), custom_call_target="tpu_custom_call" | custom-call | flops 2000000 | bytes 5000000 | tf_op jit(solution)/shard_map/share_dens/pallas_call | solution.py:239
  19.5 0.8 %collective-permute-done.3.cross_ref = f32[4,256,128]{2,1,0:T(8,128)S(1)} collective-permute-done((f32[4,256,128]{2,1,0:T(8,128)S(1)}, f32[4,256,128]{2,1,0:T(8,128)S(1)}, u32[]{:S(2)}, u32[]{:S(2)}) %collective-permute-start.3) | collective-permute-done | bytes 524320 | tf_op jit(solution)/shard_map/ppermute | solution.py:605
  20.3 1.0 %collective-permute-start.8 = (f32[4,256,128]{2,1,0:T(8,128)S(1)}, f32[4,256,128]{2,1,0:T(8,128)S(1)}, u32[]{:S(2)}, u32[]{:S(2)}) collective-permute-start(f32[4,256,128]{2,1,0:T(8,128)S(1)} %share_dens.1), channel_id=1, source_target_pairs={{0,2},{1,3},{2,0},{3,1},{4,6},{5,7},{6,4},{7,5},{8,10},{9,11},{10,... | collective-permute-start | bytes 1572872 | tf_op jit(solution)/shard_map/ppermute | solution.py:605
  21.3 2.3 %field_16.1 = (f32[4,256,128]{2,1,0:T(8,128)S(1)}, f32[4,256,128]{2,1,0:T(8,128)S(1)}) custom-call(f32[6,32]{1,0:T(8,128)S(1)} %stack.27.members_ref, f32[32,128]{1,0:T(8,128)S(1)} %broadcast_in_dim.2.radius_ref, f32[16,32,128]{2,1,0:T(8,128)S(1)} %copy-done, f32[4,256,128]{2,1,0:T(8,128)S(1)} %get-tuple-element.35.refs_0_, ...), custom_call_target="tpu_custom_call" | custom-call | flops 2000000 | bytes 5000000 | tf_op jit(solution)/shard_map/field_16/pallas_call | solution.py:699
  23.6 1.1 %collective-permute-start.14 = (f32[4,256,128]{2,1,0:T(8,128)S(1)}, f32[4,256,128]{2,1,0:T(8,128)S(1)}, u32[]{:S(2)}, u32[]{:S(2)}) collective-permute-start(f32[4,256,128]{2,1,0:T(8,128)S(1)} %get-tuple-element.49), channel_id=1, source_target_pairs={{0,2},{1,3},{2,0},{3,1},{4,6},{5,7},{6,4},{7,5},{8,10},{9,11},{10,... | collective-permute-start | bytes 1572872 | tf_op jit(solution)/shard_map/ppermute | solution.py:605
  24.7 0.7 collective-permute-start.12
  25.4 4.5 %collective-permute-start.11 = (f32[64,128]{1,0:T(8,128)S(1)}, f32[64,128]{1,0:T(8,128)S(1)}, u32[]{:S(2)}, u32[]{:S(2)}) collective-permute-start(f32[64,128]{1,0:T(8,128)S(1)} %get-tuple-element.37), channel_id=1, source_target_pairs={{0,4},{4,0},{8,12},{12,8},{16,20},{20,16},{24,28},{28,24},{32,36},... | collective-permute-start | bytes 98312 | tf_op jit(solution)/shard_map/ppermute | solution.py:605
  29.9 1.3 %keep_dens.1.kept_ref = f32[4,256,128]{2,1,0:T(8,128)S(1)} custom-call(s32[32]{0:T(128)S(1)} %copy-done.10, f32[4,256,128]{2,1,0:T(8,128)S(1)} %azimuth.1.own_ref, f32[4,256,128]{2,1,0:T(8,128)S(1)} %collective-permute-done.2.mate_ref), custom_call_target="tpu_custom_call" | custom-call | flops 2000000 | bytes 5000000 | tf_op jit(solution)/shard_map/keep_dens/pallas_call | solution.py:239
  31.2 0.0 copy-start.2
  31.2 0.0 copy-start.7
  31.2 0.0 copy-start.8
  31.2 1.3 %shift_vrad.1.vrad_ref = f32[4,256,128]{2,1,0:T(8,128)S(1)} custom-call(s32[32]{0:T(128)S(1)} %copy-done.10, f32[4,256,128]{2,1,0:T(8,128)S(1)} %bitcast.45, f32[4,256,128]{2,1,0:T(8,128)S(1)} %collective-permute-done.9.mate_ref, f32[4,256,128]{2,1,0:T(8,128)S(1)} %collective-permute-done.3.cross_ref, f32[4,256,128]{2,1,0:T(8,128)S(1)} %collective-permute-done.10.far_ref), custom_call_target="tpu_custom_call" | custom-call | flops 2000000 | bytes 5000000 | tf_op jit(solution)/shard_map/shift_vrad/pallas_call | solution.py:207
  32.5 0.0 collective-permute-done.12.second_ref
  32.6 3.2 %collective-permute-done.8.sent_ref = f32[4,256,128]{2,1,0:T(8,128)S(1)} collective-permute-done((f32[4,256,128]{2,1,0:T(8,128)S(1)}, f32[4,256,128]{2,1,0:T(8,128)S(1)}, u32[]{:S(2)}, u32[]{:S(2)}) %collective-permute-start.8) | collective-permute-done | bytes 524320 | tf_op jit(solution)/shard_map/ppermute | solution.py:605
  35.8 2.1 %transport.1 = (f32[4,256,128]{2,1,0:T(8,128)}, f32[4,256,128]{2,1,0:T(8,128)S(1)}, f32[32,512]{1,0:T(8,128)S(1)}) custom-call(f32[4,256,128]{2,1,0:T(8,128)S(1)} %keep_dens.1.kept_ref, f32[4,256,128]{2,1,0:T(8,128)S(1)} %collective-permute-done.8.sent_ref, f32[64,128]{1,0:T(8,128)S(1)} %collective-permute-done.11.first_ref, ...), custom_call_target="tpu_custom_call" | custom-call | flops 3000000 | bytes 7500000 | tf_op jit(solution)/shard_map/transport/pallas_call | solution.py:726
  37.8 6.0 %push.1 = f32[136,128]{1,0:T(8,128)S(1)} custom-call(f32[6,32]{1,0:T(8,128)S(1)} %stack.27.members_ref, f32[32,128]{1,0:T(8,128)S(1)} %broadcast_in_dim.2.radius_ref, f32[16,32,128]{2,1,0:T(8,128)S(1)} %copy-done, f32[4,256,128]{2,1,0:T(8,128)S(1)} %get-tuple-element.47.dens_ref, f32[32,512]{1,0:T(8,128)S(1)} %get-tuple-element.48.spectra_ref), custom_call_target="tpu_custom_call" | custom-call | flops 6000000 | bytes 15000000 | tf_op jit(solution)/shard_map/push/pallas_call | solution.py:746
  43.8 0.1 collective-permute-start.13
  43.9 1.2 %collective-permute-done.13 = f32[136,128]{1,0:T(8,128)S(1)} collective-permute-done((f32[136,128]{1,0:T(8,128)S(1)}, f32[136,128]{1,0:T(8,128)S(1)}, u32[]{:S(2)}, u32[]{:S(2)}) %collective-permute-start.13) | collective-permute-done | bytes 69664 | tf_op jit(solution)/shard_map/ppermute | solution.py:605
  45.2 0.0 copy-start.3
  45.2 0.0 copy-start.4
  45.2 0.0 copy-start.9
  45.2 1.1 %collective-permute-start.15 = (f32[136,128]{1,0:T(8,128)S(1)}, f32[136,128]{1,0:T(8,128)S(1)}, u32[]{:S(2)}, u32[]{:S(2)}) collective-permute-start(f32[136,128]{1,0:T(8,128)S(1)} %add.43.a_ref), channel_id=1, source_target_pairs={{0,2},{1,3},{2,0},{3,1},{4,6},{5,7},{6,4},{7,5},{8,10},{9,11},{10,... | collective-permute-start | bytes 208904 | tf_op jit(solution)/shard_map/ppermute | solution.py:605
  46.3 2.3 %field_24.1 = (f32[4,256,128]{2,1,0:T(8,128)S(1)}, f32[4,256,128]{2,1,0:T(8,128)S(1)}) custom-call(f32[6,32]{1,0:T(8,128)S(1)} %stack.27.members_ref, f32[32,128]{1,0:T(8,128)S(1)} %broadcast_in_dim.2.radius_ref, f32[16,32,128]{2,1,0:T(8,128)S(1)} %copy-done, f32[4,256,128]{2,1,0:T(8,128)S(1)} %get-tuple-element.42.refs_0_, ...), custom_call_target="tpu_custom_call" | custom-call | flops 2000000 | bytes 5000000 | tf_op jit(solution)/shard_map/field_24/pallas_call | solution.py:699
  48.6 1.0 %collective-permute-done.15.b_ref = f32[136,128]{1,0:T(8,128)S(1)} collective-permute-done((f32[136,128]{1,0:T(8,128)S(1)}, f32[136,128]{1,0:T(8,128)S(1)}, u32[]{:S(2)}, u32[]{:S(2)}) %collective-permute-start.15) | collective-permute-done | bytes 69664 | tf_op jit(solution)/shard_map/ppermute | solution.py:605
  49.6 0.0 copy-start.11
  49.7 0.0 copy-start.6
  49.7 20.8 %all_to_all.5.moments_ref = f32[32,16,128]{2,1,0:T(8,128)S(1)} all-to-all(f32[32,16,128]{2,1,0:T(8,128)S(1)} %get-tuple-element.53), channel_id=1, replica_groups=mesh['rad_0'=4,'rad_1'=2,'rad_2'=4,'az_0'=2,'az_1'=2] {'rad_0','rad_1','..., dimensions={0} | all-to-all | bytes 524288 | tf_op jit(solution)/shard_map/all_to_all | solution.py:778
  70.5 3.1 %kick.1 = (f32[4,256,128]{2,1,0:T(8,128)}, f32[4,256,128]{2,1,0:T(8,128)}, f32[2,32]{1,0:T(2,128)}) custom-call(f32[32,512]{1,0:T(8,128)S(1)} %get-tuple-element.52.spectra_ref, f32[32,16,128]{2,1,0:T(8,128)S(1)} %all_to_all.5.moments_ref, f32[8,128]{1,0:T(8,128)S(1)} %copy-done.11, f32[32,128]{1,0:T(8,128)S(1)} %broadcast_in_dim.2.radius_ref, ...), custom_call_target="tpu_custom_call" | custom-call | flops 5000000 | bytes 12500000 | tf_op jit(solution)/shard_map/kick/pallas_call | solution.py:780
  (35 shorter events, 0.2 us)
Async XLA Ops:
  0.6 4.3 %copy-start.1 = (f32[32,4096]{1,0:T(8,128)S(1)}, f32[32,4096]{1,0:T(8,128)}, u32[]{:S(2)}) copy-start(f32[32,4096]{1,0:T(8,128)} %param.18) | copy-start | bytes 1572868
  2.1 2.8 %collective-permute-start = (f32[8,8,128]{2,1,0:T(8,128)S(1)}, f32[8,8,128]{2,1,0:T(8,128)S(1)}, u32[]{:S(2)}, u32[]{:S(2)}) collective-permute-start(f32[8,8,128]{2,1,0:T(8,128)S(1)} %get-tuple-element.31), channel_id=1, source_target_pairs={{0,1},{1,0},{2,3},{3,2},{4,5},{5,4},{6,7},{7,6},{8,9},{9,8},{10,11... | collective-permute-start | bytes 98312 | tf_op jit(solution)/shard_map/ppermute | solution.py:605
  2.2 4.7 %collective-permute-start.1 = (f32[8,8,128]{2,1,0:T(8,128)S(1)}, f32[8,8,128]{2,1,0:T(8,128)S(1)}, u32[]{:S(2)}, u32[]{:S(2)}) collective-permute-start(f32[8,8,128]{2,1,0:T(8,128)S(1)} %get-tuple-element.32), channel_id=1, source_target_pairs={{0,3},{1,2},{2,1},{3,0},{4,7},{5,6},{6,5},{7,4},{8,11},{9,10},{10,... | collective-permute-start | bytes 98312 | tf_op jit(solution)/shard_map/ppermute | solution.py:605
  4.3 4.6 %copy-start.12 = (s32[32]{0:T(128)S(1)}, s32[32]{0:T(128)}, u32[]{:S(2)}) copy-start(s32[32]{0:T(128)} %param.22) | copy-start | bytes 388
  4.3 6.4 %copy-start = (f32[16,32,128]{2,1,0:T(8,128)S(1)}, f32[16,32,128]{2,1,0:T(8,128)}, u32[]{:S(2)}) copy-start(f32[16,32,128]{2,1,0:T(8,128)} %constant.55.clone.angles_ref) | copy-start | bytes 786436
  4.3 5.8 %collective-permute-start.5 = (f32[2,96,128]{2,1,0:T(8,128)S(1)}, f32[2,96,128]{2,1,0:T(8,128)}, u32[]{:S(2)}, u32[]{:S(2)}) collective-permute-start(f32[2,96,128]{2,1,0:T(8,128)S(1)} %get-tuple-element.33.own_ref), channel_id=1, source_target_pairs={{0,2},{1,3},{2,0},{3,1},{4,6},{5,7},{6,4},{7,5},{8,10},{9,11},{10,... | collective-permute-start | bytes 294920 | tf_op jit(solution)/shard_map/ppermute | solution.py:605
  4.4 5.7 %collective-permute-start.4 = (f32[2,96,128]{2,1,0:T(8,128)S(1)}, f32[2,96,128]{2,1,0:T(8,128)}, u32[]{:S(2)}, u32[]{:S(2)}) collective-permute-start(f32[2,96,128]{2,1,0:T(8,128)S(1)} %get-tuple-element.33.own_ref), channel_id=1, source_target_pairs={{0,1},{1,0},{2,3},{3,2},{4,5},{5,4},{6,7},{7,6},{8,9},{9,8},{10,11... | collective-permute-start | bytes 294920 | tf_op jit(solution)/shard_map/ppermute | solution.py:605
  4.4 11.6 %collective-permute-start.7 = (f32[4,256,128]{2,1,0:T(8,128)}, f32[4,256,128]{2,1,0:T(8,128)S(1)}, u32[]{:S(2)}, u32[]{:S(2)}) collective-permute-start(f32[4,256,128]{2,1,0:T(8,128)} %bitcast.5.phi_ref.own_ref), channel_id=1, source_target_pairs={{0,1},{1,0},{2,3},{3,2},{4,5},{5,4},{6,7},{7,6},{8,9},{9,8},{10,11... | collective-permute-start | bytes 1572872 | tf_op jit(solution)/shard_map/ppermute | solution.py:605
  4.9 15.4 %collective-permute-start.3 = (f32[4,256,128]{2,1,0:T(8,128)S(1)}, f32[4,256,128]{2,1,0:T(8,128)S(1)}, u32[]{:S(2)}, u32[]{:S(2)}) collective-permute-start(f32[4,256,128]{2,1,0:T(8,128)S(1)} %bitcast.43), channel_id=1, source_target_pairs={{0,2},{1,3},{2,0},{3,1},{4,6},{5,7},{6,4},{7,5},{8,10},{9,11},{10,... | collective-permute-start | bytes 1572872 | tf_op jit(solution)/shard_map/ppermute | solution.py:605
  8.8 0.7 copy-start.13
  8.8 0.7 copy-start.14
  8.8 9.5 %collective-permute-start.2 = (f32[4,256,128]{2,1,0:T(8,128)S(1)}, f32[4,256,128]{2,1,0:T(8,128)S(1)}, u32[]{:S(2)}, u32[]{:S(2)}) collective-permute-start(f32[4,256,128]{2,1,0:T(8,128)S(1)} %azimuth.1.own_ref), channel_id=1, source_target_pairs={{0,1},{1,0},{2,3},{3,2},{4,5},{5,4},{6,7},{7,6},{8,9},{9,8},{10,11... | collective-permute-start | bytes 1572872 | tf_op jit(solution)/shard_map/ppermute | solution.py:605
  10.1 15.3 %collective-permute-start.9 = (f32[4,256,128]{2,1,0:T(8,128)S(1)}, f32[4,256,128]{2,1,0:T(8,128)S(1)}, u32[]{:S(2)}, u32[]{:S(2)}) collective-permute-start(f32[4,256,128]{2,1,0:T(8,128)S(1)} %bitcast.44), channel_id=1, source_target_pairs={{0,1},{1,0},{2,3},{3,2},{4,5},{5,4},{6,7},{7,6},{8,9},{9,8},{10,11... | collective-permute-start | bytes 1572872 | tf_op jit(solution)/shard_map/ppermute | solution.py:605
  10.1 4.4 %collective-permute-start.6 = (f32[2,96,128]{2,1,0:T(8,128)}, f32[2,96,128]{2,1,0:T(8,128)}, u32[]{:S(2)}, u32[]{:S(2)}) collective-permute-start(f32[2,96,128]{2,1,0:T(8,128)} %collective-permute-done.5.cross_ref), channel_id=1, source_target_pairs={{0,1},{1,0},{2,3},{3,2},{4,5},{5,4},{6,7},{7,6},{8,9},{9,8},{10,11... | collective-permute-start | bytes 294920 | tf_op jit(solution)/shard_map/ppermute | solution.py:605
  10.7 3.8 %copy-start.10 = (s32[32]{0:T(128)S(1)}, s32[32]{0:T(128)}, u32[]{:S(2)}) copy-start(s32[32]{0:T(128)} %offs_ref.9) | copy-start | bytes 388
  20.3 10.9 %collective-permute-start.10 = (f32[4,256,128]{2,1,0:T(8,128)S(1)}, f32[4,256,128]{2,1,0:T(8,128)S(1)}, u32[]{:S(2)}, u32[]{:S(2)}) collective-permute-start(f32[4,256,128]{2,1,0:T(8,128)S(1)} %collective-permute-done.3.cross_ref), channel_id=1, source_target_pairs={{0,1},{1,0},{2,3},{3,2},{4,5},{5,4},{6,7},{7,6},{8,9},{9,8},{10,11... | collective-permute-start | bytes 1572872 | tf_op jit(solution)/shard_map/ppermute | solution.py:605
  20.3 15.4 %collective-permute-start.8 = (f32[4,256,128]{2,1,0:T(8,128)S(1)}, f32[4,256,128]{2,1,0:T(8,128)S(1)}, u32[]{:S(2)}, u32[]{:S(2)}) collective-permute-start(f32[4,256,128]{2,1,0:T(8,128)S(1)} %share_dens.1), channel_id=1, source_target_pairs={{0,2},{1,3},{2,0},{3,1},{4,6},{5,7},{6,4},{7,5},{8,10},{9,11},{10,... | collective-permute-start | bytes 1572872 | tf_op jit(solution)/shard_map/ppermute | solution.py:605
  23.6 25.0 %collective-permute-start.14 = (f32[4,256,128]{2,1,0:T(8,128)S(1)}, f32[4,256,128]{2,1,0:T(8,128)S(1)}, u32[]{:S(2)}, u32[]{:S(2)}) collective-permute-start(f32[4,256,128]{2,1,0:T(8,128)S(1)} %get-tuple-element.49), channel_id=1, source_target_pairs={{0,2},{1,3},{2,0},{3,1},{4,6},{5,7},{6,4},{7,5},{8,10},{9,11},{10,... | collective-permute-start | bytes 1572872 | tf_op jit(solution)/shard_map/ppermute | solution.py:605
  24.7 7.8 %collective-permute-start.12 = (f32[64,128]{1,0:T(8,128)S(1)}, f32[64,128]{1,0:T(8,128)S(1)}, u32[]{:S(2)}, u32[]{:S(2)}) collective-permute-start(f32[64,128]{1,0:T(8,128)S(1)} %get-tuple-element.44), channel_id=1, source_target_pairs={{4,8},{8,4},{12,16},{16,12},{20,24},{24,20},{28,32},{32,28},{36,40... | collective-permute-start | bytes 98312 | tf_op jit(solution)/shard_map/ppermute | solution.py:695
  25.4 7.2 %collective-permute-start.11 = (f32[64,128]{1,0:T(8,128)S(1)}, f32[64,128]{1,0:T(8,128)S(1)}, u32[]{:S(2)}, u32[]{:S(2)}) collective-permute-start(f32[64,128]{1,0:T(8,128)S(1)} %get-tuple-element.37), channel_id=1, source_target_pairs={{0,4},{4,0},{8,12},{12,8},{16,20},{20,16},{24,28},{28,24},{32,36},... | collective-permute-start | bytes 98312 | tf_op jit(solution)/shard_map/ppermute | solution.py:605
  31.2 4.6 %copy-start.2 = (f32[64,512]{1,0:T(8,128)S(1)}, f32[64,512]{1,0:T(8,128)}, u32[]{:S(2)}) copy-start(f32[64,512]{1,0:T(8,128)} %constant.58.clone.twiddle_ref) | copy-start | bytes 393220
  31.2 4.6 %copy-start.7 = (bf16[256,512]{1,0:T(8,128)(2,1)S(1)}, bf16[256,512]{1,0:T(8,128)(2,1)}, u32[]{:S(2)}) copy-start(bf16[256,512]{1,0:T(8,128)(2,1)} %constant.57.clone.low_ref) | copy-start | bytes 786436
  31.2 4.6 %copy-start.8 = (bf16[256,512]{1,0:T(8,128)(2,1)S(1)}, bf16[256,512]{1,0:T(8,128)(2,1)}, u32[]{:S(2)}) copy-start(bf16[256,512]{1,0:T(8,128)(2,1)} %constant.56.clone.high_ref) | copy-start | bytes 786436
  43.8 1.3 %collective-permute-start.13 = (f32[136,128]{1,0:T(8,128)S(1)}, f32[136,128]{1,0:T(8,128)S(1)}, u32[]{:S(2)}, u32[]{:S(2)}) collective-permute-start(f32[136,128]{1,0:T(8,128)S(1)} %push.1), channel_id=1, source_target_pairs={{0,1},{1,0},{2,3},{3,2},{4,5},{5,4},{6,7},{7,6},{8,9},{9,8},{10,11... | collective-permute-start | bytes 208904 | tf_op jit(solution)/shard_map/ppermute | solution.py:605
  45.2 4.4 %copy-start.3 = (f32[32,512]{1,0:T(8,128)S(1)}, f32[32,512]{1,0:T(8,128)}, u32[]{:S(2)}) copy-start(f32[32,512]{1,0:T(8,128)} %constant.60.clone.drop_ref) | copy-start | bytes 196612
  45.2 4.4 %copy-start.4 = (f32[32,512]{1,0:T(8,128)S(1)}, f32[32,512]{1,0:T(8,128)}, u32[]{:S(2)}) copy-start(f32[32,512]{1,0:T(8,128)} %constant.59.clone.lift_ref) | copy-start | bytes 196612
  45.2 4.4 %copy-start.9 = (f32[8,512]{1,0:T(8,128)S(1)}, f32[8,512]{1,0:T(8,128)}, u32[]{:S(2)}) copy-start(f32[8,512]{1,0:T(8,128)} %constant.61.clone.vectors_ref) | copy-start | bytes 49156
  45.2 4.4 %collective-permute-start.15 = (f32[136,128]{1,0:T(8,128)S(1)}, f32[136,128]{1,0:T(8,128)S(1)}, u32[]{:S(2)}, u32[]{:S(2)}) collective-permute-start(f32[136,128]{1,0:T(8,128)S(1)} %add.43.a_ref), channel_id=1, source_target_pairs={{0,2},{1,3},{2,0},{3,1},{4,6},{5,7},{6,4},{7,5},{8,10},{9,11},{10,... | collective-permute-start | bytes 208904 | tf_op jit(solution)/shard_map/ppermute | solution.py:605
  49.6 20.9 %copy-start.11 = (f32[8,128]{1,0:T(8,128)S(1)}, f32[8,128]{1,0:T(8,128)}, u32[]{:S(2)}) copy-start(f32[8,128]{1,0:T(8,128)} %constant.62.clone.rate_ref) | copy-start | bytes 12292
  49.7 20.9 %copy-start.5 = (bf16[512,256]{1,0:T(8,128)(2,1)S(1)}, bf16[512,256]{1,0:T(8,128)(2,1)}, u32[]{:S(2)}) copy-start(bf16[512,256]{1,0:T(8,128)(2,1)} %constant.64.clone.low_ref) | copy-start | bytes 786436
  49.7 20.8 %copy-start.6 = (bf16[512,256]{1,0:T(8,128)(2,1)S(1)}, bf16[512,256]{1,0:T(8,128)(2,1)}, u32[]{:S(2)}) copy-start(bf16[512,256]{1,0:T(8,128)(2,1)} %constant.63.clone.high_ref) | copy-start | bytes 786436

commit v7 on v6

--- a/solution.py
+++ b/solution.py
@@ -461,7 +461,7 @@
         rows = pl.ds(pl.multiple_of(member * CHUNKS, CHUNKS), CHUNKS)
         chord_ref[rows, :] = (2.0 * members_ref[0, member]) * (near * near)
 
-    @pl.loop(0, EMB, unroll=2)
+    @pl.loop(0, EMB, unroll=4)
     def _(member):
         embryo_radius = members_ref[0, member]
         soft = softening * embryo_radius
@@ -721,7 +721,7 @@
     dens_cross = after(
         dens_cross, vrad_one, *middle_field, dens_kept, vphi_sent, vphi_kept, edge_first_in, edge_second
     )
-    vphi_cross = across(after(vphi_sent, *middle_field), AZ, lambda i: i ^ 2)
+    vphi_cross = across(after(vphi_sent, vrad_one), AZ, lambda i: i ^ 2)
 
     transported, stepped, part = pl.pallas_call(
         transport_kernel,

time: 73.9 us -> 73.7 us (level)
  transfers between devices with their start and end apart: 16 -> 16, of which waited for: 5 -> 6; matrix products, arithmetic and copies ran while one was open for 0% -> 0% of each run, Pallas kernels for 35% -> 35%
where the time goes in v7:
time: 73.7 us; the launch traced here: 73.4 us
  Pallas kernels  29.9 us (41%)
  blocking collectives  20.8 us (28%)
  starting transfers between devices  13.7 us (19%)
  waiting for transfers between devices  7.32 us (10%)
  between operations  0.93 us (1%)
    all_to_all x1, blocking collectives, on_device(): lax.all_to_all(packed, RAD, split_axis=0, concat_axis=0, tiled=True)  20.8 us
    ppermute x15, starting transfers between devices, across(): lax.ppermute(value, axis, [(source, target(source)) for source in range(c...  13.1 us
    pallas_call x3, Pallas kernels, field(): pl.pallas_call(functools.partial(field_kernel, base=base, many=many), out...  8.37 us
    ppermute x15, waiting for transfers between devices, across(): lax.ppermute(value, axis, [(source, target(source)) for source in range(c...  7.32 us
    pallas_call x1, Pallas kernels, on_device(): pl.pallas_call(push_kernel, out_shape=joined_shape, in_specs=[smem()] + [...  5.89 us
    pallas_call x3, Pallas kernels, share(): pl.pallas_call(functools.partial(share_kernel, kinds=kinds), out_shape=tu...  4.72 us
    pallas_call x1, Pallas kernels, on_device(): pl.pallas_call(kick_kernel, out_shape=(tiles, tiles, jax.ShapeDtypeStruct...  3.06 us
    pallas_call x1, Pallas kernels, on_device(): pl.pallas_call(transport_kernel, out_shape=(tiles, tiles, jax.ShapeDtypeS...  2.03 us
  transfers between devices with their start and end apart: 16, of which 6 were waited for; matrix products, arithmetic and copies ran while one was open for 0% of the time, Pallas kernels for 35%

profile of v7, /device:TPU:0, one launch (start us, length us, event | category | flops | bytes accessed | tf_op | source)
XLA Modules:
  0.0 73.4 jit_solution(2846609088069891789)
XLA Ops:
  0.6 1.4 %borders.1 = (f32[8,8,128]{2,1,0:T(8,128)S(1)}, f32[8,8,128]{2,1,0:T(8,128)S(1)}, f32[2,96,128]{2,1,0:T(8,128)S(1)}) custom-call(f32[4,256,128]{2,1,0:T(8,128)} %bitcast.46, f32[4,256,128]{2,1,0:T(8,128)} %bitcast.5.phi_ref.own_ref, f32[4,256,128]{2,1,0:T(8,128)} %bitcast.42), custom_call_target="tpu_custom_call" | custom-call | flops 1000000 | bytes 2500000 | tf_op jit(solution)/shard_map/borders/pallas_call | solution.py:630
  2.1 0.1 collective-permute-start
  2.2 2.1 %collective-permute-start.1 = (f32[8,8,128]{2,1,0:T(8,128)S(1)}, f32[8,8,128]{2,1,0:T(8,128)S(1)}, u32[]{:S(2)}, u32[]{:S(2)}) collective-permute-start(f32[8,8,128]{2,1,0:T(8,128)S(1)} %get-tuple-element.32), channel_id=1, source_target_pairs={{0,3},{1,2},{2,1},{3,0},{4,7},{5,6},{6,5},{7,4},{8,11},{9,10},{10,... | collective-permute-start | bytes 98312 | tf_op jit(solution)/shard_map/ppermute | solution.py:605
  4.3 0.1 collective-permute-start.5
  4.4 0.1 collective-permute-start.4
  4.4 0.5 collective-permute-start.7
  4.9 1.9 %collective-permute-start.3 = (f32[4,256,128]{2,1,0:T(8,128)S(1)}, f32[4,256,128]{2,1,0:T(8,128)S(1)}, u32[]{:S(2)}, u32[]{:S(2)}) collective-permute-start(f32[4,256,128]{2,1,0:T(8,128)S(1)} %bitcast.43), channel_id=1, source_target_pairs={{0,2},{1,3},{2,0},{3,1},{4,6},{5,7},{6,4},{7,5},{8,10},{9,11},{10,... | collective-permute-start | bytes 1572872 | tf_op jit(solution)/shard_map/ppermute | solution.py:605
  6.9 1.9 %azimuth.1.own_ref = f32[4,256,128]{2,1,0:T(8,128)S(1)} custom-call(f32[4,256,128]{2,1,0:T(8,128)} %bitcast.47, f32[4,256,128]{2,1,0:T(8,128)} %bitcast.5.phi_ref.own_ref, f32[8,8,128]{2,1,0:T(8,128)S(1)} %collective-permute-done.mate_ref, f32[8,8,128]{2,1,0:T(8,128)S(1)} %collective-permute-done.1.far_ref), custom_call_target="tpu_custom_call" | custom-call | flops 1000000 | bytes 2500000 | tf_op jit(solution)/shard_map/azimuth/pallas_call | solution.py:662
  8.8 0.0 copy-start.13
  8.8 0.1 collective-permute-start.2
  8.9 0.1 sine_bitcast_fusion
  8.9 0.5 copy-done.13
  9.4 0.0 copy-done.14
  9.5 0.5 collective-permute-done.5.cross_ref
  10.0 0.1 broadcast_in_dim.2.radius_ref
  10.0 3.8 %field_0.1 = (f32[4,256,128]{2,1,0:T(8,128)S(1)}, f32[4,256,128]{2,1,0:T(8,128)S(1)}) custom-call(f32[6,32]{1,0:T(8,128)S(1)} %stack.27.members_ref, f32[32,128]{1,0:T(8,128)S(1)} %broadcast_in_dim.2.radius_ref, f32[16,32,128]{2,1,0:T(8,128)S(1)} %copy-done), custom_call_target="tpu_custom_call" | custom-call | flops 4000000 | bytes 10000000 | tf_op jit(solution)/shard_map/field_0/pallas_call | solution.py:699
  13.8 0.6 collective-permute-start.9
  14.4 1.1 %edges.1 = (f32[64,128]{1,0:T(8,128)S(1)}, f32[64,128]{1,0:T(8,128)S(1)}) custom-call(s32[32]{0:T(128)S(1)} %copy-done.10, f32[2,96,128]{2,1,0:T(8,128)S(1)} %get-tuple-element.33.own_ref, f32[2,96,128]{2,1,0:T(8,128)S(1)} %collective-permute-done.4.mate_ref, f32[2,96,128]{2,1,0:T(8,128)S(1)} %collective-permute-done.5.cross_ref, ...), custom_call_target="tpu_custom_call" | custom-call | flops 1000000 | bytes 2500000 | tf_op jit(solution)/shard_map/edges/pallas_call | solution.py:679
  15.6 2.2 %share_vphi.1 = (f32[4,256,128]{2,1,0:T(8,128)S(1)}, f32[4,256,128]{2,1,0:T(8,128)S(1)}) custom-call(s32[32]{0:T(128)S(1)} %copy-done.10, f32[4,256,128]{2,1,0:T(8,128)} %bitcast.5.phi_ref.own_ref, f32[4,256,128]{2,1,0:T(8,128)S(1)} %collective-permute-done.7.mate_ref), custom_call_target="tpu_custom_call" | custom-call | flops 2000000 | bytes 5000000 | tf_op jit(solution)/shard_map/share_vphi/pallas_call | solution.py:239
  17.8 1.2 %share_dens.1 = f32[4,256,128]{2,1,0:T(8,128)S(1)} custom-call(s32[32]{0:T(128)S(1)} %copy-done.10, f32[4,256,128]{2,1,0:T(8,128)S(1)} %azimuth.1.own_ref, f32[4,256,128]{2,1,0:T(8,128)S(1)} %collective-permute-done.2.mate_ref), custom_call_target="tpu_custom_call" | custom-call | flops 2000000 | bytes 5000000 | tf_op jit(solution)/shard_map/share_dens/pallas_call | solution.py:239
  19.0 1.3 %collective-permute-done.3.cross_ref = f32[4,256,128]{2,1,0:T(8,128)S(1)} collective-permute-done((f32[4,256,128]{2,1,0:T(8,128)S(1)}, f32[4,256,128]{2,1,0:T(8,128)S(1)}, u32[]{:S(2)}, u32[]{:S(2)}) %collective-permute-start.3) | collective-permute-done | bytes 524320 | tf_op jit(solution)/shard_map/ppermute | solution.py:605
  20.3 1.0 %collective-permute-start.8 = (f32[4,256,128]{2,1,0:T(8,128)S(1)}, f32[4,256,128]{2,1,0:T(8,128)S(1)}, u32[]{:S(2)}, u32[]{:S(2)}) collective-permute-start(f32[4,256,128]{2,1,0:T(8,128)S(1)} %share_dens.1), channel_id=1, source_target_pairs={{0,2},{1,3},{2,0},{3,1},{4,6},{5,7},{6,4},{7,5},{8,10},{9,11},{10,... | collective-permute-start | bytes 1572872 | tf_op jit(solution)/shard_map/ppermute | solution.py:605
  21.3 0.9 %collective-permute-done.10.far_ref = f32[4,256,128]{2,1,0:T(8,128)S(1)} collective-permute-done((f32[4,256,128]{2,1,0:T(8,128)S(1)}, f32[4,256,128]{2,1,0:T(8,128)S(1)}, u32[]{:S(2)}, u32[]{:S(2)}) %collective-permute-start.10) | collective-permute-done | bytes 524320 | tf_op jit(solution)/shard_map/ppermute | solution.py:605
  22.2 1.3 %shift_vrad.1.vrad_ref = f32[4,256,128]{2,1,0:T(8,128)S(1)} custom-call(s32[32]{0:T(128)S(1)} %copy-done.10, f32[4,256,128]{2,1,0:T(8,128)S(1)} %bitcast.45, f32[4,256,128]{2,1,0:T(8,128)S(1)} %collective-permute-done.9.mate_ref, f32[4,256,128]{2,1,0:T(8,128)S(1)} %collective-permute-done.3.cross_ref, f32[4,256,128]{2,1,0:T(8,128)S(1)} %collective-permute-done.10.far_ref), custom_call_target="tpu_custom_call" | custom-call | flops 2000000 | bytes 5000000 | tf_op jit(solution)/shard_map/shift_vrad/pallas_call | solution.py:207
  23.5 1.1 %collective-permute-start.14 = (f32[4,256,128]{2,1,0:T(8,128)S(1)}, f32[4,256,128]{2,1,0:T(8,128)S(1)}, u32[]{:S(2)}, u32[]{:S(2)}) collective-permute-start(f32[4,256,128]{2,1,0:T(8,128)S(1)} %get-tuple-element.49), channel_id=1, source_target_pairs={{0,2},{1,3},{2,0},{3,1},{4,6},{5,7},{6,4},{7,5},{8,10},{9,11},{10,... | collective-permute-start | bytes 1572872 | tf_op jit(solution)/shard_map/ppermute | solution.py:605
  24.6 0.7 collective-permute-start.12
  25.3 4.5 %collective-permute-start.11 = (f32[64,128]{1,0:T(8,128)S(1)}, f32[64,128]{1,0:T(8,128)S(1)}, u32[]{:S(2)}, u32[]{:S(2)}) collective-permute-start(f32[64,128]{1,0:T(8,128)S(1)} %get-tuple-element.37), channel_id=1, source_target_pairs={{0,4},{4,0},{8,12},{12,8},{16,20},{20,16},{24,28},{28,24},{32,36},... | collective-permute-start | bytes 98312 | tf_op jit(solution)/shard_map/ppermute | solution.py:605
  29.7 2.3 %field_16.1 = (f32[4,256,128]{2,1,0:T(8,128)S(1)}, f32[4,256,128]{2,1,0:T(8,128)S(1)}) custom-call(f32[6,32]{1,0:T(8,128)S(1)} %stack.27.members_ref, f32[32,128]{1,0:T(8,128)S(1)} %broadcast_in_dim.2.radius_ref, f32[16,32,128]{2,1,0:T(8,128)S(1)} %copy-done, f32[4,256,128]{2,1,0:T(8,128)S(1)} %get-tuple-element.35.refs_0_, ...), custom_call_target="tpu_custom_call" | custom-call | flops 2000000 | bytes 5000000 | tf_op jit(solution)/shard_map/field_16/pallas_call | solution.py:699
  32.0 0.0 copy-start.2
  32.1 0.0 copy-start.7
  32.1 0.0 copy-start.8
  32.1 1.3 %keep_dens.1.kept_ref = f32[4,256,128]{2,1,0:T(8,128)S(1)} custom-call(s32[32]{0:T(128)S(1)} %copy-done.10, f32[4,256,128]{2,1,0:T(8,128)S(1)} %azimuth.1.own_ref, f32[4,256,128]{2,1,0:T(8,128)S(1)} %collective-permute-done.2.mate_ref), custom_call_target="tpu_custom_call" | custom-call | flops 2000000 | bytes 5000000 | tf_op jit(solution)/shard_map/keep_dens/pallas_call | solution.py:239
  33.4 2.3 %collective-permute-done.8.sent_ref = f32[4,256,128]{2,1,0:T(8,128)S(1)} collective-permute-done((f32[4,256,128]{2,1,0:T(8,128)S(1)}, f32[4,256,128]{2,1,0:T(8,128)S(1)}, u32[]{:S(2)}, u32[]{:S(2)}) %collective-permute-start.8) | collective-permute-done | bytes 524320 | tf_op jit(solution)/shard_map/ppermute | solution.py:605
  35.8 2.0 %transport.1 = (f32[4,256,128]{2,1,0:T(8,128)}, f32[4,256,128]{2,1,0:T(8,128)S(1)}, f32[32,512]{1,0:T(8,128)S(1)}) custom-call(f32[4,256,128]{2,1,0:T(8,128)S(1)} %keep_dens.1.kept_ref, f32[4,256,128]{2,1,0:T(8,128)S(1)} %collective-permute-done.8.sent_ref, f32[64,128]{1,0:T(8,128)S(1)} %collective-permute-done.11.first_ref, ...), custom_call_target="tpu_custom_call" | custom-call | flops 3000000 | bytes 7500000 | tf_op jit(solution)/shard_map/transport/pallas_call | solution.py:726
  37.8 5.9 %push.1 = f32[136,128]{1,0:T(8,128)S(1)} custom-call(f32[6,32]{1,0:T(8,128)S(1)} %stack.27.members_ref, f32[32,128]{1,0:T(8,128)S(1)} %broadcast_in_dim.2.radius_ref, f32[16,32,128]{2,1,0:T(8,128)S(1)} %copy-done, f32[4,256,128]{2,1,0:T(8,128)S(1)} %get-tuple-element.47.dens_ref, f32[32,512]{1,0:T(8,128)S(1)} %get-tuple-element.48.spectra_ref), custom_call_target="tpu_custom_call" | custom-call | flops 6000000 | bytes 15000000 | tf_op jit(solution)/shard_map/push/pallas_call | solution.py:746
  43.7 0.1 collective-permute-start.13
  43.8 1.2 %collective-permute-done.13 = f32[136,128]{1,0:T(8,128)S(1)} collective-permute-done((f32[136,128]{1,0:T(8,128)S(1)}, f32[136,128]{1,0:T(8,128)S(1)}, u32[]{:S(2)}, u32[]{:S(2)}) %collective-permute-start.13) | collective-permute-done | bytes 69664 | tf_op jit(solution)/shard_map/ppermute | solution.py:605
  45.0 0.0 copy-start.3
  45.0 0.0 copy-start.4
  45.0 0.0 copy-start.9
  45.1 1.1 %collective-permute-start.15 = (f32[136,128]{1,0:T(8,128)S(1)}, f32[136,128]{1,0:T(8,128)S(1)}, u32[]{:S(2)}, u32[]{:S(2)}) collective-permute-start(f32[136,128]{1,0:T(8,128)S(1)} %add.43.a_ref), channel_id=1, source_target_pairs={{0,2},{1,3},{2,0},{3,1},{4,6},{5,7},{6,4},{7,5},{8,10},{9,11},{10,... | collective-permute-start | bytes 208904 | tf_op jit(solution)/shard_map/ppermute | solution.py:605
  46.1 2.3 %field_24.1 = (f32[4,256,128]{2,1,0:T(8,128)S(1)}, f32[4,256,128]{2,1,0:T(8,128)S(1)}) custom-call(f32[6,32]{1,0:T(8,128)S(1)} %stack.27.members_ref, f32[32,128]{1,0:T(8,128)S(1)} %broadcast_in_dim.2.radius_ref, f32[16,32,128]{2,1,0:T(8,128)S(1)} %copy-done, f32[4,256,128]{2,1,0:T(8,128)S(1)} %get-tuple-element.42.refs_0_, ...), custom_call_target="tpu_custom_call" | custom-call | flops 2000000 | bytes 5000000 | tf_op jit(solution)/shard_map/field_24/pallas_call | solution.py:699
  48.4 1.0 %collective-permute-done.15.b_ref = f32[136,128]{1,0:T(8,128)S(1)} collective-permute-done((f32[136,128]{1,0:T(8,128)S(1)}, f32[136,128]{1,0:T(8,128)S(1)}, u32[]{:S(2)}, u32[]{:S(2)}) %collective-permute-start.15) | collective-permute-done | bytes 69664 | tf_op jit(solution)/shard_map/ppermute | solution.py:605
  49.5 0.0 copy-start.11
  49.5 0.1 moments.1
  49.5 0.0 copy-start.6
  49.5 20.8 %all_to_all.5.moments_ref = f32[32,16,128]{2,1,0:T(8,128)S(1)} all-to-all(f32[32,16,128]{2,1,0:T(8,128)S(1)} %get-tuple-element.53), channel_id=1, replica_groups=mesh['rad_0'=4,'rad_1'=2,'rad_2'=4,'az_0'=2,'az_1'=2] {'rad_0','rad_1','..., dimensions={0} | all-to-all | bytes 524288 | tf_op jit(solution)/shard_map/all_to_all | solution.py:778
  70.4 3.1 %kick.1 = (f32[4,256,128]{2,1,0:T(8,128)}, f32[4,256,128]{2,1,0:T(8,128)}, f32[2,32]{1,0:T(2,128)}) custom-call(f32[32,512]{1,0:T(8,128)S(1)} %get-tuple-element.52.spectra_ref, f32[32,16,128]{2,1,0:T(8,128)S(1)} %all_to_all.5.moments_ref, f32[8,128]{1,0:T(8,128)S(1)} %copy-done.11, f32[32,128]{1,0:T(8,128)S(1)} %broadcast_in_dim.2.radius_ref, ...), custom_call_target="tpu_custom_call" | custom-call | flops 5000000 | bytes 12500000 | tf_op jit(solution)/shard_map/kick/pallas_call | solution.py:780
  (35 shorter events, 0.1 us)
Async XLA Ops:
  0.6 4.3 %copy-start.1 = (f32[32,4096]{1,0:T(8,128)S(1)}, f32[32,4096]{1,0:T(8,128)}, u32[]{:S(2)}) copy-start(f32[32,4096]{1,0:T(8,128)} %param.18) | copy-start | bytes 1572868
  2.1 2.8 %collective-permute-start = (f32[8,8,128]{2,1,0:T(8,128)S(1)}, f32[8,8,128]{2,1,0:T(8,128)S(1)}, u32[]{:S(2)}, u32[]{:S(2)}) collective-permute-start(f32[8,8,128]{2,1,0:T(8,128)S(1)} %get-tuple-element.31), channel_id=1, source_target_pairs={{0,1},{1,0},{2,3},{3,2},{4,5},{5,4},{6,7},{7,6},{8,9},{9,8},{10,11... | collective-permute-start | bytes 98312 | tf_op jit(solution)/shard_map/ppermute | solution.py:605
  2.2 4.7 %collective-permute-start.1 = (f32[8,8,128]{2,1,0:T(8,128)S(1)}, f32[8,8,128]{2,1,0:T(8,128)S(1)}, u32[]{:S(2)}, u32[]{:S(2)}) collective-permute-start(f32[8,8,128]{2,1,0:T(8,128)S(1)} %get-tuple-element.32), channel_id=1, source_target_pairs={{0,3},{1,2},{2,1},{3,0},{4,7},{5,6},{6,5},{7,4},{8,11},{9,10},{10,... | collective-permute-start | bytes 98312 | tf_op jit(solution)/shard_map/ppermute | solution.py:605
  4.3 4.6 %copy-start.12 = (s32[32]{0:T(128)S(1)}, s32[32]{0:T(128)}, u32[]{:S(2)}) copy-start(s32[32]{0:T(128)} %param.22) | copy-start | bytes 388
  4.3 5.7 %copy-start = (f32[16,32,128]{2,1,0:T(8,128)S(1)}, f32[16,32,128]{2,1,0:T(8,128)}, u32[]{:S(2)}) copy-start(f32[16,32,128]{2,1,0:T(8,128)} %constant.55.clone.angles_ref) | copy-start | bytes 786436
  4.3 5.7 %collective-permute-start.5 = (f32[2,96,128]{2,1,0:T(8,128)S(1)}, f32[2,96,128]{2,1,0:T(8,128)S(1)}, u32[]{:S(2)}, u32[]{:S(2)}) collective-permute-start(f32[2,96,128]{2,1,0:T(8,128)S(1)} %get-tuple-element.33.own_ref), channel_id=1, source_target_pairs={{0,2},{1,3},{2,0},{3,1},{4,6},{5,7},{6,4},{7,5},{8,10},{9,11},{10,... | collective-permute-start | bytes 294920 | tf_op jit(solution)/shard_map/ppermute | solution.py:605
  4.4 9.4 %collective-permute-start.4 = (f32[2,96,128]{2,1,0:T(8,128)S(1)}, f32[2,96,128]{2,1,0:T(8,128)S(1)}, u32[]{:S(2)}, u32[]{:S(2)}) collective-permute-start(f32[2,96,128]{2,1,0:T(8,128)S(1)} %get-tuple-element.33.own_ref), channel_id=1, source_target_pairs={{0,1},{1,0},{2,3},{3,2},{4,5},{5,4},{6,7},{7,6},{8,9},{9,8},{10,11... | collective-permute-start | bytes 294920 | tf_op jit(solution)/shard_map/ppermute | solution.py:605
  4.4 11.1 %collective-permute-start.7 = (f32[4,256,128]{2,1,0:T(8,128)}, f32[4,256,128]{2,1,0:T(8,128)S(1)}, u32[]{:S(2)}, u32[]{:S(2)}) collective-permute-start(f32[4,256,128]{2,1,0:T(8,128)} %bitcast.5.phi_ref.own_ref), channel_id=1, source_target_pairs={{0,1},{1,0},{2,3},{3,2},{4,5},{5,4},{6,7},{7,6},{8,9},{9,8},{10,11... | collective-permute-start | bytes 1572872 | tf_op jit(solution)/shard_map/ppermute | solution.py:605
  4.9 15.4 %collective-permute-start.3 = (f32[4,256,128]{2,1,0:T(8,128)S(1)}, f32[4,256,128]{2,1,0:T(8,128)S(1)}, u32[]{:S(2)}, u32[]{:S(2)}) collective-permute-start(f32[4,256,128]{2,1,0:T(8,128)S(1)} %bitcast.43), channel_id=1, source_target_pairs={{0,2},{1,3},{2,0},{3,1},{4,6},{5,7},{6,4},{7,5},{8,10},{9,11},{10,... | collective-permute-start | bytes 1572872 | tf_op jit(solution)/shard_map/ppermute | solution.py:605
  8.8 0.7 copy-start.13
  8.8 0.7 copy-start.14
  8.8 9.0 %collective-permute-start.2 = (f32[4,256,128]{2,1,0:T(8,128)S(1)}, f32[4,256,128]{2,1,0:T(8,128)S(1)}, u32[]{:S(2)}, u32[]{:S(2)}) collective-permute-start(f32[4,256,128]{2,1,0:T(8,128)S(1)} %azimuth.1.own_ref), channel_id=1, source_target_pairs={{0,1},{1,0},{2,3},{3,2},{4,5},{5,4},{6,7},{7,6},{8,9},{9,8},{10,11... | collective-permute-start | bytes 1572872 | tf_op jit(solution)/shard_map/ppermute | solution.py:605
  10.0 4.5 %collective-permute-start.6 = (f32[2,96,128]{2,1,0:T(8,128)S(1)}, f32[2,96,128]{2,1,0:T(8,128)S(1)}, u32[]{:S(2)}, u32[]{:S(2)}) collective-permute-start(f32[2,96,128]{2,1,0:T(8,128)S(1)} %collective-permute-done.5.cross_ref), channel_id=1, source_target_pairs={{0,1},{1,0},{2,3},{3,2},{4,5},{5,4},{6,7},{7,6},{8,9},{9,8},{10,11... | collective-permute-start | bytes 294920 | tf_op jit(solution)/shard_map/ppermute | solution.py:605
  10.0 4.4 %copy-start.10 = (s32[32]{0:T(128)S(1)}, s32[32]{0:T(128)}, u32[]{:S(2)}) copy-start(s32[32]{0:T(128)} %offs_ref.9) | copy-start | bytes 388
  13.8 7.5 %collective-permute-start.9 = (f32[4,256,128]{2,1,0:T(8,128)S(1)}, f32[4,256,128]{2,1,0:T(8,128)S(1)}, u32[]{:S(2)}, u32[]{:S(2)}) collective-permute-start(f32[4,256,128]{2,1,0:T(8,128)S(1)} %bitcast.44), channel_id=1, source_target_pairs={{0,1},{1,0},{2,3},{3,2},{4,5},{5,4},{6,7},{7,6},{8,9},{9,8},{10,11... | collective-permute-start | bytes 1572872 | tf_op jit(solution)/shard_map/ppermute | solution.py:605
  20.3 1.9 %collective-permute-start.10 = (f32[4,256,128]{2,1,0:T(8,128)S(1)}, f32[4,256,128]{2,1,0:T(8,128)S(1)}, u32[]{:S(2)}, u32[]{:S(2)}) collective-permute-start(f32[4,256,128]{2,1,0:T(8,128)S(1)} %collective-permute-done.3.cross_ref), channel_id=1, source_target_pairs={{0,1},{1,0},{2,3},{3,2},{4,5},{5,4},{6,7},{7,6},{8,9},{9,8},{10,11... | collective-permute-start | bytes 1572872 | tf_op jit(solution)/shard_map/ppermute | solution.py:605
  20.3 15.4 %collective-permute-start.8 = (f32[4,256,128]{2,1,0:T(8,128)S(1)}, f32[4,256,128]{2,1,0:T(8,128)S(1)}, u32[]{:S(2)}, u32[]{:S(2)}) collective-permute-start(f32[4,256,128]{2,1,0:T(8,128)S(1)} %share_dens.1), channel_id=1, source_target_pairs={{0,2},{1,3},{2,0},{3,1},{4,6},{5,7},{6,4},{7,5},{8,10},{9,11},{10,... | collective-permute-start | bytes 1572872 | tf_op jit(solution)/shard_map/ppermute | solution.py:605
  23.5 24.9 %collective-permute-start.14 = (f32[4,256,128]{2,1,0:T(8,128)S(1)}, f32[4,256,128]{2,1,0:T(8,128)S(1)}, u32[]{:S(2)}, u32[]{:S(2)}) collective-permute-start(f32[4,256,128]{2,1,0:T(8,128)S(1)} %get-tuple-element.49), channel_id=1, source_target_pairs={{0,2},{1,3},{2,0},{3,1},{4,6},{5,7},{6,4},{7,5},{8,10},{9,11},{10,... | collective-permute-start | bytes 1572872 | tf_op jit(solution)/shard_map/ppermute | solution.py:605
  24.6 8.8 %collective-permute-start.12 = (f32[64,128]{1,0:T(8,128)S(1)}, f32[64,128]{1,0:T(8,128)S(1)}, u32[]{:S(2)}, u32[]{:S(2)}) collective-permute-start(f32[64,128]{1,0:T(8,128)S(1)} %get-tuple-element.44), channel_id=1, source_target_pairs={{4,8},{8,4},{12,16},{16,12},{20,24},{24,20},{28,32},{32,28},{36,40... | collective-permute-start | bytes 98312 | tf_op jit(solution)/shard_map/ppermute | solution.py:695
  25.3 8.1 %collective-permute-start.11 = (f32[64,128]{1,0:T(8,128)S(1)}, f32[64,128]{1,0:T(8,128)S(1)}, u32[]{:S(2)}, u32[]{:S(2)}) collective-permute-start(f32[64,128]{1,0:T(8,128)S(1)} %get-tuple-element.37), channel_id=1, source_target_pairs={{0,4},{4,0},{8,12},{12,8},{16,20},{20,16},{24,28},{28,24},{32,36},... | collective-permute-start | bytes 98312 | tf_op jit(solution)/shard_map/ppermute | solution.py:605
  32.0 3.7 %copy-start.2 = (f32[64,512]{1,0:T(8,128)S(1)}, f32[64,512]{1,0:T(8,128)}, u32[]{:S(2)}) copy-start(f32[64,512]{1,0:T(8,128)} %constant.58.clone.twiddle_ref) | copy-start | bytes 393220
  32.1 3.7 %copy-start.7 = (bf16[256,512]{1,0:T(8,128)(2,1)S(1)}, bf16[256,512]{1,0:T(8,128)(2,1)}, u32[]{:S(2)}) copy-start(bf16[256,512]{1,0:T(8,128)(2,1)} %constant.57.clone.low_ref) | copy-start | bytes 786436
  32.1 3.7 %copy-start.8 = (bf16[256,512]{1,0:T(8,128)(2,1)S(1)}, bf16[256,512]{1,0:T(8,128)(2,1)}, u32[]{:S(2)}) copy-start(bf16[256,512]{1,0:T(8,128)(2,1)} %constant.56.clone.high_ref) | copy-start | bytes 786436
  43.7 1.3 %collective-permute-start.13 = (f32[136,128]{1,0:T(8,128)S(1)}, f32[136,128]{1,0:T(8,128)S(1)}, u32[]{:S(2)}, u32[]{:S(2)}) collective-permute-start(f32[136,128]{1,0:T(8,128)S(1)} %push.1), channel_id=1, source_target_pairs={{0,1},{1,0},{2,3},{3,2},{4,5},{5,4},{6,7},{7,6},{8,9},{9,8},{10,11... | collective-permute-start | bytes 208904 | tf_op jit(solution)/shard_map/ppermute | solution.py:605
  45.0 4.4 %copy-start.3 = (f32[32,512]{1,0:T(8,128)S(1)}, f32[32,512]{1,0:T(8,128)}, u32[]{:S(2)}) copy-start(f32[32,512]{1,0:T(8,128)} %constant.60.clone.drop_ref) | copy-start | bytes 196612
  45.0 4.4 %copy-start.4 = (f32[32,512]{1,0:T(8,128)S(1)}, f32[32,512]{1,0:T(8,128)}, u32[]{:S(2)}) copy-start(f32[32,512]{1,0:T(8,128)} %constant.59.clone.lift_ref) | copy-start | bytes 196612
  45.0 4.4 %copy-start.9 = (f32[8,512]{1,0:T(8,128)S(1)}, f32[8,512]{1,0:T(8,128)}, u32[]{:S(2)}) copy-start(f32[8,512]{1,0:T(8,128)} %constant.61.clone.vectors_ref) | copy-start | bytes 49156
  45.1 4.4 %collective-permute-start.15 = (f32[136,128]{1,0:T(8,128)S(1)}, f32[136,128]{1,0:T(8,128)S(1)}, u32[]{:S(2)}, u32[]{:S(2)}) collective-permute-start(f32[136,128]{1,0:T(8,128)S(1)} %add.43.a_ref), channel_id=1, source_target_pairs={{0,2},{1,3},{2,0},{3,1},{4,6},{5,7},{6,4},{7,5},{8,10},{9,11},{10,... | collective-permute-start | bytes 208904 | tf_op jit(solution)/shard_map/ppermute | solution.py:605
  49.5 20.9 %copy-start.11 = (f32[8,128]{1,0:T(8,128)S(1)}, f32[8,128]{1,0:T(8,128)}, u32[]{:S(2)}) copy-start(f32[8,128]{1,0:T(8,128)} %constant.62.clone.rate_ref) | copy-start | bytes 12292
  49.5 20.9 %copy-start.5 = (bf16[512,256]{1,0:T(8,128)(2,1)S(1)}, bf16[512,256]{1,0:T(8,128)(2,1)}, u32[]{:S(2)}) copy-start(bf16[512,256]{1,0:T(8,128)(2,1)} %constant.64.clone.low_ref) | copy-start | bytes 786436
  49.5 20.8 %copy-start.6 = (bf16[512,256]{1,0:T(8,128)(2,1)S(1)}, bf16[512,256]{1,0:T(8,128)(2,1)}, u32[]{:S(2)}) copy-start(bf16[512,256]{1,0:T(8,128)(2,1)} %constant.63.clone.high_ref) | copy-start | bytes 786436
